TPU v7x, 32 devices: a whole 2x2x4 slice. The times are simulated.
32 devices in a mesh: particle: 8 (over y, x, core), shard: 4 (over z).
Axes of the slice: x: 2, y: 2, z: 4, core: 2. Of those that a mesh axis runs over, the one named last changes fastest.
Arguments:
- pool: bfloat16 [4096, 1024], P('shard'), may hold values from -6 to 6
- batch_index: int32 [2048], P('shard'), may hold values from 0 to 1023
- kernel_scale: int32 [1], replicated, may hold values from 4194304 to 8388607
- cotangent: bfloat16 [8, 2048, 1024], P('particle', 'shard'), may hold values from -6 to 6
- weights: float32 [8, 1024, 2, 2048], P('particle', 'shard'), may hold values from -10 to 10
- first_moment: float32 [8, 1024, 2, 2048], P('particle', 'shard'), may hold values from -2 to 2
- second_moment: float32 [8, 1024, 2, 2048], P('particle', 'shard'), may hold values from 0.01 to 1
Outputs:
- new_weights: float32 [8, 1024, 2, 2048], P('particle', 'shard')
- new_first: float32 [8, 1024, 2, 2048], P('particle', 'shard')
- new_second: float32 [8, 1024, 2, 2048], P('particle', 'shard')
- transport: float32 [8, 1024, 2, 2048], P('particle', 'shard')
Inputs may be any that keep to these rules, and one draw needn't show every extreme that they name: `batch_index`: each entry names a row of the pool block that the same index of shard holds.
All inputs are finite; a program needn't handle non-finite values.
Results may differ from a plain program's by a relative error of at most 0.015.
Values may be sent and summed in bfloat16 or wider, within the bound.
No kernel may reach another device: no remote copies, remote signals or barrier semaphores. Data moves between devices by JAX's collectives and lax.ppermute only.
A program may use at most 192 MiB of HBM per device.

v0:
```python
import jax
import jax.numpy as jnp
from jax import lax
from jax.sharding import PartitionSpec as P


def gelu_pair(up_proj):
    cdf_part = 0.5 * (1.0 + jax.scipy.special.erf(up_proj * 0.7071067811865476))
    density = jnp.exp(-0.5 * up_proj * up_proj) * 0.3989422804014327
    return (up_proj * cdf_part, cdf_part + up_proj * density)


def local(pool, batch_index, kernel_scale, cotangent, weights, first_moment, second_moment):
    shard_count = lax.axis_size("shard")
    particles = lax.axis_size("particle")
    tok_rows = batch_index.shape[0]
    model_width = pool.shape[1]
    hidden_units = weights.shape[3]
    picked = jnp.take(pool, batch_index, axis=0).astype(jnp.float32)
    normed = (picked * lax.rsqrt(jnp.mean(picked * picked, axis=1, keepdims=True) + 1e-06)).astype(
        jnp.bfloat16
    )
    upstream = cotangent[0]
    local_b = weights[0].astype(jnp.bfloat16)
    block_rows = lax.all_gather(local_b, "shard", axis=0, tiled=True)
    left_cols = normed
    right_cols = upstream
    up_part = jnp.dot(left_cols, block_rows[:, 0, :], preferred_element_type=jnp.float32)
    back_part = jnp.dot(right_cols, block_rows[:, 1, :], preferred_element_type=jnp.float32)
    up_proj = up_part * model_width ** (-0.5)
    back_proj = back_part * hidden_units ** (-0.5)
    act_full, gelu_slope = gelu_pair(up_proj)
    activation = act_full.astype(jnp.bfloat16)
    up_grad = (back_proj * gelu_slope).astype(jnp.bfloat16)
    grad_scale = 1.0 / (tok_rows * shard_count * model_width)
    contract = (((0,), (0,)), ((), ()))
    left_cols = normed
    right_cols = upstream
    g_up = lax.dot_general(left_cols, up_grad, contract, preferred_element_type=jnp.float32)
    g_down = lax.dot_general(right_cols, activation, contract, preferred_element_type=jnp.float32)
    g_up = g_up * (model_width ** (-0.5) * grad_scale)
    g_down = g_down * (hidden_units ** (-0.5) * grad_scale)
    grad_sum = lax.psum_scatter(
        jnp.stack([g_up, g_down], axis=1).astype(jnp.bfloat16),
        "shard",
        scatter_dimension=0,
        tiled=True,
    ).astype(jnp.float32)
    score_b = (-grad_sum).astype(jnp.bfloat16)
    inverse_band = 1.0 / kernel_scale[0].astype(jnp.float32)
    repulse = 2.0 * inverse_band
    own_w = lax.optimization_barrier(local_b).astype(jnp.float32)
    all_w, all_scores = (
        lax.all_gather(local_b[None], "particle", axis=0, tiled=True),
        lax.all_gather(score_b[None], "particle", axis=0, tiled=True),
    )
    all_wf = all_w.astype(jnp.float32)
    offset_sq = own_w[None] - all_wf
    partial_row = jnp.sum(offset_sq * offset_sq, axis=(1, 2, 3))
    distances = lax.psum(partial_row, "shard")
    kernel = jnp.exp(-distances * inverse_band)
    kernel_total = jnp.sum(kernel)
    pushed_field = all_scores.astype(jnp.float32) - repulse * all_wf
    term_rows = (kernel[:, None, None, None] * pushed_field).astype(jnp.bfloat16)
    weighted = jnp.sum(lax.optimization_barrier(term_rows).astype(jnp.float32), axis=0)
    params_total = 2 * model_width * hidden_units
    transport = params_total / particles * (weighted + repulse * kernel_total * own_w)
    new_first = 0.9 * first_moment[0] - 0.1 * transport
    new_second = 0.999 * second_moment[0] + 0.001 * transport * transport
    new_weights = weights[0] - 0.01 * new_first / (jnp.sqrt(new_second) + 1e-08)
    return (new_weights[None], new_first[None], new_second[None], transport[None])


def solution(mesh):
    placed = (
        P("shard", None),
        P("shard"),
        P(),
        P("particle", "shard", None),
        P("particle", "shard", None, None),
        P("particle", "shard", None, None),
        P("particle", "shard", None, None),
    )
    return jax.shard_map(
        local,
        mesh=mesh,
        in_specs=placed,
        out_specs=(
            P("particle", "shard", None, None),
            P("particle", "shard", None, None),
            P("particle", "shard", None, None),
            P("particle", "shard", None, None),
        ),
        check_vma=False,
    )
```

profile of v0, /device:TPU:23, one launch (start us, length us, event | category | flops | bytes accessed | tf_op | source)
XLA Modules:
  0.0 495.9 jit_solution(18178249712160779709)
XLA Ops:
  8.1 5.7 %bitcast_convert_fusion = bf16[256,2,2048]{2,1,0:T(2,128)(2,1)} fusion(f32[1,256,2,2048]{3,2,1,0:T(2,128)} %param.11), kind=kLoop, calls=%fused_computation.20 | loop fusion | flops 1048576 | bytes 6291456 | tf_op jit(solution)/shard_map/convert_element_type | solution.py:24
  13.8 0.2 reduce-scatter.2.cloned.1.call-start
  14.0 2.1 gather_fusion
  16.1 0.4 fusion.10
  16.6 146.2 %all-gather.7.cloned.1.call-done = bf16[1024,2,2048]{2,1,0:T(2,128)(2,1)} async-done(((bf16[256,2,2048]{2,1,0:T(2,128)(2,1)}), bf16[1024,2,2048]{2,1,0:T(2,128)(2,1)}) %all-gather.7.cloned.1.call-update) | async-done | bytes 8388624 | tf_op jit(solution)/shard_map/all_gather | solution.py:25
  162.7 17.1 %fusion.27 = (bf16[1024,1,2048]{2,1,0:T(2,128)(2,1)}, bf16[1024,1,2048]{2,1,0:T(2,128)(2,1)S(1)}) fusion(bf16[1024,2,2048]{2,1,0:T(2,128)(2,1)} %all-gather.7.cloned.1.call-done), kind=kLoop, calls=%fused_computation.51 | loop fusion | bytes 16777216 | tf_op jit(solution)/shard_map/slice | solution.py:29
  179.9 3.1 fusion.5
  183.0 4.1 fusion.9
  187.2 11.6 %fusion.8 = bf16[1024,1,2048]{2,0,1:T(8,128)(2,1)} fusion(f32[512,2048]{1,0:T(8,128)} %copy-done.9, bf16[1024,1,2048]{2,1,0:T(2,128)(2,1)} %get-tuple-element.13, bf16[1,512,1024]{2,1,0:T(8,128)(2,1)S(1)} %copy-done.8, f32[512]{0:T(512)S(1)} %add_rsqrt_fusion, bf16[512,1024]{1,0:T(8,128)(2,1)S(1)} %gather_fusion, pred[512]{0:T(512)(128)(4,1)S(1)} %compare_and_fusion), kind=kOutput, calls=%fused_computation.27 | convolution fusion | flops 4313841664 | bytes 14682624 | tf_op jit(solution)/shard_map/dot_general | solution.py:39
  198.8 7.5 %pad_maximum_fusion = bf16[1024,2,2048]{2,0,1:T(8,128)(2,1)} fusion(bf16[1024,1,2048]{2,0,1:T(8,128)(2,1)} %fusion.9, bf16[1024,1,2048]{2,0,1:T(8,128)(2,1)} %fusion.8), kind=kLoop, calls=%fused_computation.9 | loop fusion | flops 4194304 | bytes 16777216 | tf_op jit(solution)/shard_map/stack | solution.py:44
  206.3 0.3 all-gather.5.cloned.1.call-start
  206.6 5.7 %copy.58 = bf16[1,256,2,2048]{3,1,2,0:T(8,128)(2,1)} copy(f32[1,256,2,2048]{3,2,1,0:T(2,128)} %param.11) | data formatting | bytes 6291456 | tf_op args[4]
  212.4 139.4 %reduce-scatter.2.cloned.1.call-done = bf16[256,2,2048]{2,0,1:T(8,128)(2,1)} async-done(((bf16[1024,2,2048]{2,0,1:T(8,128)(2,1)}), bf16[256,2,2048]{2,0,1:T(8,128)(2,1)}) %reduce-scatter.2.cloned.1.call-update) | async-done | bytes 2097168 | tf_op jit(solution)/shard_map/reduce_scatter | solution.py:43
  351.8 3.4 negate_convert_fusion
  355.9 3.0 copy.28
  358.9 9.9 %fusion.1 = f32[8]{0:T(128)S(1)} fusion(bf16[8,256,2,2048]{3,1,2,0:T(8,128)(2,1)} %all-gather.5.cloned.1.call-done, f32[256,2,2048]{2,0,1:T(8,128)} %copy.28), kind=kLoop, calls=%fused_computation.4 | loop fusion | flops 33554424 | bytes 20971552 | tf_op jit(solution)/shard_map/reduce_sum | solution.py:59
  368.8 6.1 %psum.7 = f32[8]{0:T(128)S(1)} all-reduce(f32[8]{0:T(128)S(1)} %fusion.1), channel_id=1, replica_groups=mesh['particle'=8,'shard'=4] {'shard'}, use_global_device_ids=true, to_apply=%region_1.2 | all-reduce | flops 8 | bytes 64 | tf_op jit(solution)/shard_map/psum | solution.py:60
  374.9 0.6 fusion.26
  376.2 68.3 %all-gather.9.cloned.1.call-done = bf16[2048,2,2048]{2,0,1:T(8,128)(2,1)} async-done(((bf16[256,2,2048]{2,0,1:T(8,128)(2,1)}), bf16[2048,2,2048]{2,0,1:T(8,128)(2,1)}) %all-gather.9.cloned.1.call-update) | async-done | bytes 16777232 | tf_op jit(solution)/shard_map/all_gather | solution.py:55
  444.4 14.6 %fusion.4 = bf16[8,256,2,2048]{3,1,2,0:T(8,128)(2,1)S(1)} fusion(bf16[8,256,2,2048]{3,1,2,0:T(8,128)(2,1)} %all-gather.5.cloned.1.call-done, f32[]{:T(128)S(6)} %mul_shard_map.3, f32[8]{0:T(128)S(1)} %get-tuple-element.9, bf16[8,256,2,2048]{3,1,0,2:T(8,128)(2,1)} %bitcast.51), kind=kLoop, calls=%fused_computation.7 | loop fusion | flops 50331648 | bytes 50331684 | tf_op jit(solution)/shard_map/convert_element_type | solution.py:64
  459.1 3.3 convert_reduce_fusion
  462.5 0.7 copy-done.5
  463.1 1.2 copy-done.6
  464.3 24.1 %fusion.25 = (f32[1,256,2,2048]{3,2,1,0:T(2,128)}, f32[1,256,2,2048]{3,2,1,0:T(2,128)}, f32[1,256,2,2048]{3,2,1,0:T(2,128)}, f32[1,256,2,2048]{3,2,1,0:T(2,128)}) fusion(f32[1,256,2,2048]{3,2,1,0:T(2,128)S(1)} %copy-done.5, bf16[256,2,2048]{2,1,0:T(2,128)(2,1)S(1)} %copy-done.4, f32[]{:T(128)S(6)} %mul.182, f32[256,2,2048]{2,0,1:T(8,128)S(1)} %convert_reduce_fusion, ...), kind=kLoop, calls=%fused_computation.49 | loop fusion | flops 15728640 | bytes 35651588 | tf_op jit(solution)/shard_map/broadcast_in_dim | solution.py:71
  (29 shorter events, 0.3 us)
Async XLA Ops:
  8.0 6.0 %copy-start = (bf16[1024,1024]{1,0:T(8,128)(2,1)S(1)}, bf16[1024,1024]{1,0:T(8,128)(2,1)}, u32[]{:S(2)}) copy-start(bf16[1024,1024]{1,0:T(8,128)(2,1)} %param.7) | copy-start | bytes 6291460
  8.0 6.0 %copy-start.7 = (s32[512]{0:T(512)S(1)}, s32[512]{0:T(512)}, u32[]{:S(2)}) copy-start(s32[512]{0:T(512)} %param.8) | copy-start | bytes 6148
  8.0 154.7 %all-gather.7.cloned.1.call-start = ((), (), s32[]{:S(2)}) async-start(), calls=%async_computation.2 | async-start | bytes 10485760 | tf_op jit(solution)/shard_map/all_gather | solution.py:25
  13.8 338.0 %reduce-scatter.2.cloned.1.call-start = ((), (), s32[]{:S(2)}) async-start(), calls=%async_computation.3 | async-start | bytes 10485760 | tf_op jit(solution)/shard_map/reduce_scatter | solution.py:43
  179.9 3.1 copy-start.8
  183.0 4.1 copy-start.9
  206.3 152.6 %all-gather.5.cloned.1.call-start = ((), (), s32[]{:S(2)}) async-start(), calls=%async_computation.1 | async-start | bytes 18874368 | tf_op jit(solution)/shard_map/all_gather | solution.py:54
  212.3 143.6 %copy-start.3 = (bf16[256,2,2048]{2,1,0:T(2,128)(2,1)S(1)}, bf16[256,2,2048]{2,1,0:T(2,128)(2,1)}, u32[]{:S(2)}) copy-start(bf16[256,2,2048]{2,1,0:T(2,128)(2,1)} %bitcast_convert_fusion) | copy-start | bytes 6291460
  212.3 232.1 %all-gather.9.cloned.1.call-start = ((), (), s32[]{:S(2)}) async-start(), calls=%async_computation.4 | async-start | bytes 18874368 | tf_op jit(solution)/shard_map/all_gather | solution.py:55
  459.1 3.4 copy-start.2
  459.1 3.4 copy-start.4
  459.1 4.1 copy-start.5
  459.1 5.2 %copy-start.6 = (f32[1,256,2,2048]{3,2,1,0:T(2,128)S(1)}, f32[1,256,2,2048]{3,2,1,0:T(2,128)}, u32[]{:S(2)}) copy-start(f32[1,256,2,2048]{3,2,1,0:T(2,128)} %param.12) | copy-start | bytes 12582916
  464.3 24.1 %copy-start.1 = (bf16[1024,1024]{1,0:T(8,128)(2,1)S(1)}, bf16[1024,1024]{1,0:T(8,128)(2,1)}, u32[]{:S(2)}) copy-start(bf16[1024,1024]{1,0:T(8,128)(2,1)} %param.7) | copy-start | bytes 6291460
Sparse Core Ops, SparseCore 0:
  13.9 148.8 all-gather.6
  206.4 145.2 reduce-scatter.1
Sparse Core Ops, SparseCore 1:
  212.4 89.2 all-gather.4
  355.3 89.1 all-gather.8
where the time goes:
time: 498 us; the launch traced here: 496 us
  waiting for transfers between devices  354 us (71%)
  other arithmetic  69.6 us (14%)
  local copies, waits for them, and re-layouts  29.8 us (6%)
  matrix products  18.9 us (4%)
  between operations  17 us (3%)
  blocking collectives  6.07 us (1%)
    all_gather x1, waiting for transfers between devices, local(): block_rows = lax.all_gather(local_b, 'shard', axis=0, tiled=True)  146 us
    reduce_scatter x1, waiting for transfers between devices, local(): lax.psum_scatter(jnp.stack([g_up, g_down], axis=1).astype(jnp.bfloat16),...  139 us
    all_gather x1, waiting for transfers between devices, local(): lax.all_gather(score_b[None], 'particle', axis=0, tiled=True)  68.3 us
    broadcast_in_dim x1, other arithmetic, local(): new_second[None]  24.1 us
    slice x1, local copies, waits for them, and re-layouts, local(): block_rows[:, 1, :]  17.1 us
    convert_element_type x1, other arithmetic, local(): (kernel[:, None, None, None] * pushed_field).astype(jnp.bfloat16)  14.6 us
    dot_general x1, matrix products, local(): lax.dot_general(left_cols, up_grad, contract, preferred_element_type=jnp....  11.6 us
  transfers between devices with their start and end apart: 4, of which 3 were waited for; matrix products, arithmetic and copies ran while one was open for 5% of the time, Pallas kernels for 0%

commit v1 on v0

v1 whole, which is shorter than its diff:
```python
import functools

import jax
import jax.numpy as jnp
from jax import lax
from jax.experimental import pallas as pl
from jax.experimental.pallas import tpu as pltpu
from jax.sharding import PartitionSpec as P

BF = jnp.bfloat16
F32 = jnp.float32
AXES = ("particle", "shard")
LANES = 128
BLOCK = 256
MIB = 1024 * 1024
NT = (((1,), (1,)), ((), ()))

COL, CORE, SHARD, PROC, PIECE = range(5)


def any_spec():
    return pl.BlockSpec(memory_space=pl.ANY)


def smem_spec():
    return pl.BlockSpec(memory_space=pltpu.SMEM)


def params(mib):
    return pltpu.CompilerParams(vmem_limit_bytes=mib * MIB)


def run_copies(copies):
    for copy in copies:
        copy.start()
    for copy in copies:
        copy.wait()


def slice_index(ids, column, core, shard, columns):
    return 2 * lax.rem(column - shard + columns * 16, columns) + core


def split_kernel(shards, ids, w, *out):
    _, rows, piece = out[0].shape
    tiles = piece // LANES
    stride = 2 * shards * tiles
    for r in range(shards):
        first = lax.rem(ids[SHARD] - r + shards, shards) * tiles
        for kind in range(2):
            for j in range(tiles):
                part = w[pl.ds(2 * (first + j) + kind, rows, stride=stride), :]
                out[r][kind, :, j * LANES : (j + 1) * LANES] = part.astype(BF)


def slice_kernel(ids, w, out):
    particles, _, rows, cols = out.shape
    tiles = cols // LANES
    stride = 2 * particles * tiles
    for p in range(particles):
        first = slice_index(ids, p // 2, p % 2, ids[SHARD], particles // 2) * tiles
        for kind in range(2):
            for j in range(tiles):
                part = w[pl.ds(2 * (first + j) + kind, rows, stride=stride), :]
                out[p, kind, :, j * LANES : (j + 1) * LANES] = part.astype(BF)


def up_kernel(shards, scale, ids, tokens, *refs):
    pieces = refs[:shards]
    act_t, slope_t, down_t, normed, up_w, down_w, up_t = refs[shards:]
    width, part = up_w.shape
    rows = width // shards

    @pl.when(pl.program_id(0) == 0)
    def _():
        for r in range(shards):
            at = pl.multiple_of(lax.rem(ids[PIECE] + r, shards) * rows, rows)
            up_w[pl.ds(at, rows), :] = pieces[r][0]
            down_w[pl.ds(at, rows), :] = pieces[r][1]
        for i in range(width // LANES):
            span = slice(i * LANES, (i + 1) * LANES)
            up_t[:, span] = up_w[span, :].astype(F32).T.astype(BF)
            down_t[:, span] = down_w[span, :].astype(F32).T.astype(BF)

    block = tokens[...].reshape(normed.shape)
    normed[...] = block
    u = lax.dot_general(up_t[...], block, NT, preferred_element_type=F32) * scale
    cdf = 0.5 * (1.0 + lax.erf(u * 0.7071067811865476))
    density = jnp.exp(-0.5 * u * u) * 0.3989422804014327
    act_t[...] = (u * cdf).astype(BF)
    slope_t[...] = (cdf + u * density).astype(BF)


def grad_kernel(shards, particles, up_scale, down_scale, back_scale, pick, ids, normed, act_t, slope_t, down_t, *refs):
    n_in = len(refs) - particles - 8
    sources, out = refs[:n_in], refs[n_in : n_in + particles]
    c, n, act, slope, grad, down, score, sems = refs[n_in + particles :]
    part, tokens = act.shape
    width = c.shape[1]
    chunk = tokens // shards
    first = [
        pltpu.make_async_copy(down_t, down, sems.at[2 * shards]),
        pltpu.make_async_copy(slope_t, slope, sems.at[2 * shards + 1]),
    ]
    later = [
        pltpu.make_async_copy(act_t, act, sems.at[2 * shards + 2]),
        pltpu.make_async_copy(normed, n, sems.at[2 * shards + 3]),
    ]
    for copy in first:
        copy.start()
    pick(ids, sources, c, sems)
    for copy in later:
        copy.start()
    for copy in first:
        copy.wait()

    def back(i, carry):
        for turn in range(2):
            here = c.at[pl.ds(0, chunk // 2), :]
            pltpu.make_async_copy(here, here, sems.at[2 * i + turn]).wait()
        at = pl.multiple_of(i * chunk, chunk)
        b = lax.dot_general(down[...], c[pl.ds(at, chunk), :], NT, preferred_element_type=F32)
        grad[:, pl.ds(at, chunk)] = (b * (slope[:, pl.ds(at, chunk)].astype(F32) * back_scale)).astype(BF)
        return carry

    lax.fori_loop(0, shards, back, 0)
    for copy in later:
        copy.wait()

    def gradient(j, carry):
        at = pl.multiple_of(j * BLOCK, BLOCK)
        g = jnp.dot(grad[...], n[:, pl.ds(at, BLOCK)], preferred_element_type=F32)
        score[0, pl.ds(at, BLOCK), :] = (g * up_scale).T.astype(BF)
        g = jnp.dot(act[...], c[:, pl.ds(at, BLOCK)], preferred_element_type=F32)
        score[1, pl.ds(at, BLOCK), :] = (g * down_scale).T.astype(BF)
        return carry

    lax.fori_loop(0, width // BLOCK, gradient, 0)
    rows = width // shards
    ratio = particles // shards
    cols = part // ratio
    mine = 2 * ids[COL] + ids[PROC]
    copies = []
    for t in range(particles):
        u = lax.rem(mine + ratio * ids[PIECE] - t + particles, particles)
        row = pl.multiple_of(lax.div(u, ratio) * rows, rows)
        col = pl.multiple_of(lax.rem(u, ratio) * cols, cols)
        copies.append(pltpu.make_async_copy(score.at[:, pl.ds(row, rows), pl.ds(col, cols)], out[t], sems.at[t]))
    run_copies(copies)


def distance_kernel(whole, out):
    particles, _, rows, cols = whole.shape
    pairs = [(i, j) for i in range(particles) for j in range(i)]
    tiles = cols // LANES

    def body(g, acc):
        kind = lax.div(g, rows // 16)
        row = pl.multiple_of(lax.rem(g, rows // 16) * 16, 16)
        for tile in range(tiles):
            w = [whole[p, kind, pl.ds(row, 16), tile * LANES : (tile + 1) * LANES].astype(F32) for p in range(particles)]
            new = []
            for a, (i, j) in zip(acc, pairs):
                d = w[i] - w[j]
                d = d * d
                new.append(a + (d[:8] + d[8:]))
            acc = tuple(new)
        return acc

    acc = lax.fori_loop(0, 2 * rows // 16, body, tuple(jnp.zeros((8, LANES), F32) for _ in pairs))
    for i, a in enumerate(acc):
        out[i] = a


def stein_kernel(shards, particles, ids, coef, whole, *refs):
    sources, out = refs[:particles], refs[particles : 2 * particles]
    scores, field, sems = refs[2 * particles :]
    columns = particles // 2
    ratio = particles // shards
    _, _, rows, cols = whole.shape
    e = slice_index(ids, ids[COL], ids[CORE], ids[SHARD], columns)
    u = ids[SHARD] * ratio + lax.rem(e, ratio) + particles * shards - ratio * lax.div(e, ratio)
    run_copies(
        [pltpu.make_async_copy(sources[t], scores.at[lax.rem(u + t, particles)], sems.at[t]) for t in range(particles)]
    )
    repulse = coef[particles * particles + particles]
    groups = rows // 16
    tiles = cols // LANES

    def body(g, carry):
        kind = lax.div(g, groups)
        row = pl.multiple_of(lax.rem(g, groups) * 16, 16)
        for tile in range(tiles):
            at = (kind, pl.ds(row, 16), slice(tile * LANES, (tile + 1) * LANES))
            w = [whole[(p,) + at].astype(F32) for p in range(particles)]
            pushed = [scores[(p,) + at].astype(F32) - repulse * w[p] for p in range(particles)]
            for i in range(particles):
                total = coef[particles * particles + i] * w[i]
                for j in range(particles):
                    total = total + coef[i * particles + j] * pushed[j]
                field[(i,) + at] = total.astype(BF)
        return carry

    lax.fori_loop(0, 2 * groups, body, 0)
    copies = []
    for k in range(columns):
        for x in range(2):
            column = lax.rem(ids[COL] + k, columns)
            core = ids[CORE] if x == 0 else 1 - ids[CORE]
            i = 2 * k + x
            copies.append(pltpu.make_async_copy(field.at[2 * column + core], out[i], sems.at[i]))
    run_copies(copies)


def adam_kernel(particles, ids, w, first, second, *refs):
    sources = refs[:particles]
    new_w, new_first, new_second, transport, field, sems = refs[particles:]
    columns = particles // 2
    _, _, hidden = field.shape
    width = hidden // particles
    step = pl.program_id(0)

    @pl.when(step == 0)
    def _():
        copies = []
        for k in range(columns):
            for x in range(2):
                column = lax.rem(ids[COL] - k + columns, columns)
                core = ids[CORE] if x == 0 else 1 - ids[CORE]
                at = pl.multiple_of(slice_index(ids, column, core, ids[SHARD], columns) * width, width)
                i = 2 * k + x
                copies.append(pltpu.make_async_copy(sources[i], field.at[:, :, pl.ds(at, width)], sems.at[i]))
        run_copies(copies)

    lane_tiles = hidden // LANES
    rows = w.shape[0] // (2 * lane_tiles)
    base = pl.multiple_of(step * rows, rows)
    for kind in range(2):
        for tile in range(lane_tiles):
            part = field[kind, pl.ds(base, rows), tile * LANES : (tile + 1) * LANES]
            transport[pl.ds(2 * tile + kind, rows, stride=2 * lane_tiles), :] = part.astype(F32)
    t = transport[...]
    m = 0.9 * first[...] - 0.1 * t
    v = 0.999 * second[...] + 0.001 * t * t
    new_first[...] = m
    new_second[...] = v
    new_w[...] = w[...] - 0.01 * m / (jnp.sqrt(v) + 1e-08)


def local(pool, batch_index, kernel_scale, cotangent, weights, first_moment, second_moment):
    shards = lax.axis_size("shard")
    particles = lax.axis_size("particle")
    columns, half = particles // 2, shards // 2
    tok_rows = batch_index.shape[0]
    width = pool.shape[1]
    _, rows, _, hidden = weights.shape
    part, cols = hidden // shards, hidden // particles
    tokens = tok_rows * shards
    blocks = tokens // BLOCK
    lane_tiles = hidden // LANES

    own = lax.axis_index("particle")
    shard = lax.axis_index("shard")
    core, column = own % 2, own // 2
    proc = shard // half
    piece = 2 * (shard % half) + core
    ids = jnp.stack([column, core, shard, proc, piece]).astype(jnp.int32)
    devices = [(m, c, s) for m in range(columns) for c in range(2) for s in range(shards)]

    def dev(m, c, s):
        return (2 * (m % columns) + c) * shards + s

    def move(x, pairs):
        if all(a == b for a, b in pairs) and len(pairs) == len(devices):
            return x
        return lax.ppermute(x, AXES, pairs)

    def swap_of(among):
        return [(dev(m, c, s), dev(m, 1 - c, s)) for m, c, s in devices if s in among]

    def flat(x):
        return x[0].reshape(rows, 2, lane_tiles, LANES).transpose(0, 2, 1, 3).reshape(-1, LANES)

    def unflat(x):
        return x.reshape(rows, lane_tiles, 2, LANES).transpose(0, 2, 1, 3).reshape(1, rows, 2, hidden)

    everyone = range(shards)
    half_rows = tok_rows // 2
    if shards == 4:
        mine = lax.dynamic_slice(cotangent[0], (core * half_rows, 0), (half_rows, width))
        give = lax.dynamic_slice(cotangent[0], ((1 - core) * half_rows, 0), (half_rows, width))
        other = move(give, swap_of(everyone))
        is_own = core == proc
        here = jnp.where(is_own, mine, other)
        away = jnp.where(is_own, other, mine)

    share = tok_rows // particles
    index = lax.dynamic_slice(batch_index, (own * share,), (share,))
    picked = jnp.take(pool, index, axis=0).astype(F32)
    normed = (picked * lax.rsqrt(jnp.mean(picked * picked, axis=1, keepdims=True) + 1e-06)).astype(BF)
    normed = lax.all_to_all(jnp.broadcast_to(normed[None], (shards, share, width)), "shard", 0, 0, tiled=True)
    normed = lax.all_gather(normed[None], "particle", axis=0, tiled=True)

    w_flat = flat(weights)
    steps = max(rows // 64, 1)
    lines = w_flat.shape[0] // steps
    w_spec = pl.BlockSpec((lines, LANES), lambda i: (i, 0))
    prepared = pl.pallas_call(
        functools.partial(split_kernel, shards),
        grid=(steps,),
        out_shape=[jax.ShapeDtypeStruct((2, rows, part), BF)] * shards,
        in_specs=[smem_spec(), w_spec],
        out_specs=[pl.BlockSpec((2, rows // steps, part), lambda i: (0, i, 0))] * shards,
        compiler_params=params(8),
        name="split",
    )(ids, w_flat)

    if shards == 4:
        here, away, w_late, *prepared = lax.optimization_barrier((here, away, w_flat, *prepared))
    else:
        w_late, *prepared = lax.optimization_barrier((w_flat, *prepared))
    w_routes = []
    for r in range(shards):
        pairs = []
        for m, c, s in devices:
            q = (s - r) % shards
            pairs.append((dev(m, c, s), dev(m, q % 2, c * half + q // 2)))
        w_routes.append(pairs)

    if shards == 4:
        inner, edge = (1, 2), (0, 3)
        far = [(dev(m, c, s), dev(m, c, 1 if s == 3 else 2)) for m, c, s in devices if s in edge]
        near = [(dev(m, c, s), dev(m, c, 3 - s)) for m, c, s in devices if s in inner]
        outward = [(dev(m, c, s), dev(m, c, s ^ 1)) for m, c, s in devices if s in inner]
        pair_c = move(here, [(dev(m, c, s), dev(m, c, s ^ 1)) for m, c, s in devices])
        near_c, far_c = move(away, near), move(away, far)
        w_pieces = [move(x, route) for x, route in zip(prepared[:2], w_routes[:2])]
        near_c, far_c, pair_c, w_pieces[0], w_pieces[1], prepared[2], prepared[3] = lax.optimization_barrier(
            (near_c, far_c, pair_c, *w_pieces, *prepared[2:])
        )
        w_pieces += [move(x, route) for x, route in zip(prepared[2:], w_routes[2:])]
        cross = jnp.concatenate([near_c, far_c])
        cross = jnp.where(jnp.logical_or(shard == 1, shard == 2), cross, move(cross, outward))
        got = jnp.concatenate([here, pair_c])
        sources = [got, cross, move(got, swap_of(everyone)), move(cross, swap_of(everyone))]

        def pick(ids, refs, held, sems):
            s, core = ids[SHARD], ids[CORE]
            low = s < 2
            place = [s, s + 1 - 2 * lax.rem(s, 2), jnp.where(low, 2, 1), jnp.where(low, 3, 0)]
            for i, ref in enumerate(refs):
                turn = core if i < 2 else 1 - core
                for k in range(2):
                    at = 2 * place[2 * (i % 2) + k] + turn
                    to = pl.multiple_of(at * half_rows, half_rows)
                    pltpu.make_async_copy(
                        ref.at[pl.ds(k * half_rows, half_rows), :], held.at[pl.ds(to, half_rows), :], sems.at[at]
                    ).start()
    else:
        full = lax.all_gather(cotangent[0], "shard", axis=0, tiled=True)
        sources = [jnp.where(core == proc, full, move(full, swap_of(everyone)))]
        w_pieces = [move(x, route) for x, route in zip(prepared, w_routes)]

        def pick(ids, refs, held, sems):
            for i in range(2 * shards):
                span = pl.ds(i * half_rows, half_rows)
                pltpu.make_async_copy(refs[0].at[span, :], held.at[span, :], sems.at[i]).start()

    slices = pl.pallas_call(
        slice_kernel,
        grid=(steps,),
        out_shape=jax.ShapeDtypeStruct((particles, 2, rows, cols), BF),
        in_specs=[smem_spec(), w_spec],
        out_specs=pl.BlockSpec((particles, 2, rows // steps, cols), lambda i: (0, 0, i, 0)),
        compiler_params=params(8),
        name="slices",
    )(ids, w_late)
    whole = lax.all_to_all(slices, "particle", 0, 0, tiled=True)
    per = BLOCK // share
    halves = tok_rows // BLOCK
    act_t, slope_t, down_t, normed = pl.pallas_call(
        functools.partial(up_kernel, shards, width ** (-0.5)),
        grid=(blocks,),
        out_shape=[
            jax.ShapeDtypeStruct((part, tokens), BF),
            jax.ShapeDtypeStruct((part, tokens), BF),
            jax.ShapeDtypeStruct((part, width), BF),
            jax.ShapeDtypeStruct((tokens, width), BF),
        ],
        in_specs=[smem_spec(), pl.BlockSpec((per, 1, share, width), lambda i: (i % halves, i // halves, 0, 0))]
        + [pl.BlockSpec((2, rows, part), lambda i: (0, 0, 0))] * shards,
        out_specs=[
            pl.BlockSpec((part, BLOCK), lambda i: (0, i)),
            pl.BlockSpec((part, BLOCK), lambda i: (0, i)),
            pl.BlockSpec((part, width), lambda i: (0, 0)),
            pl.BlockSpec((BLOCK, width), lambda i: (i, 0)),
        ],
        scratch_shapes=[pltpu.VMEM((width, part), BF), pltpu.VMEM((width, part), BF), pltpu.VMEM((part, width), BF)],
        compiler_params=params(24),
        name="up",
    )(ids, normed, *w_pieces)

    grad_scale = 1.0 / (tokens * width)
    held = 2 * (2 * tokens * width + 3 * tokens * part + 3 * width * part)
    scores = pl.pallas_call(
        functools.partial(
            grad_kernel,
            shards,
            particles,
            -(width ** (-0.5)) * grad_scale,
            -(hidden ** (-0.5)) * grad_scale,
            hidden ** (-0.5),
            pick,
        ),
        out_shape=[jax.ShapeDtypeStruct((2, rows, cols), BF)] * particles,
        in_specs=[smem_spec()] + [any_spec()] * (4 + len(sources)),
        out_specs=[any_spec()] * particles,
        scratch_shapes=[
            pltpu.VMEM((tokens, width), BF),
            pltpu.VMEM((tokens, width), BF),
            pltpu.VMEM((part, tokens), BF),
            pltpu.VMEM((part, tokens), BF),
            pltpu.VMEM((part, tokens), BF),
            pltpu.VMEM((part, width), BF),
            pltpu.VMEM((2, width, part), BF),
            pltpu.SemaphoreType.DMA((2 * shards + 4,)),
        ],
        compiler_params=params(held // MIB + 8),
        name="grads",
    )(ids, normed, act_t, slope_t, down_t, *sources)

    whole, *scores = lax.optimization_barrier((whole, *scores))
    pair_list = [(i, j) for i in range(particles) for j in range(i)]
    partial = pl.pallas_call(
        distance_kernel,
        out_shape=jax.ShapeDtypeStruct((len(pair_list), 8, LANES), F32),
        in_specs=[pl.BlockSpec(memory_space=pltpu.VMEM)],
        out_specs=pl.BlockSpec(memory_space=pltpu.VMEM),
        compiler_params=params(8),
        name="distances",
    )(whole)
    sums = jnp.sum(partial, axis=(1, 2))
    sums = jnp.pad(sums, (0, -len(pair_list) % LANES))
    for axis, count in (("particle", particles), ("shard", shards)):
        copies = jnp.broadcast_to(sums[None, None], (count, 1, sums.shape[0]))
        sums = jnp.sum(lax.all_to_all(copies, axis, 0, 0, tiled=True), axis=(0, 1))
    lookup = [
        [pair_list.index((max(i, j), min(i, j))) if i != j else len(pair_list) for j in range(particles)]
        for i in range(particles)
    ]
    table = jnp.concatenate([sums[: len(pair_list)], jnp.zeros((1,), F32)])
    distances = table[jnp.array(lookup, jnp.int32)]
    inverse_band = 1.0 / kernel_scale[0].astype(F32)
    repulse = 2.0 * inverse_band
    kernel = jnp.exp(-distances * inverse_band)
    scale = 2 * width * hidden / particles
    coef = jnp.concatenate(
        [(scale * kernel).reshape(-1), scale * repulse * jnp.sum(kernel, axis=1), repulse[None]]
    )

    ratio = particles // shards
    arrived = []
    for t in range(particles):
        pairs = []
        for m, c, s in devices:
            mine, q = 2 * m + s // half, 2 * (s % half) + c
            u = (mine + ratio * q - t) % particles
            z, e = u // ratio, q * ratio + u % ratio
            pairs.append((dev(m, c, s), dev(e // 2 + z, e % 2, z)))
        arrived.append(move(scores[t], pairs))

    fields = pl.pallas_call(
        functools.partial(stein_kernel, shards, particles),
        out_shape=[jax.ShapeDtypeStruct((2, rows, cols), BF)] * particles,
        in_specs=[smem_spec(), smem_spec(), pl.BlockSpec(memory_space=pltpu.VMEM)] + [any_spec()] * particles,
        out_specs=[any_spec()] * particles,
        scratch_shapes=[
            pltpu.VMEM((particles, 2, rows, cols), BF),
            pltpu.VMEM((particles, 2, rows, cols), BF),
            pltpu.SemaphoreType.DMA((particles,)),
        ],
        compiler_params=params(12),
        name="stein",
    )(ids, coef, whole, *arrived)

    back = []
    for k in range(columns):
        for x in range(2):
            pairs = [(dev(m, c, s), dev(m + k, c ^ x, s)) for m, c, s in devices]
            back.append(move(fields[2 * k + x], pairs))

    steps = max(rows // 32, 1)
    flat_rows = rows * 2 * lane_tiles
    state_spec = pl.BlockSpec((flat_rows // steps, LANES), lambda i: (i, 0))
    outs = pl.pallas_call(
        functools.partial(adam_kernel, particles),
        grid=(steps,),
        out_shape=[jax.ShapeDtypeStruct((flat_rows, LANES), F32)] * 4,
        in_specs=[smem_spec()] + [state_spec] * 3 + [any_spec()] * particles,
        out_specs=[state_spec] * 4,
        scratch_shapes=[pltpu.VMEM((2, rows, hidden), BF), pltpu.SemaphoreType.DMA((particles,))],
        compiler_params=params(16),
        name="adam",
    )(ids, w_flat, flat(first_moment), flat(second_moment), *back)
    return tuple(unflat(x) for x in outs)


def solution(mesh):
    state = P("particle", "shard", None, None)
    return jax.shard_map(
        local,
        mesh=mesh,
        in_specs=(P("shard", None), P("shard"), P(), P("particle", "shard", None), state, state, state),
        out_specs=(state, state, state, state),
        check_vma=False,
    )
```

time: 498 us -> 298 us (0.60)
  waiting for transfers between devices: 354 us -> 91.5 us
  starting transfers between devices: 0.57 us -> 84 us
  other arithmetic: 69.6 us -> 5.5 us
  Pallas kernels: 0 us -> 43.5 us
  blocking collectives: 6.07 us -> 30.3 us
  matrix products: 18.9 us -> 0 us
    all_gather x3 -> x1, waiting for transfers between devices: 215 us -> 0.01 us  [local(): normed = lax.all_gather(normed[None], 'particle', axis=0, tiled=True)]
    reduce_scatter x1 -> x0, waiting for transfers between devices: 139 us -> none  [local(): lax.psum_scatter(jnp.stack([g_up, g_down], axis=1).astype(jnp.bfloat16),...]
    ppermute x0 -> x26, waiting for transfers between devices: none -> 91.5 us  [move(): return lax.ppermute(x, AXES, pairs)]
    ppermute x0 -> x26, starting transfers between devices: none -> 73.8 us  [move(): return lax.ppermute(x, AXES, pairs)]
    pallas_call x0 -> x7, Pallas kernels: none -> 43.5 us  [the longest x1 12.2 us: local(): pl.pallas_call(functools.partial(grad_kernel, shards, particles, -width *...]
    all_to_all x0 -> x2, blocking collectives: none -> 30.3 us  [the longest x1 16.1 us: local(): lax.all_to_all(jnp.broadcast_to(normed[None], (shards, share, width)), 's...]
    broadcast_in_dim x1 -> x0, other arithmetic: 24.1 us -> none  [local(): new_second[None]]
    convert_element_type x3 -> x1, other arithmetic: 23.7 us -> 0.11 us  [local(): (picked * lax.rsqrt(jnp.mean(picked * picked, axis=1, keepdims=True) + 1e...]
  transfers between devices with their start and end apart: 4 -> 29, of which waited for: 3 -> 13; matrix products, arithmetic and copies ran while one was open for 5% -> 3% of each run, Pallas kernels for 0% -> 9%
where the time goes in v1:
time: 298 us; the launch traced here: 297 us
  waiting for transfers between devices  91.5 us (31%)
  starting transfers between devices  84 us (28%)
  Pallas kernels  43.5 us (15%)
  blocking collectives  30.3 us (10%)
  local copies, waits for them, and re-layouts  26.7 us (9%)
  between operations  15.1 us (5%)
  other arithmetic  5.5 us (2%)
    ppermute x26, waiting for transfers between devices, move(): return lax.ppermute(x, AXES, pairs)  91.5 us
    ppermute x26, starting transfers between devices, move(): return lax.ppermute(x, AXES, pairs)  73.8 us
    unnamed x56, local copies, waits for them, and re-layouts  21.6 us
    all_to_all x1, blocking collectives, local(): lax.all_to_all(jnp.broadcast_to(normed[None], (shards, share, width)), 's...  16.1 us
    all_to_all x1, blocking collectives, local(): sums = jnp.sum(lax.all_to_all(copies, axis, 0, 0, tiled=True), axis=(0, 1))  14.2 us
    pallas_call x1, Pallas kernels, local(): pl.pallas_call(functools.partial(grad_kernel, shards, particles, -width *...  12.2 us
    pallas_call x1, Pallas kernels, local(): pl.pallas_call(functools.partial(adam_kernel, particles), grid=(steps,),...  10.1 us
    pallas_call x1, Pallas kernels, local(): pl.pallas_call(functools.partial(up_kernel, shards, width ** (-0.5)), gri...  7.55 us
  transfers between devices with their start and end apart: 29, of which 13 were waited for; matrix products, arithmetic and copies ran while one was open for 3% of the time, Pallas kernels for 9%

profile of v1, /device:TPU:23, one launch (start us, length us, event | category | flops | bytes accessed | tf_op | source)
XLA Modules:
  0.0 296.6 jit_solution(11448912367044171740)
XLA Ops:
  9.9 16.1 %all_to_all.20 = bf16[4,64,1024]{2,1,0:T(8,128)(2,1)} all-to-all(bf16[4,64,1024]{2,1,0:T(8,128)(2,1)S(1)} %broadcast_in_dim.43), channel_id=1, replica_groups=mesh['particle'=8,'shard'=4] {'shard'}, dimensions={0} | all-to-all | bytes 1048576 | tf_op jit(solution)/shard_map/all_to_all | solution.py:301
  45.3 17.1 %collective-permute-done.1 = bf16[256,1024]{1,0:T(8,128)(2,1)S(1)} collective-permute-done((bf16[256,1024]{1,0:T(8,128)(2,1)S(1)}, bf16[256,1024]{1,0:T(8,128)(2,1)S(1)}, u32[]{:S(2)}, u32[]{:S(2)}) %collective-permute-start.1) | collective-permute-done | bytes 524320 | tf_op jit(solution)/shard_map/ppermute | solution.py:276
  65.2 5.4 %collective-permute-done.4.refs_0_ = bf16[2,256,512]{2,1,0:T(8,128)(2,1)S(1)} collective-permute-done((bf16[2,256,512]{2,1,0:T(8,128)(2,1)S(1)}, bf16[2,256,512]{2,1,0:T(8,128)(2,1)S(1)}, u32[]{:S(2)}, u32[]{:S(2)}) %collective-permute-start.4) | collective-permute-done | bytes 524320 | tf_op jit(solution)/shard_map/ppermute | solution.py:276
  71.6 16.8 %collective-permute-start.8 = (bf16[512,1024]{1,0:T(8,128)(2,1)S(1)}, bf16[512,1024]{1,0:T(8,128)(2,1)}, u32[]{:S(2)}, u32[]{:S(2)}) collective-permute-start(bf16[512,1024]{1,0:T(8,128)(2,1)S(1)} %constant_dynamic-update-slice_fusion.2), channel_id=1, source_target_pairs={{1,0},{2,3},{5,4},{6,7},{9,8},{10,11},{13,12},{14,15},{17,16},{18,... | collective-permute-start | bytes 3145736 | tf_op jit(solution)/shard_map/ppermute | solution.py:276
  88.4 3.3 %slices.1 = bf16[8,2,256,256]{3,2,1,0:T(8,128)(2,1)S(1)} custom-call(s32[5]{0:T(128)S(1)} %stack.23.ids, f32[8192,128]{1,0:T(8,128)S(1)} %bitcast.52), custom_call_target="tpu_custom_call" | custom-call | tf_op jit(solution)/shard_map/slices/pallas_call | solution.py:369
  93.0 4.2 %all-to-all-start = ((bf16[8,2,256,256]{3,2,1,0:T(8,128)(2,1)}), bf16[8,2,256,256]{3,2,1,0:T(8,128)(2,1)S(1)}, u32[]{:S(2)}, u32[]{:S(2)}) async-start(bf16[8,2,256,256]{3,2,1,0:T(8,128)(2,1)} %copy-done.5), calls=%async_computation | async-start | bytes 4194304 | tf_op jit(solution)/shard_map/all_to_all | solution.py:378
  101.3 8.6 %collective-permute-done.8 = bf16[512,1024]{1,0:T(8,128)(2,1)} collective-permute-done((bf16[512,1024]{1,0:T(8,128)(2,1)S(1)}, bf16[512,1024]{1,0:T(8,128)(2,1)}, u32[]{:S(2)}, u32[]{:S(2)}) %collective-permute-start.8) | collective-permute-done | bytes 1048608 | tf_op jit(solution)/shard_map/ppermute | solution.py:276
  112.2 4.1 %collective-permute-start.7 = (bf16[2,256,512]{2,1,0:T(8,128)(2,1)}, bf16[2,256,512]{2,1,0:T(8,128)(2,1)S(1)}, u32[]{:S(2)}, u32[]{:S(2)}) collective-permute-start(bf16[2,256,512]{2,1,0:T(8,128)(2,1)} %copy-done.17), channel_id=1, source_target_pairs={{0,4},{1,1},{2,5},{3,0},{4,6},{5,3},{6,7},{7,2},{8,12},{9,9},{10,1... | collective-permute-start | bytes 1572872 | tf_op jit(solution)/shard_map/ppermute | solution.py:276
  116.3 10.2 %collective-permute-done.6.refs_2_ = bf16[2,256,512]{2,1,0:T(8,128)(2,1)S(1)} collective-permute-done((bf16[2,256,512]{2,1,0:T(8,128)(2,1)}, bf16[2,256,512]{2,1,0:T(8,128)(2,1)S(1)}, u32[]{:S(2)}, u32[]{:S(2)}) %collective-permute-start.6) | collective-permute-done | bytes 524320 | tf_op jit(solution)/shard_map/ppermute | solution.py:276
  137.0 7.5 %up.1 = (bf16[512,2048]{1,0:T(8,128)(2,1)S(1)}, bf16[512,2048]{1,0:T(8,128)(2,1)S(1)}, bf16[512,1024]{1,0:T(8,128)(2,1)S(1)}, bf16[2048,1024]{1,0:T(8,128)(2,1)S(1)}) custom-call(s32[5]{0:T(128)S(1)} %stack.23.ids, bf16[8,4,64,1024]{3,2,1,0:T(8,128)(2,1)S(1)} %bitcast.56, bf16[2,256,512]{2,1,0:T(8,128)(2,1)S(1)} %copy-done.10, ...), custom_call_target="tpu_custom_call" | custom-call | tf_op jit(solution)/shard_map/up/pallas_call | solution.py:381
  144.6 12.2 %grads.1 = (bf16[2,256,256]{2,1,0:T(8,128)(2,1)}, bf16[2,256,256]{2,1,0:T(8,128)(2,1)}, bf16[2,256,256]{2,1,0:T(8,128)(2,1)}, bf16[2,256,256]{2,1,0:T(8,128)(2,1...) custom-call(s32[5]{0:T(128)S(1)} %stack.23.ids, ...), custom_call_target="tpu_custom_call" | custom-call | tf_op jit(solution)/shard_map/grads/pallas_call | solution.py:405
  161.9 14.2 %all_to_all.21 = f32[8,1,128]{2,1,0:T(1,128)S(1)} all-to-all(f32[8,1,128]{2,1,0:T(1,128)S(1)} %broadcast_in_dim.45), channel_id=1, replica_groups=mesh['particle'=8,'shard'=4] {'particle'}, dimensions={0} | all-to-all | bytes 8192 | tf_op jit(solution)/shard_map/all_to_all | solution.py:446
  176.7 6.0 %all-to-all-start.3 = ((f32[4,1,128]{2,1,0:T(1,128)}), f32[4,1,128]{2,1,0:T(1,128)S(1)}, u32[]{:S(2)}, u32[]{:S(2)}) async-start(f32[4,1,128]{2,1,0:T(1,128)} %broadcast_in_dim.46), calls=%async_computation.3 | async-start | bytes 4096 | tf_op jit(solution)/shard_map/all_to_all | solution.py:446
  186.3 4.8 %collective-permute-start.12 = (bf16[2,256,256]{2,1,0:T(8,128)(2,1)}, bf16[2,256,256]{2,1,0:T(8,128)(2,1)S(1)}, u32[]{:S(2)}, u32[]{:S(2)}) collective-permute-start(bf16[2,256,256]{2,1,0:T(8,128)(2,1)} %get-tuple-element.87), channel_id=1, source_target_pairs={{0,31},{1,29},{2,0},{3,2},{4,12},{5,14},{6,17},{7,19},{8,4},{9,6},... | collective-permute-start | bytes 786440 | tf_op jit(solution)/shard_map/ppermute | solution.py:276
  191.8 6.3 %collective-permute-start.14 = (bf16[2,256,256]{2,1,0:T(8,128)(2,1)}, bf16[2,256,256]{2,1,0:T(8,128)(2,1)S(1)}, u32[]{:S(2)}, u32[]{:S(2)}) collective-permute-start(bf16[2,256,256]{2,1,0:T(8,128)(2,1)} %get-tuple-element.89), channel_id=1, source_target_pairs={{0,22},{1,20},{2,27},{3,25},{4,7},{5,5},{6,8},{7,10},{8,31},{9,29}... | collective-permute-start | bytes 786440 | tf_op jit(solution)/shard_map/ppermute | solution.py:276
  207.2 8.3 %collective-permute-start.18 = (bf16[2,256,256]{2,1,0:T(8,128)(2,1)}, bf16[2,256,256]{2,1,0:T(8,128)(2,1)S(1)}, u32[]{:S(2)}, u32[]{:S(2)}) collective-permute-start(bf16[2,256,256]{2,1,0:T(8,128)(2,1)} %copy-done.19), channel_id=1, source_target_pairs={{0,4},{1,6},{2,9},{3,11},{4,21},{5,23},{6,26},{7,24},{8,13},{9,15}... | collective-permute-start | bytes 786440 | tf_op jit(solution)/shard_map/ppermute | solution.py:276
  215.7 6.3 %collective-permute-done.17.refs_6_ = bf16[2,256,256]{2,1,0:T(8,128)(2,1)S(1)} collective-permute-done((bf16[2,256,256]{2,1,0:T(8,128)(2,1)}, bf16[2,256,256]{2,1,0:T(8,128)(2,1)S(1)}, u32[]{:S(2)}, u32[]{:S(2)}) %collective-permute-start.17) | collective-permute-done | bytes 262176 | tf_op jit(solution)/shard_map/ppermute | solution.py:276
  222.1 14.5 %collective-permute-done.18.refs_7_ = bf16[2,256,256]{2,1,0:T(8,128)(2,1)S(1)} collective-permute-done((bf16[2,256,256]{2,1,0:T(8,128)(2,1)}, bf16[2,256,256]{2,1,0:T(8,128)(2,1)S(1)}, u32[]{:S(2)}, u32[]{:S(2)}) %collective-permute-start.18) | collective-permute-done | bytes 262176 | tf_op jit(solution)/shard_map/ppermute | solution.py:276
  236.6 5.0 %stein.1 = (bf16[2,256,256]{2,1,0:T(8,128)(2,1)S(1)}, bf16[2,256,256]{2,1,0:T(8,128)(2,1)S(1)}, bf16[2,256,256]{2,1,0:T(8,128)(2,1)S(1)}, bf16[2,256,256]{2,1,0:...) custom-call(s32[5]{0:T(128)S(1)} %stack.23.ids, ...), custom_call_target="tpu_custom_call" | custom-call | tf_op jit(solution)/shard_map/stein/pallas_call | solution.py:472
  244.7 5.4 %collective-permute-start.21 = (bf16[2,256,256]{2,1,0:T(8,128)(2,1)S(1)}, bf16[2,256,256]{2,1,0:T(8,128)(2,1)S(1)}, u32[]{:S(2)}, u32[]{:S(2)}) collective-permute-start(bf16[2,256,256]{2,1,0:T(8,128)(2,1)S(1)} %get-tuple-element.97), channel_id=1, source_target_pairs={{0,12},{1,13},{2,14},{3,15},{4,8},{5,9},{6,10},{7,11},{8,20},{9,21... | collective-permute-start | bytes 786440 | tf_op jit(solution)/shard_map/ppermute | solution.py:276
  252.0 5.4 %collective-permute-start.25 = (bf16[2,256,256]{2,1,0:T(8,128)(2,1)S(1)}, bf16[2,256,256]{2,1,0:T(8,128)(2,1)S(1)}, u32[]{:S(2)}, u32[]{:S(2)}) collective-permute-start(bf16[2,256,256]{2,1,0:T(8,128)(2,1)S(1)} %get-tuple-element.101), channel_id=1, source_target_pairs={{0,28},{1,29},{2,30},{3,31},{4,24},{5,25},{6,26},{7,27},{8,4},{9,5... | collective-permute-start | bytes 786440 | tf_op jit(solution)/shard_map/ppermute | solution.py:276
  257.4 9.8 %collective-permute-done.22.refs_4_ = bf16[2,256,256]{2,1,0:T(8,128)(2,1)S(1)} collective-permute-done((bf16[2,256,256]{2,1,0:T(8,128)(2,1)S(1)}, bf16[2,256,256]{2,1,0:T(8,128)(2,1)S(1)}, u32[]{:S(2)}, u32[]{:S(2)}) %collective-permute-start.22) | collective-permute-done | bytes 262176 | tf_op jit(solution)/shard_map/ppermute | solution.py:276
  267.2 7.9 %collective-permute-done.23.refs_5_ = bf16[2,256,256]{2,1,0:T(8,128)(2,1)S(1)} collective-permute-done((bf16[2,256,256]{2,1,0:T(8,128)(2,1)S(1)}, bf16[2,256,256]{2,1,0:T(8,128)(2,1)S(1)}, u32[]{:S(2)}, u32[]{:S(2)}) %collective-permute-start.23) | collective-permute-done | bytes 262176 | tf_op jit(solution)/shard_map/ppermute | solution.py:276
  279.6 10.1 %adam.1 = (f32[8192,128]{1,0:T(8,128)}, f32[8192,128]{1,0:T(8,128)}, f32[8192,128]{1,0:T(8,128)}, f32[8192,128]{1,0:T(8,128)}) custom-call(s32[5]{0:T(128)S(1)} %stack.23.ids, f32[8192,128]{1,0:T(8,128)S(1)} %bitcast.53, f32[8192,128]{1,0:T(8,128)S(1)} %bitcast.54, f32[8192,128]{1,0:T(8,128)S(1)} %bitcast.55, ...), custom_call_target="tpu_custom_call" | custom-call | tf_op jit(solution)/shard_map/adam/pallas_call | solution.py:495
  (127 shorter events, 71.7 us)
Async XLA Ops:
  7.2 123.5 %all-gather.3.cloned.1.call-start = ((), (), s32[]{:S(2)}) async-start(), calls=%async_computation.4 | async-start | bytes 4718592 | tf_op jit(solution)/shard_map/all_gather | solution.py:302
  35.6 26.8 %collective-permute-start.1 = (bf16[256,1024]{1,0:T(8,128)(2,1)S(1)}, bf16[256,1024]{1,0:T(8,128)(2,1)S(1)}, u32[]{:S(2)}, u32[]{:S(2)}) collective-permute-start(bf16[256,1024]{1,0:T(8,128)(2,1)S(1)} %get-tuple-element.60), channel_id=1, source_target_pairs={{1,2},{2,1},{5,6},{6,5},{9,10},{10,9},{13,14},{14,13},{17,18},{18,... | collective-permute-start | bytes 1572872 | tf_op jit(solution)/shard_map/ppermute | solution.py:276
  38.8 23.7 %collective-permute-start.2 = (bf16[256,1024]{1,0:T(8,128)(2,1)S(1)}, bf16[256,1024]{1,0:T(8,128)(2,1)S(1)}, u32[]{:S(2)}, u32[]{:S(2)}) collective-permute-start(bf16[256,1024]{1,0:T(8,128)(2,1)S(1)} %get-tuple-element.60), channel_id=1, source_target_pairs={{0,2},{3,1},{4,6},{7,5},{8,10},{11,9},{12,14},{15,13},{16,18},{19,... | collective-permute-start | bytes 1572872 | tf_op jit(solution)/shard_map/ppermute | solution.py:276
  40.1 25.1 %collective-permute-start.3 = (bf16[256,1024]{1,0:T(8,128)(2,1)S(1)}, bf16[256,1024]{1,0:T(8,128)(2,1)S(1)}, u32[]{:S(2)}, u32[]{:S(2)}) collective-permute-start(bf16[256,1024]{1,0:T(8,128)(2,1)S(1)} %get-tuple-element.61), channel_id=1, source_target_pairs={{0,1},{1,0},{2,3},{3,2},{4,5},{5,4},{6,7},{7,6},{8,9},{9,8},{10,11... | collective-permute-start | bytes 1572872 | tf_op jit(solution)/shard_map/ppermute | solution.py:276
  42.2 28.4 %collective-permute-start.4 = (bf16[2,256,512]{2,1,0:T(8,128)(2,1)S(1)}, bf16[2,256,512]{2,1,0:T(8,128)(2,1)S(1)}, u32[]{:S(2)}, u32[]{:S(2)}) collective-permute-start(bf16[2,256,512]{2,1,0:T(8,128)(2,1)S(1)} %get-tuple-element.62), channel_id=1, source_target_pairs={{0,0},{1,4},{2,1},{3,5},{4,2},{5,6},{6,3},{7,7},{8,8},{9,12},{10,9... | collective-permute-start | bytes 1572872 | tf_op jit(solution)/shard_map/ppermute | solution.py:276
  44.6 26.0 %collective-permute-start.5 = (bf16[2,256,512]{2,1,0:T(8,128)(2,1)S(1)}, bf16[2,256,512]{2,1,0:T(8,128)(2,1)S(1)}, u32[]{:S(2)}, u32[]{:S(2)}) collective-permute-start(bf16[2,256,512]{2,1,0:T(8,128)(2,1)S(1)} %get-tuple-element.63), channel_id=1, source_target_pairs={{0,5},{1,0},{2,4},{3,1},{4,7},{5,2},{6,6},{7,3},{8,13},{9,8},{10,1... | collective-permute-start | bytes 1572872 | tf_op jit(solution)/shard_map/ppermute | solution.py:276
  71.6 38.3 %collective-permute-start.8 = (bf16[512,1024]{1,0:T(8,128)(2,1)S(1)}, bf16[512,1024]{1,0:T(8,128)(2,1)}, u32[]{:S(2)}, u32[]{:S(2)}) collective-permute-start(bf16[512,1024]{1,0:T(8,128)(2,1)S(1)} %constant_dynamic-update-slice_fusion.2), channel_id=1, source_target_pairs={{1,0},{2,3},{5,4},{6,7},{9,8},{10,11},{13,12},{14,15},{17,16},{18,... | collective-permute-start | bytes 3145736 | tf_op jit(solution)/shard_map/ppermute | solution.py:276
  93.0 66.7 %all-to-all-start = ((bf16[8,2,256,256]{3,2,1,0:T(8,128)(2,1)}), bf16[8,2,256,256]{3,2,1,0:T(8,128)(2,1)S(1)}, u32[]{:S(2)}, u32[]{:S(2)}) async-start(bf16[8,2,256,256]{3,2,1,0:T(8,128)(2,1)} %copy-done.5), calls=%async_computation | async-start | bytes 4194304 | tf_op jit(solution)/shard_map/all_to_all | solution.py:378
  100.9 43.7 %collective-permute-start.9 = (bf16[512,1024]{1,0:T(8,128)(2,1)}, bf16[512,1024]{1,0:T(8,128)(2,1)}, u32[]{:S(2)}, u32[]{:S(2)}) collective-permute-start(bf16[512,1024]{1,0:T(8,128)(2,1)} %constant_dynamic-update-slice_fusion.refs_0_), channel_id=1, source_target_pairs={{0,4},{1,5},{2,6},{3,7},{4,0},{5,1},{6,2},{7,3},{8,12},{9,13},{10,... | collective-permute-start | bytes 3145736 | tf_op jit(solution)/shard_map/ppermute | solution.py:276
  111.2 33.4 %collective-permute-start.10 = (bf16[512,1024]{1,0:T(8,128)(2,1)S(1)}, bf16[512,1024]{1,0:T(8,128)(2,1)}, u32[]{:S(2)}, u32[]{:S(2)}) collective-permute-start(bf16[512,1024]{1,0:T(8,128)(2,1)S(1)} %broadcast_select_fusion.refs_1_), channel_id=1, source_target_pairs={{0,4},{1,5},{2,6},{3,7},{4,0},{5,1},{6,2},{7,3},{8,12},{9,13},{10,... | collective-permute-start | bytes 3145736 | tf_op jit(solution)/shard_map/ppermute | solution.py:276
  112.2 17.7 %collective-permute-start.7 = (bf16[2,256,512]{2,1,0:T(8,128)(2,1)}, bf16[2,256,512]{2,1,0:T(8,128)(2,1)S(1)}, u32[]{:S(2)}, u32[]{:S(2)}) collective-permute-start(bf16[2,256,512]{2,1,0:T(8,128)(2,1)} %copy-done.17), channel_id=1, source_target_pairs={{0,4},{1,1},{2,5},{3,0},{4,6},{5,3},{6,7},{7,2},{8,12},{9,9},{10,1... | collective-permute-start | bytes 1572872 | tf_op jit(solution)/shard_map/ppermute | solution.py:276
  176.7 23.0 %all-to-all-start.3 = ((f32[4,1,128]{2,1,0:T(1,128)}), f32[4,1,128]{2,1,0:T(1,128)S(1)}, u32[]{:S(2)}, u32[]{:S(2)}) async-start(f32[4,1,128]{2,1,0:T(1,128)} %broadcast_in_dim.46), calls=%async_computation.3 | async-start | bytes 4096 | tf_op jit(solution)/shard_map/all_to_all | solution.py:446
  183.5 17.4 %collective-permute-start.11 = (bf16[2,256,256]{2,1,0:T(8,128)(2,1)}, bf16[2,256,256]{2,1,0:T(8,128)(2,1)S(1)}, u32[]{:S(2)}, u32[]{:S(2)}) collective-permute-start(bf16[2,256,256]{2,1,0:T(8,128)(2,1)} %get-tuple-element.86), channel_id=1, source_target_pairs={{0,0},{1,2},{2,4},{3,6},{4,17},{5,19},{6,21},{7,23},{8,9},{9,11},{... | collective-permute-start | bytes 786440 | tf_op jit(solution)/shard_map/ppermute | solution.py:276
  186.3 17.7 %collective-permute-start.12 = (bf16[2,256,256]{2,1,0:T(8,128)(2,1)}, bf16[2,256,256]{2,1,0:T(8,128)(2,1)S(1)}, u32[]{:S(2)}, u32[]{:S(2)}) collective-permute-start(bf16[2,256,256]{2,1,0:T(8,128)(2,1)} %get-tuple-element.87), channel_id=1, source_target_pairs={{0,31},{1,29},{2,0},{3,2},{4,12},{5,14},{6,17},{7,19},{8,4},{9,6},... | collective-permute-start | bytes 786440 | tf_op jit(solution)/shard_map/ppermute | solution.py:276
  191.1 16.1 %collective-permute-start.13 = (bf16[2,256,256]{2,1,0:T(8,128)(2,1)}, bf16[2,256,256]{2,1,0:T(8,128)(2,1)S(1)}, u32[]{:S(2)}, u32[]{:S(2)}) collective-permute-start(bf16[2,256,256]{2,1,0:T(8,128)(2,1)} %get-tuple-element.88), channel_id=1, source_target_pairs={{0,27},{1,25},{2,31},{3,29},{4,8},{5,10},{6,12},{7,14},{8,0},{9,2}... | collective-permute-start | bytes 786440 | tf_op jit(solution)/shard_map/ppermute | solution.py:276
  191.8 23.8 %collective-permute-start.14 = (bf16[2,256,256]{2,1,0:T(8,128)(2,1)}, bf16[2,256,256]{2,1,0:T(8,128)(2,1)S(1)}, u32[]{:S(2)}, u32[]{:S(2)}) collective-permute-start(bf16[2,256,256]{2,1,0:T(8,128)(2,1)} %get-tuple-element.89), channel_id=1, source_target_pairs={{0,22},{1,20},{2,27},{3,25},{4,7},{5,5},{6,8},{7,10},{8,31},{9,29}... | collective-permute-start | bytes 786440 | tf_op jit(solution)/shard_map/ppermute | solution.py:276
  198.1 17.4 %collective-permute-start.15 = (bf16[2,256,256]{2,1,0:T(8,128)(2,1)}, bf16[2,256,256]{2,1,0:T(8,128)(2,1)S(1)}, u32[]{:S(2)}, u32[]{:S(2)}) collective-permute-start(bf16[2,256,256]{2,1,0:T(8,128)(2,1)} %copy-done.22), channel_id=1, source_target_pairs={{0,18},{1,16},{2,22},{3,20},{4,3},{5,1},{6,7},{7,5},{8,27},{9,25},... | collective-permute-start | bytes 786440 | tf_op jit(solution)/shard_map/ppermute | solution.py:276
  200.9 14.8 %collective-permute-start.16 = (bf16[2,256,256]{2,1,0:T(8,128)(2,1)}, bf16[2,256,256]{2,1,0:T(8,128)(2,1)S(1)}, u32[]{:S(2)}, u32[]{:S(2)}) collective-permute-start(bf16[2,256,256]{2,1,0:T(8,128)(2,1)} %copy-done.21), channel_id=1, source_target_pairs={{0,13},{1,15},{2,18},{3,16},{4,30},{5,28},{6,3},{7,1},{8,22},{9,20... | collective-permute-start | bytes 786440 | tf_op jit(solution)/shard_map/ppermute | solution.py:276
  204.0 18.0 %collective-permute-start.17 = (bf16[2,256,256]{2,1,0:T(8,128)(2,1)}, bf16[2,256,256]{2,1,0:T(8,128)(2,1)S(1)}, u32[]{:S(2)}, u32[]{:S(2)}) collective-permute-start(bf16[2,256,256]{2,1,0:T(8,128)(2,1)} %copy-done.20), channel_id=1, source_target_pairs={{0,9},{1,11},{2,13},{3,15},{4,26},{5,24},{6,30},{7,28},{8,18},{9,1... | collective-permute-start | bytes 786440 | tf_op jit(solution)/shard_map/ppermute | solution.py:276
  207.2 29.4 %collective-permute-start.18 = (bf16[2,256,256]{2,1,0:T(8,128)(2,1)}, bf16[2,256,256]{2,1,0:T(8,128)(2,1)S(1)}, u32[]{:S(2)}, u32[]{:S(2)}) collective-permute-start(bf16[2,256,256]{2,1,0:T(8,128)(2,1)} %copy-done.19), channel_id=1, source_target_pairs={{0,4},{1,6},{2,9},{3,11},{4,21},{5,23},{6,26},{7,24},{8,13},{9,15}... | collective-permute-start | bytes 786440 | tf_op jit(solution)/shard_map/ppermute | solution.py:276
  250.2 17.0 %collective-permute-start.22 = (bf16[2,256,256]{2,1,0:T(8,128)(2,1)S(1)}, bf16[2,256,256]{2,1,0:T(8,128)(2,1)S(1)}, u32[]{:S(2)}, u32[]{:S(2)}) collective-permute-start(bf16[2,256,256]{2,1,0:T(8,128)(2,1)S(1)} %get-tuple-element.98), channel_id=1, source_target_pairs={{0,16},{1,17},{2,18},{3,19},{4,20},{5,21},{6,22},{7,23},{8,24},{9,... | collective-permute-start | bytes 786440 | tf_op jit(solution)/shard_map/ppermute | solution.py:276
  250.2 24.9 %collective-permute-start.23 = (bf16[2,256,256]{2,1,0:T(8,128)(2,1)S(1)}, bf16[2,256,256]{2,1,0:T(8,128)(2,1)S(1)}, u32[]{:S(2)}, u32[]{:S(2)}) collective-permute-start(bf16[2,256,256]{2,1,0:T(8,128)(2,1)S(1)} %get-tuple-element.99), channel_id=1, source_target_pairs={{0,20},{1,21},{2,22},{3,23},{4,16},{5,17},{6,18},{7,19},{8,28},{9,... | collective-permute-start | bytes 786440 | tf_op jit(solution)/shard_map/ppermute | solution.py:276
  252.0 23.1 %collective-permute-start.24 = (bf16[2,256,256]{2,1,0:T(8,128)(2,1)S(1)}, bf16[2,256,256]{2,1,0:T(8,128)(2,1)S(1)}, u32[]{:S(2)}, u32[]{:S(2)}) collective-permute-start(bf16[2,256,256]{2,1,0:T(8,128)(2,1)S(1)} %get-tuple-element.100), channel_id=1, source_target_pairs={{0,24},{1,25},{2,26},{3,27},{4,28},{5,29},{6,30},{7,31},{8,0},{9,1... | collective-permute-start | bytes 786440 | tf_op jit(solution)/shard_map/ppermute | solution.py:276
  252.0 23.1 %collective-permute-start.25 = (bf16[2,256,256]{2,1,0:T(8,128)(2,1)S(1)}, bf16[2,256,256]{2,1,0:T(8,128)(2,1)S(1)}, u32[]{:S(2)}, u32[]{:S(2)}) collective-permute-start(bf16[2,256,256]{2,1,0:T(8,128)(2,1)S(1)} %get-tuple-element.101), channel_id=1, source_target_pairs={{0,28},{1,29},{2,30},{3,31},{4,24},{5,25},{6,26},{7,27},{8,4},{9,5... | collective-permute-start | bytes 786440 | tf_op jit(solution)/shard_map/ppermute | solution.py:276
  (32 other events, 413.4 us)
Sparse Core Ops, SparseCore 0:
  26.1 38.2 all-gather.2

commit v2 on v1

--- a/solution.py
+++ b/solution.py
@@ -41,7 +41,7 @@
     return 2 * lax.rem(column - shard + columns * 16, columns) + core
 
 
-def split_kernel(shards, ids, w, *out):
+def prep_kernel(shards, ids, w, *out):
     _, rows, piece = out[0].shape
     tiles = piece // LANES
     stride = 2 * shards * tiles
@@ -51,18 +51,14 @@
             for j in range(tiles):
                 part = w[pl.ds(2 * (first + j) + kind, rows, stride=stride), :]
                 out[r][kind, :, j * LANES : (j + 1) * LANES] = part.astype(BF)
-
-
-def slice_kernel(ids, w, out):
-    particles, _, rows, cols = out.shape
+    particles, _, _, cols = out[shards].shape
     tiles = cols // LANES
-    stride = 2 * particles * tiles
     for p in range(particles):
         first = slice_index(ids, p // 2, p % 2, ids[SHARD], particles // 2) * tiles
         for kind in range(2):
             for j in range(tiles):
                 part = w[pl.ds(2 * (first + j) + kind, rows, stride=stride), :]
-                out[p, kind, :, j * LANES : (j + 1) * LANES] = part.astype(BF)
+                out[shards][p, kind, :, j * LANES : (j + 1) * LANES] = part.astype(BF)
 
 
 def up_kernel(shards, scale, ids, tokens, *refs):
@@ -298,27 +294,26 @@
     index = lax.dynamic_slice(batch_index, (own * share,), (share,))
     picked = jnp.take(pool, index, axis=0).astype(F32)
     normed = (picked * lax.rsqrt(jnp.mean(picked * picked, axis=1, keepdims=True) + 1e-06)).astype(BF)
-    normed = lax.all_to_all(jnp.broadcast_to(normed[None], (shards, share, width)), "shard", 0, 0, tiled=True)
+    normed = jnp.stack(
+        [move(normed, [(dev(m, c, s), dev(m, c, (s + k) % shards)) for m, c, s in devices]) for k in range(shards)]
+    )
     normed = lax.all_gather(normed[None], "particle", axis=0, tiled=True)
 
     w_flat = flat(weights)
     steps = max(rows // 64, 1)
     lines = w_flat.shape[0] // steps
-    w_spec = pl.BlockSpec((lines, LANES), lambda i: (i, 0))
-    prepared = pl.pallas_call(
-        functools.partial(split_kernel, shards),
+    *prepared, slices = pl.pallas_call(
+        functools.partial(prep_kernel, shards),
         grid=(steps,),
-        out_shape=[jax.ShapeDtypeStruct((2, rows, part), BF)] * shards,
-        in_specs=[smem_spec(), w_spec],
-        out_specs=[pl.BlockSpec((2, rows // steps, part), lambda i: (0, i, 0))] * shards,
-        compiler_params=params(8),
-        name="split",
+        out_shape=[jax.ShapeDtypeStruct((2, rows, part), BF)] * shards
+        + [jax.ShapeDtypeStruct((particles, 2, rows, cols), BF)],
+        in_specs=[smem_spec(), pl.BlockSpec((lines, LANES), lambda i: (i, 0))],
+        out_specs=[pl.BlockSpec((2, rows // steps, part), lambda i: (0, i, 0))] * shards
+        + [pl.BlockSpec((particles, 2, rows // steps, cols), lambda i: (0, 0, i, 0))],
+        compiler_params=params(56),
+        name="prep",
     )(ids, w_flat)
 
-    if shards == 4:
-        here, away, w_late, *prepared = lax.optimization_barrier((here, away, w_flat, *prepared))
-    else:
-        w_late, *prepared = lax.optimization_barrier((w_flat, *prepared))
     w_routes = []
     for r in range(shards):
         pairs = []
@@ -328,34 +323,47 @@
         w_routes.append(pairs)
 
     if shards == 4:
+        here, away, slices, *prepared = lax.optimization_barrier((here, away, slices, *prepared))
+    whole = lax.all_to_all(slices, "particle", 0, 0, tiled=True)
+    pair_list = [(i, j) for i in range(particles) for j in range(i)]
+    partial = pl.pallas_call(
+        distance_kernel,
+        out_shape=jax.ShapeDtypeStruct((len(pair_list), 8, LANES), F32),
+        in_specs=[pl.BlockSpec(memory_space=pltpu.VMEM)],
+        out_specs=pl.BlockSpec(memory_space=pltpu.VMEM),
+        compiler_params=params(8),
+        name="distances",
+    )(whole)
+    sums = jnp.sum(partial, axis=(1, 2))
+    sums = jnp.pad(sums, (0, -len(pair_list) % LANES))
+    for axis, count in (("particle", particles), ("shard", shards)):
+        copies = jnp.broadcast_to(sums[None, None], (count, 1, sums.shape[0]))
+        sums = jnp.sum(lax.all_to_all(copies, axis, 0, 0, tiled=True), axis=(0, 1))
+    if shards == 4:
         inner, edge = (1, 2), (0, 3)
         far = [(dev(m, c, s), dev(m, c, 1 if s == 3 else 2)) for m, c, s in devices if s in edge]
         near = [(dev(m, c, s), dev(m, c, 3 - s)) for m, c, s in devices if s in inner]
         outward = [(dev(m, c, s), dev(m, c, s ^ 1)) for m, c, s in devices if s in inner]
-        pair_c = move(here, [(dev(m, c, s), dev(m, c, s ^ 1)) for m, c, s in devices])
-        near_c, far_c = move(away, near), move(away, far)
+        pair = [(dev(m, c, s), dev(m, c, s ^ 1)) for m, c, s in devices]
+        got = [move(away, near), move(away, far), move(here, pair)]
         w_pieces = [move(x, route) for x, route in zip(prepared[:2], w_routes[:2])]
-        near_c, far_c, pair_c, w_pieces[0], w_pieces[1], prepared[2], prepared[3] = lax.optimization_barrier(
-            (near_c, far_c, pair_c, *w_pieces, *prepared[2:])
-        )
-        w_pieces += [move(x, route) for x, route in zip(prepared[2:], w_routes[2:])]
-        cross = jnp.concatenate([near_c, far_c])
-        cross = jnp.where(jnp.logical_or(shard == 1, shard == 2), cross, move(cross, outward))
-        got = jnp.concatenate([here, pair_c])
-        sources = [got, cross, move(got, swap_of(everyone)), move(cross, swap_of(everyone))]
+        got, w_pieces, last, sums, normed = lax.optimization_barrier((got, w_pieces, prepared[2:], sums, normed))
+        near_c, far_c, pair_c = got
+        near_o, far_o = move(near_c, outward), move(far_c, outward)
+        w_pieces = w_pieces + [move(x, route) for x, route in zip(last, w_routes[2:])]
+        is_inner = jnp.logical_or(shard == 1, shard == 2)
+        got = [here, pair_c, jnp.where(is_inner, near_c, near_o), jnp.where(is_inner, far_c, far_o)]
+        got, w_pieces = lax.optimization_barrier((got, w_pieces))
+        sources = got + [move(x, swap_of(everyone)) for x in got]
 
         def pick(ids, refs, held, sems):
             s, core = ids[SHARD], ids[CORE]
             low = s < 2
             place = [s, s + 1 - 2 * lax.rem(s, 2), jnp.where(low, 2, 1), jnp.where(low, 3, 0)]
             for i, ref in enumerate(refs):
-                turn = core if i < 2 else 1 - core
-                for k in range(2):
-                    at = 2 * place[2 * (i % 2) + k] + turn
-                    to = pl.multiple_of(at * half_rows, half_rows)
-                    pltpu.make_async_copy(
-                        ref.at[pl.ds(k * half_rows, half_rows), :], held.at[pl.ds(to, half_rows), :], sems.at[at]
-                    ).start()
+                at = 2 * place[i % 4] + (core if i < 4 else 1 - core)
+                to = pl.multiple_of(at * half_rows, half_rows)
+                pltpu.make_async_copy(ref, held.at[pl.ds(to, half_rows), :], sems.at[at]).start()
     else:
         full = lax.all_gather(cotangent[0], "shard", axis=0, tiled=True)
         sources = [jnp.where(core == proc, full, move(full, swap_of(everyone)))]
@@ -366,42 +374,57 @@
                 span = pl.ds(i * half_rows, half_rows)
                 pltpu.make_async_copy(refs[0].at[span, :], held.at[span, :], sems.at[i]).start()
 
-    slices = pl.pallas_call(
-        slice_kernel,
-        grid=(steps,),
-        out_shape=jax.ShapeDtypeStruct((particles, 2, rows, cols), BF),
-        in_specs=[smem_spec(), w_spec],
-        out_specs=pl.BlockSpec((particles, 2, rows // steps, cols), lambda i: (0, 0, i, 0)),
-        compiler_params=params(8),
-        name="slices",
-    )(ids, w_late)
-    whole = lax.all_to_all(slices, "particle", 0, 0, tiled=True)
+    lookup = [
+        [pair_list.index((max(i, j), min(i, j))) if i != j else len(pair_list) for j in range(particles)]
+        for i in range(particles)
+    ]
+    table = jnp.concatenate([sums[: len(pair_list)], jnp.zeros((1,), F32)])
+    distances = table[jnp.array(lookup, jnp.int32)]
+    inverse_band = 1.0 / kernel_scale[0].astype(F32)
+    repulse = 2.0 * inverse_band
+    kernel = jnp.exp(-distances * inverse_band)
+    scale = 2 * width * hidden / particles
+    coef = jnp.concatenate(
+        [(scale * kernel).reshape(-1), scale * repulse * jnp.sum(kernel, axis=1), repulse[None]]
+    )
+
     per = BLOCK // share
     halves = tok_rows // BLOCK
     act_t, slope_t, down_t, normed = pl.pallas_call(
         functools.partial(up_kernel, shards, width ** (-0.5)),
-        grid=(blocks,),
+        grid_spec=pltpu.PrefetchScalarGridSpec(
+            num_scalar_prefetch=1,
+            grid=(blocks,),
+            in_specs=[
+                pl.BlockSpec(
+                    (per, 1, share, width),
+                    lambda i, ids: (i % halves, lax.rem(ids[SHARD] - i // halves + shards, shards), 0, 0),
+                )
+            ]
+            + [pl.BlockSpec((2, rows, part), lambda i, ids: (0, 0, 0))] * shards,
+            out_specs=[
+                pl.BlockSpec((part, BLOCK), lambda i, ids: (0, i)),
+                pl.BlockSpec((part, BLOCK), lambda i, ids: (0, i)),
+                pl.BlockSpec((part, width), lambda i, ids: (0, 0)),
+                pl.BlockSpec((BLOCK, width), lambda i, ids: (i, 0)),
+            ],
+            scratch_shapes=[
+                pltpu.VMEM((width, part), BF),
+                pltpu.VMEM((width, part), BF),
+                pltpu.VMEM((part, width), BF),
+            ],
+        ),
         out_shape=[
             jax.ShapeDtypeStruct((part, tokens), BF),
             jax.ShapeDtypeStruct((part, tokens), BF),
             jax.ShapeDtypeStruct((part, width), BF),
             jax.ShapeDtypeStruct((tokens, width), BF),
         ],
-        in_specs=[smem_spec(), pl.BlockSpec((per, 1, share, width), lambda i: (i % halves, i // halves, 0, 0))]
-        + [pl.BlockSpec((2, rows, part), lambda i: (0, 0, 0))] * shards,
-        out_specs=[
-            pl.BlockSpec((part, BLOCK), lambda i: (0, i)),
-            pl.BlockSpec((part, BLOCK), lambda i: (0, i)),
-            pl.BlockSpec((part, width), lambda i: (0, 0)),
-            pl.BlockSpec((BLOCK, width), lambda i: (i, 0)),
-        ],
-        scratch_shapes=[pltpu.VMEM((width, part), BF), pltpu.VMEM((width, part), BF), pltpu.VMEM((part, width), BF)],
-        compiler_params=params(24),
+        compiler_params=params(56),
         name="up",
     )(ids, normed, *w_pieces)
 
     grad_scale = 1.0 / (tokens * width)
-    held = 2 * (2 * tokens * width + 3 * tokens * part + 3 * width * part)
     scores = pl.pallas_call(
         functools.partial(
             grad_kernel,
@@ -425,38 +448,9 @@
             pltpu.VMEM((2, width, part), BF),
             pltpu.SemaphoreType.DMA((2 * shards + 4,)),
         ],
-        compiler_params=params(held // MIB + 8),
+        compiler_params=params(56),
         name="grads",
     )(ids, normed, act_t, slope_t, down_t, *sources)
-
-    whole, *scores = lax.optimization_barrier((whole, *scores))
-    pair_list = [(i, j) for i in range(particles) for j in range(i)]
-    partial = pl.pallas_call(
-        distance_kernel,
-        out_shape=jax.ShapeDtypeStruct((len(pair_list), 8, LANES), F32),
-        in_specs=[pl.BlockSpec(memory_space=pltpu.VMEM)],
-        out_specs=pl.BlockSpec(memory_space=pltpu.VMEM),
-        compiler_params=params(8),
-        name="distances",
-    )(whole)
-    sums = jnp.sum(partial, axis=(1, 2))
-    sums = jnp.pad(sums, (0, -len(pair_list) % LANES))
-    for axis, count in (("particle", particles), ("shard", shards)):
-        copies = jnp.broadcast_to(sums[None, None], (count, 1, sums.shape[0]))
-        sums = jnp.sum(lax.all_to_all(copies, axis, 0, 0, tiled=True), axis=(0, 1))
-    lookup = [
-        [pair_list.index((max(i, j), min(i, j))) if i != j else len(pair_list) for j in range(particles)]
-        for i in range(particles)
-    ]
-    table = jnp.concatenate([sums[: len(pair_list)], jnp.zeros((1,), F32)])
-    distances = table[jnp.array(lookup, jnp.int32)]
-    inverse_band = 1.0 / kernel_scale[0].astype(F32)
-    repulse = 2.0 * inverse_band
-    kernel = jnp.exp(-distances * inverse_band)
-    scale = 2 * width * hidden / particles
-    coef = jnp.concatenate(
-        [(scale * kernel).reshape(-1), scale * repulse * jnp.sum(kernel, axis=1), repulse[None]]
-    )
 
     ratio = particles // shards
     arrived = []
@@ -499,7 +493,7 @@
         in_specs=[smem_spec()] + [state_spec] * 3 + [any_spec()] * particles,
         out_specs=[state_spec] * 4,
         scratch_shapes=[pltpu.VMEM((2, rows, hidden), BF), pltpu.SemaphoreType.DMA((particles,))],
-        compiler_params=params(16),
+        compiler_params=params(56),
         name="adam",
     )(ids, w_flat, flat(first_moment), flat(second_moment), *back)
     return tuple(unflat(x) for x in outs)

time: 298 us -> 284 us (0.953)
  local copies, waits for them, and re-layouts: 26.7 us -> 5.86 us
  waiting for transfers between devices: 91.5 us -> 112 us
  blocking collectives: 30.3 us -> 15.3 us
  Pallas kernels: 43.5 us -> 55.9 us
  starting transfers between devices: 84 us -> 72.2 us
    unnamed x56 -> x38, local copies, waits for them, and re-layouts: 21.6 us -> 2.51 us
    all_to_all x1, waiting for transfers between devices: 0.01 us -> 16.9 us  [local(): whole = lax.all_to_all(slices, 'particle', 0, 0, tiled=True)]
    all_to_all x1 -> x0, blocking collectives: 16.1 us -> none  [local(): lax.all_to_all(jnp.broadcast_to(normed[None], (shards, share, width)), 's...]
    all_to_all x1 -> x0, starting transfers between devices: 6.02 us -> none  [local(): sums = jnp.sum(lax.all_to_all(copies, axis, 0, 0, tiled=True), axis=(0, 1))]
    ppermute x26 -> x32, starting transfers between devices: 73.8 us -> 68.1 us  [move(): return lax.ppermute(x, AXES, pairs)]
    pallas_call x1, Pallas kernels: 10.1 us -> 15.4 us  [local(): pl.pallas_call(functools.partial(adam_kernel, particles), grid=(steps,),...]
    pallas_call x1, Pallas kernels: 7.55 us -> 11.9 us  [local(): pl.pallas_call(functools.partial(up_kernel, shards, width ** (-0.5)), gri...]
    ppermute x26 -> x32, waiting for transfers between devices: 91.5 us -> 94.7 us  [move(): return lax.ppermute(x, AXES, pairs)]
  transfers between devices with their start and end apart: 29 -> 34, of which waited for: 13 -> 17; matrix products, arithmetic and copies ran while one was open for 3% -> 2% of each run, Pallas kernels for 9% -> 8%
where the time goes in v2:
time: 284 us; the launch traced here: 282 us
  waiting for transfers between devices  112 us (39%)
  starting transfers between devices  72.2 us (25%)
  Pallas kernels  55.9 us (20%)
  blocking collectives  15.3 us (5%)
  between operations  15.2 us (5%)
  other arithmetic  6.07 us (2%)
  local copies, waits for them, and re-layouts  5.86 us (2%)
    ppermute x32, waiting for transfers between devices, move(): return lax.ppermute(x, AXES, pairs)  94.7 us
    ppermute x32, starting transfers between devices, move(): return lax.ppermute(x, AXES, pairs)  68.1 us
    all_to_all x1, waiting for transfers between devices, local(): whole = lax.all_to_all(slices, 'particle', 0, 0, tiled=True)  16.9 us
    pallas_call x1, Pallas kernels, local(): pl.pallas_call(functools.partial(adam_kernel, particles), grid=(steps,),...  15.4 us
    all_to_all x2, blocking collectives, local(): sums = jnp.sum(lax.all_to_all(copies, axis, 0, 0, tiled=True), axis=(0, 1))  15.3 us
    pallas_call x1, Pallas kernels, local(): pl.pallas_call(functools.partial(grad_kernel, shards, particles, -width *...  13.8 us
    pallas_call x1, Pallas kernels, local(): pl.pallas_call(functools.partial(up_kernel, shards, width ** (-0.5)), gri...  11.9 us
    pallas_call x1, Pallas kernels, local(): pl.pallas_call(functools.partial(prep_kernel, shards), grid=(steps,), out...  7.76 us
  transfers between devices with their start and end apart: 34, of which 17 were waited for; matrix products, arithmetic and copies ran while one was open for 2% of the time, Pallas kernels for 8%

profile of v2, /device:TPU:23, one launch (start us, length us, event | category | flops | bytes accessed | tf_op | source)
XLA Modules:
  0.0 282.1 jit_solution(9423192084786150345)
XLA Ops:
  14.2 6.9 %collective-permute-done.7 = bf16[64,1024]{1,0:T(8,128)(2,1)S(1)} collective-permute-done((bf16[64,1024]{1,0:T(8,128)(2,1)S(1)}, bf16[64,1024]{1,0:T(8,128)(2,1)S(1)}, u32[]{:S(2)}, u32[]{:S(2)}) %collective-permute-start.7) | collective-permute-done | bytes 131104 | tf_op jit(solution)/shard_map/ppermute | solution.py:272
  28.1 7.8 %prep.1 = (bf16[2,256,512]{2,1,0:T(8,128)(2,1)}, bf16[2,256,512]{2,1,0:T(8,128)(2,1)}, bf16[2,256,512]{2,1,0:T(8,128)(2,1)}, bf16[2,256,512]{2,1,0:T(8,128)(2,1)}, bf16[8,2,256,256]{3,2,1,0:T(8,128)(2,1)}) custom-call(s32[5]{0:T(128)} %stack.36.ids, f32[8192,128]{1,0:T(8,128)} %bitcast.58), custom_call_target="tpu_custom_call" | custom-call | tf_op jit(solution)/shard_map/prep/pallas_call | solution.py:305
  36.9 4.1 %all-to-all-start = ((bf16[8,2,256,256]{3,2,1,0:T(8,128)(2,1)}), bf16[8,2,256,256]{3,2,1,0:T(8,128)(2,1)S(1)}, u32[]{:S(2)}, u32[]{:S(2)}) async-start(bf16[8,2,256,256]{3,2,1,0:T(8,128)(2,1)} %get-tuple-element.68), calls=%async_computation | async-start | bytes 4194304 | tf_op jit(solution)/shard_map/all_to_all | solution.py:327
  44.2 4.1 %collective-permute-start.3 = (bf16[256,1024]{1,0:T(8,128)(2,1)S(1)}, bf16[256,1024]{1,0:T(8,128)(2,1)}, u32[]{:S(2)}, u32[]{:S(2)}) collective-permute-start(bf16[256,1024]{1,0:T(8,128)(2,1)S(1)} %get-tuple-element.86.refs_0_), channel_id=1, source_target_pairs={{0,1},{1,0},{2,3},{3,2},{4,5},{5,4},{6,7},{7,6},{8,9},{9,8},{10,11... | collective-permute-start | bytes 1572872 | tf_op jit(solution)/shard_map/ppermute | solution.py:272
  51.0 5.4 %collective-permute-start.5 = (bf16[2,256,512]{2,1,0:T(8,128)(2,1)}, bf16[2,256,512]{2,1,0:T(8,128)(2,1)}, u32[]{:S(2)}, u32[]{:S(2)}) collective-permute-start(bf16[2,256,512]{2,1,0:T(8,128)(2,1)} %get-tuple-element.65), channel_id=1, source_target_pairs={{0,5},{1,0},{2,4},{3,1},{4,7},{5,2},{6,6},{7,3},{8,13},{9,8},{10,1... | collective-permute-start | bytes 1572872 | tf_op jit(solution)/shard_map/ppermute | solution.py:272
  56.4 16.9 %all-to-all-done.whole = bf16[8,2,256,256]{3,2,1,0:T(8,128)(2,1)S(1)} async-done(((bf16[8,2,256,256]{3,2,1,0:T(8,128)(2,1)}), bf16[8,2,256,256]{3,2,1,0:T(8,128)(2,1)S(1)}, u32[]{:S(2)}, u32[]{:S(2)}) %all-to-all-start) | async-done | bytes 2097184 | tf_op jit(solution)/shard_map/all_to_all | solution.py:327
  75.5 9.4 %all_to_all.15 = f32[8,1,128]{2,1,0:T(1,128)S(1)} all-to-all(f32[8,1,128]{2,1,0:T(1,128)S(1)} %broadcast_in_dim.38), channel_id=1, replica_groups=mesh['particle'=8,'shard'=4] {'particle'}, dimensions={0} | all-to-all | bytes 8192 | tf_op jit(solution)/shard_map/all_to_all | solution.py:341
  85.0 5.9 %all_to_all.16 = f32[4,1,128]{2,1,0:T(1,128)S(1)} all-to-all(f32[4,1,128]{2,1,0:T(1,128)S(1)} %broadcast_in_dim.39), channel_id=1, replica_groups=mesh['particle'=8,'shard'=4] {'shard'}, dimensions={0} | all-to-all | bytes 4096 | tf_op jit(solution)/shard_map/all_to_all | solution.py:341
  100.0 15.2 %collective-permute-done.9 = bf16[256,1024]{1,0:T(8,128)(2,1)} collective-permute-done((bf16[256,1024]{1,0:T(8,128)(2,1)}, bf16[256,1024]{1,0:T(8,128)(2,1)}, u32[]{:S(2)}, u32[]{:S(2)}) %collective-permute-start.9) | collective-permute-done | bytes 524320 | tf_op jit(solution)/shard_map/ppermute | solution.py:272
  116.3 15.8 %collective-permute-done.10 = bf16[256,1024]{1,0:T(8,128)(2,1)} collective-permute-done((bf16[256,1024]{1,0:T(8,128)(2,1)}, bf16[256,1024]{1,0:T(8,128)(2,1)}, u32[]{:S(2)}, u32[]{:S(2)}) %collective-permute-start.10) | collective-permute-done | bytes 524320 | tf_op jit(solution)/shard_map/ppermute | solution.py:272
  133.3 6.1 %collective-permute-done.12.refs_3_ = bf16[2,256,512]{2,1,0:T(8,128)(2,1)S(1)} collective-permute-done((bf16[2,256,512]{2,1,0:T(8,128)(2,1)}, bf16[2,256,512]{2,1,0:T(8,128)(2,1)S(1)}, u32[]{:S(2)}, u32[]{:S(2)}) %collective-permute-start.12) | collective-permute-done | bytes 524320 | tf_op jit(solution)/shard_map/ppermute | solution.py:272
  142.0 11.9 %up.1 = (bf16[512,2048]{1,0:T(8,128)(2,1)}, bf16[512,2048]{1,0:T(8,128)(2,1)}, bf16[512,1024]{1,0:T(8,128)(2,1)}, bf16[2048,1024]{1,0:T(8,128)(2,1)}) custom-call(s32[5]{0:T(128)} %stack.36.ids, bf16[8,4,64,1024]{3,2,1,0:T(8,128)(2,1)} %bitcast.62, bf16[2,256,512]{2,1,0:T(8,128)(2,1)} %copy-done.8, bf16[2,256,512]{2,1,0:T(8,128)(2,1)} %collective-permute-done.5.refs_1_, ...), custom_call_target="tpu_custom_call" | custom-call | tf_op jit(solution)/shard_map/up/pallas_call | solution.py:393
  153.9 13.8 %grads.1 = (bf16[2,256,256]{2,1,0:T(8,128)(2,1)}, bf16[2,256,256]{2,1,0:T(8,128)(2,1)}, bf16[2,256,256]{2,1,0:T(8,128)(2,1)}, bf16[2,256,256]{2,1,0:T(8,128)(2,1...) custom-call(s32[5]{0:T(128)} %stack.36.ids, ...), custom_call_target="tpu_custom_call" | custom-call | tf_op jit(solution)/shard_map/grads/pallas_call | solution.py:428
  175.4 6.3 %collective-permute-start.20 = (bf16[2,256,256]{2,1,0:T(8,128)(2,1)}, bf16[2,256,256]{2,1,0:T(8,128)(2,1)S(1)}, u32[]{:S(2)}, u32[]{:S(2)}) collective-permute-start(bf16[2,256,256]{2,1,0:T(8,128)(2,1)} %get-tuple-element.93), channel_id=1, source_target_pairs={{0,22},{1,20},{2,27},{3,25},{4,7},{5,5},{6,8},{7,10},{8,31},{9,29}... | collective-permute-start | bytes 786440 | tf_op jit(solution)/shard_map/ppermute | solution.py:272
  187.0 3.7 %collective-permute-done.19.refs_2_ = bf16[2,256,256]{2,1,0:T(8,128)(2,1)S(1)} collective-permute-done((bf16[2,256,256]{2,1,0:T(8,128)(2,1)}, bf16[2,256,256]{2,1,0:T(8,128)(2,1)S(1)}, u32[]{:S(2)}, u32[]{:S(2)}) %collective-permute-start.19) | collective-permute-done | bytes 262176 | tf_op jit(solution)/shard_map/ppermute | solution.py:272
  190.7 6.0 %collective-permute-start.24 = (bf16[2,256,256]{2,1,0:T(8,128)(2,1)}, bf16[2,256,256]{2,1,0:T(8,128)(2,1)S(1)}, u32[]{:S(2)}, u32[]{:S(2)}) collective-permute-start(bf16[2,256,256]{2,1,0:T(8,128)(2,1)} %get-tuple-element.97), channel_id=1, source_target_pairs={{0,4},{1,6},{2,9},{3,11},{4,21},{5,23},{6,26},{7,24},{8,13},{9,15}... | collective-permute-start | bytes 786440 | tf_op jit(solution)/shard_map/ppermute | solution.py:272
  199.6 14.1 %collective-permute-done.23.refs_6_ = bf16[2,256,256]{2,1,0:T(8,128)(2,1)S(1)} collective-permute-done((bf16[2,256,256]{2,1,0:T(8,128)(2,1)}, bf16[2,256,256]{2,1,0:T(8,128)(2,1)S(1)}, u32[]{:S(2)}, u32[]{:S(2)}) %collective-permute-start.23) | collective-permute-done | bytes 262176 | tf_op jit(solution)/shard_map/ppermute | solution.py:272
  213.7 3.8 %collective-permute-done.24.refs_7_ = bf16[2,256,256]{2,1,0:T(8,128)(2,1)S(1)} collective-permute-done((bf16[2,256,256]{2,1,0:T(8,128)(2,1)}, bf16[2,256,256]{2,1,0:T(8,128)(2,1)S(1)}, u32[]{:S(2)}, u32[]{:S(2)}) %collective-permute-start.24) | collective-permute-done | bytes 262176 | tf_op jit(solution)/shard_map/ppermute | solution.py:272
  217.5 5.0 %stein.1 = (bf16[2,256,256]{2,1,0:T(8,128)(2,1)S(1)}, bf16[2,256,256]{2,1,0:T(8,128)(2,1)S(1)}, bf16[2,256,256]{2,1,0:T(8,128)(2,1)S(1)}, bf16[2,256,256]{2,1,0:...) custom-call(s32[5]{0:T(128)S(1)} %copy-done.3, ...), custom_call_target="tpu_custom_call" | custom-call | tf_op jit(solution)/shard_map/stein/pallas_call | solution.py:466
  225.0 6.2 %collective-permute-start.26 = (bf16[2,256,256]{2,1,0:T(8,128)(2,1)S(1)}, bf16[2,256,256]{2,1,0:T(8,128)(2,1)S(1)}, u32[]{:S(2)}, u32[]{:S(2)}) collective-permute-start(bf16[2,256,256]{2,1,0:T(8,128)(2,1)S(1)} %get-tuple-element.100), channel_id=1, source_target_pairs={{0,8},{1,9},{2,10},{3,11},{4,12},{5,13},{6,14},{7,15},{8,16},{9,17... | collective-permute-start | bytes 786440 | tf_op jit(solution)/shard_map/ppermute | solution.py:272
  237.0 4.3 %collective-permute-start.31 = (bf16[2,256,256]{2,1,0:T(8,128)(2,1)S(1)}, bf16[2,256,256]{2,1,0:T(8,128)(2,1)S(1)}, u32[]{:S(2)}, u32[]{:S(2)}) collective-permute-start(bf16[2,256,256]{2,1,0:T(8,128)(2,1)S(1)} %get-tuple-element.105), channel_id=1, source_target_pairs={{0,28},{1,29},{2,30},{3,31},{4,24},{5,25},{6,26},{7,27},{8,4},{9,5... | collective-permute-start | bytes 786440 | tf_op jit(solution)/shard_map/ppermute | solution.py:272
  242.6 8.5 %collective-permute-done.28.refs_4_ = bf16[2,256,256]{2,1,0:T(8,128)(2,1)S(1)} collective-permute-done((bf16[2,256,256]{2,1,0:T(8,128)(2,1)S(1)}, bf16[2,256,256]{2,1,0:T(8,128)(2,1)S(1)}, u32[]{:S(2)}, u32[]{:S(2)}) %collective-permute-start.28) | collective-permute-done | bytes 262176 | tf_op jit(solution)/shard_map/ppermute | solution.py:272
  251.1 7.8 %collective-permute-done.29.refs_5_ = bf16[2,256,256]{2,1,0:T(8,128)(2,1)S(1)} collective-permute-done((bf16[2,256,256]{2,1,0:T(8,128)(2,1)S(1)}, bf16[2,256,256]{2,1,0:T(8,128)(2,1)S(1)}, u32[]{:S(2)}, u32[]{:S(2)}) %collective-permute-start.29) | collective-permute-done | bytes 262176 | tf_op jit(solution)/shard_map/ppermute | solution.py:272
  259.8 15.4 %adam.1 = (f32[8192,128]{1,0:T(8,128)}, f32[8192,128]{1,0:T(8,128)}, f32[8192,128]{1,0:T(8,128)}, f32[8192,128]{1,0:T(8,128)}) custom-call(s32[5]{0:T(128)} %stack.36.ids, f32[8192,128]{1,0:T(8,128)} %bitcast.59, f32[8192,128]{1,0:T(8,128)} %bitcast.60, f32[8192,128]{1,0:T(8,128)} %bitcast.61, bf16[2,256,256]{2,1,0:T(8,128)(2,1)} %copy-done.2, ...), custom_call_target="tpu_custom_call" | custom-call | tf_op jit(solution)/shard_map/adam/pallas_call | solution.py:489
  (119 shorter events, 62.4 us)
Async XLA Ops:
  7.2 83.8 %all-gather.3.cloned.1.call-start = ((), (), s32[]{:S(2)}) async-start(), calls=%async_computation.3 | async-start | bytes 4718592 | tf_op jit(solution)/shard_map/all_gather | solution.py:300
  36.9 36.3 %all-to-all-start = ((bf16[8,2,256,256]{3,2,1,0:T(8,128)(2,1)}), bf16[8,2,256,256]{3,2,1,0:T(8,128)(2,1)S(1)}, u32[]{:S(2)}, u32[]{:S(2)}) async-start(bf16[8,2,256,256]{3,2,1,0:T(8,128)(2,1)} %get-tuple-element.68), calls=%async_computation | async-start | bytes 4194304 | tf_op jit(solution)/shard_map/all_to_all | solution.py:327
  41.0 49.9 %collective-permute-start.1 = (bf16[256,1024]{1,0:T(8,128)(2,1)}, bf16[256,1024]{1,0:T(8,128)(2,1)}, u32[]{:S(2)}, u32[]{:S(2)}) collective-permute-start(bf16[256,1024]{1,0:T(8,128)(2,1)} %get-tuple-element.62), channel_id=1, source_target_pairs={{1,2},{2,1},{5,6},{6,5},{9,10},{10,9},{13,14},{14,13},{17,18},{18,... | collective-permute-start | bytes 1572872 | tf_op jit(solution)/shard_map/ppermute | solution.py:272
  42.9 48.0 %collective-permute-start.2 = (bf16[256,1024]{1,0:T(8,128)(2,1)}, bf16[256,1024]{1,0:T(8,128)(2,1)}, u32[]{:S(2)}, u32[]{:S(2)}) collective-permute-start(bf16[256,1024]{1,0:T(8,128)(2,1)} %get-tuple-element.62), channel_id=1, source_target_pairs={{0,2},{3,1},{4,6},{7,5},{8,10},{11,9},{12,14},{15,13},{16,18},{19,... | collective-permute-start | bytes 1572872 | tf_op jit(solution)/shard_map/ppermute | solution.py:272
  44.2 46.7 %collective-permute-start.3 = (bf16[256,1024]{1,0:T(8,128)(2,1)S(1)}, bf16[256,1024]{1,0:T(8,128)(2,1)}, u32[]{:S(2)}, u32[]{:S(2)}) collective-permute-start(bf16[256,1024]{1,0:T(8,128)(2,1)S(1)} %get-tuple-element.86.refs_0_), channel_id=1, source_target_pairs={{0,1},{1,0},{2,3},{3,2},{4,5},{5,4},{6,7},{7,6},{8,9},{9,8},{10,11... | collective-permute-start | bytes 1572872 | tf_op jit(solution)/shard_map/ppermute | solution.py:272
  48.3 42.6 %collective-permute-start.4 = (bf16[2,256,512]{2,1,0:T(8,128)(2,1)}, bf16[2,256,512]{2,1,0:T(8,128)(2,1)S(1)}, u32[]{:S(2)}, u32[]{:S(2)}) collective-permute-start(bf16[2,256,512]{2,1,0:T(8,128)(2,1)} %get-tuple-element.64), channel_id=1, source_target_pairs={{0,0},{1,4},{2,1},{3,5},{4,2},{5,6},{6,3},{7,7},{8,8},{9,12},{10,9... | collective-permute-start | bytes 1572872 | tf_op jit(solution)/shard_map/ppermute | solution.py:272
  51.0 40.0 %collective-permute-start.5 = (bf16[2,256,512]{2,1,0:T(8,128)(2,1)}, bf16[2,256,512]{2,1,0:T(8,128)(2,1)}, u32[]{:S(2)}, u32[]{:S(2)}) collective-permute-start(bf16[2,256,512]{2,1,0:T(8,128)(2,1)} %get-tuple-element.65), channel_id=1, source_target_pairs={{0,5},{1,0},{2,4},{3,1},{4,7},{5,2},{6,6},{7,3},{8,13},{9,8},{10,1... | collective-permute-start | bytes 1572872 | tf_op jit(solution)/shard_map/ppermute | solution.py:272
  91.0 24.2 %collective-permute-start.9 = (bf16[256,1024]{1,0:T(8,128)(2,1)}, bf16[256,1024]{1,0:T(8,128)(2,1)}, u32[]{:S(2)}, u32[]{:S(2)}) collective-permute-start(bf16[256,1024]{1,0:T(8,128)(2,1)} %collective-permute-done.1), channel_id=1, source_target_pairs={{1,0},{2,3},{5,4},{6,7},{9,8},{10,11},{13,12},{14,15},{17,16},{18,... | collective-permute-start | bytes 1572872 | tf_op jit(solution)/shard_map/ppermute | solution.py:272
  94.5 37.7 %collective-permute-start.10 = (bf16[256,1024]{1,0:T(8,128)(2,1)}, bf16[256,1024]{1,0:T(8,128)(2,1)}, u32[]{:S(2)}, u32[]{:S(2)}) collective-permute-start(bf16[256,1024]{1,0:T(8,128)(2,1)} %collective-permute-done.2), channel_id=1, source_target_pairs={{1,0},{2,3},{5,4},{6,7},{9,8},{10,11},{13,12},{14,15},{17,16},{18,... | collective-permute-start | bytes 1572872 | tf_op jit(solution)/shard_map/ppermute | solution.py:272
  96.6 36.7 %collective-permute-start.11 = (bf16[2,256,512]{2,1,0:T(8,128)(2,1)}, bf16[2,256,512]{2,1,0:T(8,128)(2,1)S(1)}, u32[]{:S(2)}, u32[]{:S(2)}) collective-permute-start(bf16[2,256,512]{2,1,0:T(8,128)(2,1)} %get-tuple-element.76), channel_id=1, source_target_pairs={{0,1},{1,5},{2,0},{3,4},{4,3},{5,7},{6,2},{7,6},{8,9},{9,13},{10,8... | collective-permute-start | bytes 1572872 | tf_op jit(solution)/shard_map/ppermute | solution.py:272
  98.0 41.4 %collective-permute-start.12 = (bf16[2,256,512]{2,1,0:T(8,128)(2,1)}, bf16[2,256,512]{2,1,0:T(8,128)(2,1)S(1)}, u32[]{:S(2)}, u32[]{:S(2)}) collective-permute-start(bf16[2,256,512]{2,1,0:T(8,128)(2,1)} %get-tuple-element.77), channel_id=1, source_target_pairs={{0,4},{1,1},{2,5},{3,0},{4,6},{5,3},{6,7},{7,2},{8,12},{9,9},{10,1... | collective-permute-start | bytes 1572872 | tf_op jit(solution)/shard_map/ppermute | solution.py:272
  139.4 14.5 %collective-permute-start.14 = (bf16[256,1024]{1,0:T(8,128)(2,1)}, bf16[256,1024]{1,0:T(8,128)(2,1)}, u32[]{:S(2)}, u32[]{:S(2)}) collective-permute-start(bf16[256,1024]{1,0:T(8,128)(2,1)} %collective-permute-done.3.refs_1_), channel_id=1, source_target_pairs={{0,4},{1,5},{2,6},{3,7},{4,0},{5,1},{6,2},{7,3},{8,12},{9,13},{10,... | collective-permute-start | bytes 1572872 | tf_op jit(solution)/shard_map/ppermute | solution.py:272
  167.8 15.6 %collective-permute-start.17 = (bf16[2,256,256]{2,1,0:T(8,128)(2,1)}, bf16[2,256,256]{2,1,0:T(8,128)(2,1)S(1)}, u32[]{:S(2)}, u32[]{:S(2)}) collective-permute-start(bf16[2,256,256]{2,1,0:T(8,128)(2,1)} %get-tuple-element.90), channel_id=1, source_target_pairs={{0,0},{1,2},{2,4},{3,6},{4,17},{5,19},{6,21},{7,23},{8,9},{9,11},{... | collective-permute-start | bytes 786440 | tf_op jit(solution)/shard_map/ppermute | solution.py:272
  169.7 17.2 %collective-permute-start.18 = (bf16[2,256,256]{2,1,0:T(8,128)(2,1)}, bf16[2,256,256]{2,1,0:T(8,128)(2,1)S(1)}, u32[]{:S(2)}, u32[]{:S(2)}) collective-permute-start(bf16[2,256,256]{2,1,0:T(8,128)(2,1)} %get-tuple-element.91), channel_id=1, source_target_pairs={{0,31},{1,29},{2,0},{3,2},{4,12},{5,14},{6,17},{7,19},{8,4},{9,6},... | collective-permute-start | bytes 786440 | tf_op jit(solution)/shard_map/ppermute | solution.py:272
  171.6 19.1 %collective-permute-start.19 = (bf16[2,256,256]{2,1,0:T(8,128)(2,1)}, bf16[2,256,256]{2,1,0:T(8,128)(2,1)S(1)}, u32[]{:S(2)}, u32[]{:S(2)}) collective-permute-start(bf16[2,256,256]{2,1,0:T(8,128)(2,1)} %get-tuple-element.92), channel_id=1, source_target_pairs={{0,27},{1,25},{2,31},{3,29},{4,8},{5,10},{6,12},{7,14},{8,0},{9,2}... | collective-permute-start | bytes 786440 | tf_op jit(solution)/shard_map/ppermute | solution.py:272
  175.4 21.9 %collective-permute-start.20 = (bf16[2,256,256]{2,1,0:T(8,128)(2,1)}, bf16[2,256,256]{2,1,0:T(8,128)(2,1)S(1)}, u32[]{:S(2)}, u32[]{:S(2)}) collective-permute-start(bf16[2,256,256]{2,1,0:T(8,128)(2,1)} %get-tuple-element.93), channel_id=1, source_target_pairs={{0,22},{1,20},{2,27},{3,25},{4,7},{5,5},{6,8},{7,10},{8,31},{9,29}... | collective-permute-start | bytes 786440 | tf_op jit(solution)/shard_map/ppermute | solution.py:272
  181.7 15.6 %collective-permute-start.21 = (bf16[2,256,256]{2,1,0:T(8,128)(2,1)}, bf16[2,256,256]{2,1,0:T(8,128)(2,1)S(1)}, u32[]{:S(2)}, u32[]{:S(2)}) collective-permute-start(bf16[2,256,256]{2,1,0:T(8,128)(2,1)} %get-tuple-element.94), channel_id=1, source_target_pairs={{0,18},{1,16},{2,22},{3,20},{4,3},{5,1},{6,7},{7,5},{8,27},{9,25},... | collective-permute-start | bytes 786440 | tf_op jit(solution)/shard_map/ppermute | solution.py:272
  183.4 16.3 %collective-permute-start.22 = (bf16[2,256,256]{2,1,0:T(8,128)(2,1)}, bf16[2,256,256]{2,1,0:T(8,128)(2,1)S(1)}, u32[]{:S(2)}, u32[]{:S(2)}) collective-permute-start(bf16[2,256,256]{2,1,0:T(8,128)(2,1)} %get-tuple-element.95), channel_id=1, source_target_pairs={{0,13},{1,15},{2,18},{3,16},{4,30},{5,28},{6,3},{7,1},{8,22},{9,20... | collective-permute-start | bytes 786440 | tf_op jit(solution)/shard_map/ppermute | solution.py:272
  187.0 26.8 %collective-permute-start.23 = (bf16[2,256,256]{2,1,0:T(8,128)(2,1)}, bf16[2,256,256]{2,1,0:T(8,128)(2,1)S(1)}, u32[]{:S(2)}, u32[]{:S(2)}) collective-permute-start(bf16[2,256,256]{2,1,0:T(8,128)(2,1)} %get-tuple-element.96), channel_id=1, source_target_pairs={{0,9},{1,11},{2,13},{3,15},{4,26},{5,24},{6,30},{7,28},{8,18},{9,1... | collective-permute-start | bytes 786440 | tf_op jit(solution)/shard_map/ppermute | solution.py:272
  190.7 26.8 %collective-permute-start.24 = (bf16[2,256,256]{2,1,0:T(8,128)(2,1)}, bf16[2,256,256]{2,1,0:T(8,128)(2,1)S(1)}, u32[]{:S(2)}, u32[]{:S(2)}) collective-permute-start(bf16[2,256,256]{2,1,0:T(8,128)(2,1)} %get-tuple-element.97), channel_id=1, source_target_pairs={{0,4},{1,6},{2,9},{3,11},{4,21},{5,23},{6,26},{7,24},{8,13},{9,15}... | collective-permute-start | bytes 786440 | tf_op jit(solution)/shard_map/ppermute | solution.py:272
  234.0 17.0 %collective-permute-start.28 = (bf16[2,256,256]{2,1,0:T(8,128)(2,1)S(1)}, bf16[2,256,256]{2,1,0:T(8,128)(2,1)S(1)}, u32[]{:S(2)}, u32[]{:S(2)}) collective-permute-start(bf16[2,256,256]{2,1,0:T(8,128)(2,1)S(1)} %get-tuple-element.102), channel_id=1, source_target_pairs={{0,16},{1,17},{2,18},{3,19},{4,20},{5,21},{6,22},{7,23},{8,24},{9,... | collective-permute-start | bytes 786440 | tf_op jit(solution)/shard_map/ppermute | solution.py:272
  234.0 24.9 %collective-permute-start.29 = (bf16[2,256,256]{2,1,0:T(8,128)(2,1)S(1)}, bf16[2,256,256]{2,1,0:T(8,128)(2,1)S(1)}, u32[]{:S(2)}, u32[]{:S(2)}) collective-permute-start(bf16[2,256,256]{2,1,0:T(8,128)(2,1)S(1)} %get-tuple-element.103), channel_id=1, source_target_pairs={{0,20},{1,21},{2,22},{3,23},{4,16},{5,17},{6,18},{7,19},{8,28},{9,... | collective-permute-start | bytes 786440 | tf_op jit(solution)/shard_map/ppermute | solution.py:272
  235.9 23.0 %collective-permute-start.30 = (bf16[2,256,256]{2,1,0:T(8,128)(2,1)S(1)}, bf16[2,256,256]{2,1,0:T(8,128)(2,1)S(1)}, u32[]{:S(2)}, u32[]{:S(2)}) collective-permute-start(bf16[2,256,256]{2,1,0:T(8,128)(2,1)S(1)} %get-tuple-element.104), channel_id=1, source_target_pairs={{0,24},{1,25},{2,26},{3,27},{4,28},{5,29},{6,30},{7,31},{8,0},{9,1... | collective-permute-start | bytes 786440 | tf_op jit(solution)/shard_map/ppermute | solution.py:272
  237.0 22.0 %collective-permute-start.31 = (bf16[2,256,256]{2,1,0:T(8,128)(2,1)S(1)}, bf16[2,256,256]{2,1,0:T(8,128)(2,1)S(1)}, u32[]{:S(2)}, u32[]{:S(2)}) collective-permute-start(bf16[2,256,256]{2,1,0:T(8,128)(2,1)S(1)} %get-tuple-element.105), channel_id=1, source_target_pairs={{0,28},{1,29},{2,30},{3,31},{4,24},{5,25},{6,26},{7,27},{8,4},{9,5... | collective-permute-start | bytes 786440 | tf_op jit(solution)/shard_map/ppermute | solution.py:272
  (29 other events, 552.9 us)
Sparse Core Ops, SparseCore 0:
  25.1 52.9 all-gather.2

commit v3 on v1

--- a/solution.py
+++ b/solution.py
@@ -41,7 +41,7 @@
     return 2 * lax.rem(column - shard + columns * 16, columns) + core
 
 
-def split_kernel(shards, ids, w, *out):
+def prep_kernel(shards, ids, w, *out):
     _, rows, piece = out[0].shape
     tiles = piece // LANES
     stride = 2 * shards * tiles
@@ -51,23 +51,19 @@
             for j in range(tiles):
                 part = w[pl.ds(2 * (first + j) + kind, rows, stride=stride), :]
                 out[r][kind, :, j * LANES : (j + 1) * LANES] = part.astype(BF)
-
-
-def slice_kernel(ids, w, out):
-    particles, _, rows, cols = out.shape
+    particles, _, _, cols = out[shards].shape
     tiles = cols // LANES
-    stride = 2 * particles * tiles
     for p in range(particles):
         first = slice_index(ids, p // 2, p % 2, ids[SHARD], particles // 2) * tiles
         for kind in range(2):
             for j in range(tiles):
                 part = w[pl.ds(2 * (first + j) + kind, rows, stride=stride), :]
-                out[p, kind, :, j * LANES : (j + 1) * LANES] = part.astype(BF)
+                out[shards][p, kind, :, j * LANES : (j + 1) * LANES] = part.astype(BF)
 
 
 def up_kernel(shards, scale, ids, tokens, *refs):
     pieces = refs[:shards]
-    act_t, slope_t, down_t, normed, up_w, down_w, up_t = refs[shards:]
+    act_t, slope_t, down_t, up_w, down_w, up_t = refs[shards:]
     width, part = up_w.shape
     rows = width // shards
 
@@ -82,9 +78,7 @@
             up_t[:, span] = up_w[span, :].astype(F32).T.astype(BF)
             down_t[:, span] = down_w[span, :].astype(F32).T.astype(BF)
 
-    block = tokens[...].reshape(normed.shape)
-    normed[...] = block
-    u = lax.dot_general(up_t[...], block, NT, preferred_element_type=F32) * scale
+    u = lax.dot_general(up_t[...], tokens[...], NT, preferred_element_type=F32) * scale
     cdf = 0.5 * (1.0 + lax.erf(u * 0.7071067811865476))
     density = jnp.exp(-0.5 * u * u) * 0.3989422804014327
     act_t[...] = (u * cdf).astype(BF)
@@ -99,25 +93,23 @@
     width = c.shape[1]
     chunk = tokens // shards
     first = [
-        pltpu.make_async_copy(down_t, down, sems.at[2 * shards]),
-        pltpu.make_async_copy(slope_t, slope, sems.at[2 * shards + 1]),
+        pltpu.make_async_copy(down_t, down, sems.at[1]),
+        pltpu.make_async_copy(slope_t, slope, sems.at[2]),
     ]
     later = [
-        pltpu.make_async_copy(act_t, act, sems.at[2 * shards + 2]),
-        pltpu.make_async_copy(normed, n, sems.at[2 * shards + 3]),
+        pltpu.make_async_copy(act_t, act, sems.at[3]),
+        pltpu.make_async_copy(normed, n, sems.at[4]),
     ]
     for copy in first:
         copy.start()
-    pick(ids, sources, c, sems)
+    pick(ids, sources, c, sems.at[0])
     for copy in later:
         copy.start()
     for copy in first:
         copy.wait()
+    pltpu.make_async_copy(c, c, sems.at[0]).wait()
 
     def back(i, carry):
-        for turn in range(2):
-            here = c.at[pl.ds(0, chunk // 2), :]
-            pltpu.make_async_copy(here, here, sems.at[2 * i + turn]).wait()
         at = pl.multiple_of(i * chunk, chunk)
         b = lax.dot_general(down[...], c[pl.ds(at, chunk), :], NT, preferred_element_type=F32)
         grad[:, pl.ds(at, chunk)] = (b * (slope[:, pl.ds(at, chunk)].astype(F32) * back_scale)).astype(BF)
@@ -286,39 +278,30 @@
 
     everyone = range(shards)
     half_rows = tok_rows // 2
-    if shards == 4:
-        mine = lax.dynamic_slice(cotangent[0], (core * half_rows, 0), (half_rows, width))
-        give = lax.dynamic_slice(cotangent[0], ((1 - core) * half_rows, 0), (half_rows, width))
-        other = move(give, swap_of(everyone))
-        is_own = core == proc
-        here = jnp.where(is_own, mine, other)
-        away = jnp.where(is_own, other, mine)
-
     share = tok_rows // particles
     index = lax.dynamic_slice(batch_index, (own * share,), (share,))
     picked = jnp.take(pool, index, axis=0).astype(F32)
     normed = (picked * lax.rsqrt(jnp.mean(picked * picked, axis=1, keepdims=True) + 1e-06)).astype(BF)
-    normed = lax.all_to_all(jnp.broadcast_to(normed[None], (shards, share, width)), "shard", 0, 0, tiled=True)
-    normed = lax.all_gather(normed[None], "particle", axis=0, tiled=True)
+    normed = jnp.stack(
+        [move(normed, [(dev(m, c, s), dev(m, c, (s + k) % shards)) for m, c, s in devices]) for k in range(shards)]
+    )
+    normed = lax.all_gather(normed[None], "particle", axis=0, tiled=True).reshape(tokens, width)
 
     w_flat = flat(weights)
     steps = max(rows // 64, 1)
     lines = w_flat.shape[0] // steps
-    w_spec = pl.BlockSpec((lines, LANES), lambda i: (i, 0))
-    prepared = pl.pallas_call(
-        functools.partial(split_kernel, shards),
+    *prepared, slices = pl.pallas_call(
+        functools.partial(prep_kernel, shards),
         grid=(steps,),
-        out_shape=[jax.ShapeDtypeStruct((2, rows, part), BF)] * shards,
-        in_specs=[smem_spec(), w_spec],
-        out_specs=[pl.BlockSpec((2, rows // steps, part), lambda i: (0, i, 0))] * shards,
-        compiler_params=params(8),
-        name="split",
+        out_shape=[jax.ShapeDtypeStruct((2, rows, part), BF)] * shards
+        + [jax.ShapeDtypeStruct((particles, 2, rows, cols), BF)],
+        in_specs=[smem_spec(), pl.BlockSpec((lines, LANES), lambda i: (i, 0))],
+        out_specs=[pl.BlockSpec((2, rows // steps, part), lambda i: (0, i, 0))] * shards
+        + [pl.BlockSpec((particles, 2, rows // steps, cols), lambda i: (0, 0, i, 0))],
+        compiler_params=params(56),
+        name="prep",
     )(ids, w_flat)
 
-    if shards == 4:
-        here, away, w_late, *prepared = lax.optimization_barrier((here, away, w_flat, *prepared))
-    else:
-        w_late, *prepared = lax.optimization_barrier((w_flat, *prepared))
     w_routes = []
     for r in range(shards):
         pairs = []
@@ -327,73 +310,119 @@
             pairs.append((dev(m, c, s), dev(m, q % 2, c * half + q // 2)))
         w_routes.append(pairs)
 
+    whole = lax.all_to_all(slices, "particle", 0, 0, tiled=True)
+
+    def gather_row(ids, which, turn):
+        k = lax.rem(ids[SHARD] - which + shards, shards)
+        return (turn * (particles // 2) * shards + k) * share
+
+    def place(ids, ref, held, sem, which, turn, start=0):
+        row = gather_row(ids, which, turn)
+        for i in range(particles // 2):
+            to = pl.multiple_of(row + i * shards * share, share)
+            pltpu.make_async_copy(
+                ref.at[pl.ds(start + i * share, share), :], held.at[pl.ds(to, share), :], sem
+            ).start()
+
     if shards == 4:
-        inner, edge = (1, 2), (0, 3)
-        far = [(dev(m, c, s), dev(m, c, 1 if s == 3 else 2)) for m, c, s in devices if s in edge]
-        near = [(dev(m, c, s), dev(m, c, 3 - s)) for m, c, s in devices if s in inner]
-        outward = [(dev(m, c, s), dev(m, c, s ^ 1)) for m, c, s in devices if s in inner]
-        pair_c = move(here, [(dev(m, c, s), dev(m, c, s ^ 1)) for m, c, s in devices])
-        near_c, far_c = move(away, near), move(away, far)
+        cot = cotangent[0]
+        inner = jnp.logical_or(shard == 1, shard == 2)
+        flip = jnp.where(jnp.logical_or(inner, core == proc), 0, 1)
+        first_routes, second_routes = [], []
+        for e in range(2):
+            one, two = [], []
+            for m, c, s in devices:
+                at_home, is_inner = c == s // half, s in (1, 2)
+                if not at_home:
+                    to, turn = (3 - s, e) if is_inner else (1 if s == 3 else 2, 1 - e)
+                    one.append((dev(m, c, s), dev(m, c ^ turn, to)))
+                elif is_inner:
+                    one.append((dev(m, c, s), dev(m, c ^ e, s ^ 1)))
+                else:
+                    two.append((dev(m, c, s), dev(m, c ^ e, s ^ 1)))
+                if is_inner:
+                    two.append((dev(m, c, s), dev(m, c, s ^ 1)))
+            first_routes.append(one)
+            second_routes.append(two)
+        halves = [
+            lax.dynamic_slice(cot, (((core + e + flip) % 2) * half_rows, 0), (half_rows, width)) for e in range(2)
+        ]
+        alpha = [move(x, route) for x, route in zip(halves, first_routes)]
+        own_c = move(cot, [(dev(m, c, s), dev(m, 1 - c, s)) for m, c, s in devices if c == s // half])
         w_pieces = [move(x, route) for x, route in zip(prepared[:2], w_routes[:2])]
-        near_c, far_c, pair_c, w_pieces[0], w_pieces[1], prepared[2], prepared[3] = lax.optimization_barrier(
-            (near_c, far_c, pair_c, *w_pieces, *prepared[2:])
-        )
-        w_pieces += [move(x, route) for x, route in zip(prepared[2:], w_routes[2:])]
-        cross = jnp.concatenate([near_c, far_c])
-        cross = jnp.where(jnp.logical_or(shard == 1, shard == 2), cross, move(cross, outward))
-        got = jnp.concatenate([here, pair_c])
-        sources = [got, cross, move(got, swap_of(everyone)), move(cross, swap_of(everyone))]
-
-        def pick(ids, refs, held, sems):
-            s, core = ids[SHARD], ids[CORE]
+        alpha, own_c, w_pieces, last = lax.optimization_barrier((alpha, own_c, w_pieces, prepared[2:]))
+        beta = [move(jnp.where(inner, a, x), route) for a, x, route in zip(alpha, halves, second_routes)]
+        w_pieces = w_pieces + [move(x, route) for x, route in zip(last, w_routes[2:])]
+        alpha_x = [move(x, swap_of(everyone)) for x in alpha]
+        beta, alpha_x, w_pieces, whole = lax.optimization_barrier((beta, alpha_x, w_pieces, whole))
+        beta_x = [move(x, swap_of(everyone)) for x in beta]
+        sources = [cot, own_c, *alpha, *alpha_x, *beta, *beta_x]
+
+        def pick(ids, refs, held, sem):
+            s, core, proc = ids[SHARD], ids[CORE], ids[PROC]
             low = s < 2
-            place = [s, s + 1 - 2 * lax.rem(s, 2), jnp.where(low, 2, 1), jnp.where(low, 3, 0)]
-            for i, ref in enumerate(refs):
-                turn = core if i < 2 else 1 - core
-                for k in range(2):
-                    at = 2 * place[2 * (i % 2) + k] + turn
-                    to = pl.multiple_of(at * half_rows, half_rows)
-                    pltpu.make_async_copy(
-                        ref.at[pl.ds(k * half_rows, half_rows), :], held.at[pl.ds(to, half_rows), :], sems.at[at]
-                    ).start()
+            near, far, pair = jnp.where(low, 2, 1), jnp.where(low, 3, 0), s + 1 - 2 * lax.rem(s, 2)
+            side = lax.rem(core + proc, 2)
+            is_inner = jnp.logical_or(s == 1, s == 2)
+
+            def own(ref):
+                for turn in range(2):
+                    place(ids, ref, held, sem, s, turn, turn * half_rows)
+
+            def others(main, main_x, rest, rest_x):
+                for e in range(2):
+                    same = side == e
+                    place(ids, main[e], held, sem, jnp.where(same, near, far), core)
+                    place(ids, main_x[e], held, sem, jnp.where(same, far, near), 1 - core)
+
+                    @pl.when(same)
+                    def _():
+                        place(ids, rest[e], held, sem, pair, core)
+                        place(ids, rest_x[1 - e], held, sem, pair, 1 - core)
+
+            @pl.when(side == 0)
+            def _():
+                own(refs[0])
+
+            @pl.when(side == 1)
+            def _():
+                own(refs[1])
+
+            @pl.when(is_inner)
+            def _():
+                others(refs[2:4], refs[4:6], refs[6:8], refs[8:10])
+
+            @pl.when(jnp.logical_not(is_inner))
+            def _():
+                others(refs[6:8], refs[8:10], refs[2:4], refs[4:6])
     else:
         full = lax.all_gather(cotangent[0], "shard", axis=0, tiled=True)
         sources = [jnp.where(core == proc, full, move(full, swap_of(everyone)))]
         w_pieces = [move(x, route) for x, route in zip(prepared, w_routes)]
 
-        def pick(ids, refs, held, sems):
-            for i in range(2 * shards):
-                span = pl.ds(i * half_rows, half_rows)
-                pltpu.make_async_copy(refs[0].at[span, :], held.at[span, :], sems.at[i]).start()
-
-    slices = pl.pallas_call(
-        slice_kernel,
-        grid=(steps,),
-        out_shape=jax.ShapeDtypeStruct((particles, 2, rows, cols), BF),
-        in_specs=[smem_spec(), w_spec],
-        out_specs=pl.BlockSpec((particles, 2, rows // steps, cols), lambda i: (0, 0, i, 0)),
-        compiler_params=params(8),
-        name="slices",
-    )(ids, w_late)
-    whole = lax.all_to_all(slices, "particle", 0, 0, tiled=True)
-    per = BLOCK // share
-    halves = tok_rows // BLOCK
-    act_t, slope_t, down_t, normed = pl.pallas_call(
+        def pick(ids, refs, held, sem):
+            def one(which, carry):
+                for turn in range(2):
+                    start = pl.multiple_of(which * tok_rows + turn * half_rows, half_rows)
+                    place(ids, refs[0], held, sem, which, turn, start)
+                return carry
+
+            lax.fori_loop(0, shards, one, 0)
+
+    act_t, slope_t, down_t = pl.pallas_call(
         functools.partial(up_kernel, shards, width ** (-0.5)),
         grid=(blocks,),
         out_shape=[
             jax.ShapeDtypeStruct((part, tokens), BF),
             jax.ShapeDtypeStruct((part, tokens), BF),
             jax.ShapeDtypeStruct((part, width), BF),
-            jax.ShapeDtypeStruct((tokens, width), BF),
         ],
-        in_specs=[smem_spec(), pl.BlockSpec((per, 1, share, width), lambda i: (i % halves, i // halves, 0, 0))]
+        in_specs=[smem_spec(), pl.BlockSpec((BLOCK, width), lambda i: (i, 0))]
         + [pl.BlockSpec((2, rows, part), lambda i: (0, 0, 0))] * shards,
         out_specs=[
             pl.BlockSpec((part, BLOCK), lambda i: (0, i)),
             pl.BlockSpec((part, BLOCK), lambda i: (0, i)),
             pl.BlockSpec((part, width), lambda i: (0, 0)),
-            pl.BlockSpec((BLOCK, width), lambda i: (i, 0)),
         ],
         scratch_shapes=[pltpu.VMEM((width, part), BF), pltpu.VMEM((width, part), BF), pltpu.VMEM((part, width), BF)],
         compiler_params=params(24),
@@ -401,7 +430,6 @@
     )(ids, normed, *w_pieces)
 
     grad_scale = 1.0 / (tokens * width)
-    held = 2 * (2 * tokens * width + 3 * tokens * part + 3 * width * part)
     scores = pl.pallas_call(
         functools.partial(
             grad_kernel,
@@ -423,13 +451,24 @@
             pltpu.VMEM((part, tokens), BF),
             pltpu.VMEM((part, width), BF),
             pltpu.VMEM((2, width, part), BF),
-            pltpu.SemaphoreType.DMA((2 * shards + 4,)),
+            pltpu.SemaphoreType.DMA((particles + 5,)),
         ],
-        compiler_params=params(held // MIB + 8),
+        compiler_params=params(56),
         name="grads",
     )(ids, normed, act_t, slope_t, down_t, *sources)
 
-    whole, *scores = lax.optimization_barrier((whole, *scores))
+    ratio = particles // shards
+    arrived = []
+    for t in range(particles):
+        pairs = []
+        for m, c, s in devices:
+            mine, q = 2 * m + s // half, 2 * (s % half) + c
+            u = (mine + ratio * q - t) % particles
+            z, e = u // ratio, q * ratio + u % ratio
+            pairs.append((dev(m, c, s), dev(e // 2 + z, e % 2, z)))
+        arrived.append(move(scores[t], pairs))
+
+    whole, arrived[0] = lax.optimization_barrier((whole, arrived[0]))
     pair_list = [(i, j) for i in range(particles) for j in range(i)]
     partial = pl.pallas_call(
         distance_kernel,
@@ -458,17 +497,6 @@
         [(scale * kernel).reshape(-1), scale * repulse * jnp.sum(kernel, axis=1), repulse[None]]
     )
 
-    ratio = particles // shards
-    arrived = []
-    for t in range(particles):
-        pairs = []
-        for m, c, s in devices:
-            mine, q = 2 * m + s // half, 2 * (s % half) + c
-            u = (mine + ratio * q - t) % particles
-            z, e = u // ratio, q * ratio + u % ratio
-            pairs.append((dev(m, c, s), dev(e // 2 + z, e % 2, z)))
-        arrived.append(move(scores[t], pairs))
-
     fields = pl.pallas_call(
         functools.partial(stein_kernel, shards, particles),
         out_shape=[jax.ShapeDtypeStruct((2, rows, cols), BF)] * particles,
@@ -499,7 +527,7 @@
         in_specs=[smem_spec()] + [state_spec] * 3 + [any_spec()] * particles,
         out_specs=[state_spec] * 4,
         scratch_shapes=[pltpu.VMEM((2, rows, hidden), BF), pltpu.SemaphoreType.DMA((particles,))],
-        compiler_params=params(16),
+        compiler_params=params(56),
         name="adam",
     )(ids, w_flat, flat(first_moment), flat(second_moment), *back)
     return tuple(unflat(x) for x in outs)

time: 298 us -> 296 us (level)
  blocking collectives: 30.3 us -> 6.66 us
  waiting for transfers between devices: 91.5 us -> 111 us
  local copies, waits for them, and re-layouts: 26.7 us -> 17.3 us
  Pallas kernels: 43.5 us -> 51.8 us
    ppermute x26 -> x31, waiting for transfers between devices: 91.5 us -> 111 us  [move(): return lax.ppermute(x, AXES, pairs)]
    all_to_all x1 -> x0, blocking collectives: 16.1 us -> none  [local(): lax.all_to_all(jnp.broadcast_to(normed[None], (shards, share, width)), 's...]
    unnamed x56 -> x52, local copies, waits for them, and re-layouts: 21.6 us -> 13.3 us
    all_to_all x1, blocking collectives: 14.2 us -> 6.66 us  [local(): sums = jnp.sum(lax.all_to_all(copies, axis, 0, 0, tiled=True), axis=(0, 1))]
    pallas_call x1, Pallas kernels: 10.1 us -> 15.5 us  [local(): pl.pallas_call(functools.partial(adam_kernel, particles), grid=(steps,),...]
    ppermute x26 -> x31, starting transfers between devices: 73.8 us -> 77.2 us  [move(): return lax.ppermute(x, AXES, pairs)]
    pallas_call x2 -> x1, Pallas kernels: 6.57 us -> 7.75 us  [local(): pl.pallas_call(functools.partial(prep_kernel, shards), grid=(steps,), out...]
  transfers between devices with their start and end apart: 29 -> 34, of which waited for: 13 -> 16; matrix products, arithmetic and copies ran while one was open for 3% -> 2% of each run, Pallas kernels for 9% -> 5%
where the time goes in v3:
time: 296 us; the launch traced here: 293 us
  waiting for transfers between devices  111 us (38%)
  starting transfers between devices  86.5 us (29%)
  Pallas kernels  51.8 us (18%)
  local copies, waits for them, and re-layouts  17.3 us (6%)
  between operations  15.1 us (5%)
  blocking collectives  6.66 us (2%)
  other arithmetic  5.01 us (2%)
    ppermute x31, waiting for transfers between devices, move(): return lax.ppermute(x, AXES, pairs)  111 us
    ppermute x31, starting transfers between devices, move(): return lax.ppermute(x, AXES, pairs)  77.2 us
    pallas_call x1, Pallas kernels, local(): pl.pallas_call(functools.partial(adam_kernel, particles), grid=(steps,),...  15.5 us
    pallas_call x1, Pallas kernels, local(): pl.pallas_call(functools.partial(grad_kernel, shards, particles, -width *...  13.7 us
    unnamed x52, local copies, waits for them, and re-layouts  13.3 us
    pallas_call x1, Pallas kernels, local(): pl.pallas_call(functools.partial(prep_kernel, shards), grid=(steps,), out...  7.75 us
    pallas_call x1, Pallas kernels, local(): pl.pallas_call(functools.partial(up_kernel, shards, width ** (-0.5)), gri...  6.99 us
    all_to_all x1, blocking collectives, local(): sums = jnp.sum(lax.all_to_all(copies, axis, 0, 0, tiled=True), axis=(0, 1))  6.66 us
  transfers between devices with their start and end apart: 34, of which 16 were waited for; matrix products, arithmetic and copies ran while one was open for 2% of the time, Pallas kernels for 5%

profile of v3, /device:TPU:23, one launch (start us, length us, event | category | flops | bytes accessed | tf_op | source)
XLA Modules:
  0.0 293.1 jit_solution(11800442642269253940)
XLA Ops:
  14.2 5.5 %collective-permute-done.12 = bf16[64,1024]{1,0:T(8,128)(2,1)S(1)} collective-permute-done((bf16[64,1024]{1,0:T(8,128)(2,1)S(1)}, bf16[64,1024]{1,0:T(8,128)(2,1)S(1)}, u32[]{:S(2)}, u32[]{:S(2)}) %collective-permute-start.12) | collective-permute-done | bytes 131104 | tf_op jit(solution)/shard_map/ppermute | solution.py:268
  27.5 7.8 %prep.1 = (bf16[2,256,512]{2,1,0:T(8,128)(2,1)}, bf16[2,256,512]{2,1,0:T(8,128)(2,1)}, bf16[2,256,512]{2,1,0:T(8,128)(2,1)}, bf16[2,256,512]{2,1,0:T(8,128)(2,1)}, bf16[8,2,256,256]{3,2,1,0:T(8,128)(2,1)}) custom-call(s32[5]{0:T(128)} %stack.36.ids, f32[8192,128]{1,0:T(8,128)} %bitcast.60), custom_call_target="tpu_custom_call" | custom-call | tf_op jit(solution)/shard_map/prep/pallas_call | solution.py:293
  40.6 3.9 %collective-permute-start = (bf16[256,1024]{1,0:T(8,128)(2,1)}, bf16[256,1024]{1,0:T(8,128)(2,1)}, u32[]{:S(2)}, u32[]{:S(2)}) collective-permute-start(bf16[256,1024]{1,0:T(8,128)(2,1)} %get-tuple-element.99), channel_id=1, source_target_pairs={{1,0},{2,1},{3,5},{4,2},{5,6},{6,7},{9,8},{10,9},{11,13},{12,10},{... | collective-permute-start | bytes 1572872 | tf_op jit(solution)/shard_map/ppermute | solution.py:268
  44.5 5.8 %collective-permute-start.1 = (bf16[256,1024]{1,0:T(8,128)(2,1)}, bf16[256,1024]{1,0:T(8,128)(2,1)}, u32[]{:S(2)}, u32[]{:S(2)}) collective-permute-start(bf16[256,1024]{1,0:T(8,128)(2,1)} %get-tuple-element.98), channel_id=1, source_target_pairs={{1,4},{2,5},{3,1},{4,6},{5,2},{6,3},{9,12},{10,13},{11,9},{12,14},... | collective-permute-start | bytes 1572872 | tf_op jit(solution)/shard_map/ppermute | solution.py:268
  50.3 4.0 %all-to-all-start = ((bf16[8,2,256,256]{3,2,1,0:T(8,128)(2,1)}), bf16[8,2,256,256]{3,2,1,0:T(8,128)(2,1)S(1)}, u32[]{:S(2)}, u32[]{:S(2)}) async-start(bf16[8,2,256,256]{3,2,1,0:T(8,128)(2,1)} %get-tuple-element.60), calls=%async_computation | async-start | bytes 4194304 | tf_op jit(solution)/shard_map/all_to_all | solution.py:313
  55.1 23.5 %collective-permute-done.refs_2_ = bf16[256,1024]{1,0:T(8,128)(2,1)} collective-permute-done((bf16[256,1024]{1,0:T(8,128)(2,1)}, bf16[256,1024]{1,0:T(8,128)(2,1)}, u32[]{:S(2)}, u32[]{:S(2)}) %collective-permute-start) | collective-permute-done | bytes 524320 | tf_op jit(solution)/shard_map/ppermute | solution.py:268
  81.0 7.0 %collective-permute-start.8 = (bf16[256,1024]{1,0:T(8,128)(2,1)}, bf16[256,1024]{1,0:T(8,128)(2,1)S(1)}, u32[]{:S(2)}, u32[]{:S(2)}) collective-permute-start(bf16[256,1024]{1,0:T(8,128)(2,1)} %collective-permute-done.1.refs_3_), channel_id=1, source_target_pairs={{0,4},{1,5},{2,6},{3,7},{4,0},{5,1},{6,2},{7,3},{8,12},{9,13},{10,... | collective-permute-start | bytes 1572872 | tf_op jit(solution)/shard_map/ppermute | solution.py:268
  89.2 3.7 %collective-permute-start.5 = (bf16[256,1024]{1,0:T(8,128)(2,1)S(1)}, bf16[256,1024]{1,0:T(8,128)(2,1)S(1)}, u32[]{:S(2)}, u32[]{:S(2)}) collective-permute-start(bf16[256,1024]{1,0:T(8,128)(2,1)S(1)} %broadcast_select_fusion.1), channel_id=1, source_target_pairs={{0,1},{1,0},{2,3},{5,4},{6,7},{7,6},{8,9},{9,8},{10,11},{13,12},{1... | collective-permute-start | bytes 1572872 | tf_op jit(solution)/shard_map/ppermute | solution.py:268
  96.9 24.6 %collective-permute-done.5.refs_6_ = bf16[256,1024]{1,0:T(8,128)(2,1)S(1)} collective-permute-done((bf16[256,1024]{1,0:T(8,128)(2,1)S(1)}, bf16[256,1024]{1,0:T(8,128)(2,1)S(1)}, u32[]{:S(2)}, u32[]{:S(2)}) %collective-permute-start.5) | collective-permute-done | bytes 524320 | tf_op jit(solution)/shard_map/ppermute | solution.py:268
  121.5 6.5 %collective-permute-done.10.refs_3_ = bf16[2,256,512]{2,1,0:T(8,128)(2,1)S(1)} collective-permute-done((bf16[2,256,512]{2,1,0:T(8,128)(2,1)}, bf16[2,256,512]{2,1,0:T(8,128)(2,1)S(1)}, u32[]{:S(2)}, u32[]{:S(2)}) %collective-permute-start.10) | collective-permute-done | bytes 524320 | tf_op jit(solution)/shard_map/ppermute | solution.py:268
  136.1 7.0 %up.1 = (bf16[512,2048]{1,0:T(8,128)(2,1)S(1)}, bf16[512,2048]{1,0:T(8,128)(2,1)S(1)}, bf16[512,1024]{1,0:T(8,128)(2,1)S(1)}) custom-call(s32[5]{0:T(128)S(1)} %copy-done.11, bf16[2048,1024]{1,0:T(8,128)(2,1)S(1)} %bitcast.59, bf16[2,256,512]{2,1,0:T(8,128)(2,1)S(1)} %collective-permute-done.3.refs_0_, ...), custom_call_target="tpu_custom_call" | custom-call | tf_op jit(solution)/shard_map/up/pallas_call | solution.py:412
  146.7 13.7 %grads.1 = (bf16[2,256,256]{2,1,0:T(8,128)(2,1)}, bf16[2,256,256]{2,1,0:T(8,128)(2,1)}, bf16[2,256,256]{2,1,0:T(8,128)(2,1)}, bf16[2,256,256]{2,1,0:T(8,128)(2,1...) custom-call(s32[5]{0:T(128)} %stack.36.ids, ...), custom_call_target="tpu_custom_call" | custom-call | tf_op jit(solution)/shard_map/grads/pallas_call | solution.py:433
  162.4 8.2 %collective-permute-done.16.refs_0_ = bf16[2,256,256]{2,1,0:T(8,128)(2,1)S(1)} collective-permute-done((bf16[2,256,256]{2,1,0:T(8,128)(2,1)}, bf16[2,256,256]{2,1,0:T(8,128)(2,1)S(1)}, u32[]{:S(2)}, u32[]{:S(2)}) %collective-permute-start.16) | collective-permute-done | bytes 262176 | tf_op jit(solution)/shard_map/ppermute | solution.py:268
  172.8 6.7 %all_to_all.15 = f32[8,1,128]{2,1,0:T(1,128)S(1)} all-to-all(f32[8,1,128]{2,1,0:T(1,128)S(1)} %broadcast_in_dim.44), channel_id=1, replica_groups=mesh['particle'=8,'shard'=4] {'particle'}, dimensions={0} | all-to-all | bytes 8192 | tf_op jit(solution)/shard_map/all_to_all | solution.py:485
  180.1 5.3 %all-to-all-start.2 = ((f32[4,1,128]{2,1,0:T(1,128)}), f32[4,1,128]{2,1,0:T(1,128)S(1)}, u32[]{:S(2)}, u32[]{:S(2)}) async-start(f32[4,1,128]{2,1,0:T(1,128)} %broadcast_in_dim.45), calls=%async_computation.2 | async-start | bytes 4096 | tf_op jit(solution)/shard_map/all_to_all | solution.py:485
  202.2 6.4 %collective-permute-start.23 = (bf16[2,256,256]{2,1,0:T(8,128)(2,1)}, bf16[2,256,256]{2,1,0:T(8,128)(2,1)S(1)}, u32[]{:S(2)}, u32[]{:S(2)}) collective-permute-start(bf16[2,256,256]{2,1,0:T(8,128)(2,1)} %get-tuple-element.83), channel_id=1, source_target_pairs={{0,4},{1,6},{2,9},{3,11},{4,21},{5,23},{6,26},{7,24},{8,13},{9,15}... | collective-permute-start | bytes 786440 | tf_op jit(solution)/shard_map/ppermute | solution.py:268
  211.1 3.8 %collective-permute-done.21.refs_5_ = bf16[2,256,256]{2,1,0:T(8,128)(2,1)} collective-permute-done((bf16[2,256,256]{2,1,0:T(8,128)(2,1)}, bf16[2,256,256]{2,1,0:T(8,128)(2,1)}, u32[]{:S(2)}, u32[]{:S(2)}) %collective-permute-start.21) | collective-permute-done | bytes 262176 | tf_op jit(solution)/shard_map/ppermute | solution.py:268
  215.0 4.8 %collective-permute-done.22.refs_6_ = bf16[2,256,256]{2,1,0:T(8,128)(2,1)S(1)} collective-permute-done((bf16[2,256,256]{2,1,0:T(8,128)(2,1)}, bf16[2,256,256]{2,1,0:T(8,128)(2,1)S(1)}, u32[]{:S(2)}, u32[]{:S(2)}) %collective-permute-start.22) | collective-permute-done | bytes 262176 | tf_op jit(solution)/shard_map/ppermute | solution.py:268
  219.8 5.6 %collective-permute-done.23.refs_7_ = bf16[2,256,256]{2,1,0:T(8,128)(2,1)S(1)} collective-permute-done((bf16[2,256,256]{2,1,0:T(8,128)(2,1)}, bf16[2,256,256]{2,1,0:T(8,128)(2,1)S(1)}, u32[]{:S(2)}, u32[]{:S(2)}) %collective-permute-start.23) | collective-permute-done | bytes 262176 | tf_op jit(solution)/shard_map/ppermute | solution.py:268
  225.4 5.9 %stein.1 = (bf16[2,256,256]{2,1,0:T(8,128)(2,1)S(1)}, bf16[2,256,256]{2,1,0:T(8,128)(2,1)S(1)}, bf16[2,256,256]{2,1,0:T(8,128)(2,1)S(1)}, bf16[2,256,256]{2,1,0:...) custom-call(s32[5]{0:T(128)S(1)} %copy-done.12, ...), custom_call_target="tpu_custom_call" | custom-call | tf_op jit(solution)/shard_map/stein/pallas_call | solution.py:500
  232.0 6.6 %collective-permute-start.24 = (bf16[2,256,256]{2,1,0:T(8,128)(2,1)S(1)}, bf16[2,256,256]{2,1,0:T(8,128)(2,1)S(1)}, u32[]{:S(2)}, u32[]{:S(2)}) collective-permute-start(bf16[2,256,256]{2,1,0:T(8,128)(2,1)S(1)} %get-tuple-element.85), channel_id=1, source_target_pairs={{0,4},{1,5},{2,6},{3,7},{4,0},{5,1},{6,2},{7,3},{8,12},{9,13},{10,... | collective-permute-start | bytes 786440 | tf_op jit(solution)/shard_map/ppermute | solution.py:268
  238.6 5.4 %collective-permute-start.25 = (bf16[2,256,256]{2,1,0:T(8,128)(2,1)S(1)}, bf16[2,256,256]{2,1,0:T(8,128)(2,1)S(1)}, u32[]{:S(2)}, u32[]{:S(2)}) collective-permute-start(bf16[2,256,256]{2,1,0:T(8,128)(2,1)S(1)} %get-tuple-element.86), channel_id=1, source_target_pairs={{0,8},{1,9},{2,10},{3,11},{4,12},{5,13},{6,14},{7,15},{8,16},{9,17... | collective-permute-start | bytes 786440 | tf_op jit(solution)/shard_map/ppermute | solution.py:268
  255.4 14.5 %collective-permute-done.28.refs_5_ = bf16[2,256,256]{2,1,0:T(8,128)(2,1)S(1)} collective-permute-done((bf16[2,256,256]{2,1,0:T(8,128)(2,1)S(1)}, bf16[2,256,256]{2,1,0:T(8,128)(2,1)S(1)}, u32[]{:S(2)}, u32[]{:S(2)}) %collective-permute-start.28) | collective-permute-done | bytes 262176 | tf_op jit(solution)/shard_map/ppermute | solution.py:268
  270.8 15.5 %adam.1 = (f32[8192,128]{1,0:T(8,128)}, f32[8192,128]{1,0:T(8,128)}, f32[8192,128]{1,0:T(8,128)}, f32[8192,128]{1,0:T(8,128)}) custom-call(s32[5]{0:T(128)} %stack.36.ids, f32[8192,128]{1,0:T(8,128)} %bitcast.61, f32[8192,128]{1,0:T(8,128)} %bitcast.62, f32[8192,128]{1,0:T(8,128)} %bitcast.63, bf16[2,256,256]{2,1,0:T(8,128)(2,1)} %copy-done.10, ...), custom_call_target="tpu_custom_call" | custom-call | tf_op jit(solution)/shard_map/adam/pallas_call | solution.py:523
  (131 shorter events, 76.4 us)
Async XLA Ops:
  7.2 124.6 %all-gather.3.cloned.1.call-start = ((), (), s32[]{:S(2)}) async-start(), calls=%async_computation.3 | async-start | bytes 4718592 | tf_op jit(solution)/shard_map/all_gather | solution.py:288
  23.4 55.1 %collective-permute-start.2 = (bf16[512,1024]{1,0:T(8,128)(2,1)}, bf16[512,1024]{1,0:T(8,128)(2,1)}, u32[]{:S(2)}, u32[]{:S(2)}) collective-permute-start(bf16[512,1024]{1,0:T(8,128)(2,1)} %bitcast.64), channel_id=1, source_target_pairs={{0,4},{1,5},{6,2},{7,3},{8,12},{9,13},{14,10},{15,11},{16,20},{17,... | collective-permute-start | bytes 3145736 | tf_op jit(solution)/shard_map/ppermute | solution.py:268
  35.3 19.8 %collective-permute-start.3 = (bf16[2,256,512]{2,1,0:T(8,128)(2,1)}, bf16[2,256,512]{2,1,0:T(8,128)(2,1)S(1)}, u32[]{:S(2)}, u32[]{:S(2)}) collective-permute-start(bf16[2,256,512]{2,1,0:T(8,128)(2,1)} %get-tuple-element.50), channel_id=1, source_target_pairs={{0,0},{1,4},{2,1},{3,5},{4,2},{5,6},{6,3},{7,7},{8,8},{9,12},{10,9... | collective-permute-start | bytes 1572872 | tf_op jit(solution)/shard_map/ppermute | solution.py:268
  37.8 17.2 %collective-permute-start.4 = (bf16[2,256,512]{2,1,0:T(8,128)(2,1)}, bf16[2,256,512]{2,1,0:T(8,128)(2,1)S(1)}, u32[]{:S(2)}, u32[]{:S(2)}) collective-permute-start(bf16[2,256,512]{2,1,0:T(8,128)(2,1)} %get-tuple-element.51), channel_id=1, source_target_pairs={{0,5},{1,0},{2,4},{3,1},{4,7},{5,2},{6,6},{7,3},{8,13},{9,8},{10,1... | collective-permute-start | bytes 1572872 | tf_op jit(solution)/shard_map/ppermute | solution.py:268
  40.6 37.9 %collective-permute-start = (bf16[256,1024]{1,0:T(8,128)(2,1)}, bf16[256,1024]{1,0:T(8,128)(2,1)}, u32[]{:S(2)}, u32[]{:S(2)}) collective-permute-start(bf16[256,1024]{1,0:T(8,128)(2,1)} %get-tuple-element.99), channel_id=1, source_target_pairs={{1,0},{2,1},{3,5},{4,2},{5,6},{6,7},{9,8},{10,9},{11,13},{12,10},{... | collective-permute-start | bytes 1572872 | tf_op jit(solution)/shard_map/ppermute | solution.py:268
  44.5 34.0 %collective-permute-start.1 = (bf16[256,1024]{1,0:T(8,128)(2,1)}, bf16[256,1024]{1,0:T(8,128)(2,1)}, u32[]{:S(2)}, u32[]{:S(2)}) collective-permute-start(bf16[256,1024]{1,0:T(8,128)(2,1)} %get-tuple-element.98), channel_id=1, source_target_pairs={{1,4},{2,5},{3,1},{4,6},{5,2},{6,3},{9,12},{10,13},{11,9},{12,14},... | collective-permute-start | bytes 1572872 | tf_op jit(solution)/shard_map/ppermute | solution.py:268
  50.3 81.0 %all-to-all-start = ((bf16[8,2,256,256]{3,2,1,0:T(8,128)(2,1)}), bf16[8,2,256,256]{3,2,1,0:T(8,128)(2,1)S(1)}, u32[]{:S(2)}, u32[]{:S(2)}) async-start(bf16[8,2,256,256]{3,2,1,0:T(8,128)(2,1)} %get-tuple-element.60), calls=%async_computation | async-start | bytes 4194304 | tf_op jit(solution)/shard_map/all_to_all | solution.py:313
  79.7 15.2 %collective-permute-start.6 = (bf16[256,1024]{1,0:T(8,128)(2,1)S(1)}, bf16[256,1024]{1,0:T(8,128)(2,1)S(1)}, u32[]{:S(2)}, u32[]{:S(2)}) collective-permute-start(bf16[256,1024]{1,0:T(8,128)(2,1)S(1)} %broadcast_select_fusion), channel_id=1, source_target_pairs={{0,5},{1,0},{2,3},{5,4},{6,7},{7,2},{8,13},{9,8},{10,11},{13,12},{... | collective-permute-start | bytes 1572872 | tf_op jit(solution)/shard_map/ppermute | solution.py:268
  81.0 47.8 %collective-permute-start.8 = (bf16[256,1024]{1,0:T(8,128)(2,1)}, bf16[256,1024]{1,0:T(8,128)(2,1)S(1)}, u32[]{:S(2)}, u32[]{:S(2)}) collective-permute-start(bf16[256,1024]{1,0:T(8,128)(2,1)} %collective-permute-done.1.refs_3_), channel_id=1, source_target_pairs={{0,4},{1,5},{2,6},{3,7},{4,0},{5,1},{6,2},{7,3},{8,12},{9,13},{10,... | collective-permute-start | bytes 1572872 | tf_op jit(solution)/shard_map/ppermute | solution.py:268
  88.0 40.8 %collective-permute-start.7 = (bf16[256,1024]{1,0:T(8,128)(2,1)}, bf16[256,1024]{1,0:T(8,128)(2,1)S(1)}, u32[]{:S(2)}, u32[]{:S(2)}) collective-permute-start(bf16[256,1024]{1,0:T(8,128)(2,1)} %collective-permute-done.refs_2_), channel_id=1, source_target_pairs={{0,4},{1,5},{2,6},{3,7},{4,0},{5,1},{6,2},{7,3},{8,12},{9,13},{10,... | collective-permute-start | bytes 1572872 | tf_op jit(solution)/shard_map/ppermute | solution.py:268
  89.2 32.3 %collective-permute-start.5 = (bf16[256,1024]{1,0:T(8,128)(2,1)S(1)}, bf16[256,1024]{1,0:T(8,128)(2,1)S(1)}, u32[]{:S(2)}, u32[]{:S(2)}) collective-permute-start(bf16[256,1024]{1,0:T(8,128)(2,1)S(1)} %broadcast_select_fusion.1), channel_id=1, source_target_pairs={{0,1},{1,0},{2,3},{5,4},{6,7},{7,6},{8,9},{9,8},{10,11},{13,12},{1... | collective-permute-start | bytes 1572872 | tf_op jit(solution)/shard_map/ppermute | solution.py:268
  92.9 35.1 %collective-permute-start.10 = (bf16[2,256,512]{2,1,0:T(8,128)(2,1)}, bf16[2,256,512]{2,1,0:T(8,128)(2,1)S(1)}, u32[]{:S(2)}, u32[]{:S(2)}) collective-permute-start(bf16[2,256,512]{2,1,0:T(8,128)(2,1)} %get-tuple-element.59), channel_id=1, source_target_pairs={{0,4},{1,1},{2,5},{3,0},{4,6},{5,3},{6,7},{7,2},{8,12},{9,9},{10,1... | collective-permute-start | bytes 1572872 | tf_op jit(solution)/shard_map/ppermute | solution.py:268
  94.8 35.7 %collective-permute-start.9 = (bf16[2,256,512]{2,1,0:T(8,128)(2,1)}, bf16[2,256,512]{2,1,0:T(8,128)(2,1)S(1)}, u32[]{:S(2)}, u32[]{:S(2)}) collective-permute-start(bf16[2,256,512]{2,1,0:T(8,128)(2,1)} %get-tuple-element.58), channel_id=1, source_target_pairs={{0,1},{1,5},{2,0},{3,4},{4,3},{5,7},{6,2},{7,6},{8,9},{9,13},{10,8... | collective-permute-start | bytes 1572872 | tf_op jit(solution)/shard_map/ppermute | solution.py:268
  131.3 15.4 %collective-permute-start.14 = (bf16[256,1024]{1,0:T(8,128)(2,1)}, bf16[256,1024]{1,0:T(8,128)(2,1)}, u32[]{:S(2)}, u32[]{:S(2)}) collective-permute-start(bf16[256,1024]{1,0:T(8,128)(2,1)} %copy-done.17), channel_id=1, source_target_pairs={{0,4},{1,5},{2,6},{3,7},{4,0},{5,1},{6,2},{7,3},{8,12},{9,13},{10,... | collective-permute-start | bytes 1572872 | tf_op jit(solution)/shard_map/ppermute | solution.py:268
  131.3 15.4 %collective-permute-start.15 = (bf16[256,1024]{1,0:T(8,128)(2,1)}, bf16[256,1024]{1,0:T(8,128)(2,1)}, u32[]{:S(2)}, u32[]{:S(2)}) collective-permute-start(bf16[256,1024]{1,0:T(8,128)(2,1)} %copy-done.14), channel_id=1, source_target_pairs={{0,4},{1,5},{2,6},{3,7},{4,0},{5,1},{6,2},{7,3},{8,12},{9,13},{10,... | collective-permute-start | bytes 1572872 | tf_op jit(solution)/shard_map/ppermute | solution.py:268
  180.1 17.9 %all-to-all-start.2 = ((f32[4,1,128]{2,1,0:T(1,128)}), f32[4,1,128]{2,1,0:T(1,128)S(1)}, u32[]{:S(2)}, u32[]{:S(2)}) async-start(f32[4,1,128]{2,1,0:T(1,128)} %broadcast_in_dim.45), calls=%async_computation.2 | async-start | bytes 4096 | tf_op jit(solution)/shard_map/all_to_all | solution.py:485
  192.5 18.7 %collective-permute-start.19 = (bf16[2,256,256]{2,1,0:T(8,128)(2,1)}, bf16[2,256,256]{2,1,0:T(8,128)(2,1)S(1)}, u32[]{:S(2)}, u32[]{:S(2)}) collective-permute-start(bf16[2,256,256]{2,1,0:T(8,128)(2,1)} %get-tuple-element.79), channel_id=1, source_target_pairs={{0,22},{1,20},{2,27},{3,25},{4,7},{5,5},{6,8},{7,10},{8,31},{9,29}... | collective-permute-start | bytes 786440 | tf_op jit(solution)/shard_map/ppermute | solution.py:268
  195.6 15.5 %collective-permute-start.20 = (bf16[2,256,256]{2,1,0:T(8,128)(2,1)}, bf16[2,256,256]{2,1,0:T(8,128)(2,1)S(1)}, u32[]{:S(2)}, u32[]{:S(2)}) collective-permute-start(bf16[2,256,256]{2,1,0:T(8,128)(2,1)} %get-tuple-element.80), channel_id=1, source_target_pairs={{0,18},{1,16},{2,22},{3,20},{4,3},{5,1},{6,7},{7,5},{8,27},{9,25},... | collective-permute-start | bytes 786440 | tf_op jit(solution)/shard_map/ppermute | solution.py:268
  197.2 17.8 %collective-permute-start.21 = (bf16[2,256,256]{2,1,0:T(8,128)(2,1)}, bf16[2,256,256]{2,1,0:T(8,128)(2,1)}, u32[]{:S(2)}, u32[]{:S(2)}) collective-permute-start(bf16[2,256,256]{2,1,0:T(8,128)(2,1)} %get-tuple-element.81), channel_id=1, source_target_pairs={{0,13},{1,15},{2,18},{3,16},{4,30},{5,28},{6,3},{7,1},{8,22},{9,20... | collective-permute-start | bytes 786440 | tf_op jit(solution)/shard_map/ppermute | solution.py:268
  199.2 20.6 %collective-permute-start.22 = (bf16[2,256,256]{2,1,0:T(8,128)(2,1)}, bf16[2,256,256]{2,1,0:T(8,128)(2,1)S(1)}, u32[]{:S(2)}, u32[]{:S(2)}) collective-permute-start(bf16[2,256,256]{2,1,0:T(8,128)(2,1)} %get-tuple-element.82), channel_id=1, source_target_pairs={{0,9},{1,11},{2,13},{3,15},{4,26},{5,24},{6,30},{7,28},{8,18},{9,1... | collective-permute-start | bytes 786440 | tf_op jit(solution)/shard_map/ppermute | solution.py:268
  202.2 23.2 %collective-permute-start.23 = (bf16[2,256,256]{2,1,0:T(8,128)(2,1)}, bf16[2,256,256]{2,1,0:T(8,128)(2,1)S(1)}, u32[]{:S(2)}, u32[]{:S(2)}) collective-permute-start(bf16[2,256,256]{2,1,0:T(8,128)(2,1)} %get-tuple-element.83), channel_id=1, source_target_pairs={{0,4},{1,6},{2,9},{3,11},{4,21},{5,23},{6,26},{7,24},{8,13},{9,15}... | collective-permute-start | bytes 786440 | tf_op jit(solution)/shard_map/ppermute | solution.py:268
  245.0 24.9 %collective-permute-start.28 = (bf16[2,256,256]{2,1,0:T(8,128)(2,1)S(1)}, bf16[2,256,256]{2,1,0:T(8,128)(2,1)S(1)}, u32[]{:S(2)}, u32[]{:S(2)}) collective-permute-start(bf16[2,256,256]{2,1,0:T(8,128)(2,1)S(1)} %get-tuple-element.89), channel_id=1, source_target_pairs={{0,20},{1,21},{2,22},{3,23},{4,16},{5,17},{6,18},{7,19},{8,28},{9,... | collective-permute-start | bytes 786440 | tf_op jit(solution)/shard_map/ppermute | solution.py:268
  246.8 23.0 %collective-permute-start.29 = (bf16[2,256,256]{2,1,0:T(8,128)(2,1)S(1)}, bf16[2,256,256]{2,1,0:T(8,128)(2,1)S(1)}, u32[]{:S(2)}, u32[]{:S(2)}) collective-permute-start(bf16[2,256,256]{2,1,0:T(8,128)(2,1)S(1)} %get-tuple-element.90), channel_id=1, source_target_pairs={{0,24},{1,25},{2,26},{3,27},{4,28},{5,29},{6,30},{7,31},{8,0},{9,1... | collective-permute-start | bytes 786440 | tf_op jit(solution)/shard_map/ppermute | solution.py:268
  249.7 20.1 %collective-permute-start.30 = (bf16[2,256,256]{2,1,0:T(8,128)(2,1)S(1)}, bf16[2,256,256]{2,1,0:T(8,128)(2,1)S(1)}, u32[]{:S(2)}, u32[]{:S(2)}) collective-permute-start(bf16[2,256,256]{2,1,0:T(8,128)(2,1)S(1)} %get-tuple-element.91), channel_id=1, source_target_pairs={{0,28},{1,29},{2,30},{3,31},{4,24},{5,25},{6,26},{7,27},{8,4},{9,5... | collective-permute-start | bytes 786440 | tf_op jit(solution)/shard_map/ppermute | solution.py:268
  (36 other events, 478.4 us)
Sparse Core Ops, SparseCore 0:
  23.6 47.7 all-gather.2

commit v4 on v3

--- a/solution.py
+++ b/solution.py
@@ -30,6 +30,10 @@
     return pltpu.CompilerParams(vmem_limit_bytes=mib * MIB)
 
 
+def cost(mib, flops=0):
+    return pl.CostEstimate(flops=int(flops), bytes_accessed=int(mib * MIB), transcendentals=0)
+
+
 def run_copies(copies):
     for copy in copies:
         copy.start()
@@ -42,23 +46,23 @@
 
 
 def prep_kernel(shards, ids, w, *out):
-    _, rows, piece = out[0].shape
-    tiles = piece // LANES
-    stride = 2 * shards * tiles
+    pieces, slices = out[:shards], out[shards]
+    _, rows, piece = pieces[0].shape
+    particles, _, _, cols = slices.shape
+    columns = particles // 2
+    tiles, per_slice = piece // LANES, cols // LANES
     for r in range(shards):
-        first = lax.rem(ids[SHARD] - r + shards, shards) * tiles
-        for kind in range(2):
-            for j in range(tiles):
-                part = w[pl.ds(2 * (first + j) + kind, rows, stride=stride), :]
-                out[r][kind, :, j * LANES : (j + 1) * LANES] = part.astype(BF)
-    particles, _, _, cols = out[shards].shape
-    tiles = cols // LANES
-    for p in range(particles):
-        first = slice_index(ids, p // 2, p % 2, ids[SHARD], particles // 2) * tiles
-        for kind in range(2):
-            for j in range(tiles):
-                part = w[pl.ds(2 * (first + j) + kind, rows, stride=stride), :]
-                out[shards][p, kind, :, j * LANES : (j + 1) * LANES] = part.astype(BF)
+        q = lax.rem(ids[SHARD] - r + shards, shards)
+        for j in range(tiles):
+            e = q * (tiles // per_slice) + j // per_slice
+            column = lax.rem(lax.div(e, 2) + ids[SHARD], columns)
+            p = 2 * column + lax.rem(e, 2)
+            at, within = j * LANES, j % per_slice * LANES
+            for kind in range(2):
+                line = 2 * (q * tiles + j) + kind
+                part = w[pl.ds(line, rows, stride=2 * shards * tiles), :].astype(BF)
+                pieces[r][kind, :, at : at + LANES] = part
+                slices[p, kind, :, within : within + LANES] = part
 
 
 def up_kernel(shards, scale, ids, tokens, *refs):
@@ -160,8 +164,12 @@
         return acc
 
     acc = lax.fori_loop(0, 2 * rows // 16, body, tuple(jnp.zeros((8, LANES), F32) for _ in pairs))
+    lane = lax.broadcasted_iota(jnp.int32, (8, LANES), 1)
+    row = jnp.zeros((8, LANES), F32)
     for i, a in enumerate(acc):
-        out[i] = a
+        total = jnp.sum(jnp.sum(a, axis=0, keepdims=True), axis=1, keepdims=True)
+        row = row + jnp.where(lane == i, total, 0.0)
+    out[...] = row
 
 
 def stein_kernel(shards, particles, ids, coef, whole, *refs):
@@ -282,10 +290,11 @@
     index = lax.dynamic_slice(batch_index, (own * share,), (share,))
     picked = jnp.take(pool, index, axis=0).astype(F32)
     normed = (picked * lax.rsqrt(jnp.mean(picked * picked, axis=1, keepdims=True) + 1e-06)).astype(BF)
-    normed = jnp.stack(
-        [move(normed, [(dev(m, c, s), dev(m, c, (s + k) % shards)) for m, c, s in devices]) for k in range(shards)]
-    )
-    normed = lax.all_gather(normed[None], "particle", axis=0, tiled=True).reshape(tokens, width)
+
+    def gather_tokens(x):
+        shifted = [[(dev(m, c, s), dev(m, c, (s + k) % shards)) for m, c, s in devices] for k in range(shards)]
+        x = jnp.stack([move(x, pairs) for pairs in shifted])
+        return lax.all_gather(x[None], "particle", axis=0, tiled=True)
 
     w_flat = flat(weights)
     steps = max(rows // 64, 1)
@@ -299,6 +308,7 @@
         out_specs=[pl.BlockSpec((2, rows // steps, part), lambda i: (0, i, 0))] * shards
         + [pl.BlockSpec((particles, 2, rows // steps, cols), lambda i: (0, 0, i, 0))],
         compiler_params=params(56),
+        cost_estimate=cost(16),
         name="prep",
     )(ids, w_flat)
 
@@ -311,6 +321,30 @@
         w_routes.append(pairs)
 
     whole = lax.all_to_all(slices, "particle", 0, 0, tiled=True)
+
+    pair_list = [(i, j) for i in range(particles) for j in range(i)]
+    hops = []
+    for count, stride in ((particles, shards), (shards, 1)):
+        hop = 1
+        while hop < count:
+            hops.append([(d, d + ((d // stride % count ^ hop) - d // stride % count) * stride) for d in range(len(devices))])
+            hop *= 2
+
+    def pair_sums(whole):
+        return pl.pallas_call(
+            distance_kernel,
+            out_shape=jax.ShapeDtypeStruct((8, LANES), F32),
+            in_specs=[pl.BlockSpec(memory_space=pltpu.VMEM)],
+            out_specs=pl.BlockSpec(memory_space=pltpu.VMEM),
+            compiler_params=params(8),
+            cost_estimate=cost(4),
+            name="distances",
+        )(whole)
+
+    def add_over(sums, steps):
+        for step in steps:
+            sums = sums + move(sums, hops[step])
+        return sums
 
     def gather_row(ids, which, turn):
         k = lax.rem(ids[SHARD] - which + shards, shards)
@@ -349,12 +383,17 @@
         ]
         alpha = [move(x, route) for x, route in zip(halves, first_routes)]
         own_c = move(cot, [(dev(m, c, s), dev(m, 1 - c, s)) for m, c, s in devices if c == s // half])
-        w_pieces = [move(x, route) for x, route in zip(prepared[:2], w_routes[:2])]
-        alpha, own_c, w_pieces, last = lax.optimization_barrier((alpha, own_c, w_pieces, prepared[2:]))
-        beta = [move(jnp.where(inner, a, x), route) for a, x, route in zip(alpha, halves, second_routes)]
-        w_pieces = w_pieces + [move(x, route) for x, route in zip(last, w_routes[2:])]
+        normed = gather_tokens(normed)
+        alpha, own_c, prepared = lax.optimization_barrier((alpha, own_c, prepared))
+        w_pieces = [move(x, route) for x, route in zip(prepared, w_routes)]
+        hand_on = [jnp.where(inner, a, x) for a, x in zip(alpha, halves)]
         alpha_x = [move(x, swap_of(everyone)) for x in alpha]
-        beta, alpha_x, w_pieces, whole = lax.optimization_barrier((beta, alpha_x, w_pieces, whole))
+        beta = [move(hand_on[0], second_routes[0])]
+        hand_on[1], *w_pieces[:2] = lax.optimization_barrier((hand_on[1], *w_pieces[:2]))
+        beta.append(move(hand_on[1], second_routes[1]))
+        whole, alpha_x, beta[0] = lax.optimization_barrier((whole, alpha_x, beta[0]))
+        sums = add_over(pair_sums(whole), range(len(hops) - 3))
+        w_pieces, normed, sums = lax.optimization_barrier((w_pieces, normed, sums))
         beta_x = [move(x, swap_of(everyone)) for x in beta]
         sources = [cot, own_c, *alpha, *alpha_x, *beta, *beta_x]
 
@@ -399,6 +438,8 @@
         full = lax.all_gather(cotangent[0], "shard", axis=0, tiled=True)
         sources = [jnp.where(core == proc, full, move(full, swap_of(everyone)))]
         w_pieces = [move(x, route) for x, route in zip(prepared, w_routes)]
+        normed = gather_tokens(normed)
+        sums = add_over(pair_sums(whole), range(len(hops) - 3))
 
         def pick(ids, refs, held, sem):
             def one(which, carry):
@@ -409,6 +450,7 @@
 
             lax.fori_loop(0, shards, one, 0)
 
+    normed = normed.reshape(tokens, width)
     act_t, slope_t, down_t = pl.pallas_call(
         functools.partial(up_kernel, shards, width ** (-0.5)),
         grid=(blocks,),
@@ -425,10 +467,13 @@
             pl.BlockSpec((part, width), lambda i: (0, 0)),
         ],
         scratch_shapes=[pltpu.VMEM((width, part), BF), pltpu.VMEM((width, part), BF), pltpu.VMEM((part, width), BF)],
-        compiler_params=params(24),
+        compiler_params=params(56),
+        cost_estimate=cost(24, 2 * tokens * width * part),
         name="up",
     )(ids, normed, *w_pieces)
 
+    sums = add_over(sums, [-3])
+    sums, act_t, slope_t = lax.optimization_barrier((sums, act_t, slope_t))
     grad_scale = 1.0 / (tokens * width)
     scores = pl.pallas_call(
         functools.partial(
@@ -454,8 +499,12 @@
             pltpu.SemaphoreType.DMA((particles + 5,)),
         ],
         compiler_params=params(56),
+        cost_estimate=cost(32, 6 * tokens * width * part),
         name="grads",
     )(ids, normed, act_t, slope_t, down_t, *sources)
+
+    sums = add_over(sums, [-2])
+    sums, *scores = lax.optimization_barrier((sums, *scores))
 
     ratio = particles // shards
     arrived = []
@@ -468,21 +517,10 @@
             pairs.append((dev(m, c, s), dev(e // 2 + z, e % 2, z)))
         arrived.append(move(scores[t], pairs))
 
-    whole, arrived[0] = lax.optimization_barrier((whole, arrived[0]))
-    pair_list = [(i, j) for i in range(particles) for j in range(i)]
-    partial = pl.pallas_call(
-        distance_kernel,
-        out_shape=jax.ShapeDtypeStruct((len(pair_list), 8, LANES), F32),
-        in_specs=[pl.BlockSpec(memory_space=pltpu.VMEM)],
-        out_specs=pl.BlockSpec(memory_space=pltpu.VMEM),
-        compiler_params=params(8),
-        name="distances",
-    )(whole)
-    sums = jnp.sum(partial, axis=(1, 2))
-    sums = jnp.pad(sums, (0, -len(pair_list) % LANES))
-    for axis, count in (("particle", particles), ("shard", shards)):
-        copies = jnp.broadcast_to(sums[None, None], (count, 1, sums.shape[0]))
-        sums = jnp.sum(lax.all_to_all(copies, axis, 0, 0, tiled=True), axis=(0, 1))
+    rest = move(sums, hops[-1])
+    sums, rest, *arrived[:4] = lax.optimization_barrier((sums, rest, *arrived[:4]))
+    sums = sums + rest
+    sums = sums[0]
     lookup = [
         [pair_list.index((max(i, j), min(i, j))) if i != j else len(pair_list) for j in range(particles)]
         for i in range(particles)
@@ -508,6 +546,7 @@
             pltpu.SemaphoreType.DMA((particles,)),
         ],
         compiler_params=params(12),
+        cost_estimate=cost(12),
         name="stein",
     )(ids, coef, whole, *arrived)
 
@@ -528,6 +567,7 @@
         out_specs=[state_spec] * 4,
         scratch_shapes=[pltpu.VMEM((2, rows, hidden), BF), pltpu.SemaphoreType.DMA((particles,))],
         compiler_params=params(56),
+        cost_estimate=cost(32),
         name="adam",
     )(ids, w_flat, flat(first_moment), flat(second_moment), *back)
     return tuple(unflat(x) for x in outs)

time: 296 us -> 279 us (0.943)
  starting transfers between devices: 86.5 us -> 102 us
  waiting for transfers between devices: 111 us -> 96.4 us
  local copies, waits for them, and re-layouts: 17.3 us -> 5.33 us
  blocking collectives: 6.66 us -> 0 us
    ppermute x31 -> x36, starting transfers between devices: 77.2 us -> 97.7 us  [move(): return lax.ppermute(x, AXES, pairs)]
    ppermute x31 -> x36, waiting for transfers between devices: 111 us -> 96.3 us  [move(): return lax.ppermute(x, AXES, pairs)]
    unnamed x52 -> x38, local copies, waits for them, and re-layouts: 13.3 us -> 3.03 us
    all_to_all x1 -> x0, blocking collectives: 6.66 us -> none  [local(): sums = jnp.sum(lax.all_to_all(copies, axis, 0, 0, tiled=True), axis=(0, 1))]
    all_to_all x1 -> x0, starting transfers between devices: 5.3 us -> none  [local(): sums = jnp.sum(lax.all_to_all(copies, axis, 0, 0, tiled=True), axis=(0, 1))]
    pallas_call x1, Pallas kernels: 6.99 us -> 10.4 us  [local(): pl.pallas_call(functools.partial(up_kernel, shards, width ** (-0.5)), gri...]
  transfers between devices with their start and end apart: 34 -> 38, of which waited for: 16 -> 15; matrix products, arithmetic and copies ran while one was open for 2% -> 1% of each run, Pallas kernels for 5% -> 12%
where the time goes in v4:
time: 279 us; the launch traced here: 277 us
  starting transfers between devices  102 us (37%)
  waiting for transfers between devices  96.4 us (35%)
  Pallas kernels  54.7 us (20%)
  between operations  15.1 us (5%)
  local copies, waits for them, and re-layouts  5.33 us (2%)
  other arithmetic  3.45 us (1%)
    ppermute x36, starting transfers between devices, move(): return lax.ppermute(x, AXES, pairs)  97.7 us
    ppermute x36, waiting for transfers between devices, move(): return lax.ppermute(x, AXES, pairs)  96.3 us
    pallas_call x1, Pallas kernels, local(): pl.pallas_call(functools.partial(adam_kernel, particles), grid=(steps,),...  15.4 us
    pallas_call x1, Pallas kernels, local(): pl.pallas_call(functools.partial(grad_kernel, shards, particles, -width *...  13.7 us
    pallas_call x1, Pallas kernels, local(): pl.pallas_call(functools.partial(up_kernel, shards, width ** (-0.5)), gri...  10.4 us
    pallas_call x1, Pallas kernels, local(): pl.pallas_call(functools.partial(prep_kernel, shards), grid=(steps,), out...  6.95 us
    pallas_call x1, Pallas kernels, local(): pl.pallas_call(functools.partial(stein_kernel, shards, particles), out_sh...  6.05 us
  transfers between devices with their start and end apart: 38, of which 15 were waited for; matrix products, arithmetic and copies ran while one was open for 1% of the time, Pallas kernels for 12%

profile of v4, /device:TPU:23, one launch (start us, length us, event | category | flops | bytes accessed | tf_op | source)
XLA Modules:
  0.0 276.6 jit_solution(13140543296931381107)
XLA Ops:
  14.2 5.5 %collective-permute-done.8 = bf16[64,1024]{1,0:T(8,128)(2,1)S(1)} collective-permute-done((bf16[64,1024]{1,0:T(8,128)(2,1)S(1)}, bf16[64,1024]{1,0:T(8,128)(2,1)S(1)}, u32[]{:S(2)}, u32[]{:S(2)}) %collective-permute-start.8) | collective-permute-done | bytes 131104 | tf_op jit(solution)/shard_map/ppermute | solution.py:276
  23.4 3.4 %collective-permute-start.2 = (bf16[512,1024]{1,0:T(8,128)(2,1)}, bf16[512,1024]{1,0:T(8,128)(2,1)}, u32[]{:S(2)}, u32[]{:S(2)}) collective-permute-start(bf16[512,1024]{1,0:T(8,128)(2,1)} %bitcast.62), channel_id=1, source_target_pairs={{0,4},{1,5},{6,2},{7,3},{8,12},{9,13},{14,10},{15,11},{16,20},{17,... | collective-permute-start | bytes 3145736 | tf_op jit(solution)/shard_map/ppermute | solution.py:276
  27.4 6.9 %prep.1 = (bf16[2,256,512]{2,1,0:T(8,128)(2,1)}, bf16[2,256,512]{2,1,0:T(8,128)(2,1)}, bf16[2,256,512]{2,1,0:T(8,128)(2,1)}, bf16[2,256,512]{2,1,0:T(8,128)(2,1)}, bf16[8,2,256,256]{3,2,1,0:T(8,128)(2,1)}) custom-call(s32[5]{0:T(128)} %stack.36.ids, f32[8192,128]{1,0:T(8,128)} %bitcast.58), custom_call_target="tpu_custom_call" | custom-call | bytes 16777216 | tf_op jit(solution)/shard_map/prep/pallas_call | solution.py:302
  34.4 4.0 %all-to-all-start = ((bf16[8,2,256,256]{3,2,1,0:T(8,128)(2,1)}), bf16[8,2,256,256]{3,2,1,0:T(8,128)(2,1)S(1)}, u32[]{:S(2)}, u32[]{:S(2)}) async-start(bf16[8,2,256,256]{3,2,1,0:T(8,128)(2,1)} %get-tuple-element.81), calls=%async_computation | async-start | bytes 4194304 | tf_op jit(solution)/shard_map/all_to_all | solution.py:323
  38.4 4.3 %collective-permute-start = (bf16[256,1024]{1,0:T(8,128)(2,1)S(1)}, bf16[256,1024]{1,0:T(8,128)(2,1)S(1)}, u32[]{:S(2)}, u32[]{:S(2)}) collective-permute-start(bf16[256,1024]{1,0:T(8,128)(2,1)S(1)} %get-tuple-element.139), channel_id=1, source_target_pairs={{1,0},{2,1},{3,5},{4,2},{5,6},{6,7},{9,8},{10,9},{11,13},{12,10},{... | collective-permute-start | bytes 1572872 | tf_op jit(solution)/shard_map/ppermute | solution.py:276
  45.9 14.8 %collective-permute-done.refs_2_ = bf16[256,1024]{1,0:T(8,128)(2,1)S(1)} collective-permute-done((bf16[256,1024]{1,0:T(8,128)(2,1)S(1)}, bf16[256,1024]{1,0:T(8,128)(2,1)S(1)}, u32[]{:S(2)}, u32[]{:S(2)}) %collective-permute-start) | collective-permute-done | bytes 524320 | tf_op jit(solution)/shard_map/ppermute | solution.py:276
  60.7 6.0 %collective-permute-start.10 = (bf16[256,1024]{1,0:T(8,128)(2,1)S(1)}, bf16[256,1024]{1,0:T(8,128)(2,1)S(1)}, u32[]{:S(2)}, u32[]{:S(2)}) collective-permute-start(bf16[256,1024]{1,0:T(8,128)(2,1)S(1)} %collective-permute-done.refs_2_), channel_id=1, source_target_pairs={{0,4},{1,5},{2,6},{3,7},{4,0},{5,1},{6,2},{7,3},{8,12},{9,13},{10,... | collective-permute-start | bytes 1572872 | tf_op jit(solution)/shard_map/ppermute | solution.py:276
  70.5 5.6 %collective-permute-start.12 = (bf16[256,1024]{1,0:T(8,128)(2,1)S(1)}, bf16[256,1024]{1,0:T(8,128)(2,1)S(1)}, u32[]{:S(2)}, u32[]{:S(2)}) collective-permute-start(bf16[256,1024]{1,0:T(8,128)(2,1)S(1)} %broadcast_select_fusion), channel_id=1, source_target_pairs={{0,1},{1,0},{2,3},{5,4},{6,7},{7,6},{8,9},{9,8},{10,11},{13,12},{1... | collective-permute-start | bytes 1572872 | tf_op jit(solution)/shard_map/ppermute | solution.py:276
  77.7 8.3 %collective-permute-done.3.refs_0_ = bf16[2,256,512]{2,1,0:T(8,128)(2,1)S(1)} collective-permute-done((bf16[2,256,512]{2,1,0:T(8,128)(2,1)}, bf16[2,256,512]{2,1,0:T(8,128)(2,1)S(1)}, u32[]{:S(2)}, u32[]{:S(2)}) %collective-permute-start.3) | collective-permute-done | bytes 524320 | tf_op jit(solution)/shard_map/ppermute | solution.py:276
  85.9 9.2 %collective-permute-start.17 = (bf16[256,1024]{1,0:T(8,128)(2,1)}, bf16[256,1024]{1,0:T(8,128)(2,1)}, u32[]{:S(2)}, u32[]{:S(2)}) collective-permute-start(bf16[256,1024]{1,0:T(8,128)(2,1)} %broadcast_select_fusion.1), channel_id=1, source_target_pairs={{0,5},{1,0},{2,3},{5,4},{6,7},{7,2},{8,13},{9,8},{10,11},{13,12},{... | collective-permute-start | bytes 1572872 | tf_op jit(solution)/shard_map/ppermute | solution.py:276
  103.0 13.6 %collective-permute-done.17.refs_7_ = bf16[256,1024]{1,0:T(8,128)(2,1)} collective-permute-done((bf16[256,1024]{1,0:T(8,128)(2,1)}, bf16[256,1024]{1,0:T(8,128)(2,1)}, u32[]{:S(2)}, u32[]{:S(2)}) %collective-permute-start.17) | collective-permute-done | bytes 524320 | tf_op jit(solution)/shard_map/ppermute | solution.py:276
  116.6 10.1 %collective-permute-start.19 = (bf16[256,1024]{1,0:T(8,128)(2,1)}, bf16[256,1024]{1,0:T(8,128)(2,1)}, u32[]{:S(2)}, u32[]{:S(2)}) collective-permute-start(bf16[256,1024]{1,0:T(8,128)(2,1)} %collective-permute-done.17.refs_7_), channel_id=1, source_target_pairs={{0,4},{1,5},{2,6},{3,7},{4,0},{5,1},{6,2},{7,3},{8,12},{9,13},{10,... | collective-permute-start | bytes 1572872 | tf_op jit(solution)/shard_map/ppermute | solution.py:276
  132.8 10.4 %up.1 = (bf16[512,2048]{1,0:T(8,128)(2,1)}, bf16[512,2048]{1,0:T(8,128)(2,1)}, bf16[512,1024]{1,0:T(8,128)(2,1)}) custom-call(s32[5]{0:T(128)} %stack.36.ids, bf16[2048,1024]{1,0:T(8,128)(2,1)} %bitcast.67, bf16[2,256,512]{2,1,0:T(8,128)(2,1)} %copy-done.17, bf16[2,256,512]{2,1,0:T(8,128)(2,1)} %copy-done.18, ...), custom_call_target="tpu_custom_call" | custom-call | flops 2147483648 | bytes 25165824 | tf_op jit(solution)/shard_map/up/pallas_call | solution.py:454
  145.6 13.7 %grads.1 = (bf16[2,256,256]{2,1,0:T(8,128)(2,1)}, bf16[2,256,256]{2,1,0:T(8,128)(2,1)}, bf16[2,256,256]{2,1,0:T(8,128)(2,1)}, bf16[2,256,256]{2,1,0:T(8,128)(2,1...) custom-call(s32[5]{0:T(128)} %stack.36.ids, ...), custom_call_target="tpu_custom_call" | custom-call | flops 6442450944 | bytes 33554432 | tf_op jit(solution)/shard_map/grads/pallas_call | solution.py:478
  159.3 4.5 %collective-permute-start.21 = (bf16[2,256,256]{2,1,0:T(8,128)(2,1)}, bf16[2,256,256]{2,1,0:T(8,128)(2,1)S(1)}, u32[]{:S(2)}, u32[]{:S(2)}) collective-permute-start(bf16[2,256,256]{2,1,0:T(8,128)(2,1)} %get-tuple-element.110), channel_id=1, source_target_pairs={{0,0},{1,2},{2,4},{3,6},{4,17},{5,19},{6,21},{7,23},{8,9},{9,11},{... | collective-permute-start | bytes 786440 | tf_op jit(solution)/shard_map/ppermute | solution.py:276
  163.9 5.3 %collective-permute-start.22 = (bf16[2,256,256]{2,1,0:T(8,128)(2,1)}, bf16[2,256,256]{2,1,0:T(8,128)(2,1)S(1)}, u32[]{:S(2)}, u32[]{:S(2)}) collective-permute-start(bf16[2,256,256]{2,1,0:T(8,128)(2,1)} %get-tuple-element.111), channel_id=1, source_target_pairs={{0,31},{1,29},{2,0},{3,2},{4,12},{5,14},{6,17},{7,19},{8,4},{9,6},... | collective-permute-start | bytes 786440 | tf_op jit(solution)/shard_map/ppermute | solution.py:276
  174.3 13.2 %collective-permute-done.20 = f32[8,128]{1,0:T(8,128)S(1)} collective-permute-done((f32[8,128]{1,0:T(8,128)S(1)}, f32[8,128]{1,0:T(8,128)S(1)}, u32[]{:S(2)}, u32[]{:S(2)}) %collective-permute-start.20) | collective-permute-done | bytes 4128 | tf_op jit(solution)/shard_map/ppermute | solution.py:276
  196.9 5.2 %collective-permute-done.26.refs_5_ = bf16[2,256,256]{2,1,0:T(8,128)(2,1)} collective-permute-done((bf16[2,256,256]{2,1,0:T(8,128)(2,1)}, bf16[2,256,256]{2,1,0:T(8,128)(2,1)}, u32[]{:S(2)}, u32[]{:S(2)}) %collective-permute-start.26) | collective-permute-done | bytes 262176 | tf_op jit(solution)/shard_map/ppermute | solution.py:276
  205.4 5.8 %collective-permute-done.28.refs_7_ = bf16[2,256,256]{2,1,0:T(8,128)(2,1)} collective-permute-done((bf16[2,256,256]{2,1,0:T(8,128)(2,1)}, bf16[2,256,256]{2,1,0:T(8,128)(2,1)}, u32[]{:S(2)}, u32[]{:S(2)}) %collective-permute-start.28) | collective-permute-done | bytes 262176 | tf_op jit(solution)/shard_map/ppermute | solution.py:276
  211.3 6.0 %stein.1 = (bf16[2,256,256]{2,1,0:T(8,128)(2,1)S(1)}, bf16[2,256,256]{2,1,0:T(8,128)(2,1)S(1)}, bf16[2,256,256]{2,1,0:T(8,128)(2,1)S(1)}, bf16[2,256,256]{2,1,0:...) custom-call(s32[5]{0:T(128)S(1)} %copy-done.3, ...), custom_call_target="tpu_custom_call" | custom-call | bytes 12582912 | tf_op jit(solution)/shard_map/stein/pallas_call | solution.py:538
  218.0 4.4 %collective-permute-start.29 = (bf16[2,256,256]{2,1,0:T(8,128)(2,1)S(1)}, bf16[2,256,256]{2,1,0:T(8,128)(2,1)S(1)}, u32[]{:S(2)}, u32[]{:S(2)}) collective-permute-start(bf16[2,256,256]{2,1,0:T(8,128)(2,1)S(1)} %get-tuple-element.125), channel_id=1, source_target_pairs={{0,4},{1,5},{2,6},{3,7},{4,0},{5,1},{6,2},{7,3},{8,12},{9,13},{10,... | collective-permute-start | bytes 786440 | tf_op jit(solution)/shard_map/ppermute | solution.py:276
  231.5 4.2 %collective-permute-start.35 = (bf16[2,256,256]{2,1,0:T(8,128)(2,1)S(1)}, bf16[2,256,256]{2,1,0:T(8,128)(2,1)S(1)}, u32[]{:S(2)}, u32[]{:S(2)}) collective-permute-start(bf16[2,256,256]{2,1,0:T(8,128)(2,1)S(1)} %get-tuple-element.131), channel_id=1, source_target_pairs={{0,28},{1,29},{2,30},{3,31},{4,24},{5,25},{6,26},{7,27},{8,4},{9,5... | collective-permute-start | bytes 786440 | tf_op jit(solution)/shard_map/ppermute | solution.py:276
  237.1 16.2 %collective-permute-done.33.refs_5_ = bf16[2,256,256]{2,1,0:T(8,128)(2,1)S(1)} collective-permute-done((bf16[2,256,256]{2,1,0:T(8,128)(2,1)S(1)}, bf16[2,256,256]{2,1,0:T(8,128)(2,1)S(1)}, u32[]{:S(2)}, u32[]{:S(2)}) %collective-permute-start.33) | collective-permute-done | bytes 262176 | tf_op jit(solution)/shard_map/ppermute | solution.py:276
  254.3 15.4 %adam.1 = (f32[8192,128]{1,0:T(8,128)}, f32[8192,128]{1,0:T(8,128)}, f32[8192,128]{1,0:T(8,128)}, f32[8192,128]{1,0:T(8,128)}) custom-call(s32[5]{0:T(128)} %stack.36.ids, f32[8192,128]{1,0:T(8,128)} %bitcast.59, f32[8192,128]{1,0:T(8,128)} %bitcast.60, f32[8192,128]{1,0:T(8,128)} %bitcast.61, bf16[2,256,256]{2,1,0:T(8,128)(2,1)} %copy-done.2, ...), custom_call_target="tpu_custom_call" | custom-call | bytes 33554432 | tf_op jit(solution)/shard_map/adam/pallas_call | solution.py:562
  (124 shorter events, 65.3 us)
Async XLA Ops:
  7.2 125.3 %all-gather.3.cloned.1.call-start = ((), (), s32[]{:S(2)}) async-start(), calls=%async_computation.1 | async-start | bytes 4718592 | tf_op jit(solution)/shard_map/all_gather | solution.py:297
  23.4 37.3 %collective-permute-start.2 = (bf16[512,1024]{1,0:T(8,128)(2,1)}, bf16[512,1024]{1,0:T(8,128)(2,1)}, u32[]{:S(2)}, u32[]{:S(2)}) collective-permute-start(bf16[512,1024]{1,0:T(8,128)(2,1)} %bitcast.62), channel_id=1, source_target_pairs={{0,4},{1,5},{6,2},{7,3},{8,12},{9,13},{14,10},{15,11},{16,20},{17,... | collective-permute-start | bytes 3145736 | tf_op jit(solution)/shard_map/ppermute | solution.py:276
  34.4 66.9 %all-to-all-start = ((bf16[8,2,256,256]{3,2,1,0:T(8,128)(2,1)}), bf16[8,2,256,256]{3,2,1,0:T(8,128)(2,1)S(1)}, u32[]{:S(2)}, u32[]{:S(2)}) async-start(bf16[8,2,256,256]{3,2,1,0:T(8,128)(2,1)} %get-tuple-element.81), calls=%async_computation | async-start | bytes 4194304 | tf_op jit(solution)/shard_map/all_to_all | solution.py:323
  38.4 22.3 %collective-permute-start = (bf16[256,1024]{1,0:T(8,128)(2,1)S(1)}, bf16[256,1024]{1,0:T(8,128)(2,1)S(1)}, u32[]{:S(2)}, u32[]{:S(2)}) collective-permute-start(bf16[256,1024]{1,0:T(8,128)(2,1)S(1)} %get-tuple-element.139), channel_id=1, source_target_pairs={{1,0},{2,1},{3,5},{4,2},{5,6},{6,7},{9,8},{10,9},{11,13},{12,10},{... | collective-permute-start | bytes 1572872 | tf_op jit(solution)/shard_map/ppermute | solution.py:276
  42.8 18.0 %collective-permute-start.1 = (bf16[256,1024]{1,0:T(8,128)(2,1)S(1)}, bf16[256,1024]{1,0:T(8,128)(2,1)S(1)}, u32[]{:S(2)}, u32[]{:S(2)}) collective-permute-start(bf16[256,1024]{1,0:T(8,128)(2,1)S(1)} %get-tuple-element.138), channel_id=1, source_target_pairs={{1,4},{2,5},{3,1},{4,6},{5,2},{6,3},{9,12},{10,13},{11,9},{12,14},... | collective-permute-start | bytes 1572872 | tf_op jit(solution)/shard_map/ppermute | solution.py:276
  60.7 39.7 %collective-permute-start.10 = (bf16[256,1024]{1,0:T(8,128)(2,1)S(1)}, bf16[256,1024]{1,0:T(8,128)(2,1)S(1)}, u32[]{:S(2)}, u32[]{:S(2)}) collective-permute-start(bf16[256,1024]{1,0:T(8,128)(2,1)S(1)} %collective-permute-done.refs_2_), channel_id=1, source_target_pairs={{0,4},{1,5},{2,6},{3,7},{4,0},{5,1},{6,2},{7,3},{8,12},{9,13},{10,... | collective-permute-start | bytes 1572872 | tf_op jit(solution)/shard_map/ppermute | solution.py:276
  66.7 19.2 %collective-permute-start.3 = (bf16[2,256,512]{2,1,0:T(8,128)(2,1)}, bf16[2,256,512]{2,1,0:T(8,128)(2,1)S(1)}, u32[]{:S(2)}, u32[]{:S(2)}) collective-permute-start(bf16[2,256,512]{2,1,0:T(8,128)(2,1)} %get-tuple-element.75), channel_id=1, source_target_pairs={{0,0},{1,4},{2,1},{3,5},{4,2},{5,6},{6,3},{7,7},{8,8},{9,12},{10,9... | collective-permute-start | bytes 1572872 | tf_op jit(solution)/shard_map/ppermute | solution.py:276
  68.6 17.3 %collective-permute-start.4 = (bf16[2,256,512]{2,1,0:T(8,128)(2,1)}, bf16[2,256,512]{2,1,0:T(8,128)(2,1)S(1)}, u32[]{:S(2)}, u32[]{:S(2)}) collective-permute-start(bf16[2,256,512]{2,1,0:T(8,128)(2,1)} %get-tuple-element.76), channel_id=1, source_target_pairs={{0,5},{1,0},{2,4},{3,1},{4,7},{5,2},{6,6},{7,3},{8,13},{9,8},{10,1... | collective-permute-start | bytes 1572872 | tf_op jit(solution)/shard_map/ppermute | solution.py:276
  70.5 26.7 %collective-permute-start.12 = (bf16[256,1024]{1,0:T(8,128)(2,1)S(1)}, bf16[256,1024]{1,0:T(8,128)(2,1)S(1)}, u32[]{:S(2)}, u32[]{:S(2)}) collective-permute-start(bf16[256,1024]{1,0:T(8,128)(2,1)S(1)} %broadcast_select_fusion), channel_id=1, source_target_pairs={{0,1},{1,0},{2,3},{5,4},{6,7},{7,6},{8,9},{9,8},{10,11},{13,12},{1... | collective-permute-start | bytes 1572872 | tf_op jit(solution)/shard_map/ppermute | solution.py:276
  76.0 25.3 %collective-permute-start.11 = (bf16[256,1024]{1,0:T(8,128)(2,1)S(1)}, bf16[256,1024]{1,0:T(8,128)(2,1)}, u32[]{:S(2)}, u32[]{:S(2)}) collective-permute-start(bf16[256,1024]{1,0:T(8,128)(2,1)S(1)} %collective-permute-done.1.refs_3_), channel_id=1, source_target_pairs={{0,4},{1,5},{2,6},{3,7},{4,0},{5,1},{6,2},{7,3},{8,12},{9,13},{10,... | collective-permute-start | bytes 1572872 | tf_op jit(solution)/shard_map/ppermute | solution.py:276
  85.9 30.7 %collective-permute-start.17 = (bf16[256,1024]{1,0:T(8,128)(2,1)}, bf16[256,1024]{1,0:T(8,128)(2,1)}, u32[]{:S(2)}, u32[]{:S(2)}) collective-permute-start(bf16[256,1024]{1,0:T(8,128)(2,1)} %broadcast_select_fusion.1), channel_id=1, source_target_pairs={{0,5},{1,0},{2,3},{5,4},{6,7},{7,2},{8,13},{9,8},{10,11},{13,12},{... | collective-permute-start | bytes 1572872 | tf_op jit(solution)/shard_map/ppermute | solution.py:276
  95.1 37.3 %collective-permute-start.5 = (bf16[2,256,512]{2,1,0:T(8,128)(2,1)}, bf16[2,256,512]{2,1,0:T(8,128)(2,1)}, u32[]{:S(2)}, u32[]{:S(2)}) collective-permute-start(bf16[2,256,512]{2,1,0:T(8,128)(2,1)} %get-tuple-element.79), channel_id=1, source_target_pairs={{0,1},{1,5},{2,0},{3,4},{4,3},{5,7},{6,2},{7,6},{8,9},{9,13},{10,8... | collective-permute-start | bytes 1572872 | tf_op jit(solution)/shard_map/ppermute | solution.py:276
  97.2 35.2 %collective-permute-start.6 = (bf16[2,256,512]{2,1,0:T(8,128)(2,1)}, bf16[2,256,512]{2,1,0:T(8,128)(2,1)}, u32[]{:S(2)}, u32[]{:S(2)}) collective-permute-start(bf16[2,256,512]{2,1,0:T(8,128)(2,1)} %get-tuple-element.80), channel_id=1, source_target_pairs={{0,4},{1,1},{2,5},{3,0},{4,6},{5,3},{6,7},{7,2},{8,12},{9,9},{10,1... | collective-permute-start | bytes 1572872 | tf_op jit(solution)/shard_map/ppermute | solution.py:276
  101.3 44.2 %collective-permute-start.18 = (bf16[256,1024]{1,0:T(8,128)(2,1)}, bf16[256,1024]{1,0:T(8,128)(2,1)}, u32[]{:S(2)}, u32[]{:S(2)}) collective-permute-start(bf16[256,1024]{1,0:T(8,128)(2,1)} %copy-done.16), channel_id=1, source_target_pairs={{0,4},{1,5},{2,6},{3,7},{4,0},{5,1},{6,2},{7,3},{8,12},{9,13},{10,... | collective-permute-start | bytes 1572872 | tf_op jit(solution)/shard_map/ppermute | solution.py:276
  116.6 29.0 %collective-permute-start.19 = (bf16[256,1024]{1,0:T(8,128)(2,1)}, bf16[256,1024]{1,0:T(8,128)(2,1)}, u32[]{:S(2)}, u32[]{:S(2)}) collective-permute-start(bf16[256,1024]{1,0:T(8,128)(2,1)} %collective-permute-done.17.refs_7_), channel_id=1, source_target_pairs={{0,4},{1,5},{2,6},{3,7},{4,0},{5,1},{6,2},{7,3},{8,12},{9,13},{10,... | collective-permute-start | bytes 1572872 | tf_op jit(solution)/shard_map/ppermute | solution.py:276
  143.3 16.0 %collective-permute-start.16 = (f32[8,128]{1,0:T(8,128)S(1)}, f32[8,128]{1,0:T(8,128)S(1)}, u32[]{:S(2)}, u32[]{:S(2)}) collective-permute-start(f32[8,128]{1,0:T(8,128)S(1)} %add.93), channel_id=1, source_target_pairs={{0,1},{1,0},{2,3},{3,2},{4,5},{5,4},{6,7},{7,6},{8,9},{9,8},{10,11... | collective-permute-start | bytes 12296 | tf_op jit(solution)/shard_map/ppermute | solution.py:276
  159.3 29.8 %collective-permute-start.21 = (bf16[2,256,256]{2,1,0:T(8,128)(2,1)}, bf16[2,256,256]{2,1,0:T(8,128)(2,1)S(1)}, u32[]{:S(2)}, u32[]{:S(2)}) collective-permute-start(bf16[2,256,256]{2,1,0:T(8,128)(2,1)} %get-tuple-element.110), channel_id=1, source_target_pairs={{0,0},{1,2},{2,4},{3,6},{4,17},{5,19},{6,21},{7,23},{8,9},{9,11},{... | collective-permute-start | bytes 786440 | tf_op jit(solution)/shard_map/ppermute | solution.py:276
  163.9 28.0 %collective-permute-start.22 = (bf16[2,256,256]{2,1,0:T(8,128)(2,1)}, bf16[2,256,256]{2,1,0:T(8,128)(2,1)S(1)}, u32[]{:S(2)}, u32[]{:S(2)}) collective-permute-start(bf16[2,256,256]{2,1,0:T(8,128)(2,1)} %get-tuple-element.111), channel_id=1, source_target_pairs={{0,31},{1,29},{2,0},{3,2},{4,12},{5,14},{6,17},{7,19},{8,4},{9,6},... | collective-permute-start | bytes 786440 | tf_op jit(solution)/shard_map/ppermute | solution.py:276
  169.2 25.0 %collective-permute-start.23 = (bf16[2,256,256]{2,1,0:T(8,128)(2,1)}, bf16[2,256,256]{2,1,0:T(8,128)(2,1)S(1)}, u32[]{:S(2)}, u32[]{:S(2)}) collective-permute-start(bf16[2,256,256]{2,1,0:T(8,128)(2,1)} %get-tuple-element.112), channel_id=1, source_target_pairs={{0,27},{1,25},{2,31},{3,29},{4,8},{5,10},{6,12},{7,14},{8,0},{9,2}... | collective-permute-start | bytes 786440 | tf_op jit(solution)/shard_map/ppermute | solution.py:276
  169.3 26.4 %collective-permute-start.24 = (bf16[2,256,256]{2,1,0:T(8,128)(2,1)}, bf16[2,256,256]{2,1,0:T(8,128)(2,1)S(1)}, u32[]{:S(2)}, u32[]{:S(2)}) collective-permute-start(bf16[2,256,256]{2,1,0:T(8,128)(2,1)} %get-tuple-element.113), channel_id=1, source_target_pairs={{0,22},{1,20},{2,27},{3,25},{4,7},{5,5},{6,8},{7,10},{8,31},{9,29}... | collective-permute-start | bytes 786440 | tf_op jit(solution)/shard_map/ppermute | solution.py:276
  194.2 17.1 %collective-permute-start.28 = (bf16[2,256,256]{2,1,0:T(8,128)(2,1)}, bf16[2,256,256]{2,1,0:T(8,128)(2,1)}, u32[]{:S(2)}, u32[]{:S(2)}) collective-permute-start(bf16[2,256,256]{2,1,0:T(8,128)(2,1)} %get-tuple-element.123), channel_id=1, source_target_pairs={{0,4},{1,6},{2,9},{3,11},{4,21},{5,23},{6,26},{7,24},{8,13},{9,15}... | collective-permute-start | bytes 786440 | tf_op jit(solution)/shard_map/ppermute | solution.py:276
  228.5 24.9 %collective-permute-start.33 = (bf16[2,256,256]{2,1,0:T(8,128)(2,1)S(1)}, bf16[2,256,256]{2,1,0:T(8,128)(2,1)S(1)}, u32[]{:S(2)}, u32[]{:S(2)}) collective-permute-start(bf16[2,256,256]{2,1,0:T(8,128)(2,1)S(1)} %get-tuple-element.129), channel_id=1, source_target_pairs={{0,20},{1,21},{2,22},{3,23},{4,16},{5,17},{6,18},{7,19},{8,28},{9,... | collective-permute-start | bytes 786440 | tf_op jit(solution)/shard_map/ppermute | solution.py:276
  230.4 23.0 %collective-permute-start.34 = (bf16[2,256,256]{2,1,0:T(8,128)(2,1)S(1)}, bf16[2,256,256]{2,1,0:T(8,128)(2,1)S(1)}, u32[]{:S(2)}, u32[]{:S(2)}) collective-permute-start(bf16[2,256,256]{2,1,0:T(8,128)(2,1)S(1)} %get-tuple-element.130), channel_id=1, source_target_pairs={{0,24},{1,25},{2,26},{3,27},{4,28},{5,29},{6,30},{7,31},{8,0},{9,1... | collective-permute-start | bytes 786440 | tf_op jit(solution)/shard_map/ppermute | solution.py:276
  231.5 21.9 %collective-permute-start.35 = (bf16[2,256,256]{2,1,0:T(8,128)(2,1)S(1)}, bf16[2,256,256]{2,1,0:T(8,128)(2,1)S(1)}, u32[]{:S(2)}, u32[]{:S(2)}) collective-permute-start(bf16[2,256,256]{2,1,0:T(8,128)(2,1)S(1)} %get-tuple-element.131), channel_id=1, source_target_pairs={{0,28},{1,29},{2,30},{3,31},{4,24},{5,25},{6,26},{7,27},{8,4},{9,5... | collective-permute-start | bytes 786440 | tf_op jit(solution)/shard_map/ppermute | solution.py:276
  (33 other events, 518.9 us)
Sparse Core Ops, SparseCore 0:
  23.6 52.9 all-gather.2

commit v5 on v4

--- a/solution.py
+++ b/solution.py
@@ -30,10 +30,6 @@
     return pltpu.CompilerParams(vmem_limit_bytes=mib * MIB)
 
 
-def cost(mib, flops=0):
-    return pl.CostEstimate(flops=int(flops), bytes_accessed=int(mib * MIB), transcendentals=0)
-
-
 def run_copies(copies):
     for copy in copies:
         copy.start()
@@ -45,24 +41,27 @@
     return 2 * lax.rem(column - shard + columns * 16, columns) + core
 
 
-def prep_kernel(shards, ids, w, *out):
-    pieces, slices = out[:shards], out[shards]
+def prep_kernel(shards, batches, ids, w, *out):
+    pieces, slices = out[:-1], out[-1]
     _, rows, piece = pieces[0].shape
     particles, _, _, cols = slices.shape
     columns = particles // 2
-    tiles, per_slice = piece // LANES, cols // LANES
+    ratio = particles // shards
+    tiles, per_slice = piece // LANES, cols // batches // LANES
+    stride = 2 * shards * batches * tiles
     for r in range(shards):
         q = lax.rem(ids[SHARD] - r + shards, shards)
-        for j in range(tiles):
-            e = q * (tiles // per_slice) + j // per_slice
-            column = lax.rem(lax.div(e, 2) + ids[SHARD], columns)
-            p = 2 * column + lax.rem(e, 2)
-            at, within = j * LANES, j % per_slice * LANES
-            for kind in range(2):
-                line = 2 * (q * tiles + j) + kind
-                part = w[pl.ds(line, rows, stride=2 * shards * tiles), :].astype(BF)
-                pieces[r][kind, :, at : at + LANES] = part
-                slices[p, kind, :, within : within + LANES] = part
+        for batch in range(batches):
+            for j in range(tiles):
+                e = q * ratio + j // per_slice
+                column = lax.rem(lax.div(e, 2) + ids[SHARD], columns)
+                p = 2 * column + lax.rem(e, 2)
+                at, within = j * LANES, (batch * per_slice + j % per_slice) * LANES
+                for kind in range(2):
+                    line = 2 * ((q * batches + batch) * tiles + j) + kind
+                    part = w[pl.ds(line, rows, stride=stride), :].astype(BF)
+                    pieces[batch * shards + r][kind, :, at : at + LANES] = part
+                    slices[p, kind, :, within : within + LANES] = part
 
 
 def up_kernel(shards, scale, ids, tokens, *refs):
@@ -212,12 +211,14 @@
     run_copies(copies)
 
 
-def adam_kernel(particles, ids, w, first, second, *refs):
-    sources = refs[:particles]
-    new_w, new_first, new_second, transport, field, sems = refs[particles:]
+def adam_kernel(shards, particles, batches, ids, w, first, second, *refs):
+    sources = refs[: batches * particles]
+    new_w, new_first, new_second, transport, field, sems = refs[batches * particles :]
     columns = particles // 2
     _, _, hidden = field.shape
-    width = hidden // particles
+    ratio = particles // shards
+    piece = hidden // shards // batches
+    width = piece // ratio
     step = pl.program_id(0)
 
     @pl.when(step == 0)
@@ -227,9 +228,12 @@
             for x in range(2):
                 column = lax.rem(ids[COL] - k + columns, columns)
                 core = ids[CORE] if x == 0 else 1 - ids[CORE]
-                at = pl.multiple_of(slice_index(ids, column, core, ids[SHARD], columns) * width, width)
-                i = 2 * k + x
-                copies.append(pltpu.make_async_copy(sources[i], field.at[:, :, pl.ds(at, width)], sems.at[i]))
+                e = slice_index(ids, column, core, ids[SHARD], columns)
+                for batch in range(batches):
+                    at = (lax.div(e, ratio) * batches + batch) * piece + lax.rem(e, ratio) * width
+                    at = pl.multiple_of(at, width)
+                    i = batch * particles + 2 * k + x
+                    copies.append(pltpu.make_async_copy(sources[i], field.at[:, :, pl.ds(at, width)], sems.at[i]))
         run_copies(copies)
 
     lane_tiles = hidden // LANES
@@ -254,7 +258,8 @@
     tok_rows = batch_index.shape[0]
     width = pool.shape[1]
     _, rows, _, hidden = weights.shape
-    part, cols = hidden // shards, hidden // particles
+    batches = 2 if hidden // particles >= 2 * LANES else 1
+    part, cols = hidden // shards // batches, hidden // particles
     tokens = tok_rows * shards
     blocks = tokens // BLOCK
     lane_tiles = hidden // LANES
@@ -291,24 +296,22 @@
     picked = jnp.take(pool, index, axis=0).astype(F32)
     normed = (picked * lax.rsqrt(jnp.mean(picked * picked, axis=1, keepdims=True) + 1e-06)).astype(BF)
 
-    def gather_tokens(x):
+    def shift_tokens(x):
         shifted = [[(dev(m, c, s), dev(m, c, (s + k) % shards)) for m, c, s in devices] for k in range(shards)]
-        x = jnp.stack([move(x, pairs) for pairs in shifted])
-        return lax.all_gather(x[None], "particle", axis=0, tiled=True)
+        return jnp.stack([move(x, pairs) for pairs in shifted])
 
     w_flat = flat(weights)
     steps = max(rows // 64, 1)
     lines = w_flat.shape[0] // steps
     *prepared, slices = pl.pallas_call(
-        functools.partial(prep_kernel, shards),
+        functools.partial(prep_kernel, shards, batches),
         grid=(steps,),
-        out_shape=[jax.ShapeDtypeStruct((2, rows, part), BF)] * shards
+        out_shape=[jax.ShapeDtypeStruct((2, rows, part), BF)] * (batches * shards)
         + [jax.ShapeDtypeStruct((particles, 2, rows, cols), BF)],
         in_specs=[smem_spec(), pl.BlockSpec((lines, LANES), lambda i: (i, 0))],
-        out_specs=[pl.BlockSpec((2, rows // steps, part), lambda i: (0, i, 0))] * shards
+        out_specs=[pl.BlockSpec((2, rows // steps, part), lambda i: (0, i, 0))] * (batches * shards)
         + [pl.BlockSpec((particles, 2, rows // steps, cols), lambda i: (0, 0, i, 0))],
         compiler_params=params(56),
-        cost_estimate=cost(16),
         name="prep",
     )(ids, w_flat)
 
@@ -337,8 +340,7 @@
             in_specs=[pl.BlockSpec(memory_space=pltpu.VMEM)],
             out_specs=pl.BlockSpec(memory_space=pltpu.VMEM),
             compiler_params=params(8),
-            cost_estimate=cost(4),
-            name="distances",
+                name="distances",
         )(whole)
 
     def add_over(sums, steps):
@@ -383,17 +385,13 @@
         ]
         alpha = [move(x, route) for x, route in zip(halves, first_routes)]
         own_c = move(cot, [(dev(m, c, s), dev(m, 1 - c, s)) for m, c, s in devices if c == s // half])
-        normed = gather_tokens(normed)
-        alpha, own_c, prepared = lax.optimization_barrier((alpha, own_c, prepared))
-        w_pieces = [move(x, route) for x, route in zip(prepared, w_routes)]
-        hand_on = [jnp.where(inner, a, x) for a, x in zip(alpha, halves)]
+        normed = shift_tokens(normed)
+        alpha, own_c, prepared, normed = lax.optimization_barrier((alpha, own_c, prepared, normed))
+        normed = lax.all_gather(normed[None], "particle", axis=0, tiled=True)
+        w_pieces = [move(x, w_routes[i % shards]) for i, x in enumerate(prepared)]
+        beta = [move(jnp.where(inner, a, x), route) for a, x, route in zip(alpha, halves, second_routes)]
         alpha_x = [move(x, swap_of(everyone)) for x in alpha]
-        beta = [move(hand_on[0], second_routes[0])]
-        hand_on[1], *w_pieces[:2] = lax.optimization_barrier((hand_on[1], *w_pieces[:2]))
-        beta.append(move(hand_on[1], second_routes[1]))
-        whole, alpha_x, beta[0] = lax.optimization_barrier((whole, alpha_x, beta[0]))
-        sums = add_over(pair_sums(whole), range(len(hops) - 3))
-        w_pieces, normed, sums = lax.optimization_barrier((w_pieces, normed, sums))
+        beta, alpha_x, w_pieces[:shards], normed = lax.optimization_barrier((beta, alpha_x, w_pieces[:shards], normed))
         beta_x = [move(x, swap_of(everyone)) for x in beta]
         sources = [cot, own_c, *alpha, *alpha_x, *beta, *beta_x]
 
@@ -437,9 +435,8 @@
     else:
         full = lax.all_gather(cotangent[0], "shard", axis=0, tiled=True)
         sources = [jnp.where(core == proc, full, move(full, swap_of(everyone)))]
-        w_pieces = [move(x, route) for x, route in zip(prepared, w_routes)]
-        normed = gather_tokens(normed)
-        sums = add_over(pair_sums(whole), range(len(hops) - 3))
+        w_pieces = [move(x, w_routes[i % shards]) for i, x in enumerate(prepared)]
+        normed = lax.all_gather(shift_tokens(normed)[None], "particle", axis=0, tiled=True)
 
         def pick(ids, refs, held, sem):
             def one(which, carry):
@@ -451,63 +448,9 @@
             lax.fori_loop(0, shards, one, 0)
 
     normed = normed.reshape(tokens, width)
-    act_t, slope_t, down_t = pl.pallas_call(
-        functools.partial(up_kernel, shards, width ** (-0.5)),
-        grid=(blocks,),
-        out_shape=[
-            jax.ShapeDtypeStruct((part, tokens), BF),
-            jax.ShapeDtypeStruct((part, tokens), BF),
-            jax.ShapeDtypeStruct((part, width), BF),
-        ],
-        in_specs=[smem_spec(), pl.BlockSpec((BLOCK, width), lambda i: (i, 0))]
-        + [pl.BlockSpec((2, rows, part), lambda i: (0, 0, 0))] * shards,
-        out_specs=[
-            pl.BlockSpec((part, BLOCK), lambda i: (0, i)),
-            pl.BlockSpec((part, BLOCK), lambda i: (0, i)),
-            pl.BlockSpec((part, width), lambda i: (0, 0)),
-        ],
-        scratch_shapes=[pltpu.VMEM((width, part), BF), pltpu.VMEM((width, part), BF), pltpu.VMEM((part, width), BF)],
-        compiler_params=params(56),
-        cost_estimate=cost(24, 2 * tokens * width * part),
-        name="up",
-    )(ids, normed, *w_pieces)
-
-    sums = add_over(sums, [-3])
-    sums, act_t, slope_t = lax.optimization_barrier((sums, act_t, slope_t))
     grad_scale = 1.0 / (tokens * width)
-    scores = pl.pallas_call(
-        functools.partial(
-            grad_kernel,
-            shards,
-            particles,
-            -(width ** (-0.5)) * grad_scale,
-            -(hidden ** (-0.5)) * grad_scale,
-            hidden ** (-0.5),
-            pick,
-        ),
-        out_shape=[jax.ShapeDtypeStruct((2, rows, cols), BF)] * particles,
-        in_specs=[smem_spec()] + [any_spec()] * (4 + len(sources)),
-        out_specs=[any_spec()] * particles,
-        scratch_shapes=[
-            pltpu.VMEM((tokens, width), BF),
-            pltpu.VMEM((tokens, width), BF),
-            pltpu.VMEM((part, tokens), BF),
-            pltpu.VMEM((part, tokens), BF),
-            pltpu.VMEM((part, tokens), BF),
-            pltpu.VMEM((part, width), BF),
-            pltpu.VMEM((2, width, part), BF),
-            pltpu.SemaphoreType.DMA((particles + 5,)),
-        ],
-        compiler_params=params(56),
-        cost_estimate=cost(32, 6 * tokens * width * part),
-        name="grads",
-    )(ids, normed, act_t, slope_t, down_t, *sources)
-
-    sums = add_over(sums, [-2])
-    sums, *scores = lax.optimization_barrier((sums, *scores))
-
     ratio = particles // shards
-    arrived = []
+    score_routes = []
     for t in range(particles):
         pairs = []
         for m, c, s in devices:
@@ -515,10 +458,78 @@
             u = (mine + ratio * q - t) % particles
             z, e = u // ratio, q * ratio + u % ratio
             pairs.append((dev(m, c, s), dev(e // 2 + z, e % 2, z)))
-        arrived.append(move(scores[t], pairs))
-
+        score_routes.append(pairs)
+
+    def up(pieces):
+        return pl.pallas_call(
+            functools.partial(up_kernel, shards, width ** (-0.5)),
+            grid=(blocks,),
+            out_shape=[
+                jax.ShapeDtypeStruct((part, tokens), BF),
+                jax.ShapeDtypeStruct((part, tokens), BF),
+                jax.ShapeDtypeStruct((part, width), BF),
+            ],
+            in_specs=[smem_spec(), pl.BlockSpec((BLOCK, width), lambda i: (i, 0))]
+            + [pl.BlockSpec((2, rows, part), lambda i: (0, 0, 0))] * shards,
+            out_specs=[
+                pl.BlockSpec((part, BLOCK), lambda i: (0, i)),
+                pl.BlockSpec((part, BLOCK), lambda i: (0, i)),
+                pl.BlockSpec((part, width), lambda i: (0, 0)),
+            ],
+            scratch_shapes=[
+                pltpu.VMEM((width, part), BF),
+                pltpu.VMEM((width, part), BF),
+                pltpu.VMEM((part, width), BF),
+            ],
+            compiler_params=params(56),
+            name="up",
+        )(ids, normed, *pieces)
+
+    def gradients(act_t, slope_t, down_t):
+        return pl.pallas_call(
+            functools.partial(
+                grad_kernel,
+                shards,
+                particles,
+                -(width ** (-0.5)) * grad_scale,
+                -(hidden ** (-0.5)) * grad_scale,
+                hidden ** (-0.5),
+                pick,
+            ),
+            out_shape=[jax.ShapeDtypeStruct((2, rows, cols // batches), BF)] * particles,
+            in_specs=[smem_spec()] + [any_spec()] * (4 + len(sources)),
+            out_specs=[any_spec()] * particles,
+            scratch_shapes=[
+                pltpu.VMEM((tokens, width), BF),
+                pltpu.VMEM((tokens, width), BF),
+                pltpu.VMEM((part, tokens), BF),
+                pltpu.VMEM((part, tokens), BF),
+                pltpu.VMEM((part, tokens), BF),
+                pltpu.VMEM((part, width), BF),
+                pltpu.VMEM((2, width, part), BF),
+                pltpu.SemaphoreType.DMA((particles + 5,)),
+            ],
+            compiler_params=params(56),
+            name="grads",
+        )(ids, normed, act_t, slope_t, down_t, *sources)
+
+    arrived, sums = [], None
+    for batch in range(batches):
+        act_t, slope_t, down_t = up(w_pieces[batch * shards : (batch + 1) * shards])
+        if batch == 0:
+            whole, act_t = lax.optimization_barrier((whole, act_t))
+            sums = add_over(pair_sums(whole), range(len(hops) - 3))
+        else:
+            sums = add_over(sums, [-3])
+            sums, act_t = lax.optimization_barrier((sums, act_t))
+        scores = gradients(act_t, slope_t, down_t)
+        sums, *scores = lax.optimization_barrier((sums, *scores))
+        arrived.append([move(x, route) for x, route in zip(scores, score_routes)])
+    if batches == 1:
+        sums = add_over(sums, [-3])
+    sums = add_over(sums, [-2])
     rest = move(sums, hops[-1])
-    sums, rest, *arrived[:4] = lax.optimization_barrier((sums, rest, *arrived[:4]))
+    sums, rest, arrived[0] = lax.optimization_barrier((sums, rest, arrived[0]))
     sums = sums + rest
     sums = sums[0]
     lookup = [
@@ -535,39 +546,43 @@
         [(scale * kernel).reshape(-1), scale * repulse * jnp.sum(kernel, axis=1), repulse[None]]
     )
 
-    fields = pl.pallas_call(
-        functools.partial(stein_kernel, shards, particles),
-        out_shape=[jax.ShapeDtypeStruct((2, rows, cols), BF)] * particles,
-        in_specs=[smem_spec(), smem_spec(), pl.BlockSpec(memory_space=pltpu.VMEM)] + [any_spec()] * particles,
-        out_specs=[any_spec()] * particles,
-        scratch_shapes=[
-            pltpu.VMEM((particles, 2, rows, cols), BF),
-            pltpu.VMEM((particles, 2, rows, cols), BF),
-            pltpu.SemaphoreType.DMA((particles,)),
-        ],
-        compiler_params=params(12),
-        cost_estimate=cost(12),
-        name="stein",
-    )(ids, coef, whole, *arrived)
-
     back = []
-    for k in range(columns):
-        for x in range(2):
-            pairs = [(dev(m, c, s), dev(m + k, c ^ x, s)) for m, c, s in devices]
-            back.append(move(fields[2 * k + x], pairs))
+    for batch in range(batches):
+        fields = pl.pallas_call(
+            functools.partial(stein_kernel, shards, particles),
+            grid=(1,),
+            out_shape=[jax.ShapeDtypeStruct((2, rows, cols // batches), BF)] * particles,
+            in_specs=[
+                smem_spec(),
+                smem_spec(),
+                pl.BlockSpec((particles, 2, rows, cols // batches), lambda i, batch=batch: (0, 0, 0, batch)),
+            ]
+            + [any_spec()] * particles,
+            out_specs=[any_spec()] * particles,
+            scratch_shapes=[
+                pltpu.VMEM((particles, 2, rows, cols // batches), BF),
+                pltpu.VMEM((particles, 2, rows, cols // batches), BF),
+                pltpu.SemaphoreType.DMA((particles,)),
+            ],
+            compiler_params=params(12),
+            name="stein",
+        )(ids, coef, whole, *arrived[batch])
+        for k in range(columns):
+            for x in range(2):
+                pairs = [(dev(m, c, s), dev(m + k, c ^ x, s)) for m, c, s in devices]
+                back.append(move(fields[2 * k + x], pairs))
 
     steps = max(rows // 32, 1)
     flat_rows = rows * 2 * lane_tiles
     state_spec = pl.BlockSpec((flat_rows // steps, LANES), lambda i: (i, 0))
     outs = pl.pallas_call(
-        functools.partial(adam_kernel, particles),
+        functools.partial(adam_kernel, shards, particles, batches),
         grid=(steps,),
         out_shape=[jax.ShapeDtypeStruct((flat_rows, LANES), F32)] * 4,
-        in_specs=[smem_spec()] + [state_spec] * 3 + [any_spec()] * particles,
+        in_specs=[smem_spec()] + [state_spec] * 3 + [any_spec()] * len(back),
         out_specs=[state_spec] * 4,
-        scratch_shapes=[pltpu.VMEM((2, rows, hidden), BF), pltpu.SemaphoreType.DMA((particles,))],
+        scratch_shapes=[pltpu.VMEM((2, rows, hidden), BF), pltpu.SemaphoreType.DMA((len(back),))],
         compiler_params=params(56),
-        cost_estimate=cost(32),
         name="adam",
     )(ids, w_flat, flat(first_moment), flat(second_moment), *back)
     return tuple(unflat(x) for x in outs)

time: 279 us -> 283 us (1.014)
  waiting for transfers between devices: 96.4 us -> 51.6 us
  starting transfers between devices: 102 us -> 126 us
  Pallas kernels: 54.7 us -> 73.4 us
  local copies, waits for them, and re-layouts: 5.33 us -> 9.49 us
    ppermute x36 -> x55, waiting for transfers between devices: 96.3 us -> 51.6 us  [move(): return lax.ppermute(x, AXES, pairs)]
    ppermute x36 -> x55, starting transfers between devices: 97.7 us -> 118 us  [move(): return lax.ppermute(x, AXES, pairs)]
    pallas_call x5 -> x8, Pallas kernels: 52.6 us -> 71.3 us  [the longest x2 19.6 us: gradients(): pl.pallas_call(functools.partial(grad_kernel, shards, particles, -width *...]
    all_to_all x1, starting transfers between devices: 3.95 us -> 8.2 us  [local(): whole = lax.all_to_all(slices, 'particle', 0, 0, tiled=True)]
  transfers between devices with their start and end apart: 38 -> 57, of which waited for: 15 -> 12; matrix products, arithmetic and copies ran while one was open for 1% -> 2% of each run, Pallas kernels for 12% -> 21%
where the time goes in v5:
time: 283 us; the launch traced here: 279 us
  starting transfers between devices  126 us (45%)
  Pallas kernels  73.4 us (26%)
  waiting for transfers between devices  51.6 us (18%)
  between operations  15.5 us (5%)
  local copies, waits for them, and re-layouts  9.49 us (3%)
    ppermute x55, starting transfers between devices, move(): return lax.ppermute(x, AXES, pairs)  118 us
    ppermute x55, waiting for transfers between devices, move(): return lax.ppermute(x, AXES, pairs)  51.6 us
    pallas_call x2, Pallas kernels, gradients(): pl.pallas_call(functools.partial(grad_kernel, shards, particles, -width *...  19.6 us
    pallas_call x2, Pallas kernels, up(): pl.pallas_call(functools.partial(up_kernel, shards, width ** (-0.5)), gri...  16.8 us
    pallas_call x1, Pallas kernels, local(): pl.pallas_call(functools.partial(adam_kernel, shards, particles, batches)...  15.5 us
    pallas_call x2, Pallas kernels, local(): pl.pallas_call(functools.partial(stein_kernel, shards, particles), grid=(...  12.6 us
    all_to_all x1, starting transfers between devices, local(): whole = lax.all_to_all(slices, 'particle', 0, 0, tiled=True)  8.2 us
    pallas_call x1, Pallas kernels, local(): pl.pallas_call(functools.partial(prep_kernel, shards, batches), grid=(ste...  6.86 us
  transfers between devices with their start and end apart: 57, of which 12 were waited for; matrix products, arithmetic and copies ran while one was open for 2% of the time, Pallas kernels for 21%

profile of v5, /device:TPU:23, one launch (start us, length us, event | category | flops | bytes accessed | tf_op | source)
XLA Modules:
  0.0 278.5 jit_solution(3358003046283882651)
XLA Ops:
  9.7 3.8 %collective-permute-start.1 = (bf16[256,1024]{1,0:T(8,128)(2,1)}, bf16[256,1024]{1,0:T(8,128)(2,1)S(1)}, u32[]{:S(2)}, u32[]{:S(2)}) collective-permute-start(bf16[256,1024]{1,0:T(8,128)(2,1)} %get-tuple-element.214), channel_id=1, source_target_pairs={{1,4},{2,5},{3,1},{4,6},{5,2},{6,3},{9,12},{10,13},{11,9},{12,14},... | collective-permute-start | bytes 1572872 | tf_op jit(solution)/shard_map/ppermute | solution.py:281
  20.0 4.0 %collective-permute-start.4 = (bf16[64,1024]{1,0:T(8,128)(2,1)S(1)}, bf16[64,1024]{1,0:T(8,128)(2,1)S(1)}, u32[]{:S(2)}, u32[]{:S(2)}) collective-permute-start(bf16[64,1024]{1,0:T(8,128)(2,1)S(1)} %fusion.1), channel_id=1, source_target_pairs={{0,2},{1,3},{2,0},{3,1},{4,6},{5,7},{6,4},{7,5},{8,10},{9,11},{10,... | collective-permute-start | bytes 393224 | tf_op jit(solution)/shard_map/ppermute | solution.py:281
  24.6 6.9 %prep.1 = (bf16[2,256,256]{2,1,0:T(8,128)(2,1)}, bf16[2,256,256]{2,1,0:T(8,128)(2,1)}, bf16[2,256,256]{2,1,0:T(8,128)(2,1)}, bf16[2,256,256]{2,1,0:T(8,128)(2,1)...) custom-call(s32[5]{0:T(128)} %stack.36.ids, ...), custom_call_target="tpu_custom_call" | custom-call | tf_op jit(solution)/shard_map/prep/pallas_call | solution.py:306
  31.9 5.2 %collective-permute-done.4 = bf16[64,1024]{1,0:T(8,128)(2,1)S(1)} collective-permute-done((bf16[64,1024]{1,0:T(8,128)(2,1)S(1)}, bf16[64,1024]{1,0:T(8,128)(2,1)S(1)}, u32[]{:S(2)}, u32[]{:S(2)}) %collective-permute-start.4) | collective-permute-done | bytes 131104 | tf_op jit(solution)/shard_map/ppermute | solution.py:281
  37.1 9.9 %collective-permute-done.3 = bf16[64,1024]{1,0:T(8,128)(2,1)S(1)} collective-permute-done((bf16[64,1024]{1,0:T(8,128)(2,1)S(1)}, bf16[64,1024]{1,0:T(8,128)(2,1)S(1)}, u32[]{:S(2)}, u32[]{:S(2)}) %collective-permute-start.3) | collective-permute-done | bytes 131104 | tf_op jit(solution)/shard_map/ppermute | solution.py:281
  47.9 8.2 %all-to-all-start = ((bf16[8,2,256,256]{3,2,1,0:T(8,128)(2,1)}), bf16[8,2,256,256]{3,2,1,0:T(8,128)(2,1)S(1)}, u32[]{:S(2)}, u32[]{:S(2)}) async-start(bf16[8,2,256,256]{3,2,1,0:T(8,128)(2,1)} %get-tuple-element.108), calls=%async_computation | async-start | bytes 4194304 | tf_op jit(solution)/shard_map/all_to_all | solution.py:326
  63.8 4.6 %collective-permute-start.7 = (bf16[256,1024]{1,0:T(8,128)(2,1)S(1)}, bf16[256,1024]{1,0:T(8,128)(2,1)S(1)}, u32[]{:S(2)}, u32[]{:S(2)}) collective-permute-start(bf16[256,1024]{1,0:T(8,128)(2,1)S(1)} %broadcast_select_fusion), channel_id=1, source_target_pairs={{0,5},{1,0},{2,3},{5,4},{6,7},{7,2},{8,13},{9,8},{10,11},{13,12},{... | collective-permute-start | bytes 1572872 | tf_op jit(solution)/shard_map/ppermute | solution.py:281
  70.8 4.0 %collective-permute-start.9 = (bf16[256,1024]{1,0:T(8,128)(2,1)S(1)}, bf16[256,1024]{1,0:T(8,128)(2,1)}, u32[]{:S(2)}, u32[]{:S(2)}) collective-permute-start(bf16[256,1024]{1,0:T(8,128)(2,1)S(1)} %collective-permute-done.1.refs_3_), channel_id=1, source_target_pairs={{0,4},{1,5},{2,6},{3,7},{4,0},{5,1},{6,2},{7,3},{8,12},{9,13},{10,... | collective-permute-start | bytes 1572872 | tf_op jit(solution)/shard_map/ppermute | solution.py:281
  74.8 6.4 %collective-permute-start.13 = (bf16[2,256,256]{2,1,0:T(8,128)(2,1)S(1)}, bf16[2,256,256]{2,1,0:T(8,128)(2,1)S(1)}, u32[]{:S(2)}, u32[]{:S(2)}) collective-permute-start(bf16[2,256,256]{2,1,0:T(8,128)(2,1)S(1)} %copy-done.32), channel_id=1, source_target_pairs={{0,4},{1,1},{2,5},{3,0},{4,6},{5,3},{6,7},{7,2},{8,12},{9,9},{10,1... | collective-permute-start | bytes 786440 | tf_op jit(solution)/shard_map/ppermute | solution.py:281
  81.2 21.7 %collective-permute-done.13.refs_3_ = bf16[2,256,256]{2,1,0:T(8,128)(2,1)S(1)} collective-permute-done((bf16[2,256,256]{2,1,0:T(8,128)(2,1)S(1)}, bf16[2,256,256]{2,1,0:T(8,128)(2,1)S(1)}, u32[]{:S(2)}, u32[]{:S(2)}) %collective-permute-start.13) | collective-permute-done | bytes 262176 | tf_op jit(solution)/shard_map/ppermute | solution.py:281
  105.3 3.8 %collective-permute-start.19 = (bf16[2,256,256]{2,1,0:T(8,128)(2,1)}, bf16[2,256,256]{2,1,0:T(8,128)(2,1)S(1)}, u32[]{:S(2)}, u32[]{:S(2)}) collective-permute-start(bf16[2,256,256]{2,1,0:T(8,128)(2,1)} %get-tuple-element.148), channel_id=1, source_target_pairs={{0,0},{1,4},{2,1},{3,5},{4,2},{5,6},{6,3},{7,7},{8,8},{9,12},{10,9... | collective-permute-start | bytes 786440 | tf_op jit(solution)/shard_map/ppermute | solution.py:281
  112.7 8.4 %up.2 = (bf16[256,2048]{1,0:T(8,128)(2,1)}, bf16[256,2048]{1,0:T(8,128)(2,1)}, bf16[256,1024]{1,0:T(8,128)(2,1)}) custom-call(s32[5]{0:T(128)} %stack.36.ids, bf16[2048,1024]{1,0:T(8,128)(2,1)} %bitcast.58, bf16[2,256,256]{2,1,0:T(8,128)(2,1)} %copy-done.11, bf16[2,256,256]{2,1,0:T(8,128)(2,1)} %copy-done.12, bf16[2,256,256]{2,1,0:T(8,128)(2,1)} %copy-done.13, ...), custom_call_target="tpu_custom_call" | custom-call | tf_op jit(solution)/shard_map/up/pallas_call | solution.py:464
  130.3 9.8 %grads.2 = (bf16[2,256,128]{2,1,0:T(8,128)(2,1)}, bf16[2,256,128]{2,1,0:T(8,128)(2,1)}, bf16[2,256,128]{2,1,0:T(8,128)(2,1)}, bf16[2,256,128]{2,1,0:T(8,128)(2,1...) custom-call(s32[5]{0:T(128)} %stack.36.ids, ...), custom_call_target="tpu_custom_call" | custom-call | tf_op jit(solution)/shard_map/grads/pallas_call | solution.py:489
  140.1 4.5 %collective-permute-start.25 = (bf16[2,256,128]{2,1,0:T(8,128)(2,1)}, bf16[2,256,128]{2,1,0:T(8,128)(2,1)S(1)}, u32[]{:S(2)}, u32[]{:S(2)}) collective-permute-start(bf16[2,256,128]{2,1,0:T(8,128)(2,1)} %get-tuple-element.166), channel_id=1, source_target_pairs={{0,0},{1,2},{2,4},{3,6},{4,17},{5,19},{6,21},{7,23},{8,9},{9,11},{... | collective-permute-start | bytes 393224 | tf_op jit(solution)/shard_map/ppermute | solution.py:281
  150.6 8.4 %up.3 = (bf16[256,2048]{1,0:T(8,128)(2,1)}, bf16[256,2048]{1,0:T(8,128)(2,1)}, bf16[256,1024]{1,0:T(8,128)(2,1)}) custom-call(s32[5]{0:T(128)} %stack.36.ids, bf16[2048,1024]{1,0:T(8,128)(2,1)} %bitcast.60, bf16[2,256,256]{2,1,0:T(8,128)(2,1)} %copy-done.10, bf16[2,256,256]{2,1,0:T(8,128)(2,1)} %collective-permute-done.20.refs_1_, ...), custom_call_target="tpu_custom_call" | custom-call | tf_op jit(solution)/shard_map/up/pallas_call | solution.py:464
  159.0 9.8 %grads.3 = (bf16[2,256,128]{2,1,0:T(8,128)(2,1)}, bf16[2,256,128]{2,1,0:T(8,128)(2,1)}, bf16[2,256,128]{2,1,0:T(8,128)(2,1)}, bf16[2,256,128]{2,1,0:T(8,128)(2,1...) custom-call(s32[5]{0:T(128)} %stack.36.ids, ...), custom_call_target="tpu_custom_call" | custom-call | tf_op jit(solution)/shard_map/grads/pallas_call | solution.py:489
  185.7 4.1 %collective-permute-start.40 = (bf16[2,256,128]{2,1,0:T(8,128)(2,1)}, bf16[2,256,128]{2,1,0:T(8,128)(2,1)S(1)}, u32[]{:S(2)}, u32[]{:S(2)}) collective-permute-start(bf16[2,256,128]{2,1,0:T(8,128)(2,1)} %get-tuple-element.192), channel_id=1, source_target_pairs={{0,0},{1,2},{2,4},{3,6},{4,17},{5,19},{6,21},{7,23},{8,9},{9,11},{... | collective-permute-start | bytes 393224 | tf_op jit(solution)/shard_map/ppermute | solution.py:281
  189.8 4.1 %collective-permute-start.41 = (bf16[2,256,128]{2,1,0:T(8,128)(2,1)}, bf16[2,256,128]{2,1,0:T(8,128)(2,1)S(1)}, u32[]{:S(2)}, u32[]{:S(2)}) collective-permute-start(bf16[2,256,128]{2,1,0:T(8,128)(2,1)} %get-tuple-element.193), channel_id=1, source_target_pairs={{0,31},{1,29},{2,0},{3,2},{4,12},{5,14},{6,17},{7,19},{8,4},{9,6},... | collective-permute-start | bytes 393224 | tf_op jit(solution)/shard_map/ppermute | solution.py:281
  196.7 6.3 %collective-permute-start.43 = (bf16[2,256,128]{2,1,0:T(8,128)(2,1)}, bf16[2,256,128]{2,1,0:T(8,128)(2,1)S(1)}, u32[]{:S(2)}, u32[]{:S(2)}) collective-permute-start(bf16[2,256,128]{2,1,0:T(8,128)(2,1)} %get-tuple-element.195), channel_id=1, source_target_pairs={{0,22},{1,20},{2,27},{3,25},{4,7},{5,5},{6,8},{7,10},{8,31},{9,29}... | collective-permute-start | bytes 393224 | tf_op jit(solution)/shard_map/ppermute | solution.py:281
  209.2 5.9 %collective-permute-start.47 = (bf16[2,256,128]{2,1,0:T(8,128)(2,1)}, bf16[2,256,128]{2,1,0:T(8,128)(2,1)S(1)}, u32[]{:S(2)}, u32[]{:S(2)}) collective-permute-start(bf16[2,256,128]{2,1,0:T(8,128)(2,1)} %get-tuple-element.199), channel_id=1, source_target_pairs={{0,4},{1,6},{2,9},{3,11},{4,21},{5,23},{6,26},{7,24},{8,13},{9,15}... | collective-permute-start | bytes 393224 | tf_op jit(solution)/shard_map/ppermute | solution.py:281
  215.0 6.5 %stein.2 = (bf16[2,256,128]{2,1,0:T(8,128)(2,1)S(1)}, bf16[2,256,128]{2,1,0:T(8,128)(2,1)S(1)}, bf16[2,256,128]{2,1,0:T(8,128)(2,1)S(1)}, bf16[2,256,128]{2,1,0:...) custom-call(s32[5]{0:T(128)S(1)} %copy-done.4, ...), custom_call_target="tpu_custom_call" | custom-call | tf_op jit(solution)/shard_map/stein/pallas_call | solution.py:551
  228.2 6.1 %stein.3 = (bf16[2,256,128]{2,1,0:T(8,128)(2,1)S(1)}, bf16[2,256,128]{2,1,0:T(8,128)(2,1)S(1)}, bf16[2,256,128]{2,1,0:T(8,128)(2,1)S(1)}, bf16[2,256,128]{2,1,0:...) custom-call(s32[5]{0:T(128)S(1)} %copy-done.4, ...), custom_call_target="tpu_custom_call" | custom-call | tf_op jit(solution)/shard_map/stein/pallas_call | solution.py:551
  250.7 4.7 %collective-permute-done.52.refs_13_ = bf16[2,256,128]{2,1,0:T(8,128)(2,1)S(1)} collective-permute-done((bf16[2,256,128]{2,1,0:T(8,128)(2,1)S(1)}, bf16[2,256,128]{2,1,0:T(8,128)(2,1)S(1)}, u32[]{:S(2)}, u32[]{:S(2)}) %collective-permute-start.52) | collective-permute-done | bytes 131104 | tf_op jit(solution)/shard_map/ppermute | solution.py:281
  256.1 15.5 %adam.1 = (f32[8192,128]{1,0:T(8,128)}, f32[8192,128]{1,0:T(8,128)}, f32[8192,128]{1,0:T(8,128)}, f32[8192,128]{1,0:T(8,128)}) custom-call(s32[5]{0:T(128)} %stack.36.ids, f32[8192,128]{1,0:T(8,128)} %bitcast.63, f32[8192,128]{1,0:T(8,128)} %bitcast.67, f32[8192,128]{1,0:T(8,128)} %bitcast.68, bf16[2,256,128]{2,1,0:T(8,128)(2,1)} %copy-done.2, ...), custom_call_target="tpu_custom_call" | custom-call | tf_op jit(solution)/shard_map/adam/pallas_call | solution.py:578
  (199 shorter events, 90.6 us)
Async XLA Ops:
  7.2 97.6 %all-gather.3.cloned.1.call-start = ((), (), s32[]{:S(2)}) async-start(), calls=%async_computation.1 | async-start | bytes 4718592 | tf_op jit(solution)/shard_map/all_gather | solution.py:390
  9.7 38.2 %collective-permute-start.1 = (bf16[256,1024]{1,0:T(8,128)(2,1)}, bf16[256,1024]{1,0:T(8,128)(2,1)S(1)}, u32[]{:S(2)}, u32[]{:S(2)}) collective-permute-start(bf16[256,1024]{1,0:T(8,128)(2,1)} %get-tuple-element.214), channel_id=1, source_target_pairs={{1,4},{2,5},{3,1},{4,6},{5,2},{6,3},{9,12},{10,13},{11,9},{12,14},... | collective-permute-start | bytes 1572872 | tf_op jit(solution)/shard_map/ppermute | solution.py:281
  13.4 34.5 %collective-permute-start = (bf16[256,1024]{1,0:T(8,128)(2,1)}, bf16[256,1024]{1,0:T(8,128)(2,1)S(1)}, u32[]{:S(2)}, u32[]{:S(2)}) collective-permute-start(bf16[256,1024]{1,0:T(8,128)(2,1)} %get-tuple-element.215), channel_id=1, source_target_pairs={{1,0},{2,1},{3,5},{4,2},{5,6},{6,7},{9,8},{10,9},{11,13},{12,10},{... | collective-permute-start | bytes 1572872 | tf_op jit(solution)/shard_map/ppermute | solution.py:281
  15.3 32.6 %collective-permute-start.2 = (bf16[512,1024]{1,0:T(8,128)(2,1)}, bf16[512,1024]{1,0:T(8,128)(2,1)}, u32[]{:S(2)}, u32[]{:S(2)}) collective-permute-start(bf16[512,1024]{1,0:T(8,128)(2,1)} %bitcast.64), channel_id=1, source_target_pairs={{0,4},{1,5},{6,2},{7,3},{8,12},{9,13},{14,10},{15,11},{16,20},{17,... | collective-permute-start | bytes 3145736 | tf_op jit(solution)/shard_map/ppermute | solution.py:281
  47.9 73.1 %all-to-all-start = ((bf16[8,2,256,256]{3,2,1,0:T(8,128)(2,1)}), bf16[8,2,256,256]{3,2,1,0:T(8,128)(2,1)S(1)}, u32[]{:S(2)}, u32[]{:S(2)}) async-start(bf16[8,2,256,256]{3,2,1,0:T(8,128)(2,1)} %get-tuple-element.108), calls=%async_computation | async-start | bytes 4194304 | tf_op jit(solution)/shard_map/all_to_all | solution.py:326
  63.0 39.9 %collective-permute-start.8 = (bf16[256,1024]{1,0:T(8,128)(2,1)S(1)}, bf16[256,1024]{1,0:T(8,128)(2,1)S(1)}, u32[]{:S(2)}, u32[]{:S(2)}) collective-permute-start(bf16[256,1024]{1,0:T(8,128)(2,1)S(1)} %collective-permute-done.refs_2_), channel_id=1, source_target_pairs={{0,4},{1,5},{2,6},{3,7},{4,0},{5,1},{6,2},{7,3},{8,12},{9,13},{10,... | collective-permute-start | bytes 1572872 | tf_op jit(solution)/shard_map/ppermute | solution.py:281
  63.8 39.1 %collective-permute-start.7 = (bf16[256,1024]{1,0:T(8,128)(2,1)S(1)}, bf16[256,1024]{1,0:T(8,128)(2,1)S(1)}, u32[]{:S(2)}, u32[]{:S(2)}) collective-permute-start(bf16[256,1024]{1,0:T(8,128)(2,1)S(1)} %broadcast_select_fusion), channel_id=1, source_target_pairs={{0,5},{1,0},{2,3},{5,4},{6,7},{7,2},{8,13},{9,8},{10,11},{13,12},{... | collective-permute-start | bytes 1572872 | tf_op jit(solution)/shard_map/ppermute | solution.py:281
  68.9 34.0 %collective-permute-start.6 = (bf16[256,1024]{1,0:T(8,128)(2,1)S(1)}, bf16[256,1024]{1,0:T(8,128)(2,1)S(1)}, u32[]{:S(2)}, u32[]{:S(2)}) collective-permute-start(bf16[256,1024]{1,0:T(8,128)(2,1)S(1)} %broadcast_select_fusion.1), channel_id=1, source_target_pairs={{0,1},{1,0},{2,3},{5,4},{6,7},{7,6},{8,9},{9,8},{10,11},{13,12},{1... | collective-permute-start | bytes 1572872 | tf_op jit(solution)/shard_map/ppermute | solution.py:281
  70.8 34.0 %collective-permute-start.9 = (bf16[256,1024]{1,0:T(8,128)(2,1)S(1)}, bf16[256,1024]{1,0:T(8,128)(2,1)}, u32[]{:S(2)}, u32[]{:S(2)}) collective-permute-start(bf16[256,1024]{1,0:T(8,128)(2,1)S(1)} %collective-permute-done.1.refs_3_), channel_id=1, source_target_pairs={{0,4},{1,5},{2,6},{3,7},{4,0},{5,1},{6,2},{7,3},{8,12},{9,13},{10,... | collective-permute-start | bytes 1572872 | tf_op jit(solution)/shard_map/ppermute | solution.py:281
  74.8 28.1 %collective-permute-start.13 = (bf16[2,256,256]{2,1,0:T(8,128)(2,1)S(1)}, bf16[2,256,256]{2,1,0:T(8,128)(2,1)S(1)}, u32[]{:S(2)}, u32[]{:S(2)}) collective-permute-start(bf16[2,256,256]{2,1,0:T(8,128)(2,1)S(1)} %copy-done.32), channel_id=1, source_target_pairs={{0,4},{1,1},{2,5},{3,0},{4,6},{5,3},{6,7},{7,2},{8,12},{9,9},{10,1... | collective-permute-start | bytes 786440 | tf_op jit(solution)/shard_map/ppermute | solution.py:281
  104.8 23.4 %collective-permute-start.16 = (bf16[256,1024]{1,0:T(8,128)(2,1)}, bf16[256,1024]{1,0:T(8,128)(2,1)}, u32[]{:S(2)}, u32[]{:S(2)}) collective-permute-start(bf16[256,1024]{1,0:T(8,128)(2,1)} %copy-done.9), channel_id=1, source_target_pairs={{0,4},{1,5},{2,6},{3,7},{4,0},{5,1},{6,2},{7,3},{8,12},{9,13},{10,... | collective-permute-start | bytes 1572872 | tf_op jit(solution)/shard_map/ppermute | solution.py:281
  104.8 25.4 %collective-permute-start.17 = (bf16[256,1024]{1,0:T(8,128)(2,1)}, bf16[256,1024]{1,0:T(8,128)(2,1)}, u32[]{:S(2)}, u32[]{:S(2)}) collective-permute-start(bf16[256,1024]{1,0:T(8,128)(2,1)} %copy-done.8), channel_id=1, source_target_pairs={{0,4},{1,5},{2,6},{3,7},{4,0},{5,1},{6,2},{7,3},{8,12},{9,13},{10,... | collective-permute-start | bytes 1572872 | tf_op jit(solution)/shard_map/ppermute | solution.py:281
  105.3 39.2 %collective-permute-start.19 = (bf16[2,256,256]{2,1,0:T(8,128)(2,1)}, bf16[2,256,256]{2,1,0:T(8,128)(2,1)S(1)}, u32[]{:S(2)}, u32[]{:S(2)}) collective-permute-start(bf16[2,256,256]{2,1,0:T(8,128)(2,1)} %get-tuple-element.148), channel_id=1, source_target_pairs={{0,0},{1,4},{2,1},{3,5},{4,2},{5,6},{6,3},{7,7},{8,8},{9,12},{10,9... | collective-permute-start | bytes 786440 | tf_op jit(solution)/shard_map/ppermute | solution.py:281
  109.1 37.8 %collective-permute-start.20 = (bf16[2,256,256]{2,1,0:T(8,128)(2,1)}, bf16[2,256,256]{2,1,0:T(8,128)(2,1)}, u32[]{:S(2)}, u32[]{:S(2)}) collective-permute-start(bf16[2,256,256]{2,1,0:T(8,128)(2,1)} %get-tuple-element.149), channel_id=1, source_target_pairs={{0,5},{1,0},{2,4},{3,1},{4,7},{5,2},{6,6},{7,3},{8,13},{9,8},{10,1... | collective-permute-start | bytes 786440 | tf_op jit(solution)/shard_map/ppermute | solution.py:281
  126.9 22.3 %collective-permute-start.21 = (bf16[2,256,256]{2,1,0:T(8,128)(2,1)}, bf16[2,256,256]{2,1,0:T(8,128)(2,1)S(1)}, u32[]{:S(2)}, u32[]{:S(2)}) collective-permute-start(bf16[2,256,256]{2,1,0:T(8,128)(2,1)} %get-tuple-element.150), channel_id=1, source_target_pairs={{0,1},{1,5},{2,0},{3,4},{4,3},{5,7},{6,2},{7,6},{8,9},{9,13},{10,8... | collective-permute-start | bytes 786440 | tf_op jit(solution)/shard_map/ppermute | solution.py:281
  128.2 21.4 %collective-permute-start.22 = (bf16[2,256,256]{2,1,0:T(8,128)(2,1)}, bf16[2,256,256]{2,1,0:T(8,128)(2,1)S(1)}, u32[]{:S(2)}, u32[]{:S(2)}) collective-permute-start(bf16[2,256,256]{2,1,0:T(8,128)(2,1)} %get-tuple-element.151), channel_id=1, source_target_pairs={{0,4},{1,1},{2,5},{3,0},{4,6},{5,3},{6,7},{7,2},{8,12},{9,9},{10,1... | collective-permute-start | bytes 786440 | tf_op jit(solution)/shard_map/ppermute | solution.py:281
  140.1 39.2 %collective-permute-start.25 = (bf16[2,256,128]{2,1,0:T(8,128)(2,1)}, bf16[2,256,128]{2,1,0:T(8,128)(2,1)S(1)}, u32[]{:S(2)}, u32[]{:S(2)}) collective-permute-start(bf16[2,256,128]{2,1,0:T(8,128)(2,1)} %get-tuple-element.166), channel_id=1, source_target_pairs={{0,0},{1,2},{2,4},{3,6},{4,17},{5,19},{6,21},{7,23},{8,9},{9,11},{... | collective-permute-start | bytes 393224 | tf_op jit(solution)/shard_map/ppermute | solution.py:281
  144.6 36.5 %collective-permute-start.26 = (bf16[2,256,128]{2,1,0:T(8,128)(2,1)}, bf16[2,256,128]{2,1,0:T(8,128)(2,1)S(1)}, u32[]{:S(2)}, u32[]{:S(2)}) collective-permute-start(bf16[2,256,128]{2,1,0:T(8,128)(2,1)} %get-tuple-element.167), channel_id=1, source_target_pairs={{0,31},{1,29},{2,0},{3,2},{4,12},{5,14},{6,17},{7,19},{8,4},{9,6},... | collective-permute-start | bytes 393224 | tf_op jit(solution)/shard_map/ppermute | solution.py:281
  146.9 37.0 %collective-permute-start.27 = (bf16[2,256,128]{2,1,0:T(8,128)(2,1)}, bf16[2,256,128]{2,1,0:T(8,128)(2,1)S(1)}, u32[]{:S(2)}, u32[]{:S(2)}) collective-permute-start(bf16[2,256,128]{2,1,0:T(8,128)(2,1)} %get-tuple-element.168), channel_id=1, source_target_pairs={{0,27},{1,25},{2,31},{3,29},{4,8},{5,10},{6,12},{7,14},{8,0},{9,2}... | collective-permute-start | bytes 393224 | tf_op jit(solution)/shard_map/ppermute | solution.py:281
  183.9 19.2 %collective-permute-start.32 = (bf16[2,256,128]{2,1,0:T(8,128)(2,1)}, bf16[2,256,128]{2,1,0:T(8,128)(2,1)}, u32[]{:S(2)}, u32[]{:S(2)}) collective-permute-start(bf16[2,256,128]{2,1,0:T(8,128)(2,1)} %get-tuple-element.173), channel_id=1, source_target_pairs={{0,4},{1,6},{2,9},{3,11},{4,21},{5,23},{6,26},{7,24},{8,13},{9,15}... | collective-permute-start | bytes 393224 | tf_op jit(solution)/shard_map/ppermute | solution.py:281
  185.7 20.6 %collective-permute-start.40 = (bf16[2,256,128]{2,1,0:T(8,128)(2,1)}, bf16[2,256,128]{2,1,0:T(8,128)(2,1)S(1)}, u32[]{:S(2)}, u32[]{:S(2)}) collective-permute-start(bf16[2,256,128]{2,1,0:T(8,128)(2,1)} %get-tuple-element.192), channel_id=1, source_target_pairs={{0,0},{1,2},{2,4},{3,6},{4,17},{5,19},{6,21},{7,23},{8,9},{9,11},{... | collective-permute-start | bytes 393224 | tf_op jit(solution)/shard_map/ppermute | solution.py:281
  189.8 19.2 %collective-permute-start.41 = (bf16[2,256,128]{2,1,0:T(8,128)(2,1)}, bf16[2,256,128]{2,1,0:T(8,128)(2,1)S(1)}, u32[]{:S(2)}, u32[]{:S(2)}) collective-permute-start(bf16[2,256,128]{2,1,0:T(8,128)(2,1)} %get-tuple-element.193), channel_id=1, source_target_pairs={{0,31},{1,29},{2,0},{3,2},{4,12},{5,14},{6,17},{7,19},{8,4},{9,6},... | collective-permute-start | bytes 393224 | tf_op jit(solution)/shard_map/ppermute | solution.py:281
  196.7 25.5 %collective-permute-start.43 = (bf16[2,256,128]{2,1,0:T(8,128)(2,1)}, bf16[2,256,128]{2,1,0:T(8,128)(2,1)S(1)}, u32[]{:S(2)}, u32[]{:S(2)}) collective-permute-start(bf16[2,256,128]{2,1,0:T(8,128)(2,1)} %get-tuple-element.195), channel_id=1, source_target_pairs={{0,22},{1,20},{2,27},{3,25},{4,7},{5,5},{6,8},{7,10},{8,31},{9,29}... | collective-permute-start | bytes 393224 | tf_op jit(solution)/shard_map/ppermute | solution.py:281
  203.1 19.1 %collective-permute-start.44 = (bf16[2,256,128]{2,1,0:T(8,128)(2,1)}, bf16[2,256,128]{2,1,0:T(8,128)(2,1)}, u32[]{:S(2)}, u32[]{:S(2)}) collective-permute-start(bf16[2,256,128]{2,1,0:T(8,128)(2,1)} %get-tuple-element.196), channel_id=1, source_target_pairs={{0,18},{1,16},{2,22},{3,20},{4,3},{5,1},{6,7},{7,5},{8,27},{9,25},... | collective-permute-start | bytes 393224 | tf_op jit(solution)/shard_map/ppermute | solution.py:281
  (69 other events, 961.2 us)
Sparse Core Ops, SparseCore 0:
  48.1 51.5 all-gather.2

commit v6 on v4

--- a/solution.py
+++ b/solution.py
@@ -28,10 +28,6 @@
 
 def params(mib):
     return pltpu.CompilerParams(vmem_limit_bytes=mib * MIB)
-
-
-def cost(mib, flops=0):
-    return pl.CostEstimate(flops=int(flops), bytes_accessed=int(mib * MIB), transcendentals=0)
 
 
 def run_copies(copies):
@@ -174,7 +170,7 @@
 
 def stein_kernel(shards, particles, ids, coef, whole, *refs):
     sources, out = refs[:particles], refs[particles : 2 * particles]
-    scores, field, sems = refs[2 * particles :]
+    scores, field, pushed, sems = refs[2 * particles :]
     columns = particles // 2
     ratio = particles // shards
     _, _, rows, cols = whole.shape
@@ -184,18 +180,19 @@
         [pltpu.make_async_copy(sources[t], scores.at[lax.rem(u + t, particles)], sems.at[t]) for t in range(particles)]
     )
     repulse = coef[particles * particles + particles]
-    groups = rows // 16
+    chunk = min(rows, 64)
+    groups = rows // chunk
     tiles = cols // LANES
 
     def body(g, carry):
         kind = lax.div(g, groups)
-        row = pl.multiple_of(lax.rem(g, groups) * 16, 16)
+        row = pl.multiple_of(lax.rem(g, groups) * chunk, chunk)
         for tile in range(tiles):
-            at = (kind, pl.ds(row, 16), slice(tile * LANES, (tile + 1) * LANES))
-            w = [whole[(p,) + at].astype(F32) for p in range(particles)]
-            pushed = [scores[(p,) + at].astype(F32) - repulse * w[p] for p in range(particles)]
+            at = (kind, pl.ds(row, chunk), slice(tile * LANES, (tile + 1) * LANES))
+            for p in range(particles):
+                pushed[p] = scores[(p,) + at].astype(F32) - repulse * whole[(p,) + at].astype(F32)
             for i in range(particles):
-                total = coef[particles * particles + i] * w[i]
+                total = coef[particles * particles + i] * whole[(i,) + at].astype(F32)
                 for j in range(particles):
                     total = total + coef[i * particles + j] * pushed[j]
                 field[(i,) + at] = total.astype(BF)
@@ -291,10 +288,9 @@
     picked = jnp.take(pool, index, axis=0).astype(F32)
     normed = (picked * lax.rsqrt(jnp.mean(picked * picked, axis=1, keepdims=True) + 1e-06)).astype(BF)
 
-    def gather_tokens(x):
+    def shift_tokens(x):
         shifted = [[(dev(m, c, s), dev(m, c, (s + k) % shards)) for m, c, s in devices] for k in range(shards)]
-        x = jnp.stack([move(x, pairs) for pairs in shifted])
-        return lax.all_gather(x[None], "particle", axis=0, tiled=True)
+        return jnp.stack([move(x, pairs) for pairs in shifted])
 
     w_flat = flat(weights)
     steps = max(rows // 64, 1)
@@ -308,7 +304,6 @@
         out_specs=[pl.BlockSpec((2, rows // steps, part), lambda i: (0, i, 0))] * shards
         + [pl.BlockSpec((particles, 2, rows // steps, cols), lambda i: (0, 0, i, 0))],
         compiler_params=params(56),
-        cost_estimate=cost(16),
         name="prep",
     )(ids, w_flat)
 
@@ -337,8 +332,7 @@
             in_specs=[pl.BlockSpec(memory_space=pltpu.VMEM)],
             out_specs=pl.BlockSpec(memory_space=pltpu.VMEM),
             compiler_params=params(8),
-            cost_estimate=cost(4),
-            name="distances",
+                name="distances",
         )(whole)
 
     def add_over(sums, steps):
@@ -383,15 +377,15 @@
         ]
         alpha = [move(x, route) for x, route in zip(halves, first_routes)]
         own_c = move(cot, [(dev(m, c, s), dev(m, 1 - c, s)) for m, c, s in devices if c == s // half])
-        normed = gather_tokens(normed)
-        alpha, own_c, prepared = lax.optimization_barrier((alpha, own_c, prepared))
+        normed = shift_tokens(normed)
+        alpha, own_c, prepared, normed = lax.optimization_barrier((alpha, own_c, prepared, normed))
+        normed = lax.all_gather(normed[None], "particle", axis=0, tiled=True)
         w_pieces = [move(x, route) for x, route in zip(prepared, w_routes)]
         hand_on = [jnp.where(inner, a, x) for a, x in zip(alpha, halves)]
         alpha_x = [move(x, swap_of(everyone)) for x in alpha]
         beta = [move(hand_on[0], second_routes[0])]
-        hand_on[1], *w_pieces[:2] = lax.optimization_barrier((hand_on[1], *w_pieces[:2]))
+        hand_on[1], whole, *w_pieces[:2] = lax.optimization_barrier((hand_on[1], whole, *w_pieces[:2]))
         beta.append(move(hand_on[1], second_routes[1]))
-        whole, alpha_x, beta[0] = lax.optimization_barrier((whole, alpha_x, beta[0]))
         sums = add_over(pair_sums(whole), range(len(hops) - 3))
         w_pieces, normed, sums = lax.optimization_barrier((w_pieces, normed, sums))
         beta_x = [move(x, swap_of(everyone)) for x in beta]
@@ -438,7 +432,7 @@
         full = lax.all_gather(cotangent[0], "shard", axis=0, tiled=True)
         sources = [jnp.where(core == proc, full, move(full, swap_of(everyone)))]
         w_pieces = [move(x, route) for x, route in zip(prepared, w_routes)]
-        normed = gather_tokens(normed)
+        normed = lax.all_gather(shift_tokens(normed)[None], "particle", axis=0, tiled=True)
         sums = add_over(pair_sums(whole), range(len(hops) - 3))
 
         def pick(ids, refs, held, sem):
@@ -468,7 +462,6 @@
         ],
         scratch_shapes=[pltpu.VMEM((width, part), BF), pltpu.VMEM((width, part), BF), pltpu.VMEM((part, width), BF)],
         compiler_params=params(56),
-        cost_estimate=cost(24, 2 * tokens * width * part),
         name="up",
     )(ids, normed, *w_pieces)
 
@@ -499,7 +492,6 @@
             pltpu.SemaphoreType.DMA((particles + 5,)),
         ],
         compiler_params=params(56),
-        cost_estimate=cost(32, 6 * tokens * width * part),
         name="grads",
     )(ids, normed, act_t, slope_t, down_t, *sources)
 
@@ -543,10 +535,10 @@
         scratch_shapes=[
             pltpu.VMEM((particles, 2, rows, cols), BF),
             pltpu.VMEM((particles, 2, rows, cols), BF),
+            pltpu.VMEM((particles, min(rows, 64), LANES), F32),
             pltpu.SemaphoreType.DMA((particles,)),
         ],
         compiler_params=params(12),
-        cost_estimate=cost(12),
         name="stein",
     )(ids, coef, whole, *arrived)
 
@@ -567,7 +559,6 @@
         out_specs=[state_spec] * 4,
         scratch_shapes=[pltpu.VMEM((2, rows, hidden), BF), pltpu.SemaphoreType.DMA((particles,))],
         compiler_params=params(56),
-        cost_estimate=cost(32),
         name="adam",
     )(ids, w_flat, flat(first_moment), flat(second_moment), *back)
     return tuple(unflat(x) for x in outs)

time: 279 us -> 259 us (0.928)
  starting transfers between devices: 102 us -> 72.8 us
  waiting for transfers between devices: 96.4 us -> 105 us
    ppermute x36, starting transfers between devices: 97.7 us -> 68.8 us  [move(): return lax.ppermute(x, AXES, pairs)]
    all_to_all x1, waiting for transfers between devices: 0.01 us -> 11.3 us  [local(): whole = lax.all_to_all(slices, 'particle', 0, 0, tiled=True)]
  transfers between devices with their start and end apart: 38 -> 38, of which waited for: 15 -> 13; matrix products, arithmetic and copies ran while one was open for 1% -> 2% of each run, Pallas kernels for 12% -> 13%
where the time goes in v6:
time: 259 us; the launch traced here: 258 us
  waiting for transfers between devices  105 us (41%)
  starting transfers between devices  72.8 us (28%)
  Pallas kernels  53.9 us (21%)
  between operations  15.1 us (6%)
  local copies, waits for them, and re-layouts  6.97 us (3%)
  other arithmetic  4.16 us (2%)
    ppermute x36, waiting for transfers between devices, move(): return lax.ppermute(x, AXES, pairs)  93.6 us
    ppermute x36, starting transfers between devices, move(): return lax.ppermute(x, AXES, pairs)  68.8 us
    pallas_call x1, Pallas kernels, local(): pl.pallas_call(functools.partial(adam_kernel, particles), grid=(steps,),...  15.5 us
    pallas_call x1, Pallas kernels, local(): pl.pallas_call(functools.partial(grad_kernel, shards, particles, -width *...  13.7 us
    all_to_all x1, waiting for transfers between devices, local(): whole = lax.all_to_all(slices, 'particle', 0, 0, tiled=True)  11.3 us
    pallas_call x1, Pallas kernels, local(): pl.pallas_call(functools.partial(up_kernel, shards, width ** (-0.5)), gri...  10.4 us
    pallas_call x1, Pallas kernels, local(): pl.pallas_call(functools.partial(prep_kernel, shards), grid=(steps,), out...  6.86 us
    pallas_call x1, Pallas kernels, local(): pl.pallas_call(functools.partial(stein_kernel, shards, particles), out_sh...  5.37 us
  transfers between devices with their start and end apart: 38, of which 13 were waited for; matrix products, arithmetic and copies ran while one was open for 2% of the time, Pallas kernels for 13%

profile of v6, /device:TPU:23, one launch (start us, length us, event | category | flops | bytes accessed | tf_op | source)
XLA Modules:
  0.0 257.9 jit_solution(3125003580515588471)
XLA Ops:
  21.6 6.9 %prep.1 = (bf16[2,256,512]{2,1,0:T(8,128)(2,1)}, bf16[2,256,512]{2,1,0:T(8,128)(2,1)}, bf16[2,256,512]{2,1,0:T(8,128)(2,1)}, bf16[2,256,512]{2,1,0:T(8,128)(2,1)}, bf16[8,2,256,256]{3,2,1,0:T(8,128)(2,1)}) custom-call(s32[5]{0:T(128)} %stack.36.ids, f32[8192,128]{1,0:T(8,128)} %bitcast.58), custom_call_target="tpu_custom_call" | custom-call | tf_op jit(solution)/shard_map/prep/pallas_call | solution.py:298
  28.5 18.0 %collective-permute-done.3 = bf16[64,1024]{1,0:T(8,128)(2,1)S(1)} collective-permute-done((bf16[64,1024]{1,0:T(8,128)(2,1)S(1)}, bf16[64,1024]{1,0:T(8,128)(2,1)S(1)}, u32[]{:S(2)}, u32[]{:S(2)}) %collective-permute-start.3) | collective-permute-done | bytes 131104 | tf_op jit(solution)/shard_map/ppermute | solution.py:273
  46.6 3.7 %collective-permute-done.5 = bf16[64,1024]{1,0:T(8,128)(2,1)S(1)} collective-permute-done((bf16[64,1024]{1,0:T(8,128)(2,1)S(1)}, bf16[64,1024]{1,0:T(8,128)(2,1)S(1)}, u32[]{:S(2)}, u32[]{:S(2)}) %collective-permute-start.5) | collective-permute-done | bytes 131104 | tf_op jit(solution)/shard_map/ppermute | solution.py:273
  51.3 4.0 %all-to-all-start = ((bf16[8,2,256,256]{3,2,1,0:T(8,128)(2,1)}), bf16[8,2,256,256]{3,2,1,0:T(8,128)(2,1)S(1)}, u32[]{:S(2)}, u32[]{:S(2)}) async-start(bf16[8,2,256,256]{3,2,1,0:T(8,128)(2,1)} %get-tuple-element.73), calls=%async_computation | async-start | bytes 4194304 | tf_op jit(solution)/shard_map/all_to_all | solution.py:318
  57.1 5.4 %collective-permute-start.7 = (bf16[2,256,512]{2,1,0:T(8,128)(2,1)}, bf16[2,256,512]{2,1,0:T(8,128)(2,1)}, u32[]{:S(2)}, u32[]{:S(2)}) collective-permute-start(bf16[2,256,512]{2,1,0:T(8,128)(2,1)} %get-tuple-element.75), channel_id=1, source_target_pairs={{0,5},{1,0},{2,4},{3,1},{4,7},{5,2},{6,6},{7,3},{8,13},{9,8},{10,1... | collective-permute-start | bytes 1572872 | tf_op jit(solution)/shard_map/ppermute | solution.py:273
  63.5 4.4 %collective-permute-start.16 = (bf16[256,1024]{1,0:T(8,128)(2,1)}, bf16[256,1024]{1,0:T(8,128)(2,1)}, u32[]{:S(2)}, u32[]{:S(2)}) collective-permute-start(bf16[256,1024]{1,0:T(8,128)(2,1)} %broadcast_select_fusion), channel_id=1, source_target_pairs={{0,1},{1,0},{2,3},{5,4},{6,7},{7,6},{8,9},{9,8},{10,11},{13,12},{1... | collective-permute-start | bytes 1572872 | tf_op jit(solution)/shard_map/ppermute | solution.py:273
  68.8 4.0 %collective-permute-done.6.refs_0_ = bf16[2,256,512]{2,1,0:T(8,128)(2,1)S(1)} collective-permute-done((bf16[2,256,512]{2,1,0:T(8,128)(2,1)}, bf16[2,256,512]{2,1,0:T(8,128)(2,1)S(1)}, u32[]{:S(2)}, u32[]{:S(2)}) %collective-permute-start.6) | collective-permute-done | bytes 524320 | tf_op jit(solution)/shard_map/ppermute | solution.py:273
  73.5 11.3 %all-to-all-done.whole = bf16[8,2,256,256]{3,2,1,0:T(8,128)(2,1)S(1)} async-done(((bf16[8,2,256,256]{3,2,1,0:T(8,128)(2,1)}), bf16[8,2,256,256]{3,2,1,0:T(8,128)(2,1)S(1)}, u32[]{:S(2)}, u32[]{:S(2)}) %all-to-all-start) | async-done | bytes 2097184 | tf_op jit(solution)/shard_map/all_to_all | solution.py:318
  87.2 4.0 %collective-permute-start.9 = (bf16[2,256,512]{2,1,0:T(8,128)(2,1)}, bf16[2,256,512]{2,1,0:T(8,128)(2,1)}, u32[]{:S(2)}, u32[]{:S(2)}) collective-permute-start(bf16[2,256,512]{2,1,0:T(8,128)(2,1)} %get-tuple-element.79), channel_id=1, source_target_pairs={{0,4},{1,1},{2,5},{3,0},{4,6},{5,3},{6,7},{7,2},{8,12},{9,9},{10,1... | collective-permute-start | bytes 1572872 | tf_op jit(solution)/shard_map/ppermute | solution.py:273
  100.3 13.1 %collective-permute-done.17.refs_7_ = bf16[256,1024]{1,0:T(8,128)(2,1)} collective-permute-done((bf16[256,1024]{1,0:T(8,128)(2,1)}, bf16[256,1024]{1,0:T(8,128)(2,1)}, u32[]{:S(2)}, u32[]{:S(2)}) %collective-permute-start.17) | collective-permute-done | bytes 524320 | tf_op jit(solution)/shard_map/ppermute | solution.py:273
  113.5 5.5 %collective-permute-done.9.refs_3_ = bf16[2,256,512]{2,1,0:T(8,128)(2,1)} collective-permute-done((bf16[2,256,512]{2,1,0:T(8,128)(2,1)}, bf16[2,256,512]{2,1,0:T(8,128)(2,1)}, u32[]{:S(2)}, u32[]{:S(2)}) %collective-permute-start.9) | collective-permute-done | bytes 524320 | tf_op jit(solution)/shard_map/ppermute | solution.py:273
  119.3 10.4 %up.1 = (bf16[512,2048]{1,0:T(8,128)(2,1)}, bf16[512,2048]{1,0:T(8,128)(2,1)}, bf16[512,1024]{1,0:T(8,128)(2,1)}) custom-call(s32[5]{0:T(128)} %stack.36.ids, bf16[2048,1024]{1,0:T(8,128)(2,1)} %bitcast.60, bf16[2,256,512]{2,1,0:T(8,128)(2,1)} %copy-done.6, bf16[2,256,512]{2,1,0:T(8,128)(2,1)} %collective-permute-done.7.refs_1_, ...), custom_call_target="tpu_custom_call" | custom-call | tf_op jit(solution)/shard_map/up/pallas_call | solution.py:448
  131.7 13.7 %grads.1 = (bf16[2,256,256]{2,1,0:T(8,128)(2,1)}, bf16[2,256,256]{2,1,0:T(8,128)(2,1)}, bf16[2,256,256]{2,1,0:T(8,128)(2,1)}, bf16[2,256,256]{2,1,0:T(8,128)(2,1...) custom-call(s32[5]{0:T(128)} %stack.36.ids, ...), custom_call_target="tpu_custom_call" | custom-call | tf_op jit(solution)/shard_map/grads/pallas_call | solution.py:471
  150.3 3.6 %collective-permute-start.24 = (bf16[2,256,256]{2,1,0:T(8,128)(2,1)}, bf16[2,256,256]{2,1,0:T(8,128)(2,1)S(1)}, u32[]{:S(2)}, u32[]{:S(2)}) collective-permute-start(bf16[2,256,256]{2,1,0:T(8,128)(2,1)} %get-tuple-element.109), channel_id=1, source_target_pairs={{0,22},{1,20},{2,27},{3,25},{4,7},{5,5},{6,8},{7,10},{8,31},{9,29}... | collective-permute-start | bytes 786440 | tf_op jit(solution)/shard_map/ppermute | solution.py:273
  156.8 12.8 %collective-permute-done.20 = f32[8,128]{1,0:T(8,128)S(1)} collective-permute-done((f32[8,128]{1,0:T(8,128)S(1)}, f32[8,128]{1,0:T(8,128)S(1)}, u32[]{:S(2)}, u32[]{:S(2)}) %collective-permute-start.20) | collective-permute-done | bytes 4128 | tf_op jit(solution)/shard_map/ppermute | solution.py:273
  179.6 9.0 %collective-permute-done.26.refs_5_ = bf16[2,256,256]{2,1,0:T(8,128)(2,1)} collective-permute-done((bf16[2,256,256]{2,1,0:T(8,128)(2,1)}, bf16[2,256,256]{2,1,0:T(8,128)(2,1)}, u32[]{:S(2)}, u32[]{:S(2)}) %collective-permute-start.26) | collective-permute-done | bytes 262176 | tf_op jit(solution)/shard_map/ppermute | solution.py:273
  188.6 6.3 %collective-permute-done.28.refs_7_ = bf16[2,256,256]{2,1,0:T(8,128)(2,1)} collective-permute-done((bf16[2,256,256]{2,1,0:T(8,128)(2,1)}, bf16[2,256,256]{2,1,0:T(8,128)(2,1)}, u32[]{:S(2)}, u32[]{:S(2)}) %collective-permute-start.28) | collective-permute-done | bytes 262176 | tf_op jit(solution)/shard_map/ppermute | solution.py:273
  194.9 5.4 %stein.1 = (bf16[2,256,256]{2,1,0:T(8,128)(2,1)S(1)}, bf16[2,256,256]{2,1,0:T(8,128)(2,1)S(1)}, bf16[2,256,256]{2,1,0:T(8,128)(2,1)S(1)}, bf16[2,256,256]{2,1,0:...) custom-call(s32[5]{0:T(128)S(1)} %copy-done.3, ...), custom_call_target="tpu_custom_call" | custom-call | tf_op jit(solution)/shard_map/stein/pallas_call | solution.py:530
  201.8 3.6 %collective-permute-start.30 = (bf16[2,256,256]{2,1,0:T(8,128)(2,1)S(1)}, bf16[2,256,256]{2,1,0:T(8,128)(2,1)S(1)}, u32[]{:S(2)}, u32[]{:S(2)}) collective-permute-start(bf16[2,256,256]{2,1,0:T(8,128)(2,1)S(1)} %get-tuple-element.122), channel_id=1, source_target_pairs={{0,8},{1,9},{2,10},{3,11},{4,12},{5,13},{6,14},{7,15},{8,16},{9,17... | collective-permute-start | bytes 786440 | tf_op jit(solution)/shard_map/ppermute | solution.py:273
  205.4 4.3 %collective-permute-start.31 = (bf16[2,256,256]{2,1,0:T(8,128)(2,1)S(1)}, bf16[2,256,256]{2,1,0:T(8,128)(2,1)S(1)}, u32[]{:S(2)}, u32[]{:S(2)}) collective-permute-start(bf16[2,256,256]{2,1,0:T(8,128)(2,1)S(1)} %get-tuple-element.123), channel_id=1, source_target_pairs={{0,12},{1,13},{2,14},{3,15},{4,8},{5,9},{6,10},{7,11},{8,20},{9,21... | collective-permute-start | bytes 786440 | tf_op jit(solution)/shard_map/ppermute | solution.py:273
  211.7 5.4 %collective-permute-start.35 = (bf16[2,256,256]{2,1,0:T(8,128)(2,1)S(1)}, bf16[2,256,256]{2,1,0:T(8,128)(2,1)S(1)}, u32[]{:S(2)}, u32[]{:S(2)}) collective-permute-start(bf16[2,256,256]{2,1,0:T(8,128)(2,1)S(1)} %get-tuple-element.127), channel_id=1, source_target_pairs={{0,28},{1,29},{2,30},{3,31},{4,24},{5,25},{6,26},{7,27},{8,4},{9,5... | collective-permute-start | bytes 786440 | tf_op jit(solution)/shard_map/ppermute | solution.py:273
  217.0 9.6 %collective-permute-done.32.refs_4_ = bf16[2,256,256]{2,1,0:T(8,128)(2,1)S(1)} collective-permute-done((bf16[2,256,256]{2,1,0:T(8,128)(2,1)S(1)}, bf16[2,256,256]{2,1,0:T(8,128)(2,1)S(1)}, u32[]{:S(2)}, u32[]{:S(2)}) %collective-permute-start.32) | collective-permute-done | bytes 262176 | tf_op jit(solution)/shard_map/ppermute | solution.py:273
  226.7 8.0 %collective-permute-done.33.refs_5_ = bf16[2,256,256]{2,1,0:T(8,128)(2,1)S(1)} collective-permute-done((bf16[2,256,256]{2,1,0:T(8,128)(2,1)S(1)}, bf16[2,256,256]{2,1,0:T(8,128)(2,1)S(1)}, u32[]{:S(2)}, u32[]{:S(2)}) %collective-permute-start.33) | collective-permute-done | bytes 262176 | tf_op jit(solution)/shard_map/ppermute | solution.py:273
  235.6 15.5 %adam.1 = (f32[8192,128]{1,0:T(8,128)}, f32[8192,128]{1,0:T(8,128)}, f32[8192,128]{1,0:T(8,128)}, f32[8192,128]{1,0:T(8,128)}) custom-call(s32[5]{0:T(128)} %stack.36.ids, f32[8192,128]{1,0:T(8,128)} %bitcast.59, f32[8192,128]{1,0:T(8,128)} %bitcast.62, f32[8192,128]{1,0:T(8,128)} %bitcast.63, bf16[2,256,256]{2,1,0:T(8,128)(2,1)} %copy-done.2, ...), custom_call_target="tpu_custom_call" | custom-call | tf_op jit(solution)/shard_map/adam/pallas_call | solution.py:554
  (116 shorter events, 54.8 us)
Async XLA Ops:
  7.2 111.8 %all-gather.3.cloned.1.call-start = ((), (), s32[]{:S(2)}) async-start(), calls=%async_computation.1 | async-start | bytes 4718592 | tf_op jit(solution)/shard_map/all_gather | solution.py:382
  9.7 41.5 %collective-permute-start = (bf16[256,1024]{1,0:T(8,128)(2,1)}, bf16[256,1024]{1,0:T(8,128)(2,1)S(1)}, u32[]{:S(2)}, u32[]{:S(2)}) collective-permute-start(bf16[256,1024]{1,0:T(8,128)(2,1)} %get-tuple-element.135), channel_id=1, source_target_pairs={{1,0},{2,1},{3,5},{4,2},{5,6},{6,7},{9,8},{10,9},{11,13},{12,10},{... | collective-permute-start | bytes 1572872 | tf_op jit(solution)/shard_map/ppermute | solution.py:273
  12.9 38.3 %collective-permute-start.1 = (bf16[256,1024]{1,0:T(8,128)(2,1)}, bf16[256,1024]{1,0:T(8,128)(2,1)S(1)}, u32[]{:S(2)}, u32[]{:S(2)}) collective-permute-start(bf16[256,1024]{1,0:T(8,128)(2,1)} %get-tuple-element.134), channel_id=1, source_target_pairs={{1,4},{2,5},{3,1},{4,6},{5,2},{6,3},{9,12},{10,13},{11,9},{12,14},... | collective-permute-start | bytes 1572872 | tf_op jit(solution)/shard_map/ppermute | solution.py:273
  15.2 36.1 %collective-permute-start.2 = (bf16[512,1024]{1,0:T(8,128)(2,1)}, bf16[512,1024]{1,0:T(8,128)(2,1)}, u32[]{:S(2)}, u32[]{:S(2)}) collective-permute-start(bf16[512,1024]{1,0:T(8,128)(2,1)} %bitcast.64), channel_id=1, source_target_pairs={{0,4},{1,5},{6,2},{7,3},{8,12},{9,13},{14,10},{15,11},{16,20},{17,... | collective-permute-start | bytes 3145736 | tf_op jit(solution)/shard_map/ppermute | solution.py:273
  20.1 26.4 %collective-permute-start.3 = (bf16[64,1024]{1,0:T(8,128)(2,1)S(1)}, bf16[64,1024]{1,0:T(8,128)(2,1)S(1)}, u32[]{:S(2)}, u32[]{:S(2)}) collective-permute-start(bf16[64,1024]{1,0:T(8,128)(2,1)S(1)} %fusion.1), channel_id=1, source_target_pairs={{0,1},{1,2},{2,3},{3,0},{4,5},{5,6},{6,7},{7,4},{8,9},{9,10},{10,1... | collective-permute-start | bytes 393224 | tf_op jit(solution)/shard_map/ppermute | solution.py:273
  21.0 25.6 %collective-permute-start.4 = (bf16[64,1024]{1,0:T(8,128)(2,1)S(1)}, bf16[64,1024]{1,0:T(8,128)(2,1)S(1)}, u32[]{:S(2)}, u32[]{:S(2)}) collective-permute-start(bf16[64,1024]{1,0:T(8,128)(2,1)S(1)} %fusion.1), channel_id=1, source_target_pairs={{0,2},{1,3},{2,0},{3,1},{4,6},{5,7},{6,4},{7,5},{8,10},{9,11},{10,... | collective-permute-start | bytes 393224 | tf_op jit(solution)/shard_map/ppermute | solution.py:273
  51.3 33.5 %all-to-all-start = ((bf16[8,2,256,256]{3,2,1,0:T(8,128)(2,1)}), bf16[8,2,256,256]{3,2,1,0:T(8,128)(2,1)S(1)}, u32[]{:S(2)}, u32[]{:S(2)}) async-start(bf16[8,2,256,256]{3,2,1,0:T(8,128)(2,1)} %get-tuple-element.73), calls=%async_computation | async-start | bytes 4194304 | tf_op jit(solution)/shard_map/all_to_all | solution.py:318
  55.2 17.5 %collective-permute-start.6 = (bf16[2,256,512]{2,1,0:T(8,128)(2,1)}, bf16[2,256,512]{2,1,0:T(8,128)(2,1)S(1)}, u32[]{:S(2)}, u32[]{:S(2)}) collective-permute-start(bf16[2,256,512]{2,1,0:T(8,128)(2,1)} %get-tuple-element.74), channel_id=1, source_target_pairs={{0,0},{1,4},{2,1},{3,5},{4,2},{5,6},{6,3},{7,7},{8,8},{9,12},{10,9... | collective-permute-start | bytes 1572872 | tf_op jit(solution)/shard_map/ppermute | solution.py:273
  62.6 33.9 %collective-permute-start.8 = (bf16[2,256,512]{2,1,0:T(8,128)(2,1)}, bf16[2,256,512]{2,1,0:T(8,128)(2,1)}, u32[]{:S(2)}, u32[]{:S(2)}) collective-permute-start(bf16[2,256,512]{2,1,0:T(8,128)(2,1)} %get-tuple-element.78), channel_id=1, source_target_pairs={{0,1},{1,5},{2,0},{3,4},{4,3},{5,7},{6,2},{7,6},{8,9},{9,13},{10,8... | collective-permute-start | bytes 1572872 | tf_op jit(solution)/shard_map/ppermute | solution.py:273
  63.5 36.3 %collective-permute-start.16 = (bf16[256,1024]{1,0:T(8,128)(2,1)}, bf16[256,1024]{1,0:T(8,128)(2,1)}, u32[]{:S(2)}, u32[]{:S(2)}) collective-permute-start(bf16[256,1024]{1,0:T(8,128)(2,1)} %broadcast_select_fusion), channel_id=1, source_target_pairs={{0,1},{1,0},{2,3},{5,4},{6,7},{7,6},{8,9},{9,8},{10,11},{13,12},{1... | collective-permute-start | bytes 1572872 | tf_op jit(solution)/shard_map/ppermute | solution.py:273
  84.8 28.6 %collective-permute-start.17 = (bf16[256,1024]{1,0:T(8,128)(2,1)}, bf16[256,1024]{1,0:T(8,128)(2,1)}, u32[]{:S(2)}, u32[]{:S(2)}) collective-permute-start(bf16[256,1024]{1,0:T(8,128)(2,1)} %broadcast_select_fusion.1), channel_id=1, source_target_pairs={{0,5},{1,0},{2,3},{5,4},{6,7},{7,2},{8,13},{9,8},{10,11},{13,12},{... | collective-permute-start | bytes 1572872 | tf_op jit(solution)/shard_map/ppermute | solution.py:273
  87.2 31.8 %collective-permute-start.9 = (bf16[2,256,512]{2,1,0:T(8,128)(2,1)}, bf16[2,256,512]{2,1,0:T(8,128)(2,1)}, u32[]{:S(2)}, u32[]{:S(2)}) collective-permute-start(bf16[2,256,512]{2,1,0:T(8,128)(2,1)} %get-tuple-element.79), channel_id=1, source_target_pairs={{0,4},{1,1},{2,5},{3,0},{4,6},{5,3},{6,7},{7,2},{8,12},{9,9},{10,1... | collective-permute-start | bytes 1572872 | tf_op jit(solution)/shard_map/ppermute | solution.py:273
  96.4 35.3 %collective-permute-start.14 = (bf16[256,1024]{1,0:T(8,128)(2,1)S(1)}, bf16[256,1024]{1,0:T(8,128)(2,1)}, u32[]{:S(2)}, u32[]{:S(2)}) collective-permute-start(bf16[256,1024]{1,0:T(8,128)(2,1)S(1)} %collective-permute-done.refs_2_), channel_id=1, source_target_pairs={{0,4},{1,5},{2,6},{3,7},{4,0},{5,1},{6,2},{7,3},{8,12},{9,13},{10,... | collective-permute-start | bytes 1572872 | tf_op jit(solution)/shard_map/ppermute | solution.py:273
  99.8 31.9 %collective-permute-start.15 = (bf16[256,1024]{1,0:T(8,128)(2,1)S(1)}, bf16[256,1024]{1,0:T(8,128)(2,1)}, u32[]{:S(2)}, u32[]{:S(2)}) collective-permute-start(bf16[256,1024]{1,0:T(8,128)(2,1)S(1)} %collective-permute-done.1.refs_3_), channel_id=1, source_target_pairs={{0,4},{1,5},{2,6},{3,7},{4,0},{5,1},{6,2},{7,3},{8,12},{9,13},{10,... | collective-permute-start | bytes 1572872 | tf_op jit(solution)/shard_map/ppermute | solution.py:273
  99.8 31.9 %collective-permute-start.18 = (bf16[256,1024]{1,0:T(8,128)(2,1)}, bf16[256,1024]{1,0:T(8,128)(2,1)}, u32[]{:S(2)}, u32[]{:S(2)}) collective-permute-start(bf16[256,1024]{1,0:T(8,128)(2,1)} %collective-permute-done.16.refs_6_), channel_id=1, source_target_pairs={{0,4},{1,5},{2,6},{3,7},{4,0},{5,1},{6,2},{7,3},{8,12},{9,13},{10,... | collective-permute-start | bytes 1572872 | tf_op jit(solution)/shard_map/ppermute | solution.py:273
  113.4 18.3 %collective-permute-start.19 = (bf16[256,1024]{1,0:T(8,128)(2,1)}, bf16[256,1024]{1,0:T(8,128)(2,1)}, u32[]{:S(2)}, u32[]{:S(2)}) collective-permute-start(bf16[256,1024]{1,0:T(8,128)(2,1)} %collective-permute-done.17.refs_7_), channel_id=1, source_target_pairs={{0,4},{1,5},{2,6},{3,7},{4,0},{5,1},{6,2},{7,3},{8,12},{9,13},{10,... | collective-permute-start | bytes 1572872 | tf_op jit(solution)/shard_map/ppermute | solution.py:273
  145.5 25.8 %collective-permute-start.21 = (bf16[2,256,256]{2,1,0:T(8,128)(2,1)}, bf16[2,256,256]{2,1,0:T(8,128)(2,1)S(1)}, u32[]{:S(2)}, u32[]{:S(2)}) collective-permute-start(bf16[2,256,256]{2,1,0:T(8,128)(2,1)} %get-tuple-element.106), channel_id=1, source_target_pairs={{0,0},{1,2},{2,4},{3,6},{4,17},{5,19},{6,21},{7,23},{8,9},{9,11},{... | collective-permute-start | bytes 786440 | tf_op jit(solution)/shard_map/ppermute | solution.py:273
  147.4 26.6 %collective-permute-start.22 = (bf16[2,256,256]{2,1,0:T(8,128)(2,1)}, bf16[2,256,256]{2,1,0:T(8,128)(2,1)S(1)}, u32[]{:S(2)}, u32[]{:S(2)}) collective-permute-start(bf16[2,256,256]{2,1,0:T(8,128)(2,1)} %get-tuple-element.107), channel_id=1, source_target_pairs={{0,31},{1,29},{2,0},{3,2},{4,12},{5,14},{6,17},{7,19},{8,4},{9,6},... | collective-permute-start | bytes 786440 | tf_op jit(solution)/shard_map/ppermute | solution.py:273
  149.3 26.6 %collective-permute-start.23 = (bf16[2,256,256]{2,1,0:T(8,128)(2,1)}, bf16[2,256,256]{2,1,0:T(8,128)(2,1)S(1)}, u32[]{:S(2)}, u32[]{:S(2)}) collective-permute-start(bf16[2,256,256]{2,1,0:T(8,128)(2,1)} %get-tuple-element.108), channel_id=1, source_target_pairs={{0,27},{1,25},{2,31},{3,29},{4,8},{5,10},{6,12},{7,14},{8,0},{9,2}... | collective-permute-start | bytes 786440 | tf_op jit(solution)/shard_map/ppermute | solution.py:273
  150.3 28.0 %collective-permute-start.24 = (bf16[2,256,256]{2,1,0:T(8,128)(2,1)}, bf16[2,256,256]{2,1,0:T(8,128)(2,1)S(1)}, u32[]{:S(2)}, u32[]{:S(2)}) collective-permute-start(bf16[2,256,256]{2,1,0:T(8,128)(2,1)} %get-tuple-element.109), channel_id=1, source_target_pairs={{0,22},{1,20},{2,27},{3,25},{4,7},{5,5},{6,8},{7,10},{8,31},{9,29}... | collective-permute-start | bytes 786440 | tf_op jit(solution)/shard_map/ppermute | solution.py:273
  176.0 18.9 %collective-permute-start.28 = (bf16[2,256,256]{2,1,0:T(8,128)(2,1)}, bf16[2,256,256]{2,1,0:T(8,128)(2,1)}, u32[]{:S(2)}, u32[]{:S(2)}) collective-permute-start(bf16[2,256,256]{2,1,0:T(8,128)(2,1)} %get-tuple-element.119), channel_id=1, source_target_pairs={{0,4},{1,6},{2,9},{3,11},{4,21},{5,23},{6,26},{7,24},{8,13},{9,15}... | collective-permute-start | bytes 786440 | tf_op jit(solution)/shard_map/ppermute | solution.py:273
  209.8 24.9 %collective-permute-start.33 = (bf16[2,256,256]{2,1,0:T(8,128)(2,1)S(1)}, bf16[2,256,256]{2,1,0:T(8,128)(2,1)S(1)}, u32[]{:S(2)}, u32[]{:S(2)}) collective-permute-start(bf16[2,256,256]{2,1,0:T(8,128)(2,1)S(1)} %get-tuple-element.125), channel_id=1, source_target_pairs={{0,20},{1,21},{2,22},{3,23},{4,16},{5,17},{6,18},{7,19},{8,28},{9,... | collective-permute-start | bytes 786440 | tf_op jit(solution)/shard_map/ppermute | solution.py:273
  211.6 23.0 %collective-permute-start.34 = (bf16[2,256,256]{2,1,0:T(8,128)(2,1)S(1)}, bf16[2,256,256]{2,1,0:T(8,128)(2,1)S(1)}, u32[]{:S(2)}, u32[]{:S(2)}) collective-permute-start(bf16[2,256,256]{2,1,0:T(8,128)(2,1)S(1)} %get-tuple-element.126), channel_id=1, source_target_pairs={{0,24},{1,25},{2,26},{3,27},{4,28},{5,29},{6,30},{7,31},{8,0},{9,1... | collective-permute-start | bytes 786440 | tf_op jit(solution)/shard_map/ppermute | solution.py:273
  211.7 23.0 %collective-permute-start.35 = (bf16[2,256,256]{2,1,0:T(8,128)(2,1)S(1)}, bf16[2,256,256]{2,1,0:T(8,128)(2,1)S(1)}, u32[]{:S(2)}, u32[]{:S(2)}) collective-permute-start(bf16[2,256,256]{2,1,0:T(8,128)(2,1)S(1)} %get-tuple-element.127), channel_id=1, source_target_pairs={{0,28},{1,29},{2,30},{3,31},{4,24},{5,25},{6,26},{7,27},{8,4},{9,5... | collective-permute-start | bytes 786440 | tf_op jit(solution)/shard_map/ppermute | solution.py:273
  (29 other events, 431.1 us)
Sparse Core Ops, SparseCore 0:
  51.4 47.4 all-gather.2

commit v7 on v6

--- a/solution.py
+++ b/solution.py
@@ -42,8 +42,8 @@
 
 
 def prep_kernel(shards, ids, w, *out):
-    pieces, slices = out[:shards], out[shards]
-    _, rows, piece = pieces[0].shape
+    pieces, slices = out[:-1], out[-1]
+    rows, piece = pieces[0].shape
     particles, _, _, cols = slices.shape
     columns = particles // 2
     tiles, per_slice = piece // LANES, cols // LANES
@@ -57,26 +57,28 @@
             for kind in range(2):
                 line = 2 * (q * tiles + j) + kind
                 part = w[pl.ds(line, rows, stride=2 * shards * tiles), :].astype(BF)
-                pieces[r][kind, :, at : at + LANES] = part
+                pieces[kind * shards + r][:, at : at + LANES] = part
                 slices[p, kind, :, within : within + LANES] = part
+
+
+def transpose_pieces(shards, ids, pieces, straight, turned):
+    width = straight.shape[0]
+    rows = width // shards
+    for r in range(shards):
+        at = pl.multiple_of(lax.rem(ids[PIECE] + r, shards) * rows, rows)
+        straight[pl.ds(at, rows), :] = pieces[r][...]
+    for i in range(width // LANES):
+        span = slice(i * LANES, (i + 1) * LANES)
+        turned[:, span] = straight[span, :].astype(F32).T.astype(BF)
 
 
 def up_kernel(shards, scale, ids, tokens, *refs):
     pieces = refs[:shards]
-    act_t, slope_t, down_t, up_w, down_w, up_t = refs[shards:]
-    width, part = up_w.shape
-    rows = width // shards
+    act_t, slope_t, up_w, up_t = refs[shards:]
 
     @pl.when(pl.program_id(0) == 0)
     def _():
-        for r in range(shards):
-            at = pl.multiple_of(lax.rem(ids[PIECE] + r, shards) * rows, rows)
-            up_w[pl.ds(at, rows), :] = pieces[r][0]
-            down_w[pl.ds(at, rows), :] = pieces[r][1]
-        for i in range(width // LANES):
-            span = slice(i * LANES, (i + 1) * LANES)
-            up_t[:, span] = up_w[span, :].astype(F32).T.astype(BF)
-            down_t[:, span] = down_w[span, :].astype(F32).T.astype(BF)
+        transpose_pieces(shards, ids, pieces, up_w, up_t)
 
     u = lax.dot_general(up_t[...], tokens[...], NT, preferred_element_type=F32) * scale
     cdf = 0.5 * (1.0 + lax.erf(u * 0.7071067811865476))
@@ -85,17 +87,14 @@
     slope_t[...] = (cdf + u * density).astype(BF)
 
 
-def grad_kernel(shards, particles, up_scale, down_scale, back_scale, pick, ids, normed, act_t, slope_t, down_t, *refs):
-    n_in = len(refs) - particles - 8
-    sources, out = refs[:n_in], refs[n_in : n_in + particles]
-    c, n, act, slope, grad, down, score, sems = refs[n_in + particles :]
+def grad_kernel(shards, particles, up_scale, down_scale, back_scale, pick, ids, normed, act_t, slope_t, *refs):
+    n_in = len(refs) - particles - 9
+    pieces, sources, out = refs[:shards], refs[shards:n_in], refs[n_in : n_in + particles]
+    c, n, act, slope, grad, down_w, down, score, sems = refs[n_in + particles :]
     part, tokens = act.shape
     width = c.shape[1]
     chunk = tokens // shards
-    first = [
-        pltpu.make_async_copy(down_t, down, sems.at[1]),
-        pltpu.make_async_copy(slope_t, slope, sems.at[2]),
-    ]
+    first = [pltpu.make_async_copy(slope_t, slope, sems.at[1])]
     later = [
         pltpu.make_async_copy(act_t, act, sems.at[3]),
         pltpu.make_async_copy(normed, n, sems.at[4]),
@@ -105,6 +104,7 @@
     pick(ids, sources, c, sems.at[0])
     for copy in later:
         copy.start()
+    transpose_pieces(shards, ids, pieces, down_w, down)
     for copy in first:
         copy.wait()
     pltpu.make_async_copy(c, c, sems.at[0]).wait()
@@ -298,10 +298,10 @@
     *prepared, slices = pl.pallas_call(
         functools.partial(prep_kernel, shards),
         grid=(steps,),
-        out_shape=[jax.ShapeDtypeStruct((2, rows, part), BF)] * shards
+        out_shape=[jax.ShapeDtypeStruct((rows, part), BF)] * (2 * shards)
         + [jax.ShapeDtypeStruct((particles, 2, rows, cols), BF)],
         in_specs=[smem_spec(), pl.BlockSpec((lines, LANES), lambda i: (i, 0))],
-        out_specs=[pl.BlockSpec((2, rows // steps, part), lambda i: (0, i, 0))] * shards
+        out_specs=[pl.BlockSpec((rows // steps, part), lambda i: (i, 0))] * (2 * shards)
         + [pl.BlockSpec((particles, 2, rows // steps, cols), lambda i: (0, 0, i, 0))],
         compiler_params=params(56),
         name="prep",
@@ -380,14 +380,13 @@
         normed = shift_tokens(normed)
         alpha, own_c, prepared, normed = lax.optimization_barrier((alpha, own_c, prepared, normed))
         normed = lax.all_gather(normed[None], "particle", axis=0, tiled=True)
-        w_pieces = [move(x, route) for x, route in zip(prepared, w_routes)]
+        w_pieces = [move(x, w_routes[i % shards]) for i, x in enumerate(prepared)]
         hand_on = [jnp.where(inner, a, x) for a, x in zip(alpha, halves)]
         alpha_x = [move(x, swap_of(everyone)) for x in alpha]
         beta = [move(hand_on[0], second_routes[0])]
-        hand_on[1], whole, *w_pieces[:2] = lax.optimization_barrier((hand_on[1], whole, *w_pieces[:2]))
+        hand_on[1], *w_pieces[:2] = lax.optimization_barrier((hand_on[1], *w_pieces[:2]))
         beta.append(move(hand_on[1], second_routes[1]))
-        sums = add_over(pair_sums(whole), range(len(hops) - 3))
-        w_pieces, normed, sums = lax.optimization_barrier((w_pieces, normed, sums))
+        w_pieces[:shards], normed = lax.optimization_barrier((w_pieces[:shards], normed))
         beta_x = [move(x, swap_of(everyone)) for x in beta]
         sources = [cot, own_c, *alpha, *alpha_x, *beta, *beta_x]
 
@@ -431,9 +430,8 @@
     else:
         full = lax.all_gather(cotangent[0], "shard", axis=0, tiled=True)
         sources = [jnp.where(core == proc, full, move(full, swap_of(everyone)))]
-        w_pieces = [move(x, route) for x, route in zip(prepared, w_routes)]
+        w_pieces = [move(x, w_routes[i % shards]) for i, x in enumerate(prepared)]
         normed = lax.all_gather(shift_tokens(normed)[None], "particle", axis=0, tiled=True)
-        sums = add_over(pair_sums(whole), range(len(hops) - 3))
 
         def pick(ids, refs, held, sem):
             def one(which, carry):
@@ -445,28 +443,29 @@
             lax.fori_loop(0, shards, one, 0)
 
     normed = normed.reshape(tokens, width)
-    act_t, slope_t, down_t = pl.pallas_call(
+    act_t, slope_t = pl.pallas_call(
         functools.partial(up_kernel, shards, width ** (-0.5)),
         grid=(blocks,),
         out_shape=[
             jax.ShapeDtypeStruct((part, tokens), BF),
             jax.ShapeDtypeStruct((part, tokens), BF),
-            jax.ShapeDtypeStruct((part, width), BF),
         ],
         in_specs=[smem_spec(), pl.BlockSpec((BLOCK, width), lambda i: (i, 0))]
-        + [pl.BlockSpec((2, rows, part), lambda i: (0, 0, 0))] * shards,
+        + [pl.BlockSpec((rows, part), lambda i: (0, 0))] * shards,
         out_specs=[
             pl.BlockSpec((part, BLOCK), lambda i: (0, i)),
             pl.BlockSpec((part, BLOCK), lambda i: (0, i)),
-            pl.BlockSpec((part, width), lambda i: (0, 0)),
         ],
-        scratch_shapes=[pltpu.VMEM((width, part), BF), pltpu.VMEM((width, part), BF), pltpu.VMEM((part, width), BF)],
+        scratch_shapes=[pltpu.VMEM((width, part), BF), pltpu.VMEM((part, width), BF)],
         compiler_params=params(56),
         name="up",
-    )(ids, normed, *w_pieces)
-
+    )(ids, normed, *w_pieces[:shards])
+
+    whole, act_t = lax.optimization_barrier((whole, act_t))
+    sums = add_over(pair_sums(whole), range(len(hops) - 3))
+    sums, w_pieces[shards:] = lax.optimization_barrier((sums, w_pieces[shards:]))
     sums = add_over(sums, [-3])
-    sums, act_t, slope_t = lax.optimization_barrier((sums, act_t, slope_t))
+    sums, slope_t = lax.optimization_barrier((sums, slope_t))
     grad_scale = 1.0 / (tokens * width)
     scores = pl.pallas_call(
         functools.partial(
@@ -479,7 +478,10 @@
             pick,
         ),
         out_shape=[jax.ShapeDtypeStruct((2, rows, cols), BF)] * particles,
-        in_specs=[smem_spec()] + [any_spec()] * (4 + len(sources)),
+        in_specs=[smem_spec()]
+        + [any_spec()] * 3
+        + [pl.BlockSpec(memory_space=pltpu.VMEM)] * shards
+        + [any_spec()] * len(sources),
         out_specs=[any_spec()] * particles,
         scratch_shapes=[
             pltpu.VMEM((tokens, width), BF),
@@ -487,13 +489,14 @@
             pltpu.VMEM((part, tokens), BF),
             pltpu.VMEM((part, tokens), BF),
             pltpu.VMEM((part, tokens), BF),
+            pltpu.VMEM((width, part), BF),
             pltpu.VMEM((part, width), BF),
             pltpu.VMEM((2, width, part), BF),
             pltpu.SemaphoreType.DMA((particles + 5,)),
         ],
         compiler_params=params(56),
         name="grads",
-    )(ids, normed, act_t, slope_t, down_t, *sources)
+    )(ids, normed, act_t, slope_t, *w_pieces[shards:], *sources)
 
     sums = add_over(sums, [-2])
     sums, *scores = lax.optimization_barrier((sums, *scores))

time: 259 us -> 276 us (1.066)
  starting transfers between devices: 72.8 us -> 86.7 us
  waiting for transfers between devices: 105 us -> 102 us
    ppermute x36 -> x40, starting transfers between devices: 68.8 us -> 82.3 us  [move(): return lax.ppermute(x, AXES, pairs)]
    all_to_all x1, waiting for transfers between devices: 11.3 us -> 0.01 us  [local(): whole = lax.all_to_all(slices, 'particle', 0, 0, tiled=True)]
    ppermute x36 -> x40, waiting for transfers between devices: 93.6 us -> 102 us  [move(): return lax.ppermute(x, AXES, pairs)]
  transfers between devices with their start and end apart: 38 -> 42, of which waited for: 13 -> 15; matrix products, arithmetic and copies ran while one was open for 2% -> 3% of each run, Pallas kernels for 13% -> 12%
where the time goes in v7:
time: 276 us; the launch traced here: 273 us
  waiting for transfers between devices  102 us (37%)
  starting transfers between devices  86.7 us (31%)
  Pallas kernels  55.8 us (20%)
  between operations  15.3 us (6%)
  local copies, waits for them, and re-layouts  8.14 us (3%)
  other arithmetic  5.03 us (2%)
    ppermute x40, waiting for transfers between devices, move(): return lax.ppermute(x, AXES, pairs)  102 us
    ppermute x40, starting transfers between devices, move(): return lax.ppermute(x, AXES, pairs)  82.3 us
    pallas_call x1, Pallas kernels, local(): pl.pallas_call(functools.partial(adam_kernel, particles), grid=(steps,),...  15.4 us
    pallas_call x1, Pallas kernels, local(): pl.pallas_call(functools.partial(grad_kernel, shards, particles, -width *...  14 us
    pallas_call x1, Pallas kernels, local(): pl.pallas_call(functools.partial(up_kernel, shards, width ** (-0.5)), gri...  9.74 us
    pallas_call x1, Pallas kernels, local(): pl.pallas_call(functools.partial(prep_kernel, shards), grid=(steps,), out...  6.56 us
    pallas_call x1, Pallas kernels, local(): pl.pallas_call(functools.partial(stein_kernel, shards, particles), out_sh...  6.42 us
  transfers between devices with their start and end apart: 42, of which 15 were waited for; matrix products, arithmetic and copies ran while one was open for 3% of the time, Pallas kernels for 12%

profile of v7, /device:TPU:23, one launch (start us, length us, event | category | flops | bytes accessed | tf_op | source)
XLA Modules:
  0.0 272.7 jit_solution(7601590265015370388)
XLA Ops:
  21.7 6.6 %prep.1 = (bf16[256,512]{1,0:T(8,128)(2,1)}, bf16[256,512]{1,0:T(8,128)(2,1)}, bf16[256,512]{1,0:T(8,128)(2,1)}, bf16[256,512]{1,0:T(8,128)(2,1)}, bf16[256,512]...) custom-call(s32[5]{0:T(128)} %stack.36.ids, ...), custom_call_target="tpu_custom_call" | custom-call | tf_op jit(solution)/shard_map/prep/pallas_call | solution.py:298
  28.3 18.2 %collective-permute-done.3 = bf16[64,1024]{1,0:T(8,128)(2,1)S(1)} collective-permute-done((bf16[64,1024]{1,0:T(8,128)(2,1)S(1)}, bf16[64,1024]{1,0:T(8,128)(2,1)S(1)}, u32[]{:S(2)}, u32[]{:S(2)}) %collective-permute-start.3) | collective-permute-done | bytes 131104 | tf_op jit(solution)/shard_map/ppermute | solution.py:273
  46.6 3.7 %collective-permute-done.5 = bf16[64,1024]{1,0:T(8,128)(2,1)S(1)} collective-permute-done((bf16[64,1024]{1,0:T(8,128)(2,1)S(1)}, bf16[64,1024]{1,0:T(8,128)(2,1)S(1)}, u32[]{:S(2)}, u32[]{:S(2)}) %collective-permute-start.5) | collective-permute-done | bytes 131104 | tf_op jit(solution)/shard_map/ppermute | solution.py:273
  52.1 4.3 %all-to-all-start = ((bf16[8,2,256,256]{3,2,1,0:T(8,128)(2,1)}), bf16[8,2,256,256]{3,2,1,0:T(8,128)(2,1)}, u32[]{:S(2)}, u32[]{:S(2)}) async-start(bf16[8,2,256,256]{3,2,1,0:T(8,128)(2,1)} %get-tuple-element.79), calls=%async_computation | async-start | bytes 4194304 | tf_op jit(solution)/shard_map/all_to_all | solution.py:318
  59.1 3.9 %collective-permute-start.8 = (bf16[256,512]{1,0:T(8,128)(2,1)}, bf16[256,512]{1,0:T(8,128)(2,1)}, u32[]{:S(2)}, u32[]{:S(2)}) collective-permute-start(bf16[256,512]{1,0:T(8,128)(2,1)} %get-tuple-element.93), channel_id=1, source_target_pairs={{0,1},{1,5},{2,0},{3,4},{4,3},{5,7},{6,2},{7,6},{8,9},{9,13},{10,8... | collective-permute-start | bytes 786440 | tf_op jit(solution)/shard_map/ppermute | solution.py:273
  68.9 5.3 %collective-permute-start.21 = (bf16[256,1024]{1,0:T(8,128)(2,1)}, bf16[256,1024]{1,0:T(8,128)(2,1)}, u32[]{:S(2)}, u32[]{:S(2)}) collective-permute-start(bf16[256,1024]{1,0:T(8,128)(2,1)} %broadcast_select_fusion.1), channel_id=1, source_target_pairs={{0,5},{1,0},{2,3},{5,4},{6,7},{7,2},{8,13},{9,8},{10,11},{13,12},{... | collective-permute-start | bytes 1572872 | tf_op jit(solution)/shard_map/ppermute | solution.py:273
  74.2 5.8 %collective-permute-start.9 = (bf16[256,512]{1,0:T(8,128)(2,1)}, bf16[256,512]{1,0:T(8,128)(2,1)}, u32[]{:S(2)}, u32[]{:S(2)}) collective-permute-start(bf16[256,512]{1,0:T(8,128)(2,1)} %get-tuple-element.94), channel_id=1, source_target_pairs={{0,4},{1,1},{2,5},{3,0},{4,6},{5,3},{6,7},{7,2},{8,12},{9,9},{10,1... | collective-permute-start | bytes 786440 | tf_op jit(solution)/shard_map/ppermute | solution.py:273
  85.9 21.6 %collective-permute-done.9.refs_3_ = bf16[256,512]{1,0:T(8,128)(2,1)} collective-permute-done((bf16[256,512]{1,0:T(8,128)(2,1)}, bf16[256,512]{1,0:T(8,128)(2,1)}, u32[]{:S(2)}, u32[]{:S(2)}) %collective-permute-start.9) | collective-permute-done | bytes 262176 | tf_op jit(solution)/shard_map/ppermute | solution.py:273
  107.5 9.7 %up.1 = (bf16[512,2048]{1,0:T(8,128)(2,1)}, bf16[512,2048]{1,0:T(8,128)(2,1)}) custom-call(s32[5]{0:T(128)} %stack.36.ids, bf16[2048,1024]{1,0:T(8,128)(2,1)} %bitcast.60, bf16[256,512]{1,0:T(8,128)(2,1)} %copy-done.18, bf16[256,512]{1,0:T(8,128)(2,1)} %copy-done.19, bf16[256,512]{1,0:T(8,128)(2,1)} %collective-permute-done.8.refs_2_, ...), custom_call_target="tpu_custom_call" | custom-call | tf_op jit(solution)/shard_map/up/pallas_call | solution.py:446
  124.8 3.8 %collective-permute-start.15 = (bf16[256,512]{1,0:T(8,128)(2,1)}, bf16[256,512]{1,0:T(8,128)(2,1)S(1)}, u32[]{:S(2)}, u32[]{:S(2)}) collective-permute-start(bf16[256,512]{1,0:T(8,128)(2,1)} %get-tuple-element.106), channel_id=1, source_target_pairs={{0,4},{1,1},{2,5},{3,0},{4,6},{5,3},{6,7},{7,2},{8,12},{9,9},{10,1... | collective-permute-start | bytes 786440 | tf_op jit(solution)/shard_map/ppermute | solution.py:273
  128.6 4.5 %collective-permute-done.15.refs_3_ = bf16[256,512]{1,0:T(8,128)(2,1)S(1)} collective-permute-done((bf16[256,512]{1,0:T(8,128)(2,1)}, bf16[256,512]{1,0:T(8,128)(2,1)S(1)}, u32[]{:S(2)}, u32[]{:S(2)}) %collective-permute-start.15) | collective-permute-done | bytes 262176 | tf_op jit(solution)/shard_map/ppermute | solution.py:273
  139.6 14.0 %grads.1 = (bf16[2,256,256]{2,1,0:T(8,128)(2,1)}, bf16[2,256,256]{2,1,0:T(8,128)(2,1)}, bf16[2,256,256]{2,1,0:T(8,128)(2,1)}, bf16[2,256,256]{2,1,0:T(8,128)(2,1...) custom-call(s32[5]{0:T(128)} %stack.36.ids, ...), custom_call_target="tpu_custom_call" | custom-call | tf_op jit(solution)/shard_map/grads/pallas_call | solution.py:470
  153.7 6.3 %collective-permute-start.25 = (bf16[2,256,256]{2,1,0:T(8,128)(2,1)}, bf16[2,256,256]{2,1,0:T(8,128)(2,1)S(1)}, u32[]{:S(2)}, u32[]{:S(2)}) collective-permute-start(bf16[2,256,256]{2,1,0:T(8,128)(2,1)} %get-tuple-element.128), channel_id=1, source_target_pairs={{0,0},{1,2},{2,4},{3,6},{4,17},{5,19},{6,21},{7,23},{8,9},{9,11},{... | collective-permute-start | bytes 786440 | tf_op jit(solution)/shard_map/ppermute | solution.py:273
  159.9 4.6 %collective-permute-start.26 = (bf16[2,256,256]{2,1,0:T(8,128)(2,1)}, bf16[2,256,256]{2,1,0:T(8,128)(2,1)S(1)}, u32[]{:S(2)}, u32[]{:S(2)}) collective-permute-start(bf16[2,256,256]{2,1,0:T(8,128)(2,1)} %get-tuple-element.129), channel_id=1, source_target_pairs={{0,31},{1,29},{2,0},{3,2},{4,12},{5,14},{6,17},{7,19},{8,4},{9,6},... | collective-permute-start | bytes 786440 | tf_op jit(solution)/shard_map/ppermute | solution.py:273
  164.6 5.0 %collective-permute-start.28 = (bf16[2,256,256]{2,1,0:T(8,128)(2,1)}, bf16[2,256,256]{2,1,0:T(8,128)(2,1)S(1)}, u32[]{:S(2)}, u32[]{:S(2)}) collective-permute-start(bf16[2,256,256]{2,1,0:T(8,128)(2,1)} %get-tuple-element.131), channel_id=1, source_target_pairs={{0,22},{1,20},{2,27},{3,25},{4,7},{5,5},{6,8},{7,10},{8,31},{9,29}... | collective-permute-start | bytes 786440 | tf_op jit(solution)/shard_map/ppermute | solution.py:273
  170.4 12.9 %collective-permute-done.24 = f32[8,128]{1,0:T(8,128)S(1)} collective-permute-done((f32[8,128]{1,0:T(8,128)S(1)}, f32[8,128]{1,0:T(8,128)S(1)}, u32[]{:S(2)}, u32[]{:S(2)}) %collective-permute-start.24) | collective-permute-done | bytes 4128 | tf_op jit(solution)/shard_map/ppermute | solution.py:273
  192.5 4.8 %collective-permute-done.30.refs_5_ = bf16[2,256,256]{2,1,0:T(8,128)(2,1)} collective-permute-done((bf16[2,256,256]{2,1,0:T(8,128)(2,1)}, bf16[2,256,256]{2,1,0:T(8,128)(2,1)}, u32[]{:S(2)}, u32[]{:S(2)}) %collective-permute-start.30) | collective-permute-done | bytes 262176 | tf_op jit(solution)/shard_map/ppermute | solution.py:273
  197.3 4.0 %collective-permute-done.31.refs_6_ = bf16[2,256,256]{2,1,0:T(8,128)(2,1)} collective-permute-done((bf16[2,256,256]{2,1,0:T(8,128)(2,1)}, bf16[2,256,256]{2,1,0:T(8,128)(2,1)}, u32[]{:S(2)}, u32[]{:S(2)}) %collective-permute-start.31) | collective-permute-done | bytes 262176 | tf_op jit(solution)/shard_map/ppermute | solution.py:273
  201.3 6.3 %collective-permute-done.32.refs_7_ = bf16[2,256,256]{2,1,0:T(8,128)(2,1)} collective-permute-done((bf16[2,256,256]{2,1,0:T(8,128)(2,1)}, bf16[2,256,256]{2,1,0:T(8,128)(2,1)}, u32[]{:S(2)}, u32[]{:S(2)}) %collective-permute-start.32) | collective-permute-done | bytes 262176 | tf_op jit(solution)/shard_map/ppermute | solution.py:273
  207.7 6.4 %stein.1 = (bf16[2,256,256]{2,1,0:T(8,128)(2,1)S(1)}, bf16[2,256,256]{2,1,0:T(8,128)(2,1)S(1)}, bf16[2,256,256]{2,1,0:T(8,128)(2,1)S(1)}, bf16[2,256,256]{2,1,0:...) custom-call(s32[5]{0:T(128)S(1)} %copy-done.2, ...), custom_call_target="tpu_custom_call" | custom-call | tf_op jit(solution)/shard_map/stein/pallas_call | solution.py:533
  214.8 4.7 %collective-permute-start.33 = (bf16[2,256,256]{2,1,0:T(8,128)(2,1)S(1)}, bf16[2,256,256]{2,1,0:T(8,128)(2,1)S(1)}, u32[]{:S(2)}, u32[]{:S(2)}) collective-permute-start(bf16[2,256,256]{2,1,0:T(8,128)(2,1)S(1)} %get-tuple-element.143), channel_id=1, source_target_pairs={{0,4},{1,5},{2,6},{3,7},{4,0},{5,1},{6,2},{7,3},{8,12},{9,13},{10,... | collective-permute-start | bytes 786440 | tf_op jit(solution)/shard_map/ppermute | solution.py:273
  227.6 4.3 %collective-permute-start.39 = (bf16[2,256,256]{2,1,0:T(8,128)(2,1)S(1)}, bf16[2,256,256]{2,1,0:T(8,128)(2,1)S(1)}, u32[]{:S(2)}, u32[]{:S(2)}) collective-permute-start(bf16[2,256,256]{2,1,0:T(8,128)(2,1)S(1)} %get-tuple-element.149), channel_id=1, source_target_pairs={{0,28},{1,29},{2,30},{3,31},{4,24},{5,25},{6,26},{7,27},{8,4},{9,5... | collective-permute-start | bytes 786440 | tf_op jit(solution)/shard_map/ppermute | solution.py:273
  233.8 15.7 %collective-permute-done.37.refs_5_ = bf16[2,256,256]{2,1,0:T(8,128)(2,1)S(1)} collective-permute-done((bf16[2,256,256]{2,1,0:T(8,128)(2,1)S(1)}, bf16[2,256,256]{2,1,0:T(8,128)(2,1)S(1)}, u32[]{:S(2)}, u32[]{:S(2)}) %collective-permute-start.37) | collective-permute-done | bytes 262176 | tf_op jit(solution)/shard_map/ppermute | solution.py:273
  250.4 15.4 %adam.1 = (f32[8192,128]{1,0:T(8,128)}, f32[8192,128]{1,0:T(8,128)}, f32[8192,128]{1,0:T(8,128)}, f32[8192,128]{1,0:T(8,128)}) custom-call(s32[5]{0:T(128)} %stack.36.ids, f32[8192,128]{1,0:T(8,128)} %bitcast.59, f32[8192,128]{1,0:T(8,128)} %bitcast.62, f32[8192,128]{1,0:T(8,128)} %bitcast.63, bf16[2,256,256]{2,1,0:T(8,128)(2,1)} %copy-done.1, ...), custom_call_target="tpu_custom_call" | custom-call | tf_op jit(solution)/shard_map/adam/pallas_call | solution.py:557
  (138 shorter events, 65.7 us)
Async XLA Ops:
  7.2 100.3 %all-gather.3.cloned.1.call-start = ((), (), s32[]{:S(2)}) async-start(), calls=%async_computation.1 | async-start | bytes 4718592 | tf_op jit(solution)/shard_map/all_gather | solution.py:382
  9.7 42.4 %collective-permute-start = (bf16[256,1024]{1,0:T(8,128)(2,1)}, bf16[256,1024]{1,0:T(8,128)(2,1)S(1)}, u32[]{:S(2)}, u32[]{:S(2)}) collective-permute-start(bf16[256,1024]{1,0:T(8,128)(2,1)} %get-tuple-element.157), channel_id=1, source_target_pairs={{1,0},{2,1},{3,5},{4,2},{5,6},{6,7},{9,8},{10,9},{11,13},{12,10},{... | collective-permute-start | bytes 1572872 | tf_op jit(solution)/shard_map/ppermute | solution.py:273
  12.9 39.2 %collective-permute-start.1 = (bf16[256,1024]{1,0:T(8,128)(2,1)}, bf16[256,1024]{1,0:T(8,128)(2,1)S(1)}, u32[]{:S(2)}, u32[]{:S(2)}) collective-permute-start(bf16[256,1024]{1,0:T(8,128)(2,1)} %get-tuple-element.156), channel_id=1, source_target_pairs={{1,4},{2,5},{3,1},{4,6},{5,2},{6,3},{9,12},{10,13},{11,9},{12,14},... | collective-permute-start | bytes 1572872 | tf_op jit(solution)/shard_map/ppermute | solution.py:273
  15.1 37.0 %collective-permute-start.2 = (bf16[512,1024]{1,0:T(8,128)(2,1)}, bf16[512,1024]{1,0:T(8,128)(2,1)}, u32[]{:S(2)}, u32[]{:S(2)}) collective-permute-start(bf16[512,1024]{1,0:T(8,128)(2,1)} %bitcast.64), channel_id=1, source_target_pairs={{0,4},{1,5},{6,2},{7,3},{8,12},{9,13},{14,10},{15,11},{16,20},{17,... | collective-permute-start | bytes 3145736 | tf_op jit(solution)/shard_map/ppermute | solution.py:273
  20.1 26.4 %collective-permute-start.3 = (bf16[64,1024]{1,0:T(8,128)(2,1)S(1)}, bf16[64,1024]{1,0:T(8,128)(2,1)S(1)}, u32[]{:S(2)}, u32[]{:S(2)}) collective-permute-start(bf16[64,1024]{1,0:T(8,128)(2,1)S(1)} %fusion.1), channel_id=1, source_target_pairs={{0,1},{1,2},{2,3},{3,0},{4,5},{5,6},{6,7},{7,4},{8,9},{9,10},{10,1... | collective-permute-start | bytes 393224 | tf_op jit(solution)/shard_map/ppermute | solution.py:273
  21.0 25.6 %collective-permute-start.4 = (bf16[64,1024]{1,0:T(8,128)(2,1)S(1)}, bf16[64,1024]{1,0:T(8,128)(2,1)}, u32[]{:S(2)}, u32[]{:S(2)}) collective-permute-start(bf16[64,1024]{1,0:T(8,128)(2,1)S(1)} %fusion.1), channel_id=1, source_target_pairs={{0,2},{1,3},{2,0},{3,1},{4,6},{5,7},{6,4},{7,5},{8,10},{9,11},{10,... | collective-permute-start | bytes 393224 | tf_op jit(solution)/shard_map/ppermute | solution.py:273
  52.1 65.1 %all-to-all-start = ((bf16[8,2,256,256]{3,2,1,0:T(8,128)(2,1)}), bf16[8,2,256,256]{3,2,1,0:T(8,128)(2,1)}, u32[]{:S(2)}, u32[]{:S(2)}) async-start(bf16[8,2,256,256]{3,2,1,0:T(8,128)(2,1)} %get-tuple-element.79), calls=%async_computation | async-start | bytes 4194304 | tf_op jit(solution)/shard_map/all_to_all | solution.py:318
  59.1 23.1 %collective-permute-start.8 = (bf16[256,512]{1,0:T(8,128)(2,1)}, bf16[256,512]{1,0:T(8,128)(2,1)}, u32[]{:S(2)}, u32[]{:S(2)}) collective-permute-start(bf16[256,512]{1,0:T(8,128)(2,1)} %get-tuple-element.93), channel_id=1, source_target_pairs={{0,1},{1,5},{2,0},{3,4},{4,3},{5,7},{6,2},{7,6},{8,9},{9,13},{10,8... | collective-permute-start | bytes 786440 | tf_op jit(solution)/shard_map/ppermute | solution.py:273
  63.9 57.6 %collective-permute-start.20 = (bf16[256,1024]{1,0:T(8,128)(2,1)}, bf16[256,1024]{1,0:T(8,128)(2,1)}, u32[]{:S(2)}, u32[]{:S(2)}) collective-permute-start(bf16[256,1024]{1,0:T(8,128)(2,1)} %broadcast_select_fusion), channel_id=1, source_target_pairs={{0,1},{1,0},{2,3},{5,4},{6,7},{7,6},{8,9},{9,8},{10,11},{13,12},{1... | collective-permute-start | bytes 1572872 | tf_op jit(solution)/shard_map/ppermute | solution.py:273
  68.9 52.7 %collective-permute-start.21 = (bf16[256,1024]{1,0:T(8,128)(2,1)}, bf16[256,1024]{1,0:T(8,128)(2,1)}, u32[]{:S(2)}, u32[]{:S(2)}) collective-permute-start(bf16[256,1024]{1,0:T(8,128)(2,1)} %broadcast_select_fusion.1), channel_id=1, source_target_pairs={{0,5},{1,0},{2,3},{5,4},{6,7},{7,2},{8,13},{9,8},{10,11},{13,12},{... | collective-permute-start | bytes 1572872 | tf_op jit(solution)/shard_map/ppermute | solution.py:273
  74.2 33.3 %collective-permute-start.9 = (bf16[256,512]{1,0:T(8,128)(2,1)}, bf16[256,512]{1,0:T(8,128)(2,1)}, u32[]{:S(2)}, u32[]{:S(2)}) collective-permute-start(bf16[256,512]{1,0:T(8,128)(2,1)} %get-tuple-element.94), channel_id=1, source_target_pairs={{0,4},{1,1},{2,5},{3,0},{4,6},{5,3},{6,7},{7,2},{8,12},{9,9},{10,1... | collective-permute-start | bytes 786440 | tf_op jit(solution)/shard_map/ppermute | solution.py:273
  80.0 40.9 %collective-permute-start.12 = (bf16[256,512]{1,0:T(8,128)(2,1)}, bf16[256,512]{1,0:T(8,128)(2,1)S(1)}, u32[]{:S(2)}, u32[]{:S(2)}) collective-permute-start(bf16[256,512]{1,0:T(8,128)(2,1)} %get-tuple-element.103), channel_id=1, source_target_pairs={{0,0},{1,4},{2,1},{3,5},{4,2},{5,6},{6,3},{7,7},{8,8},{9,12},{10,9... | collective-permute-start | bytes 786440 | tf_op jit(solution)/shard_map/ppermute | solution.py:273
  82.2 38.7 %collective-permute-start.13 = (bf16[256,512]{1,0:T(8,128)(2,1)}, bf16[256,512]{1,0:T(8,128)(2,1)}, u32[]{:S(2)}, u32[]{:S(2)}) collective-permute-start(bf16[256,512]{1,0:T(8,128)(2,1)} %get-tuple-element.104), channel_id=1, source_target_pairs={{0,5},{1,0},{2,4},{3,1},{4,7},{5,2},{6,6},{7,3},{8,13},{9,8},{10,1... | collective-permute-start | bytes 786440 | tf_op jit(solution)/shard_map/ppermute | solution.py:273
  121.0 16.7 %collective-permute-start.18 = (bf16[256,1024]{1,0:T(8,128)(2,1)S(1)}, bf16[256,1024]{1,0:T(8,128)(2,1)S(1)}, u32[]{:S(2)}, u32[]{:S(2)}) collective-permute-start(bf16[256,1024]{1,0:T(8,128)(2,1)S(1)} %collective-permute-done.refs_6_), channel_id=1, source_target_pairs={{0,4},{1,5},{2,6},{3,7},{4,0},{5,1},{6,2},{7,3},{8,12},{9,13},{10,... | collective-permute-start | bytes 1572872 | tf_op jit(solution)/shard_map/ppermute | solution.py:273
  121.5 16.2 %collective-permute-start.19 = (bf16[256,1024]{1,0:T(8,128)(2,1)S(1)}, bf16[256,1024]{1,0:T(8,128)(2,1)S(1)}, u32[]{:S(2)}, u32[]{:S(2)}) collective-permute-start(bf16[256,1024]{1,0:T(8,128)(2,1)S(1)} %collective-permute-done.1.refs_7_), channel_id=1, source_target_pairs={{0,4},{1,5},{2,6},{3,7},{4,0},{5,1},{6,2},{7,3},{8,12},{9,13},{10,... | collective-permute-start | bytes 1572872 | tf_op jit(solution)/shard_map/ppermute | solution.py:273
  135.8 17.8 %collective-permute-start.17 = (f32[8,128]{1,0:T(8,128)S(1)}, f32[8,128]{1,0:T(8,128)S(1)}, u32[]{:S(2)}, u32[]{:S(2)}) collective-permute-start(f32[8,128]{1,0:T(8,128)S(1)} %add.93), channel_id=1, source_target_pairs={{0,1},{1,0},{2,3},{3,2},{4,5},{5,4},{6,7},{7,6},{8,9},{9,8},{10,11... | collective-permute-start | bytes 12296 | tf_op jit(solution)/shard_map/ppermute | solution.py:273
  153.7 31.3 %collective-permute-start.25 = (bf16[2,256,256]{2,1,0:T(8,128)(2,1)}, bf16[2,256,256]{2,1,0:T(8,128)(2,1)S(1)}, u32[]{:S(2)}, u32[]{:S(2)}) collective-permute-start(bf16[2,256,256]{2,1,0:T(8,128)(2,1)} %get-tuple-element.128), channel_id=1, source_target_pairs={{0,0},{1,2},{2,4},{3,6},{4,17},{5,19},{6,21},{7,23},{8,9},{9,11},{... | collective-permute-start | bytes 786440 | tf_op jit(solution)/shard_map/ppermute | solution.py:273
  159.9 28.6 %collective-permute-start.26 = (bf16[2,256,256]{2,1,0:T(8,128)(2,1)}, bf16[2,256,256]{2,1,0:T(8,128)(2,1)S(1)}, u32[]{:S(2)}, u32[]{:S(2)}) collective-permute-start(bf16[2,256,256]{2,1,0:T(8,128)(2,1)} %get-tuple-element.129), channel_id=1, source_target_pairs={{0,31},{1,29},{2,0},{3,2},{4,12},{5,14},{6,17},{7,19},{8,4},{9,6},... | collective-permute-start | bytes 786440 | tf_op jit(solution)/shard_map/ppermute | solution.py:273
  164.5 26.0 %collective-permute-start.27 = (bf16[2,256,256]{2,1,0:T(8,128)(2,1)}, bf16[2,256,256]{2,1,0:T(8,128)(2,1)S(1)}, u32[]{:S(2)}, u32[]{:S(2)}) collective-permute-start(bf16[2,256,256]{2,1,0:T(8,128)(2,1)} %get-tuple-element.130), channel_id=1, source_target_pairs={{0,27},{1,25},{2,31},{3,29},{4,8},{5,10},{6,12},{7,14},{8,0},{9,2}... | collective-permute-start | bytes 786440 | tf_op jit(solution)/shard_map/ppermute | solution.py:273
  164.6 26.7 %collective-permute-start.28 = (bf16[2,256,256]{2,1,0:T(8,128)(2,1)}, bf16[2,256,256]{2,1,0:T(8,128)(2,1)S(1)}, u32[]{:S(2)}, u32[]{:S(2)}) collective-permute-start(bf16[2,256,256]{2,1,0:T(8,128)(2,1)} %get-tuple-element.131), channel_id=1, source_target_pairs={{0,22},{1,20},{2,27},{3,25},{4,7},{5,5},{6,8},{7,10},{8,31},{9,29}... | collective-permute-start | bytes 786440 | tf_op jit(solution)/shard_map/ppermute | solution.py:273
  190.6 17.1 %collective-permute-start.32 = (bf16[2,256,256]{2,1,0:T(8,128)(2,1)}, bf16[2,256,256]{2,1,0:T(8,128)(2,1)}, u32[]{:S(2)}, u32[]{:S(2)}) collective-permute-start(bf16[2,256,256]{2,1,0:T(8,128)(2,1)} %get-tuple-element.141), channel_id=1, source_target_pairs={{0,4},{1,6},{2,9},{3,11},{4,21},{5,23},{6,26},{7,24},{8,13},{9,15}... | collective-permute-start | bytes 786440 | tf_op jit(solution)/shard_map/ppermute | solution.py:273
  224.7 24.9 %collective-permute-start.37 = (bf16[2,256,256]{2,1,0:T(8,128)(2,1)S(1)}, bf16[2,256,256]{2,1,0:T(8,128)(2,1)S(1)}, u32[]{:S(2)}, u32[]{:S(2)}) collective-permute-start(bf16[2,256,256]{2,1,0:T(8,128)(2,1)S(1)} %get-tuple-element.147), channel_id=1, source_target_pairs={{0,20},{1,21},{2,22},{3,23},{4,16},{5,17},{6,18},{7,19},{8,28},{9,... | collective-permute-start | bytes 786440 | tf_op jit(solution)/shard_map/ppermute | solution.py:273
  226.5 23.0 %collective-permute-start.38 = (bf16[2,256,256]{2,1,0:T(8,128)(2,1)S(1)}, bf16[2,256,256]{2,1,0:T(8,128)(2,1)S(1)}, u32[]{:S(2)}, u32[]{:S(2)}) collective-permute-start(bf16[2,256,256]{2,1,0:T(8,128)(2,1)S(1)} %get-tuple-element.148), channel_id=1, source_target_pairs={{0,24},{1,25},{2,26},{3,27},{4,28},{5,29},{6,30},{7,31},{8,0},{9,1... | collective-permute-start | bytes 786440 | tf_op jit(solution)/shard_map/ppermute | solution.py:273
  227.6 21.9 %collective-permute-start.39 = (bf16[2,256,256]{2,1,0:T(8,128)(2,1)S(1)}, bf16[2,256,256]{2,1,0:T(8,128)(2,1)S(1)}, u32[]{:S(2)}, u32[]{:S(2)}) collective-permute-start(bf16[2,256,256]{2,1,0:T(8,128)(2,1)S(1)} %get-tuple-element.149), channel_id=1, source_target_pairs={{0,28},{1,29},{2,30},{3,31},{4,24},{5,25},{6,26},{7,27},{8,4},{9,5... | collective-permute-start | bytes 786440 | tf_op jit(solution)/shard_map/ppermute | solution.py:273
  (40 other events, 544.5 us)
Sparse Core Ops, SparseCore 0:
  52.3 46.9 all-gather.2

commit v8 on v6

--- a/solution.py
+++ b/solution.py
@@ -237,8 +237,8 @@
             part = field[kind, pl.ds(base, rows), tile * LANES : (tile + 1) * LANES]
             transport[pl.ds(2 * tile + kind, rows, stride=2 * lane_tiles), :] = part.astype(F32)
     t = transport[...]
-    m = 0.9 * first[...] - 0.1 * t
-    v = 0.999 * second[...] + 0.001 * t * t
+    m = first[...] - 0.1 * t
+    v = second[...] + 0.001 * t * t
     new_first[...] = m
     new_second[...] = v
     new_w[...] = w[...] - 0.01 * m / (jnp.sqrt(v) + 1e-08)
@@ -381,12 +381,10 @@
         alpha, own_c, prepared, normed = lax.optimization_barrier((alpha, own_c, prepared, normed))
         normed = lax.all_gather(normed[None], "particle", axis=0, tiled=True)
         w_pieces = [move(x, route) for x, route in zip(prepared, w_routes)]
-        hand_on = [jnp.where(inner, a, x) for a, x in zip(alpha, halves)]
+        beta = [move(jnp.where(inner, a, x), route) for a, x, route in zip(alpha, halves, second_routes)]
         alpha_x = [move(x, swap_of(everyone)) for x in alpha]
-        beta = [move(hand_on[0], second_routes[0])]
-        hand_on[1], whole, *w_pieces[:2] = lax.optimization_barrier((hand_on[1], whole, *w_pieces[:2]))
-        beta.append(move(hand_on[1], second_routes[1]))
-        sums = add_over(pair_sums(whole), range(len(hops) - 3))
+        whole, *w_pieces[:3] = lax.optimization_barrier((whole, *w_pieces[:3]))
+        sums = add_over(pair_sums(whole), range(len(hops) - 2))
         w_pieces, normed, sums = lax.optimization_barrier((w_pieces, normed, sums))
         beta_x = [move(x, swap_of(everyone)) for x in beta]
         sources = [cot, own_c, *alpha, *alpha_x, *beta, *beta_x]
@@ -433,7 +431,7 @@
         sources = [jnp.where(core == proc, full, move(full, swap_of(everyone)))]
         w_pieces = [move(x, route) for x, route in zip(prepared, w_routes)]
         normed = lax.all_gather(shift_tokens(normed)[None], "particle", axis=0, tiled=True)
-        sums = add_over(pair_sums(whole), range(len(hops) - 3))
+        sums = add_over(pair_sums(whole), range(len(hops) - 2))
 
         def pick(ids, refs, held, sem):
             def one(which, carry):
@@ -465,7 +463,7 @@
         name="up",
     )(ids, normed, *w_pieces)
 
-    sums = add_over(sums, [-3])
+    sums = add_over(sums, [-2])
     sums, act_t, slope_t = lax.optimization_barrier((sums, act_t, slope_t))
     grad_scale = 1.0 / (tokens * width)
     scores = pl.pallas_call(
@@ -495,7 +493,7 @@
         name="grads",
     )(ids, normed, act_t, slope_t, down_t, *sources)
 
-    sums = add_over(sums, [-2])
+    sums = add_over(sums, [-1])
     sums, *scores = lax.optimization_barrier((sums, *scores))
 
     ratio = particles // shards
@@ -509,9 +507,10 @@
             pairs.append((dev(m, c, s), dev(e // 2 + z, e % 2, z)))
         arrived.append(move(scores[t], pairs))
 
-    rest = move(sums, hops[-1])
-    sums, rest, *arrived[:4] = lax.optimization_barrier((sums, rest, *arrived[:4]))
-    sums = sums + rest
+    first_moment, second_moment, sums, *arrived[:5] = lax.optimization_barrier(
+        (flat(first_moment), flat(second_moment), sums, *arrived[:5])
+    )
+    first_moment, second_moment = 0.9 * first_moment, 0.999 * second_moment
     sums = sums[0]
     lookup = [
         [pair_list.index((max(i, j), min(i, j))) if i != j else len(pair_list) for j in range(particles)]
@@ -558,9 +557,9 @@
         in_specs=[smem_spec()] + [state_spec] * 3 + [any_spec()] * particles,
         out_specs=[state_spec] * 4,
         scratch_shapes=[pltpu.VMEM((2, rows, hidden), BF), pltpu.SemaphoreType.DMA((particles,))],
-        compiler_params=params(56),
+        compiler_params=params(20),
         name="adam",
-    )(ids, w_flat, flat(first_moment), flat(second_moment), *back)
+    )(ids, w_flat, first_moment, second_moment, *back)
     return tuple(unflat(x) for x in outs)
 
 

time: 259 us -> 252 us (0.973)
  waiting for transfers between devices: 105 us -> 86.6 us
  starting transfers between devices: 72.8 us -> 85.2 us
  Pallas kernels: 53.9 us -> 48 us
  other arithmetic: 4.16 us -> 8.33 us
    ppermute x36, waiting for transfers between devices: 93.6 us -> 76.8 us  [move(): return lax.ppermute(x, AXES, pairs)]
    ppermute x36, starting transfers between devices: 68.8 us -> 77.1 us  [move(): return lax.ppermute(x, AXES, pairs)]
    pallas_call x1, Pallas kernels: 15.5 us -> 9.52 us  [local(): pl.pallas_call(functools.partial(adam_kernel, particles), grid=(steps,),...]
    mul x0 -> x1, other arithmetic: none -> 4.19 us  [local(): first_moment, second_moment = (0.9 * first_moment, 0.999 * second_moment)]
    all_to_all x1, starting transfers between devices: 3.96 us -> 8.07 us  [local(): whole = lax.all_to_all(slices, 'particle', 0, 0, tiled=True)]
  transfers between devices with their start and end apart: 38 -> 38, of which waited for: 13 -> 12; matrix products, arithmetic and copies ran while one was open for 2% -> 4% of each run, Pallas kernels for 13% -> 13%
where the time goes in v8:
time: 252 us; the launch traced here: 249 us
  waiting for transfers between devices  86.6 us (34%)
  starting transfers between devices  85.2 us (34%)
  Pallas kernels  48 us (19%)
  between operations  15.2 us (6%)
  other arithmetic  8.33 us (3%)
  local copies, waits for them, and re-layouts  6.26 us (2%)
    ppermute x36, starting transfers between devices, move(): return lax.ppermute(x, AXES, pairs)  77.1 us
    ppermute x36, waiting for transfers between devices, move(): return lax.ppermute(x, AXES, pairs)  76.8 us
    pallas_call x1, Pallas kernels, local(): pl.pallas_call(functools.partial(grad_kernel, shards, particles, -width *...  13.7 us
    pallas_call x1, Pallas kernels, local(): pl.pallas_call(functools.partial(up_kernel, shards, width ** (-0.5)), gri...  10.4 us
    all_to_all x1, waiting for transfers between devices, local(): whole = lax.all_to_all(slices, 'particle', 0, 0, tiled=True)  9.72 us
    pallas_call x1, Pallas kernels, local(): pl.pallas_call(functools.partial(adam_kernel, particles), grid=(steps,),...  9.52 us
    all_to_all x1, starting transfers between devices, local(): whole = lax.all_to_all(slices, 'particle', 0, 0, tiled=True)  8.07 us
    pallas_call x1, Pallas kernels, local(): pl.pallas_call(functools.partial(prep_kernel, shards), grid=(steps,), out...  6.86 us
  transfers between devices with their start and end apart: 38, of which 12 were waited for; matrix products, arithmetic and copies ran while one was open for 4% of the time, Pallas kernels for 13%

profile of v8, /device:TPU:23, one launch (start us, length us, event | category | flops | bytes accessed | tf_op | source)
XLA Modules:
  0.0 249.5 jit_solution(17978469887533167114)
XLA Ops:
  9.7 3.8 %collective-permute-start.1 = (bf16[256,1024]{1,0:T(8,128)(2,1)}, bf16[256,1024]{1,0:T(8,128)(2,1)S(1)}, u32[]{:S(2)}, u32[]{:S(2)}) collective-permute-start(bf16[256,1024]{1,0:T(8,128)(2,1)} %get-tuple-element.138), channel_id=1, source_target_pairs={{1,4},{2,5},{3,1},{4,6},{5,2},{6,3},{9,12},{10,13},{11,9},{12,14},... | collective-permute-start | bytes 1572872 | tf_op jit(solution)/shard_map/ppermute | solution.py:273
  20.0 4.0 %collective-permute-start.4 = (bf16[64,1024]{1,0:T(8,128)(2,1)S(1)}, bf16[64,1024]{1,0:T(8,128)(2,1)S(1)}, u32[]{:S(2)}, u32[]{:S(2)}) collective-permute-start(bf16[64,1024]{1,0:T(8,128)(2,1)S(1)} %fusion.1), channel_id=1, source_target_pairs={{0,2},{1,3},{2,0},{3,1},{4,6},{5,7},{6,4},{7,5},{8,10},{9,11},{10,... | collective-permute-start | bytes 393224 | tf_op jit(solution)/shard_map/ppermute | solution.py:273
  24.6 6.9 %prep.1 = (bf16[2,256,512]{2,1,0:T(8,128)(2,1)}, bf16[2,256,512]{2,1,0:T(8,128)(2,1)}, bf16[2,256,512]{2,1,0:T(8,128)(2,1)}, bf16[2,256,512]{2,1,0:T(8,128)(2,1)}, bf16[8,2,256,256]{3,2,1,0:T(8,128)(2,1)}) custom-call(s32[5]{0:T(128)} %stack.36.ids, f32[8192,128]{1,0:T(8,128)} %bitcast.58), custom_call_target="tpu_custom_call" | custom-call | tf_op jit(solution)/shard_map/prep/pallas_call | solution.py:298
  31.9 5.2 %collective-permute-done.4 = bf16[64,1024]{1,0:T(8,128)(2,1)S(1)} collective-permute-done((bf16[64,1024]{1,0:T(8,128)(2,1)S(1)}, bf16[64,1024]{1,0:T(8,128)(2,1)S(1)}, u32[]{:S(2)}, u32[]{:S(2)}) %collective-permute-start.4) | collective-permute-done | bytes 131104 | tf_op jit(solution)/shard_map/ppermute | solution.py:273
  37.1 9.9 %collective-permute-done.3 = bf16[64,1024]{1,0:T(8,128)(2,1)S(1)} collective-permute-done((bf16[64,1024]{1,0:T(8,128)(2,1)S(1)}, bf16[64,1024]{1,0:T(8,128)(2,1)S(1)}, u32[]{:S(2)}, u32[]{:S(2)}) %collective-permute-start.3) | collective-permute-done | bytes 131104 | tf_op jit(solution)/shard_map/ppermute | solution.py:273
  48.0 8.1 %all-to-all-start = ((bf16[8,2,256,256]{3,2,1,0:T(8,128)(2,1)}), bf16[8,2,256,256]{3,2,1,0:T(8,128)(2,1)S(1)}, u32[]{:S(2)}, u32[]{:S(2)}) async-start(bf16[8,2,256,256]{3,2,1,0:T(8,128)(2,1)} %get-tuple-element.70), calls=%async_computation | async-start | bytes 4194304 | tf_op jit(solution)/shard_map/all_to_all | solution.py:318
  59.7 3.2 %collective-permute-start.8 = (bf16[2,256,512]{2,1,0:T(8,128)(2,1)}, bf16[2,256,512]{2,1,0:T(8,128)(2,1)}, u32[]{:S(2)}, u32[]{:S(2)}) collective-permute-start(bf16[2,256,512]{2,1,0:T(8,128)(2,1)} %get-tuple-element.77), channel_id=1, source_target_pairs={{0,1},{1,5},{2,0},{3,4},{4,3},{5,7},{6,2},{7,6},{8,9},{9,13},{10,8... | collective-permute-start | bytes 1572872 | tf_op jit(solution)/shard_map/ppermute | solution.py:273
  63.8 4.1 %collective-permute-start.18 = (bf16[256,1024]{1,0:T(8,128)(2,1)}, bf16[256,1024]{1,0:T(8,128)(2,1)}, u32[]{:S(2)}, u32[]{:S(2)}) collective-permute-start(bf16[256,1024]{1,0:T(8,128)(2,1)} %broadcast_select_fusion), channel_id=1, source_target_pairs={{0,5},{1,0},{2,3},{5,4},{6,7},{7,2},{8,13},{9,8},{10,11},{13,12},{... | collective-permute-start | bytes 1572872 | tf_op jit(solution)/shard_map/ppermute | solution.py:273
  76.0 9.7 %all-to-all-done.whole = bf16[8,2,256,256]{3,2,1,0:T(8,128)(2,1)S(1)} async-done(((bf16[8,2,256,256]{3,2,1,0:T(8,128)(2,1)}), bf16[8,2,256,256]{3,2,1,0:T(8,128)(2,1)S(1)}, u32[]{:S(2)}, u32[]{:S(2)}) %all-to-all-start) | async-done | bytes 2097184 | tf_op jit(solution)/shard_map/all_to_all | solution.py:318
  87.8 9.8 %collective-permute-start.10 = (f32[8,128]{1,0:T(8,128)S(1)}, f32[8,128]{1,0:T(8,128)S(1)}, u32[]{:S(2)}, u32[]{:S(2)}) collective-permute-start(f32[8,128]{1,0:T(8,128)S(1)} %distances.1), channel_id=1, source_target_pairs={{0,4},{1,5},{2,6},{3,7},{4,0},{5,1},{6,2},{7,3},{8,12},{9,13},{10,... | collective-permute-start | bytes 12296 | tf_op jit(solution)/shard_map/ppermute | solution.py:273
  107.0 7.4 %collective-permute-start.20 = (bf16[256,1024]{1,0:T(8,128)(2,1)}, bf16[256,1024]{1,0:T(8,128)(2,1)}, u32[]{:S(2)}, u32[]{:S(2)}) collective-permute-start(bf16[256,1024]{1,0:T(8,128)(2,1)} %collective-permute-done.18.refs_7_), channel_id=1, source_target_pairs={{0,4},{1,5},{2,6},{3,7},{4,0},{5,1},{6,2},{7,3},{8,12},{9,13},{10,... | collective-permute-start | bytes 1572872 | tf_op jit(solution)/shard_map/ppermute | solution.py:273
  114.5 4.0 %collective-permute-done.9.refs_3_ = bf16[2,256,512]{2,1,0:T(8,128)(2,1)} collective-permute-done((bf16[2,256,512]{2,1,0:T(8,128)(2,1)}, bf16[2,256,512]{2,1,0:T(8,128)(2,1)}, u32[]{:S(2)}, u32[]{:S(2)}) %collective-permute-start.9) | collective-permute-done | bytes 524320 | tf_op jit(solution)/shard_map/ppermute | solution.py:273
  120.4 10.4 %up.1 = (bf16[512,2048]{1,0:T(8,128)(2,1)}, bf16[512,2048]{1,0:T(8,128)(2,1)}, bf16[512,1024]{1,0:T(8,128)(2,1)}) custom-call(s32[5]{0:T(128)} %stack.36.ids, bf16[2048,1024]{1,0:T(8,128)(2,1)} %bitcast.60, bf16[2,256,512]{2,1,0:T(8,128)(2,1)} %copy-done.6, bf16[2,256,512]{2,1,0:T(8,128)(2,1)} %copy-done.7, ...), custom_call_target="tpu_custom_call" | custom-call | tf_op jit(solution)/shard_map/up/pallas_call | solution.py:446
  131.0 13.7 %grads.1 = (bf16[2,256,256]{2,1,0:T(8,128)(2,1)}, bf16[2,256,256]{2,1,0:T(8,128)(2,1)}, bf16[2,256,256]{2,1,0:T(8,128)(2,1)}, bf16[2,256,256]{2,1,0:T(8,128)(2,1...) custom-call(s32[5]{0:T(128)} %stack.36.ids, ...), custom_call_target="tpu_custom_call" | custom-call | tf_op jit(solution)/shard_map/grads/pallas_call | solution.py:469
  144.7 4.2 %collective-permute-start.21 = (bf16[2,256,256]{2,1,0:T(8,128)(2,1)}, bf16[2,256,256]{2,1,0:T(8,128)(2,1)S(1)}, u32[]{:S(2)}, u32[]{:S(2)}) collective-permute-start(bf16[2,256,256]{2,1,0:T(8,128)(2,1)} %get-tuple-element.108), channel_id=1, source_target_pairs={{0,0},{1,2},{2,4},{3,6},{4,17},{5,19},{6,21},{7,23},{8,9},{9,11},{... | collective-permute-start | bytes 786440 | tf_op jit(solution)/shard_map/ppermute | solution.py:273
  153.6 4.2 %collective-permute-start.24 = (bf16[2,256,256]{2,1,0:T(8,128)(2,1)}, bf16[2,256,256]{2,1,0:T(8,128)(2,1)S(1)}, u32[]{:S(2)}, u32[]{:S(2)}) collective-permute-start(bf16[2,256,256]{2,1,0:T(8,128)(2,1)} %get-tuple-element.111), channel_id=1, source_target_pairs={{0,22},{1,20},{2,27},{3,25},{4,7},{5,5},{6,8},{7,10},{8,31},{9,29}... | collective-permute-start | bytes 786440 | tf_op jit(solution)/shard_map/ppermute | solution.py:273
  160.2 18.4 %collective-permute-done.22.refs_1_ = bf16[2,256,256]{2,1,0:T(8,128)(2,1)S(1)} collective-permute-done((bf16[2,256,256]{2,1,0:T(8,128)(2,1)}, bf16[2,256,256]{2,1,0:T(8,128)(2,1)S(1)}, u32[]{:S(2)}, u32[]{:S(2)}) %collective-permute-start.22) | collective-permute-done | bytes 262176 | tf_op jit(solution)/shard_map/ppermute | solution.py:273
  179.9 7.9 %collective-permute-done.27.refs_6_ = bf16[2,256,256]{2,1,0:T(8,128)(2,1)} collective-permute-done((bf16[2,256,256]{2,1,0:T(8,128)(2,1)}, bf16[2,256,256]{2,1,0:T(8,128)(2,1)}, u32[]{:S(2)}, u32[]{:S(2)}) %collective-permute-start.27) | collective-permute-done | bytes 262176 | tf_op jit(solution)/shard_map/ppermute | solution.py:273
  187.7 7.2 %collective-permute-done.28.refs_7_ = bf16[2,256,256]{2,1,0:T(8,128)(2,1)} collective-permute-done((bf16[2,256,256]{2,1,0:T(8,128)(2,1)}, bf16[2,256,256]{2,1,0:T(8,128)(2,1)}, u32[]{:S(2)}, u32[]{:S(2)}) %collective-permute-start.28) | collective-permute-done | bytes 262176 | tf_op jit(solution)/shard_map/ppermute | solution.py:273
  194.9 5.4 %stein.1 = (bf16[2,256,256]{2,1,0:T(8,128)(2,1)S(1)}, bf16[2,256,256]{2,1,0:T(8,128)(2,1)S(1)}, bf16[2,256,256]{2,1,0:T(8,128)(2,1)S(1)}, bf16[2,256,256]{2,1,0:...) custom-call(s32[5]{0:T(128)S(1)} %copy-done.3, ...), custom_call_target="tpu_custom_call" | custom-call | tf_op jit(solution)/shard_map/stein/pallas_call | solution.py:529
  201.0 5.5 %collective-permute-start.30 = (bf16[2,256,256]{2,1,0:T(8,128)(2,1)S(1)}, bf16[2,256,256]{2,1,0:T(8,128)(2,1)S(1)}, u32[]{:S(2)}, u32[]{:S(2)}) collective-permute-start(bf16[2,256,256]{2,1,0:T(8,128)(2,1)S(1)} %get-tuple-element.126), channel_id=1, source_target_pairs={{0,8},{1,9},{2,10},{3,11},{4,12},{5,13},{6,14},{7,15},{8,16},{9,17... | collective-permute-start | bytes 786440 | tf_op jit(solution)/shard_map/ppermute | solution.py:273
  215.5 4.2 %broadcast_multiply_fusion = (f32[8192,128]{1,0:T(8,128)S(1)}, f32[8192,128]{1,0:T(8,128)S(1)}) fusion(f32[8192,128]{1,0:T(8,128)} %bitcast.64, f32[8192,128]{1,0:T(8,128)} %bitcast.65), kind=kLoop, calls=%fused_computation.2 | loop fusion | flops 2097152 | bytes 16777216 | tf_op jit(solution)/shard_map/mul | solution.py:513
  219.7 13.4 %collective-permute-done.33.refs_5_ = bf16[2,256,256]{2,1,0:T(8,128)(2,1)S(1)} collective-permute-done((bf16[2,256,256]{2,1,0:T(8,128)(2,1)S(1)}, bf16[2,256,256]{2,1,0:T(8,128)(2,1)S(1)}, u32[]{:S(2)}, u32[]{:S(2)}) %collective-permute-start.33) | collective-permute-done | bytes 262176 | tf_op jit(solution)/shard_map/ppermute | solution.py:273
  233.1 9.5 %adam.1 = (f32[8192,128]{1,0:T(8,128)}, f32[8192,128]{1,0:T(8,128)}, f32[8192,128]{1,0:T(8,128)}, f32[8192,128]{1,0:T(8,128)}) custom-call(s32[5]{0:T(128)S(1)} %copy-done.3, f32[8192,128]{1,0:T(8,128)S(1)} %bitcast.59, f32[8192,128]{1,0:T(8,128)S(1)} %get-tuple-element.143.first, f32[8192,128]{1,0:T(8,128)S(1)} %get-tuple-element.142.second, ...), custom_call_target="tpu_custom_call" | custom-call | tf_op jit(solution)/shard_map/adam/pallas_call | solution.py:553
  (105 shorter events, 54.3 us)
Async XLA Ops:
  7.2 111.3 %all-gather.3.cloned.1.call-start = ((), (), s32[]{:S(2)}) async-start(), calls=%async_computation.1 | async-start | bytes 4718592 | tf_op jit(solution)/shard_map/all_gather | solution.py:382
  9.7 38.2 %collective-permute-start.1 = (bf16[256,1024]{1,0:T(8,128)(2,1)}, bf16[256,1024]{1,0:T(8,128)(2,1)S(1)}, u32[]{:S(2)}, u32[]{:S(2)}) collective-permute-start(bf16[256,1024]{1,0:T(8,128)(2,1)} %get-tuple-element.138), channel_id=1, source_target_pairs={{1,4},{2,5},{3,1},{4,6},{5,2},{6,3},{9,12},{10,13},{11,9},{12,14},... | collective-permute-start | bytes 1572872 | tf_op jit(solution)/shard_map/ppermute | solution.py:273
  13.4 34.5 %collective-permute-start = (bf16[256,1024]{1,0:T(8,128)(2,1)}, bf16[256,1024]{1,0:T(8,128)(2,1)S(1)}, u32[]{:S(2)}, u32[]{:S(2)}) collective-permute-start(bf16[256,1024]{1,0:T(8,128)(2,1)} %get-tuple-element.139), channel_id=1, source_target_pairs={{1,0},{2,1},{3,5},{4,2},{5,6},{6,7},{9,8},{10,9},{11,13},{12,10},{... | collective-permute-start | bytes 1572872 | tf_op jit(solution)/shard_map/ppermute | solution.py:273
  15.4 32.6 %collective-permute-start.2 = (bf16[512,1024]{1,0:T(8,128)(2,1)}, bf16[512,1024]{1,0:T(8,128)(2,1)}, u32[]{:S(2)}, u32[]{:S(2)}) collective-permute-start(bf16[512,1024]{1,0:T(8,128)(2,1)} %bitcast.62), channel_id=1, source_target_pairs={{0,4},{1,5},{6,2},{7,3},{8,12},{9,13},{14,10},{15,11},{16,20},{17,... | collective-permute-start | bytes 3145736 | tf_op jit(solution)/shard_map/ppermute | solution.py:273
  20.0 17.1 %collective-permute-start.4 = (bf16[64,1024]{1,0:T(8,128)(2,1)S(1)}, bf16[64,1024]{1,0:T(8,128)(2,1)S(1)}, u32[]{:S(2)}, u32[]{:S(2)}) collective-permute-start(bf16[64,1024]{1,0:T(8,128)(2,1)S(1)} %fusion.1), channel_id=1, source_target_pairs={{0,2},{1,3},{2,0},{3,1},{4,6},{5,7},{6,4},{7,5},{8,10},{9,11},{10,... | collective-permute-start | bytes 393224 | tf_op jit(solution)/shard_map/ppermute | solution.py:273
  48.0 37.7 %all-to-all-start = ((bf16[8,2,256,256]{3,2,1,0:T(8,128)(2,1)}), bf16[8,2,256,256]{3,2,1,0:T(8,128)(2,1)S(1)}, u32[]{:S(2)}, u32[]{:S(2)}) async-start(bf16[8,2,256,256]{3,2,1,0:T(8,128)(2,1)} %get-tuple-element.70), calls=%async_computation | async-start | bytes 4194304 | tf_op jit(solution)/shard_map/all_to_all | solution.py:318
  56.0 18.4 %collective-permute-start.6 = (bf16[2,256,512]{2,1,0:T(8,128)(2,1)}, bf16[2,256,512]{2,1,0:T(8,128)(2,1)S(1)}, u32[]{:S(2)}, u32[]{:S(2)}) collective-permute-start(bf16[2,256,512]{2,1,0:T(8,128)(2,1)} %get-tuple-element.75), channel_id=1, source_target_pairs={{0,0},{1,4},{2,1},{3,5},{4,2},{5,6},{6,3},{7,7},{8,8},{9,12},{10,9... | collective-permute-start | bytes 1572872 | tf_op jit(solution)/shard_map/ppermute | solution.py:273
  57.9 16.4 %collective-permute-start.7 = (bf16[2,256,512]{2,1,0:T(8,128)(2,1)}, bf16[2,256,512]{2,1,0:T(8,128)(2,1)S(1)}, u32[]{:S(2)}, u32[]{:S(2)}) collective-permute-start(bf16[2,256,512]{2,1,0:T(8,128)(2,1)} %get-tuple-element.76), channel_id=1, source_target_pairs={{0,5},{1,0},{2,4},{3,1},{4,7},{5,2},{6,6},{7,3},{8,13},{9,8},{10,1... | collective-permute-start | bytes 1572872 | tf_op jit(solution)/shard_map/ppermute | solution.py:273
  59.7 16.3 %collective-permute-start.8 = (bf16[2,256,512]{2,1,0:T(8,128)(2,1)}, bf16[2,256,512]{2,1,0:T(8,128)(2,1)}, u32[]{:S(2)}, u32[]{:S(2)}) collective-permute-start(bf16[2,256,512]{2,1,0:T(8,128)(2,1)} %get-tuple-element.77), channel_id=1, source_target_pairs={{0,1},{1,5},{2,0},{3,4},{4,3},{5,7},{6,2},{7,6},{8,9},{9,13},{10,8... | collective-permute-start | bytes 1572872 | tf_op jit(solution)/shard_map/ppermute | solution.py:273
  63.8 40.0 %collective-permute-start.18 = (bf16[256,1024]{1,0:T(8,128)(2,1)}, bf16[256,1024]{1,0:T(8,128)(2,1)}, u32[]{:S(2)}, u32[]{:S(2)}) collective-permute-start(bf16[256,1024]{1,0:T(8,128)(2,1)} %broadcast_select_fusion), channel_id=1, source_target_pairs={{0,5},{1,0},{2,3},{5,4},{6,7},{7,2},{8,13},{9,8},{10,11},{13,12},{... | collective-permute-start | bytes 1572872 | tf_op jit(solution)/shard_map/ppermute | solution.py:273
  68.8 38.3 %collective-permute-start.17 = (bf16[256,1024]{1,0:T(8,128)(2,1)}, bf16[256,1024]{1,0:T(8,128)(2,1)}, u32[]{:S(2)}, u32[]{:S(2)}) collective-permute-start(bf16[256,1024]{1,0:T(8,128)(2,1)} %broadcast_select_fusion.1), channel_id=1, source_target_pairs={{0,1},{1,0},{2,3},{5,4},{6,7},{7,6},{8,9},{9,8},{10,11},{13,12},{1... | collective-permute-start | bytes 1572872 | tf_op jit(solution)/shard_map/ppermute | solution.py:273
  97.6 20.9 %collective-permute-start.9 = (bf16[2,256,512]{2,1,0:T(8,128)(2,1)}, bf16[2,256,512]{2,1,0:T(8,128)(2,1)}, u32[]{:S(2)}, u32[]{:S(2)}) collective-permute-start(bf16[2,256,512]{2,1,0:T(8,128)(2,1)} %get-tuple-element.81), channel_id=1, source_target_pairs={{0,4},{1,1},{2,5},{3,0},{4,6},{5,3},{6,7},{7,2},{8,12},{9,9},{10,1... | collective-permute-start | bytes 1572872 | tf_op jit(solution)/shard_map/ppermute | solution.py:273
  103.3 27.6 %collective-permute-start.15 = (bf16[256,1024]{1,0:T(8,128)(2,1)S(1)}, bf16[256,1024]{1,0:T(8,128)(2,1)}, u32[]{:S(2)}, u32[]{:S(2)}) collective-permute-start(bf16[256,1024]{1,0:T(8,128)(2,1)S(1)} %collective-permute-done.refs_2_), channel_id=1, source_target_pairs={{0,4},{1,5},{2,6},{3,7},{4,0},{5,1},{6,2},{7,3},{8,12},{9,13},{10,... | collective-permute-start | bytes 1572872 | tf_op jit(solution)/shard_map/ppermute | solution.py:273
  103.8 27.1 %collective-permute-start.16 = (bf16[256,1024]{1,0:T(8,128)(2,1)S(1)}, bf16[256,1024]{1,0:T(8,128)(2,1)}, u32[]{:S(2)}, u32[]{:S(2)}) collective-permute-start(bf16[256,1024]{1,0:T(8,128)(2,1)S(1)} %collective-permute-done.1.refs_3_), channel_id=1, source_target_pairs={{0,4},{1,5},{2,6},{3,7},{4,0},{5,1},{6,2},{7,3},{8,12},{9,13},{10,... | collective-permute-start | bytes 1572872 | tf_op jit(solution)/shard_map/ppermute | solution.py:273
  107.0 23.9 %collective-permute-start.20 = (bf16[256,1024]{1,0:T(8,128)(2,1)}, bf16[256,1024]{1,0:T(8,128)(2,1)}, u32[]{:S(2)}, u32[]{:S(2)}) collective-permute-start(bf16[256,1024]{1,0:T(8,128)(2,1)} %collective-permute-done.18.refs_7_), channel_id=1, source_target_pairs={{0,4},{1,5},{2,6},{3,7},{4,0},{5,1},{6,2},{7,3},{8,12},{9,13},{10,... | collective-permute-start | bytes 1572872 | tf_op jit(solution)/shard_map/ppermute | solution.py:273
  114.5 16.5 %collective-permute-start.19 = (bf16[256,1024]{1,0:T(8,128)(2,1)}, bf16[256,1024]{1,0:T(8,128)(2,1)}, u32[]{:S(2)}, u32[]{:S(2)}) collective-permute-start(bf16[256,1024]{1,0:T(8,128)(2,1)} %collective-permute-done.17.refs_6_), channel_id=1, source_target_pairs={{0,4},{1,5},{2,6},{3,7},{4,0},{5,1},{6,2},{7,3},{8,12},{9,13},{10,... | collective-permute-start | bytes 1572872 | tf_op jit(solution)/shard_map/ppermute | solution.py:273
  149.0 29.6 %collective-permute-start.22 = (bf16[2,256,256]{2,1,0:T(8,128)(2,1)}, bf16[2,256,256]{2,1,0:T(8,128)(2,1)S(1)}, u32[]{:S(2)}, u32[]{:S(2)}) collective-permute-start(bf16[2,256,256]{2,1,0:T(8,128)(2,1)} %get-tuple-element.109), channel_id=1, source_target_pairs={{0,31},{1,29},{2,0},{3,2},{4,12},{5,14},{6,17},{7,19},{8,4},{9,6},... | collective-permute-start | bytes 786440 | tf_op jit(solution)/shard_map/ppermute | solution.py:273
  150.9 27.7 %collective-permute-start.23 = (bf16[2,256,256]{2,1,0:T(8,128)(2,1)}, bf16[2,256,256]{2,1,0:T(8,128)(2,1)S(1)}, u32[]{:S(2)}, u32[]{:S(2)}) collective-permute-start(bf16[2,256,256]{2,1,0:T(8,128)(2,1)} %get-tuple-element.110), channel_id=1, source_target_pairs={{0,27},{1,25},{2,31},{3,29},{4,8},{5,10},{6,12},{7,14},{8,0},{9,2}... | collective-permute-start | bytes 786440 | tf_op jit(solution)/shard_map/ppermute | solution.py:273
  153.6 25.0 %collective-permute-start.24 = (bf16[2,256,256]{2,1,0:T(8,128)(2,1)}, bf16[2,256,256]{2,1,0:T(8,128)(2,1)S(1)}, u32[]{:S(2)}, u32[]{:S(2)}) collective-permute-start(bf16[2,256,256]{2,1,0:T(8,128)(2,1)} %get-tuple-element.111), channel_id=1, source_target_pairs={{0,22},{1,20},{2,27},{3,25},{4,7},{5,5},{6,8},{7,10},{8,31},{9,29}... | collective-permute-start | bytes 786440 | tf_op jit(solution)/shard_map/ppermute | solution.py:273
  157.8 20.8 %collective-permute-start.25 = (bf16[2,256,256]{2,1,0:T(8,128)(2,1)}, bf16[2,256,256]{2,1,0:T(8,128)(2,1)S(1)}, u32[]{:S(2)}, u32[]{:S(2)}) collective-permute-start(bf16[2,256,256]{2,1,0:T(8,128)(2,1)} %get-tuple-element.112), channel_id=1, source_target_pairs={{0,18},{1,16},{2,22},{3,20},{4,3},{5,1},{6,7},{7,5},{8,27},{9,25},... | collective-permute-start | bytes 786440 | tf_op jit(solution)/shard_map/ppermute | solution.py:273
  160.1 19.8 %collective-permute-start.26 = (bf16[2,256,256]{2,1,0:T(8,128)(2,1)}, bf16[2,256,256]{2,1,0:T(8,128)(2,1)}, u32[]{:S(2)}, u32[]{:S(2)}) collective-permute-start(bf16[2,256,256]{2,1,0:T(8,128)(2,1)} %get-tuple-element.121), channel_id=1, source_target_pairs={{0,13},{1,15},{2,18},{3,16},{4,30},{5,28},{6,3},{7,1},{8,22},{9,20... | collective-permute-start | bytes 786440 | tf_op jit(solution)/shard_map/ppermute | solution.py:273
  208.2 24.9 %collective-permute-start.33 = (bf16[2,256,256]{2,1,0:T(8,128)(2,1)S(1)}, bf16[2,256,256]{2,1,0:T(8,128)(2,1)S(1)}, u32[]{:S(2)}, u32[]{:S(2)}) collective-permute-start(bf16[2,256,256]{2,1,0:T(8,128)(2,1)S(1)} %get-tuple-element.129), channel_id=1, source_target_pairs={{0,20},{1,21},{2,22},{3,23},{4,16},{5,17},{6,18},{7,19},{8,28},{9,... | collective-permute-start | bytes 786440 | tf_op jit(solution)/shard_map/ppermute | solution.py:273
  210.0 23.1 %collective-permute-start.34 = (bf16[2,256,256]{2,1,0:T(8,128)(2,1)S(1)}, bf16[2,256,256]{2,1,0:T(8,128)(2,1)S(1)}, u32[]{:S(2)}, u32[]{:S(2)}) collective-permute-start(bf16[2,256,256]{2,1,0:T(8,128)(2,1)S(1)} %get-tuple-element.130), channel_id=1, source_target_pairs={{0,24},{1,25},{2,26},{3,27},{4,28},{5,29},{6,30},{7,31},{8,0},{9,1... | collective-permute-start | bytes 786440 | tf_op jit(solution)/shard_map/ppermute | solution.py:273
  212.3 20.8 %collective-permute-start.35 = (bf16[2,256,256]{2,1,0:T(8,128)(2,1)S(1)}, bf16[2,256,256]{2,1,0:T(8,128)(2,1)S(1)}, u32[]{:S(2)}, u32[]{:S(2)}) collective-permute-start(bf16[2,256,256]{2,1,0:T(8,128)(2,1)S(1)} %get-tuple-element.131), channel_id=1, source_target_pairs={{0,28},{1,29},{2,30},{3,31},{4,24},{5,25},{6,26},{7,27},{8,4},{9,5... | collective-permute-start | bytes 786440 | tf_op jit(solution)/shard_map/ppermute | solution.py:273
  (23 other events, 400.6 us)
Sparse Core Ops, SparseCore 0:
  48.1 51.6 all-gather.2

commit v9 on v8

--- a/solution.py
+++ b/solution.py
@@ -92,53 +92,70 @@
     part, tokens = act.shape
     width = c.shape[1]
     chunk = tokens // shards
-    first = [
-        pltpu.make_async_copy(down_t, down, sems.at[1]),
-        pltpu.make_async_copy(slope_t, slope, sems.at[2]),
-    ]
-    later = [
-        pltpu.make_async_copy(act_t, act, sems.at[3]),
-        pltpu.make_async_copy(normed, n, sems.at[4]),
-    ]
-    for copy in first:
-        copy.start()
-    pick(ids, sources, c, sems.at[0])
-    for copy in later:
-        copy.start()
-    for copy in first:
-        copy.wait()
-    pltpu.make_async_copy(c, c, sems.at[0]).wait()
+    per_turn, per_part = shards // 2, max(shards // 4, 1)
+
+    def chunk_of(i):
+        rest = lax.rem(i, 2 * per_part)
+        return lax.div(rest, per_part) * per_turn + lax.div(i, 2 * per_part) * per_part + lax.rem(rest, per_part)
+
+    def slope_copy(i):
+        at = pl.multiple_of(chunk_of(i) * chunk, chunk)
+        span = (slice(None), pl.ds(at, chunk))
+        return pltpu.make_async_copy(slope_t.at[span], slope.at[span], sems.at[shards + chunk_of(i)])
+
+    down_copy = pltpu.make_async_copy(down_t, down, sems.at[2 * shards])
+    act_copy = pltpu.make_async_copy(act_t, act, sems.at[2 * shards + 1])
+    n_copy = pltpu.make_async_copy(normed, n, sems.at[2 * shards + 2])
+    down_copy.start()
+    for i in range(2):
+        pick(ids, sources, c, sems, i)
+        for j in range(i * shards // 2, (i + 1) * shards // 2):
+            slope_copy(jnp.int32(j)).start()
+    act_copy.start()
+    n_copy.start()
+    down_copy.wait()
 
     def back(i, carry):
-        at = pl.multiple_of(i * chunk, chunk)
+        at = pl.multiple_of(chunk_of(i) * chunk, chunk)
+        rows = c.at[pl.ds(at, chunk), :]
+        pltpu.make_async_copy(rows, rows, sems.at[chunk_of(i)]).wait()
+        slope_copy(i).wait()
         b = lax.dot_general(down[...], c[pl.ds(at, chunk), :], NT, preferred_element_type=F32)
         grad[:, pl.ds(at, chunk)] = (b * (slope[:, pl.ds(at, chunk)].astype(F32) * back_scale)).astype(BF)
         return carry
 
     lax.fori_loop(0, shards, back, 0)
-    for copy in later:
-        copy.wait()
-
-    def gradient(j, carry):
-        at = pl.multiple_of(j * BLOCK, BLOCK)
-        g = jnp.dot(grad[...], n[:, pl.ds(at, BLOCK)], preferred_element_type=F32)
-        score[0, pl.ds(at, BLOCK), :] = (g * up_scale).T.astype(BF)
-        g = jnp.dot(act[...], c[:, pl.ds(at, BLOCK)], preferred_element_type=F32)
-        score[1, pl.ds(at, BLOCK), :] = (g * down_scale).T.astype(BF)
-        return carry
-
-    lax.fori_loop(0, width // BLOCK, gradient, 0)
     rows = width // shards
     ratio = particles // shards
     cols = part // ratio
     mine = 2 * ids[COL] + ids[PROC]
     copies = []
-    for t in range(particles):
-        u = lax.rem(mine + ratio * ids[PIECE] - t + particles, particles)
-        row = pl.multiple_of(lax.div(u, ratio) * rows, rows)
-        col = pl.multiple_of(lax.rem(u, ratio) * cols, cols)
-        copies.append(pltpu.make_async_copy(score.at[:, pl.ds(row, rows), pl.ds(col, cols)], out[t], sems.at[t]))
-    run_copies(copies)
+
+    def send(kind):
+        for t in range(particles):
+            u = lax.rem(mine + ratio * ids[PIECE] - t + particles, particles)
+            row = pl.multiple_of(lax.div(u, ratio) * rows, rows)
+            col = pl.multiple_of(lax.rem(u, ratio) * cols, cols)
+            source = score.at[kind, pl.ds(row, rows), pl.ds(col, cols)]
+            copies.append(pltpu.make_async_copy(source, out[t].at[kind], sems.at[2 * shards + 3 + kind * particles + t]))
+            copies[-1].start()
+
+    def gradient(left, right, scale, kind):
+        def tile(j, carry):
+            at = pl.multiple_of(j * BLOCK, BLOCK)
+            g = jnp.dot(left[...], right[:, pl.ds(at, BLOCK)], preferred_element_type=F32)
+            score[kind, pl.ds(at, BLOCK), :] = (g * scale).T.astype(BF)
+            return carry
+
+        lax.fori_loop(0, width // BLOCK, tile, 0)
+        send(kind)
+
+    act_copy.wait()
+    gradient(act, c, down_scale, 1)
+    n_copy.wait()
+    gradient(grad, n, up_scale, 0)
+    for copy in copies:
+        copy.wait()
 
 
 def distance_kernel(whole, out):
@@ -344,10 +361,12 @@
         k = lax.rem(ids[SHARD] - which + shards, shards)
         return (turn * (particles // 2) * shards + k) * share
 
-    def place(ids, ref, held, sem, which, turn, start=0):
+    def place(ids, ref, held, sems, part, which, turn, start=0):
+        quarter = max(particles // 4, 1)
         row = gather_row(ids, which, turn)
-        for i in range(particles // 2):
+        for i in range(part * quarter, (part + 1) * quarter):
             to = pl.multiple_of(row + i * shards * share, share)
+            sem = sems.at[lax.div(to, tokens // shards)]
             pltpu.make_async_copy(
                 ref.at[pl.ds(start + i * share, share), :], held.at[pl.ds(to, share), :], sem
             ).start()
@@ -381,15 +400,14 @@
         alpha, own_c, prepared, normed = lax.optimization_barrier((alpha, own_c, prepared, normed))
         normed = lax.all_gather(normed[None], "particle", axis=0, tiled=True)
         w_pieces = [move(x, route) for x, route in zip(prepared, w_routes)]
-        beta = [move(jnp.where(inner, a, x), route) for a, x, route in zip(alpha, halves, second_routes)]
+        hand_on = [jnp.where(inner, a, x) for a, x in zip(alpha, halves)]
         alpha_x = [move(x, swap_of(everyone)) for x in alpha]
-        whole, *w_pieces[:3] = lax.optimization_barrier((whole, *w_pieces[:3]))
-        sums = add_over(pair_sums(whole), range(len(hops) - 2))
-        w_pieces, normed, sums = lax.optimization_barrier((w_pieces, normed, sums))
-        beta_x = [move(x, swap_of(everyone)) for x in beta]
-        sources = [cot, own_c, *alpha, *alpha_x, *beta, *beta_x]
-
-        def pick(ids, refs, held, sem):
+        beta = [move(hand_on[0], second_routes[0])]
+        w_pieces, normed, whole, hand_on[1], alpha_x = lax.optimization_barrier(
+            (w_pieces, normed, whole, hand_on[1], alpha_x)
+        )
+        beta.append(move(hand_on[1], second_routes[1]))
+        def pick(ids, refs, held, sems, part):
             s, core, proc = ids[SHARD], ids[CORE], ids[PROC]
             low = s < 2
             near, far, pair = jnp.where(low, 2, 1), jnp.where(low, 3, 0), s + 1 - 2 * lax.rem(s, 2)
@@ -398,18 +416,18 @@
 
             def own(ref):
                 for turn in range(2):
-                    place(ids, ref, held, sem, s, turn, turn * half_rows)
+                    place(ids, ref, held, sems, part, s, turn, turn * half_rows)
 
             def others(main, main_x, rest, rest_x):
                 for e in range(2):
                     same = side == e
-                    place(ids, main[e], held, sem, jnp.where(same, near, far), core)
-                    place(ids, main_x[e], held, sem, jnp.where(same, far, near), 1 - core)
+                    place(ids, main[e], held, sems, part, jnp.where(same, near, far), core)
+                    place(ids, main_x[e], held, sems, part, jnp.where(same, far, near), 1 - core)
 
                     @pl.when(same)
                     def _():
-                        place(ids, rest[e], held, sem, pair, core)
-                        place(ids, rest_x[1 - e], held, sem, pair, 1 - core)
+                        place(ids, rest[e], held, sems, part, pair, core)
+                        place(ids, rest_x[1 - e], held, sems, part, pair, 1 - core)
 
             @pl.when(side == 0)
             def _():
@@ -431,13 +449,12 @@
         sources = [jnp.where(core == proc, full, move(full, swap_of(everyone)))]
         w_pieces = [move(x, route) for x, route in zip(prepared, w_routes)]
         normed = lax.all_gather(shift_tokens(normed)[None], "particle", axis=0, tiled=True)
-        sums = add_over(pair_sums(whole), range(len(hops) - 2))
-
-        def pick(ids, refs, held, sem):
+
+        def pick(ids, refs, held, sems, part):
             def one(which, carry):
                 for turn in range(2):
                     start = pl.multiple_of(which * tok_rows + turn * half_rows, half_rows)
-                    place(ids, refs[0], held, sem, which, turn, start)
+                    place(ids, refs[0], held, sems, part, which, turn, start)
                 return carry
 
             lax.fori_loop(0, shards, one, 0)
@@ -463,8 +480,14 @@
         name="up",
     )(ids, normed, *w_pieces)
 
-    sums = add_over(sums, [-2])
-    sums, act_t, slope_t = lax.optimization_barrier((sums, act_t, slope_t))
+    sums = add_over(pair_sums(whole), [0])
+    sums, act_t = lax.optimization_barrier((sums, act_t))
+    if shards == 4:
+        beta[1], act_t = lax.optimization_barrier((beta[1], act_t))
+        beta_x = [move(x, swap_of(everyone)) for x in beta]
+        sources = [cot, own_c, *alpha, *alpha_x, *beta, *beta_x]
+    sums = add_over(sums, range(1, len(hops) - 2))
+    sums, slope_t = lax.optimization_barrier((sums, slope_t))
     grad_scale = 1.0 / (tokens * width)
     scores = pl.pallas_call(
         functools.partial(
@@ -487,13 +510,13 @@
             pltpu.VMEM((part, tokens), BF),
             pltpu.VMEM((part, width), BF),
             pltpu.VMEM((2, width, part), BF),
-            pltpu.SemaphoreType.DMA((particles + 5,)),
+            pltpu.SemaphoreType.DMA((2 * shards + 3 + 2 * particles,)),
         ],
         compiler_params=params(56),
         name="grads",
     )(ids, normed, act_t, slope_t, down_t, *sources)
 
-    sums = add_over(sums, [-1])
+    sums = add_over(sums, [-2])
     sums, *scores = lax.optimization_barrier((sums, *scores))
 
     ratio = particles // shards
@@ -507,9 +530,11 @@
             pairs.append((dev(m, c, s), dev(e // 2 + z, e % 2, z)))
         arrived.append(move(scores[t], pairs))
 
-    first_moment, second_moment, sums, *arrived[:5] = lax.optimization_barrier(
-        (flat(first_moment), flat(second_moment), sums, *arrived[:5])
+    rest = move(sums, hops[-1])
+    first_moment, second_moment, sums, rest, *arrived[:4] = lax.optimization_barrier(
+        (flat(first_moment), flat(second_moment), sums, rest, *arrived[:4])
     )
+    sums = sums + rest
     first_moment, second_moment = 0.9 * first_moment, 0.999 * second_moment
     sums = sums[0]
     lookup = [

time: 252 us -> 259 us (1.028)
  starting transfers between devices: 85.2 us -> 91 us
    ppermute x36, waiting for transfers between devices: 76.8 us -> 87.5 us  [move(): return lax.ppermute(x, AXES, pairs)]
    all_to_all x1, waiting for transfers between devices: 9.72 us -> 0.01 us  [local(): whole = lax.all_to_all(slices, 'particle', 0, 0, tiled=True)]
    ppermute x36, starting transfers between devices: 77.1 us -> 82.9 us  [move(): return lax.ppermute(x, AXES, pairs)]
  transfers between devices with their start and end apart: 38 -> 38, of which waited for: 12 -> 13; matrix products, arithmetic and copies ran while one was open for 4% -> 4% of each run, Pallas kernels for 13% -> 8%
where the time goes in v9:
time: 259 us; the launch traced here: 257 us
  starting transfers between devices  91 us (35%)
  waiting for transfers between devices  87.5 us (34%)
  Pallas kernels  47.9 us (18%)
  between operations  15.2 us (6%)
  other arithmetic  8.34 us (3%)
  local copies, waits for them, and re-layouts  7.5 us (3%)
    ppermute x36, waiting for transfers between devices, move(): return lax.ppermute(x, AXES, pairs)  87.5 us
    ppermute x36, starting transfers between devices, move(): return lax.ppermute(x, AXES, pairs)  82.9 us
    pallas_call x1, Pallas kernels, local(): pl.pallas_call(functools.partial(grad_kernel, shards, particles, -width *...  13.6 us
    pallas_call x1, Pallas kernels, local(): pl.pallas_call(functools.partial(up_kernel, shards, width ** (-0.5)), gri...  10.4 us
    pallas_call x1, Pallas kernels, local(): pl.pallas_call(functools.partial(adam_kernel, particles), grid=(steps,),...  9.52 us
    all_to_all x1, starting transfers between devices, local(): whole = lax.all_to_all(slices, 'particle', 0, 0, tiled=True)  8.07 us
    pallas_call x1, Pallas kernels, local(): pl.pallas_call(functools.partial(prep_kernel, shards), grid=(steps,), out...  6.86 us
    pallas_call x1, Pallas kernels, local(): pl.pallas_call(functools.partial(stein_kernel, shards, particles), out_sh...  5.37 us
  transfers between devices with their start and end apart: 38, of which 13 were waited for; matrix products, arithmetic and copies ran while one was open for 4% of the time, Pallas kernels for 8%

profile of v9, /device:TPU:23, one launch (start us, length us, event | category | flops | bytes accessed | tf_op | source)
XLA Modules:
  0.0 257.4 jit_solution(17683397171514193333)
XLA Ops:
  9.7 3.8 %collective-permute-start.1 = (bf16[256,1024]{1,0:T(8,128)(2,1)}, bf16[256,1024]{1,0:T(8,128)(2,1)S(1)}, u32[]{:S(2)}, u32[]{:S(2)}) collective-permute-start(bf16[256,1024]{1,0:T(8,128)(2,1)} %get-tuple-element.142), channel_id=1, source_target_pairs={{1,4},{2,5},{3,1},{4,6},{5,2},{6,3},{9,12},{10,13},{11,9},{12,14},... | collective-permute-start | bytes 1572872 | tf_op jit(solution)/shard_map/ppermute | solution.py:290
  20.1 4.0 %collective-permute-start.4 = (bf16[64,1024]{1,0:T(8,128)(2,1)S(1)}, bf16[64,1024]{1,0:T(8,128)(2,1)S(1)}, u32[]{:S(2)}, u32[]{:S(2)}) collective-permute-start(bf16[64,1024]{1,0:T(8,128)(2,1)S(1)} %fusion.1), channel_id=1, source_target_pairs={{0,2},{1,3},{2,0},{3,1},{4,6},{5,7},{6,4},{7,5},{8,10},{9,11},{10,... | collective-permute-start | bytes 393224 | tf_op jit(solution)/shard_map/ppermute | solution.py:290
  24.7 6.9 %prep.1 = (bf16[2,256,512]{2,1,0:T(8,128)(2,1)}, bf16[2,256,512]{2,1,0:T(8,128)(2,1)}, bf16[2,256,512]{2,1,0:T(8,128)(2,1)}, bf16[2,256,512]{2,1,0:T(8,128)(2,1)}, bf16[8,2,256,256]{3,2,1,0:T(8,128)(2,1)}) custom-call(s32[5]{0:T(128)} %stack.36.ids, f32[8192,128]{1,0:T(8,128)} %bitcast.58), custom_call_target="tpu_custom_call" | custom-call | tf_op jit(solution)/shard_map/prep/pallas_call | solution.py:315
  32.0 5.2 %collective-permute-done.4 = bf16[64,1024]{1,0:T(8,128)(2,1)S(1)} collective-permute-done((bf16[64,1024]{1,0:T(8,128)(2,1)S(1)}, bf16[64,1024]{1,0:T(8,128)(2,1)S(1)}, u32[]{:S(2)}, u32[]{:S(2)}) %collective-permute-start.4) | collective-permute-done | bytes 131104 | tf_op jit(solution)/shard_map/ppermute | solution.py:290
  37.2 9.9 %collective-permute-done.3 = bf16[64,1024]{1,0:T(8,128)(2,1)S(1)} collective-permute-done((bf16[64,1024]{1,0:T(8,128)(2,1)S(1)}, bf16[64,1024]{1,0:T(8,128)(2,1)S(1)}, u32[]{:S(2)}, u32[]{:S(2)}) %collective-permute-start.3) | collective-permute-done | bytes 131104 | tf_op jit(solution)/shard_map/ppermute | solution.py:290
  48.1 8.1 %all-to-all-start = ((bf16[8,2,256,256]{3,2,1,0:T(8,128)(2,1)}), bf16[8,2,256,256]{3,2,1,0:T(8,128)(2,1)S(1)}, u32[]{:S(2)}, u32[]{:S(2)}) async-start(bf16[8,2,256,256]{3,2,1,0:T(8,128)(2,1)} %get-tuple-element.81), calls=%async_computation | async-start | bytes 4194304 | tf_op jit(solution)/shard_map/all_to_all | solution.py:335
  66.9 8.8 %collective-permute-done.6.refs_0_ = bf16[2,256,512]{2,1,0:T(8,128)(2,1)} collective-permute-done((bf16[2,256,512]{2,1,0:T(8,128)(2,1)}, bf16[2,256,512]{2,1,0:T(8,128)(2,1)}, u32[]{:S(2)}, u32[]{:S(2)}) %collective-permute-start.6) | collective-permute-done | bytes 524320 | tf_op jit(solution)/shard_map/ppermute | solution.py:290
  76.6 6.7 %collective-permute-start.17 = (bf16[256,1024]{1,0:T(8,128)(2,1)}, bf16[256,1024]{1,0:T(8,128)(2,1)}, u32[]{:S(2)}, u32[]{:S(2)}) collective-permute-start(bf16[256,1024]{1,0:T(8,128)(2,1)} %broadcast_select_fusion), channel_id=1, source_target_pairs={{0,1},{1,0},{2,3},{5,4},{6,7},{7,6},{8,9},{9,8},{10,11},{13,12},{1... | collective-permute-start | bytes 1572872 | tf_op jit(solution)/shard_map/ppermute | solution.py:290
  84.2 16.9 %collective-permute-done.9.refs_3_ = bf16[2,256,512]{2,1,0:T(8,128)(2,1)S(1)} collective-permute-done((bf16[2,256,512]{2,1,0:T(8,128)(2,1)}, bf16[2,256,512]{2,1,0:T(8,128)(2,1)S(1)}, u32[]{:S(2)}, u32[]{:S(2)}) %collective-permute-start.9) | collective-permute-done | bytes 524320 | tf_op jit(solution)/shard_map/ppermute | solution.py:290
  106.6 7.3 %collective-permute-start.12 = (f32[8,128]{1,0:T(8,128)S(1)}, f32[8,128]{1,0:T(8,128)S(1)}, u32[]{:S(2)}, u32[]{:S(2)}) collective-permute-start(f32[8,128]{1,0:T(8,128)S(1)} %distances.1), channel_id=1, source_target_pairs={{0,4},{1,5},{2,6},{3,7},{4,0},{5,1},{6,2},{7,3},{8,12},{9,13},{10,... | collective-permute-start | bytes 12296 | tf_op jit(solution)/shard_map/ppermute | solution.py:290
  114.0 10.4 %up.1 = (bf16[512,2048]{1,0:T(8,128)(2,1)}, bf16[512,2048]{1,0:T(8,128)(2,1)}, bf16[512,1024]{1,0:T(8,128)(2,1)}) custom-call(s32[5]{0:T(128)} %stack.36.ids, bf16[2048,1024]{1,0:T(8,128)(2,1)} %bitcast.60, bf16[2,256,512]{2,1,0:T(8,128)(2,1)} %collective-permute-done.6.refs_0_, bf16[2,256,512]{2,1,0:T(8,128)(2,1)} %copy-done.8, ...), custom_call_target="tpu_custom_call" | custom-call | tf_op jit(solution)/shard_map/up/pallas_call | solution.py:463
  133.5 13.6 %grads.1 = (bf16[2,256,256]{2,1,0:T(8,128)(2,1)}, bf16[2,256,256]{2,1,0:T(8,128)(2,1)}, bf16[2,256,256]{2,1,0:T(8,128)(2,1)}, bf16[2,256,256]{2,1,0:T(8,128)(2,1...) custom-call(s32[5]{0:T(128)} %stack.36.ids, ...), custom_call_target="tpu_custom_call" | custom-call | tf_op jit(solution)/shard_map/grads/pallas_call | solution.py:492
  150.6 5.6 %collective-permute-start.22 = (bf16[2,256,256]{2,1,0:T(8,128)(2,1)}, bf16[2,256,256]{2,1,0:T(8,128)(2,1)S(1)}, u32[]{:S(2)}, u32[]{:S(2)}) collective-permute-start(bf16[2,256,256]{2,1,0:T(8,128)(2,1)} %get-tuple-element.113), channel_id=1, source_target_pairs={{0,31},{1,29},{2,0},{3,2},{4,12},{5,14},{6,17},{7,19},{8,4},{9,6},... | collective-permute-start | bytes 786440 | tf_op jit(solution)/shard_map/ppermute | solution.py:290
  156.3 6.0 %collective-permute-start.24 = (bf16[2,256,256]{2,1,0:T(8,128)(2,1)}, bf16[2,256,256]{2,1,0:T(8,128)(2,1)S(1)}, u32[]{:S(2)}, u32[]{:S(2)}) collective-permute-start(bf16[2,256,256]{2,1,0:T(8,128)(2,1)} %get-tuple-element.115), channel_id=1, source_target_pairs={{0,22},{1,20},{2,27},{3,25},{4,7},{5,5},{6,8},{7,10},{8,31},{9,29}... | collective-permute-start | bytes 786440 | tf_op jit(solution)/shard_map/ppermute | solution.py:290
  163.1 11.2 %collective-permute-done.20 = f32[8,128]{1,0:T(8,128)S(1)} collective-permute-done((f32[8,128]{1,0:T(8,128)S(1)}, f32[8,128]{1,0:T(8,128)S(1)}, u32[]{:S(2)}, u32[]{:S(2)}) %collective-permute-start.20) | collective-permute-done | bytes 4128 | tf_op jit(solution)/shard_map/ppermute | solution.py:290
  175.9 5.2 %collective-permute-start.26 = (bf16[2,256,256]{2,1,0:T(8,128)(2,1)}, bf16[2,256,256]{2,1,0:T(8,128)(2,1)}, u32[]{:S(2)}, u32[]{:S(2)}) collective-permute-start(bf16[2,256,256]{2,1,0:T(8,128)(2,1)} %get-tuple-element.125), channel_id=1, source_target_pairs={{0,13},{1,15},{2,18},{3,16},{4,30},{5,28},{6,3},{7,1},{8,22},{9,20... | collective-permute-start | bytes 786440 | tf_op jit(solution)/shard_map/ppermute | solution.py:290
  186.1 5.7 %collective-permute-done.27.refs_6_ = bf16[2,256,256]{2,1,0:T(8,128)(2,1)} collective-permute-done((bf16[2,256,256]{2,1,0:T(8,128)(2,1)}, bf16[2,256,256]{2,1,0:T(8,128)(2,1)}, u32[]{:S(2)}, u32[]{:S(2)}) %collective-permute-start.27) | collective-permute-done | bytes 262176 | tf_op jit(solution)/shard_map/ppermute | solution.py:290
  191.8 8.4 %collective-permute-done.28.refs_7_ = bf16[2,256,256]{2,1,0:T(8,128)(2,1)} collective-permute-done((bf16[2,256,256]{2,1,0:T(8,128)(2,1)}, bf16[2,256,256]{2,1,0:T(8,128)(2,1)}, u32[]{:S(2)}, u32[]{:S(2)}) %collective-permute-start.28) | collective-permute-done | bytes 262176 | tf_op jit(solution)/shard_map/ppermute | solution.py:290
  200.2 5.4 %stein.1 = (bf16[2,256,256]{2,1,0:T(8,128)(2,1)S(1)}, bf16[2,256,256]{2,1,0:T(8,128)(2,1)S(1)}, bf16[2,256,256]{2,1,0:T(8,128)(2,1)S(1)}, bf16[2,256,256]{2,1,0:...) custom-call(s32[5]{0:T(128)S(1)} %copy-done.3, ...), custom_call_target="tpu_custom_call" | custom-call | tf_op jit(solution)/shard_map/stein/pallas_call | solution.py:554
  208.7 4.1 %collective-permute-start.30 = (bf16[2,256,256]{2,1,0:T(8,128)(2,1)S(1)}, bf16[2,256,256]{2,1,0:T(8,128)(2,1)S(1)}, u32[]{:S(2)}, u32[]{:S(2)}) collective-permute-start(bf16[2,256,256]{2,1,0:T(8,128)(2,1)S(1)} %get-tuple-element.130), channel_id=1, source_target_pairs={{0,8},{1,9},{2,10},{3,11},{4,12},{5,13},{6,14},{7,15},{8,16},{9,17... | collective-permute-start | bytes 786440 | tf_op jit(solution)/shard_map/ppermute | solution.py:290
  218.5 4.8 %collective-permute-start.35 = (bf16[2,256,256]{2,1,0:T(8,128)(2,1)S(1)}, bf16[2,256,256]{2,1,0:T(8,128)(2,1)S(1)}, u32[]{:S(2)}, u32[]{:S(2)}) collective-permute-start(bf16[2,256,256]{2,1,0:T(8,128)(2,1)S(1)} %get-tuple-element.135), channel_id=1, source_target_pairs={{0,28},{1,29},{2,30},{3,31},{4,24},{5,25},{6,26},{7,27},{8,4},{9,5... | collective-permute-start | bytes 786440 | tf_op jit(solution)/shard_map/ppermute | solution.py:290
  223.3 4.2 %broadcast_multiply_fusion = (f32[8192,128]{1,0:T(8,128)S(1)}, f32[8192,128]{1,0:T(8,128)S(1)}) fusion(f32[8192,128]{1,0:T(8,128)} %bitcast.64, f32[8192,128]{1,0:T(8,128)} %bitcast.65), kind=kLoop, calls=%fused_computation.2 | loop fusion | flops 2097152 | bytes 16777216 | tf_op jit(solution)/shard_map/mul | solution.py:538
  227.5 13.4 %collective-permute-done.33.refs_5_ = bf16[2,256,256]{2,1,0:T(8,128)(2,1)S(1)} collective-permute-done((bf16[2,256,256]{2,1,0:T(8,128)(2,1)S(1)}, bf16[2,256,256]{2,1,0:T(8,128)(2,1)S(1)}, u32[]{:S(2)}, u32[]{:S(2)}) %collective-permute-start.33) | collective-permute-done | bytes 262176 | tf_op jit(solution)/shard_map/ppermute | solution.py:290
  241.0 9.5 %adam.1 = (f32[8192,128]{1,0:T(8,128)}, f32[8192,128]{1,0:T(8,128)}, f32[8192,128]{1,0:T(8,128)}, f32[8192,128]{1,0:T(8,128)}) custom-call(s32[5]{0:T(128)S(1)} %copy-done.3, f32[8192,128]{1,0:T(8,128)S(1)} %bitcast.59, f32[8192,128]{1,0:T(8,128)S(1)} %get-tuple-element.147.first, f32[8192,128]{1,0:T(8,128)S(1)} %get-tuple-element.146.second, ...), custom_call_target="tpu_custom_call" | custom-call | tf_op jit(solution)/shard_map/adam/pallas_call | solution.py:578
  (115 shorter events, 57.1 us)
Async XLA Ops:
  7.2 95.6 %all-gather.3.cloned.1.call-start = ((), (), s32[]{:S(2)}) async-start(), calls=%async_computation.1 | async-start | bytes 4718592 | tf_op jit(solution)/shard_map/all_gather | solution.py:401
  9.7 38.3 %collective-permute-start.1 = (bf16[256,1024]{1,0:T(8,128)(2,1)}, bf16[256,1024]{1,0:T(8,128)(2,1)S(1)}, u32[]{:S(2)}, u32[]{:S(2)}) collective-permute-start(bf16[256,1024]{1,0:T(8,128)(2,1)} %get-tuple-element.142), channel_id=1, source_target_pairs={{1,4},{2,5},{3,1},{4,6},{5,2},{6,3},{9,12},{10,13},{11,9},{12,14},... | collective-permute-start | bytes 1572872 | tf_op jit(solution)/shard_map/ppermute | solution.py:290
  13.5 34.5 %collective-permute-start = (bf16[256,1024]{1,0:T(8,128)(2,1)}, bf16[256,1024]{1,0:T(8,128)(2,1)S(1)}, u32[]{:S(2)}, u32[]{:S(2)}) collective-permute-start(bf16[256,1024]{1,0:T(8,128)(2,1)} %get-tuple-element.143), channel_id=1, source_target_pairs={{1,0},{2,1},{3,5},{4,2},{5,6},{6,7},{9,8},{10,9},{11,13},{12,10},{... | collective-permute-start | bytes 1572872 | tf_op jit(solution)/shard_map/ppermute | solution.py:290
  15.4 32.6 %collective-permute-start.2 = (bf16[512,1024]{1,0:T(8,128)(2,1)}, bf16[512,1024]{1,0:T(8,128)(2,1)}, u32[]{:S(2)}, u32[]{:S(2)}) collective-permute-start(bf16[512,1024]{1,0:T(8,128)(2,1)} %bitcast.62), channel_id=1, source_target_pairs={{0,4},{1,5},{6,2},{7,3},{8,12},{9,13},{14,10},{15,11},{16,20},{17,... | collective-permute-start | bytes 3145736 | tf_op jit(solution)/shard_map/ppermute | solution.py:290
  20.1 17.1 %collective-permute-start.4 = (bf16[64,1024]{1,0:T(8,128)(2,1)S(1)}, bf16[64,1024]{1,0:T(8,128)(2,1)S(1)}, u32[]{:S(2)}, u32[]{:S(2)}) collective-permute-start(bf16[64,1024]{1,0:T(8,128)(2,1)S(1)} %fusion.1), channel_id=1, source_target_pairs={{0,2},{1,3},{2,0},{3,1},{4,6},{5,7},{6,4},{7,5},{8,10},{9,11},{10,... | collective-permute-start | bytes 393224 | tf_op jit(solution)/shard_map/ppermute | solution.py:290
  48.1 54.7 %all-to-all-start = ((bf16[8,2,256,256]{3,2,1,0:T(8,128)(2,1)}), bf16[8,2,256,256]{3,2,1,0:T(8,128)(2,1)S(1)}, u32[]{:S(2)}, u32[]{:S(2)}) async-start(bf16[8,2,256,256]{3,2,1,0:T(8,128)(2,1)} %get-tuple-element.81), calls=%async_computation | async-start | bytes 4194304 | tf_op jit(solution)/shard_map/all_to_all | solution.py:335
  56.2 19.5 %collective-permute-start.6 = (bf16[2,256,512]{2,1,0:T(8,128)(2,1)}, bf16[2,256,512]{2,1,0:T(8,128)(2,1)}, u32[]{:S(2)}, u32[]{:S(2)}) collective-permute-start(bf16[2,256,512]{2,1,0:T(8,128)(2,1)} %get-tuple-element.76), channel_id=1, source_target_pairs={{0,0},{1,4},{2,1},{3,5},{4,2},{5,6},{6,3},{7,7},{8,8},{9,12},{10,9... | collective-permute-start | bytes 1572872 | tf_op jit(solution)/shard_map/ppermute | solution.py:290
  58.1 18.5 %collective-permute-start.7 = (bf16[2,256,512]{2,1,0:T(8,128)(2,1)}, bf16[2,256,512]{2,1,0:T(8,128)(2,1)S(1)}, u32[]{:S(2)}, u32[]{:S(2)}) collective-permute-start(bf16[2,256,512]{2,1,0:T(8,128)(2,1)} %get-tuple-element.77), channel_id=1, source_target_pairs={{0,5},{1,0},{2,4},{3,1},{4,7},{5,2},{6,6},{7,3},{8,13},{9,8},{10,1... | collective-permute-start | bytes 1572872 | tf_op jit(solution)/shard_map/ppermute | solution.py:290
  59.8 24.4 %collective-permute-start.8 = (bf16[2,256,512]{2,1,0:T(8,128)(2,1)}, bf16[2,256,512]{2,1,0:T(8,128)(2,1)S(1)}, u32[]{:S(2)}, u32[]{:S(2)}) collective-permute-start(bf16[2,256,512]{2,1,0:T(8,128)(2,1)} %get-tuple-element.78), channel_id=1, source_target_pairs={{0,1},{1,5},{2,0},{3,4},{4,3},{5,7},{6,2},{7,6},{8,9},{9,13},{10,8... | collective-permute-start | bytes 1572872 | tf_op jit(solution)/shard_map/ppermute | solution.py:290
  63.0 38.1 %collective-permute-start.9 = (bf16[2,256,512]{2,1,0:T(8,128)(2,1)}, bf16[2,256,512]{2,1,0:T(8,128)(2,1)S(1)}, u32[]{:S(2)}, u32[]{:S(2)}) collective-permute-start(bf16[2,256,512]{2,1,0:T(8,128)(2,1)} %get-tuple-element.79), channel_id=1, source_target_pairs={{0,4},{1,1},{2,5},{3,0},{4,6},{5,3},{6,7},{7,2},{8,12},{9,9},{10,1... | collective-permute-start | bytes 1572872 | tf_op jit(solution)/shard_map/ppermute | solution.py:290
  65.3 35.9 %collective-permute-start.11 = (bf16[256,1024]{1,0:T(8,128)(2,1)S(1)}, bf16[256,1024]{1,0:T(8,128)(2,1)S(1)}, u32[]{:S(2)}, u32[]{:S(2)}) collective-permute-start(bf16[256,1024]{1,0:T(8,128)(2,1)S(1)} %collective-permute-done.1.refs_3_), channel_id=1, source_target_pairs={{0,4},{1,5},{2,6},{3,7},{4,0},{5,1},{6,2},{7,3},{8,12},{9,13},{10,... | collective-permute-start | bytes 1572872 | tf_op jit(solution)/shard_map/ppermute | solution.py:290
  75.7 27.1 %collective-permute-start.10 = (bf16[256,1024]{1,0:T(8,128)(2,1)S(1)}, bf16[256,1024]{1,0:T(8,128)(2,1)}, u32[]{:S(2)}, u32[]{:S(2)}) collective-permute-start(bf16[256,1024]{1,0:T(8,128)(2,1)S(1)} %collective-permute-done.refs_2_), channel_id=1, source_target_pairs={{0,4},{1,5},{2,6},{3,7},{4,0},{5,1},{6,2},{7,3},{8,12},{9,13},{10,... | collective-permute-start | bytes 1572872 | tf_op jit(solution)/shard_map/ppermute | solution.py:290
  76.6 37.4 %collective-permute-start.17 = (bf16[256,1024]{1,0:T(8,128)(2,1)}, bf16[256,1024]{1,0:T(8,128)(2,1)}, u32[]{:S(2)}, u32[]{:S(2)}) collective-permute-start(bf16[256,1024]{1,0:T(8,128)(2,1)} %broadcast_select_fusion), channel_id=1, source_target_pairs={{0,1},{1,0},{2,3},{5,4},{6,7},{7,6},{8,9},{9,8},{10,11},{13,12},{1... | collective-permute-start | bytes 1572872 | tf_op jit(solution)/shard_map/ppermute | solution.py:290
  102.8 21.6 %collective-permute-start.16 = (bf16[256,1024]{1,0:T(8,128)(2,1)}, bf16[256,1024]{1,0:T(8,128)(2,1)S(1)}, u32[]{:S(2)}, u32[]{:S(2)}) collective-permute-start(bf16[256,1024]{1,0:T(8,128)(2,1)} %broadcast_select_fusion.1), channel_id=1, source_target_pairs={{0,5},{1,0},{2,3},{5,4},{6,7},{7,2},{8,13},{9,8},{10,11},{13,12},{... | collective-permute-start | bytes 1572872 | tf_op jit(solution)/shard_map/ppermute | solution.py:290
  106.6 17.9 %collective-permute-start.12 = (f32[8,128]{1,0:T(8,128)S(1)}, f32[8,128]{1,0:T(8,128)S(1)}, u32[]{:S(2)}, u32[]{:S(2)}) collective-permute-start(f32[8,128]{1,0:T(8,128)S(1)} %distances.1), channel_id=1, source_target_pairs={{0,4},{1,5},{2,6},{3,7},{4,0},{5,1},{6,2},{7,3},{8,12},{9,13},{10,... | collective-permute-start | bytes 12296 | tf_op jit(solution)/shard_map/ppermute | solution.py:290
  113.9 18.5 %collective-permute-start.18 = (bf16[256,1024]{1,0:T(8,128)(2,1)}, bf16[256,1024]{1,0:T(8,128)(2,1)S(1)}, u32[]{:S(2)}, u32[]{:S(2)}) collective-permute-start(bf16[256,1024]{1,0:T(8,128)(2,1)} %collective-permute-done.17.refs_6_), channel_id=1, source_target_pairs={{0,4},{1,5},{2,6},{3,7},{4,0},{5,1},{6,2},{7,3},{8,12},{9,13},{10,... | collective-permute-start | bytes 1572872 | tf_op jit(solution)/shard_map/ppermute | solution.py:290
  147.1 28.9 %collective-permute-start.21 = (bf16[2,256,256]{2,1,0:T(8,128)(2,1)}, bf16[2,256,256]{2,1,0:T(8,128)(2,1)S(1)}, u32[]{:S(2)}, u32[]{:S(2)}) collective-permute-start(bf16[2,256,256]{2,1,0:T(8,128)(2,1)} %get-tuple-element.112), channel_id=1, source_target_pairs={{0,0},{1,2},{2,4},{3,6},{4,17},{5,19},{6,21},{7,23},{8,9},{9,11},{... | collective-permute-start | bytes 786440 | tf_op jit(solution)/shard_map/ppermute | solution.py:290
  150.6 30.5 %collective-permute-start.22 = (bf16[2,256,256]{2,1,0:T(8,128)(2,1)}, bf16[2,256,256]{2,1,0:T(8,128)(2,1)S(1)}, u32[]{:S(2)}, u32[]{:S(2)}) collective-permute-start(bf16[2,256,256]{2,1,0:T(8,128)(2,1)} %get-tuple-element.113), channel_id=1, source_target_pairs={{0,31},{1,29},{2,0},{3,2},{4,12},{5,14},{6,17},{7,19},{8,4},{9,6},... | collective-permute-start | bytes 786440 | tf_op jit(solution)/shard_map/ppermute | solution.py:290
  156.3 27.1 %collective-permute-start.23 = (bf16[2,256,256]{2,1,0:T(8,128)(2,1)}, bf16[2,256,256]{2,1,0:T(8,128)(2,1)S(1)}, u32[]{:S(2)}, u32[]{:S(2)}) collective-permute-start(bf16[2,256,256]{2,1,0:T(8,128)(2,1)} %get-tuple-element.114), channel_id=1, source_target_pairs={{0,27},{1,25},{2,31},{3,29},{4,8},{5,10},{6,12},{7,14},{8,0},{9,2}... | collective-permute-start | bytes 786440 | tf_op jit(solution)/shard_map/ppermute | solution.py:290
  156.3 28.0 %collective-permute-start.24 = (bf16[2,256,256]{2,1,0:T(8,128)(2,1)}, bf16[2,256,256]{2,1,0:T(8,128)(2,1)S(1)}, u32[]{:S(2)}, u32[]{:S(2)}) collective-permute-start(bf16[2,256,256]{2,1,0:T(8,128)(2,1)} %get-tuple-element.115), channel_id=1, source_target_pairs={{0,22},{1,20},{2,27},{3,25},{4,7},{5,5},{6,8},{7,10},{8,31},{9,29}... | collective-permute-start | bytes 786440 | tf_op jit(solution)/shard_map/ppermute | solution.py:290
  183.3 16.9 %collective-permute-start.28 = (bf16[2,256,256]{2,1,0:T(8,128)(2,1)}, bf16[2,256,256]{2,1,0:T(8,128)(2,1)}, u32[]{:S(2)}, u32[]{:S(2)}) collective-permute-start(bf16[2,256,256]{2,1,0:T(8,128)(2,1)} %get-tuple-element.127), channel_id=1, source_target_pairs={{0,4},{1,6},{2,9},{3,11},{4,21},{5,23},{6,26},{7,24},{8,13},{9,15}... | collective-permute-start | bytes 786440 | tf_op jit(solution)/shard_map/ppermute | solution.py:290
  216.1 24.9 %collective-permute-start.33 = (bf16[2,256,256]{2,1,0:T(8,128)(2,1)S(1)}, bf16[2,256,256]{2,1,0:T(8,128)(2,1)S(1)}, u32[]{:S(2)}, u32[]{:S(2)}) collective-permute-start(bf16[2,256,256]{2,1,0:T(8,128)(2,1)S(1)} %get-tuple-element.133), channel_id=1, source_target_pairs={{0,20},{1,21},{2,22},{3,23},{4,16},{5,17},{6,18},{7,19},{8,28},{9,... | collective-permute-start | bytes 786440 | tf_op jit(solution)/shard_map/ppermute | solution.py:290
  217.9 23.1 %collective-permute-start.34 = (bf16[2,256,256]{2,1,0:T(8,128)(2,1)S(1)}, bf16[2,256,256]{2,1,0:T(8,128)(2,1)S(1)}, u32[]{:S(2)}, u32[]{:S(2)}) collective-permute-start(bf16[2,256,256]{2,1,0:T(8,128)(2,1)S(1)} %get-tuple-element.134), channel_id=1, source_target_pairs={{0,24},{1,25},{2,26},{3,27},{4,28},{5,29},{6,30},{7,31},{8,0},{9,1... | collective-permute-start | bytes 786440 | tf_op jit(solution)/shard_map/ppermute | solution.py:290
  218.5 22.4 %collective-permute-start.35 = (bf16[2,256,256]{2,1,0:T(8,128)(2,1)S(1)}, bf16[2,256,256]{2,1,0:T(8,128)(2,1)S(1)}, u32[]{:S(2)}, u32[]{:S(2)}) collective-permute-start(bf16[2,256,256]{2,1,0:T(8,128)(2,1)S(1)} %get-tuple-element.135), channel_id=1, source_target_pairs={{0,28},{1,29},{2,30},{3,31},{4,24},{5,25},{6,26},{7,27},{8,4},{9,5... | collective-permute-start | bytes 786440 | tf_op jit(solution)/shard_map/ppermute | solution.py:290
  (28 other events, 430.7 us)
Sparse Core Ops, SparseCore 0:
  48.2 51.6 all-gather.2

commit v10 on v8

--- a/solution.py
+++ b/solution.py
@@ -376,17 +376,20 @@
             lax.dynamic_slice(cot, (((core + e + flip) % 2) * half_rows, 0), (half_rows, width)) for e in range(2)
         ]
         alpha = [move(x, route) for x, route in zip(halves, first_routes)]
-        own_c = move(cot, [(dev(m, c, s), dev(m, 1 - c, s)) for m, c, s in devices if c == s // half])
         normed = shift_tokens(normed)
-        alpha, own_c, prepared, normed = lax.optimization_barrier((alpha, own_c, prepared, normed))
+        alpha, prepared, normed = lax.optimization_barrier((alpha, prepared, normed))
         normed = lax.all_gather(normed[None], "particle", axis=0, tiled=True)
         w_pieces = [move(x, route) for x, route in zip(prepared, w_routes)]
         beta = [move(jnp.where(inner, a, x), route) for a, x, route in zip(alpha, halves, second_routes)]
         alpha_x = [move(x, swap_of(everyone)) for x in alpha]
-        whole, *w_pieces[:3] = lax.optimization_barrier((whole, *w_pieces[:3]))
+        whole, w_pieces[:3], beta = lax.optimization_barrier((whole, w_pieces[:3], beta))
         sums = add_over(pair_sums(whole), range(len(hops) - 2))
-        w_pieces, normed, sums = lax.optimization_barrier((w_pieces, normed, sums))
-        beta_x = [move(x, swap_of(everyone)) for x in beta]
+        beta_x = [move(beta[0], swap_of(everyone))]
+        w_pieces, normed, sums, cot, alpha_x, beta_x = lax.optimization_barrier(
+            (w_pieces, normed, sums, cot, alpha_x, beta_x)
+        )
+        own_c = move(cot, [(dev(m, c, s), dev(m, 1 - c, s)) for m, c, s in devices if c == s // half])
+        beta_x.append(move(beta[1], swap_of(everyone)))
         sources = [cot, own_c, *alpha, *alpha_x, *beta, *beta_x]
 
         def pick(ids, refs, held, sem):

time: 252 us -> 266 us (1.056)
  starting transfers between devices: 85.2 us -> 96.8 us
    ppermute x36, starting transfers between devices: 77.1 us -> 92.7 us  [move(): return lax.ppermute(x, AXES, pairs)]
    ppermute x36, waiting for transfers between devices: 76.8 us -> 88.1 us  [move(): return lax.ppermute(x, AXES, pairs)]
    all_to_all x1, waiting for transfers between devices: 9.72 us -> 0.01 us  [local(): whole = lax.all_to_all(slices, 'particle', 0, 0, tiled=True)]
    all_to_all x1, starting transfers between devices: 8.07 us -> 4.08 us  [local(): whole = lax.all_to_all(slices, 'particle', 0, 0, tiled=True)]
  transfers between devices with their start and end apart: 38 -> 38, of which waited for: 12 -> 15; matrix products, arithmetic and copies ran while one was open for 4% -> 4% of each run, Pallas kernels for 13% -> 7%
where the time goes in v10:
time: 266 us; the launch traced here: 265 us
  starting transfers between devices  96.8 us (36%)
  waiting for transfers between devices  88.2 us (33%)
  Pallas kernels  48.1 us (18%)
  between operations  15.2 us (6%)
  other arithmetic  8.75 us (3%)
  local copies, waits for them, and re-layouts  7.56 us (3%)
    ppermute x36, starting transfers between devices, move(): return lax.ppermute(x, AXES, pairs)  92.7 us
    ppermute x36, waiting for transfers between devices, move(): return lax.ppermute(x, AXES, pairs)  88.1 us
    pallas_call x1, Pallas kernels, local(): pl.pallas_call(functools.partial(grad_kernel, shards, particles, -width *...  13.9 us
    pallas_call x1, Pallas kernels, local(): pl.pallas_call(functools.partial(up_kernel, shards, width ** (-0.5)), gri...  10.4 us
    pallas_call x1, Pallas kernels, local(): pl.pallas_call(functools.partial(adam_kernel, particles), grid=(steps,),...  9.52 us
    pallas_call x1, Pallas kernels, local(): pl.pallas_call(functools.partial(prep_kernel, shards), grid=(steps,), out...  6.86 us
    pallas_call x1, Pallas kernels, local(): pl.pallas_call(functools.partial(stein_kernel, shards, particles), out_sh...  5.37 us
  transfers between devices with their start and end apart: 38, of which 15 were waited for; matrix products, arithmetic and copies ran while one was open for 4% of the time, Pallas kernels for 7%

profile of v10, /device:TPU:23, one launch (start us, length us, event | category | flops | bytes accessed | tf_op | source)
XLA Modules:
  0.0 264.6 jit_solution(3750927477808104791)
XLA Ops:
  20.6 6.9 %prep.1 = (bf16[2,256,512]{2,1,0:T(8,128)(2,1)}, bf16[2,256,512]{2,1,0:T(8,128)(2,1)}, bf16[2,256,512]{2,1,0:T(8,128)(2,1)}, bf16[2,256,512]{2,1,0:T(8,128)(2,1)}, bf16[8,2,256,256]{3,2,1,0:T(8,128)(2,1)}) custom-call(s32[5]{0:T(128)} %stack.36.ids, f32[8192,128]{1,0:T(8,128)} %bitcast.58), custom_call_target="tpu_custom_call" | custom-call | tf_op jit(solution)/shard_map/prep/pallas_call | solution.py:298
  31.6 5.6 %collective-permute-done.3 = bf16[64,1024]{1,0:T(8,128)(2,1)S(1)} collective-permute-done((bf16[64,1024]{1,0:T(8,128)(2,1)S(1)}, bf16[64,1024]{1,0:T(8,128)(2,1)S(1)}, u32[]{:S(2)}, u32[]{:S(2)}) %collective-permute-start.3) | collective-permute-done | bytes 131104 | tf_op jit(solution)/shard_map/ppermute | solution.py:273
  37.2 11.3 %collective-permute-done.2 = bf16[64,1024]{1,0:T(8,128)(2,1)S(1)} collective-permute-done((bf16[64,1024]{1,0:T(8,128)(2,1)S(1)}, bf16[64,1024]{1,0:T(8,128)(2,1)S(1)}, u32[]{:S(2)}, u32[]{:S(2)}) %collective-permute-start.2) | collective-permute-done | bytes 131104 | tf_op jit(solution)/shard_map/ppermute | solution.py:273
  64.8 4.2 %collective-permute-start.8 = (bf16[256,1024]{1,0:T(8,128)(2,1)S(1)}, bf16[256,1024]{1,0:T(8,128)(2,1)}, u32[]{:S(2)}, u32[]{:S(2)}) collective-permute-start(bf16[256,1024]{1,0:T(8,128)(2,1)S(1)} %broadcast_select_fusion.1), channel_id=1, source_target_pairs={{0,1},{1,0},{2,3},{5,4},{6,7},{7,6},{8,9},{9,8},{10,11},{13,12},{1... | collective-permute-start | bytes 1572872 | tf_op jit(solution)/shard_map/ppermute | solution.py:273
  71.9 11.5 %collective-permute-start.15 = (bf16[256,1024]{1,0:T(8,128)(2,1)}, bf16[256,1024]{1,0:T(8,128)(2,1)}, u32[]{:S(2)}, u32[]{:S(2)}) collective-permute-start(bf16[256,1024]{1,0:T(8,128)(2,1)} %copy-done.5), channel_id=1, source_target_pairs={{0,4},{1,5},{2,6},{3,7},{4,0},{5,1},{6,2},{7,3},{8,12},{9,13},{10,... | collective-permute-start | bytes 1572872 | tf_op jit(solution)/shard_map/ppermute | solution.py:273
  83.4 12.4 %collective-permute-start.10 = (bf16[2,256,512]{2,1,0:T(8,128)(2,1)}, bf16[2,256,512]{2,1,0:T(8,128)(2,1)}, u32[]{:S(2)}, u32[]{:S(2)}) collective-permute-start(bf16[2,256,512]{2,1,0:T(8,128)(2,1)} %get-tuple-element.88), channel_id=1, source_target_pairs={{0,4},{1,1},{2,5},{3,0},{4,6},{5,3},{6,7},{7,2},{8,12},{9,9},{10,1... | collective-permute-start | bytes 1572872 | tf_op jit(solution)/shard_map/ppermute | solution.py:273
  96.6 11.1 %collective-permute-done.8.refs_6_ = bf16[256,1024]{1,0:T(8,128)(2,1)} collective-permute-done((bf16[256,1024]{1,0:T(8,128)(2,1)S(1)}, bf16[256,1024]{1,0:T(8,128)(2,1)}, u32[]{:S(2)}, u32[]{:S(2)}) %collective-permute-start.8) | collective-permute-done | bytes 524320 | tf_op jit(solution)/shard_map/ppermute | solution.py:273
  107.7 5.2 %collective-permute-start.16 = (bf16[256,1024]{1,0:T(8,128)(2,1)}, bf16[256,1024]{1,0:T(8,128)(2,1)}, u32[]{:S(2)}, u32[]{:S(2)}) collective-permute-start(bf16[256,1024]{1,0:T(8,128)(2,1)} %collective-permute-done.8.refs_6_), channel_id=1, source_target_pairs={{0,4},{1,5},{2,6},{3,7},{4,0},{5,1},{6,2},{7,3},{8,12},{9,13},{10,... | collective-permute-start | bytes 1572872 | tf_op jit(solution)/shard_map/ppermute | solution.py:273
  121.3 4.4 %collective-permute-start.19 = (bf16[512,1024]{1,0:T(8,128)(2,1)S(1)}, bf16[512,1024]{1,0:T(8,128)(2,1)S(1)}, u32[]{:S(2)}, u32[]{:S(2)}) collective-permute-start(bf16[512,1024]{1,0:T(8,128)(2,1)S(1)} %bitcast.63), channel_id=1, source_target_pairs={{0,4},{1,5},{6,2},{7,3},{8,12},{9,13},{14,10},{15,11},{16,20},{17,... | collective-permute-start | bytes 3145736 | tf_op jit(solution)/shard_map/ppermute | solution.py:273
  128.2 10.4 %up.1 = (bf16[512,2048]{1,0:T(8,128)(2,1)}, bf16[512,2048]{1,0:T(8,128)(2,1)}, bf16[512,1024]{1,0:T(8,128)(2,1)}) custom-call(s32[5]{0:T(128)} %stack.36.ids, bf16[2048,1024]{1,0:T(8,128)(2,1)} %bitcast.60, bf16[2,256,512]{2,1,0:T(8,128)(2,1)} %copy-done.9, bf16[2,256,512]{2,1,0:T(8,128)(2,1)} %copy-done.10, bf16[2,256,512]{2,1,0:T(8,128)(2,1)} %copy-done.11, ...), custom_call_target="tpu_custom_call" | custom-call | tf_op jit(solution)/shard_map/up/pallas_call | solution.py:449
  143.2 13.9 %grads.1 = (bf16[2,256,256]{2,1,0:T(8,128)(2,1)}, bf16[2,256,256]{2,1,0:T(8,128)(2,1)}, bf16[2,256,256]{2,1,0:T(8,128)(2,1)}, bf16[2,256,256]{2,1,0:T(8,128)(2,1...) custom-call(s32[5]{0:T(128)} %stack.36.ids, ...), custom_call_target="tpu_custom_call" | custom-call | tf_op jit(solution)/shard_map/grads/pallas_call | solution.py:472
  157.1 4.2 %collective-permute-start.21 = (bf16[2,256,256]{2,1,0:T(8,128)(2,1)}, bf16[2,256,256]{2,1,0:T(8,128)(2,1)S(1)}, u32[]{:S(2)}, u32[]{:S(2)}) collective-permute-start(bf16[2,256,256]{2,1,0:T(8,128)(2,1)} %get-tuple-element.118), channel_id=1, source_target_pairs={{0,0},{1,2},{2,4},{3,6},{4,17},{5,19},{6,21},{7,23},{8,9},{9,11},{... | collective-permute-start | bytes 786440 | tf_op jit(solution)/shard_map/ppermute | solution.py:273
  161.3 5.0 %collective-permute-start.22 = (bf16[2,256,256]{2,1,0:T(8,128)(2,1)}, bf16[2,256,256]{2,1,0:T(8,128)(2,1)S(1)}, u32[]{:S(2)}, u32[]{:S(2)}) collective-permute-start(bf16[2,256,256]{2,1,0:T(8,128)(2,1)} %get-tuple-element.119), channel_id=1, source_target_pairs={{0,31},{1,29},{2,0},{3,2},{4,12},{5,14},{6,17},{7,19},{8,4},{9,6},... | collective-permute-start | bytes 786440 | tf_op jit(solution)/shard_map/ppermute | solution.py:273
  166.4 4.6 %collective-permute-start.24 = (bf16[2,256,256]{2,1,0:T(8,128)(2,1)}, bf16[2,256,256]{2,1,0:T(8,128)(2,1)S(1)}, u32[]{:S(2)}, u32[]{:S(2)}) collective-permute-start(bf16[2,256,256]{2,1,0:T(8,128)(2,1)} %get-tuple-element.121), channel_id=1, source_target_pairs={{0,22},{1,20},{2,27},{3,25},{4,7},{5,5},{6,8},{7,10},{8,31},{9,29}... | collective-permute-start | bytes 786440 | tf_op jit(solution)/shard_map/ppermute | solution.py:273
  173.9 14.2 %collective-permute-done.22.refs_1_ = bf16[2,256,256]{2,1,0:T(8,128)(2,1)S(1)} collective-permute-done((bf16[2,256,256]{2,1,0:T(8,128)(2,1)}, bf16[2,256,256]{2,1,0:T(8,128)(2,1)S(1)}, u32[]{:S(2)}, u32[]{:S(2)}) %collective-permute-start.22) | collective-permute-done | bytes 262176 | tf_op jit(solution)/shard_map/ppermute | solution.py:273
  191.4 8.0 %collective-permute-done.27.refs_6_ = bf16[2,256,256]{2,1,0:T(8,128)(2,1)} collective-permute-done((bf16[2,256,256]{2,1,0:T(8,128)(2,1)}, bf16[2,256,256]{2,1,0:T(8,128)(2,1)}, u32[]{:S(2)}, u32[]{:S(2)}) %collective-permute-start.27) | collective-permute-done | bytes 262176 | tf_op jit(solution)/shard_map/ppermute | solution.py:273
  199.4 10.1 %collective-permute-done.28.refs_7_ = bf16[2,256,256]{2,1,0:T(8,128)(2,1)} collective-permute-done((bf16[2,256,256]{2,1,0:T(8,128)(2,1)}, bf16[2,256,256]{2,1,0:T(8,128)(2,1)}, u32[]{:S(2)}, u32[]{:S(2)}) %collective-permute-start.28) | collective-permute-done | bytes 262176 | tf_op jit(solution)/shard_map/ppermute | solution.py:273
  209.6 5.4 %stein.1 = (bf16[2,256,256]{2,1,0:T(8,128)(2,1)S(1)}, bf16[2,256,256]{2,1,0:T(8,128)(2,1)S(1)}, bf16[2,256,256]{2,1,0:T(8,128)(2,1)S(1)}, bf16[2,256,256]{2,1,0:...) custom-call(s32[5]{0:T(128)S(1)} %copy-done.3, ...), custom_call_target="tpu_custom_call" | custom-call | tf_op jit(solution)/shard_map/stein/pallas_call | solution.py:532
  215.0 5.3 %collective-permute-start.30 = (bf16[2,256,256]{2,1,0:T(8,128)(2,1)S(1)}, bf16[2,256,256]{2,1,0:T(8,128)(2,1)S(1)}, u32[]{:S(2)}, u32[]{:S(2)}) collective-permute-start(bf16[2,256,256]{2,1,0:T(8,128)(2,1)S(1)} %get-tuple-element.136), channel_id=1, source_target_pairs={{0,8},{1,9},{2,10},{3,11},{4,12},{5,13},{6,14},{7,15},{8,16},{9,17... | collective-permute-start | bytes 786440 | tf_op jit(solution)/shard_map/ppermute | solution.py:273
  226.0 4.5 %collective-permute-start.35 = (bf16[2,256,256]{2,1,0:T(8,128)(2,1)S(1)}, bf16[2,256,256]{2,1,0:T(8,128)(2,1)S(1)}, u32[]{:S(2)}, u32[]{:S(2)}) collective-permute-start(bf16[2,256,256]{2,1,0:T(8,128)(2,1)S(1)} %get-tuple-element.141), channel_id=1, source_target_pairs={{0,28},{1,29},{2,30},{3,31},{4,24},{5,25},{6,26},{7,27},{8,4},{9,5... | collective-permute-start | bytes 786440 | tf_op jit(solution)/shard_map/ppermute | solution.py:273
  230.6 4.2 %broadcast_multiply_fusion = (f32[8192,128]{1,0:T(8,128)S(1)}, f32[8192,128]{1,0:T(8,128)S(1)}) fusion(f32[8192,128]{1,0:T(8,128)} %bitcast.64, f32[8192,128]{1,0:T(8,128)} %bitcast.65), kind=kLoop, calls=%fused_computation.2 | loop fusion | flops 2097152 | bytes 16777216 | tf_op jit(solution)/shard_map/mul | solution.py:516
  234.8 5.6 %collective-permute-done.32.refs_4_ = bf16[2,256,256]{2,1,0:T(8,128)(2,1)S(1)} collective-permute-done((bf16[2,256,256]{2,1,0:T(8,128)(2,1)S(1)}, bf16[2,256,256]{2,1,0:T(8,128)(2,1)S(1)}, u32[]{:S(2)}, u32[]{:S(2)}) %collective-permute-start.32) | collective-permute-done | bytes 262176 | tf_op jit(solution)/shard_map/ppermute | solution.py:273
  240.3 7.9 %collective-permute-done.33.refs_5_ = bf16[2,256,256]{2,1,0:T(8,128)(2,1)S(1)} collective-permute-done((bf16[2,256,256]{2,1,0:T(8,128)(2,1)S(1)}, bf16[2,256,256]{2,1,0:T(8,128)(2,1)S(1)}, u32[]{:S(2)}, u32[]{:S(2)}) %collective-permute-start.33) | collective-permute-done | bytes 262176 | tf_op jit(solution)/shard_map/ppermute | solution.py:273
  248.2 9.5 %adam.1 = (f32[8192,128]{1,0:T(8,128)}, f32[8192,128]{1,0:T(8,128)}, f32[8192,128]{1,0:T(8,128)}, f32[8192,128]{1,0:T(8,128)}) custom-call(s32[5]{0:T(128)S(1)} %copy-done.3, f32[8192,128]{1,0:T(8,128)S(1)} %bitcast.59, f32[8192,128]{1,0:T(8,128)S(1)} %get-tuple-element.153.first, f32[8192,128]{1,0:T(8,128)S(1)} %get-tuple-element.152.second, ...), custom_call_target="tpu_custom_call" | custom-call | tf_op jit(solution)/shard_map/adam/pallas_call | solution.py:556
  (115 shorter events, 64.1 us)
Async XLA Ops:
  7.2 114.1 %all-gather.3.cloned.1.call-start = ((), (), s32[]{:S(2)}) async-start(), calls=%async_computation.1 | async-start | bytes 4718592 | tf_op jit(solution)/shard_map/all_gather | solution.py:381
  9.7 39.6 %collective-permute-start.1 = (bf16[256,1024]{1,0:T(8,128)(2,1)}, bf16[256,1024]{1,0:T(8,128)(2,1)S(1)}, u32[]{:S(2)}, u32[]{:S(2)}) collective-permute-start(bf16[256,1024]{1,0:T(8,128)(2,1)} %get-tuple-element.148), channel_id=1, source_target_pairs={{1,4},{2,5},{3,1},{4,6},{5,2},{6,3},{9,12},{10,13},{11,9},{12,14},... | collective-permute-start | bytes 1572872 | tf_op jit(solution)/shard_map/ppermute | solution.py:273
  13.4 35.9 %collective-permute-start = (bf16[256,1024]{1,0:T(8,128)(2,1)}, bf16[256,1024]{1,0:T(8,128)(2,1)S(1)}, u32[]{:S(2)}, u32[]{:S(2)}) collective-permute-start(bf16[256,1024]{1,0:T(8,128)(2,1)} %get-tuple-element.149), channel_id=1, source_target_pairs={{1,0},{2,1},{3,5},{4,2},{5,6},{6,7},{9,8},{10,9},{11,13},{12,10},{... | collective-permute-start | bytes 1572872 | tf_op jit(solution)/shard_map/ppermute | solution.py:273
  18.7 18.5 %collective-permute-start.3 = (bf16[64,1024]{1,0:T(8,128)(2,1)S(1)}, bf16[64,1024]{1,0:T(8,128)(2,1)S(1)}, u32[]{:S(2)}, u32[]{:S(2)}) collective-permute-start(bf16[64,1024]{1,0:T(8,128)(2,1)S(1)} %fusion.1), channel_id=1, source_target_pairs={{0,2},{1,3},{2,0},{3,1},{4,6},{5,7},{6,4},{7,5},{8,10},{9,11},{10,... | collective-permute-start | bytes 393224 | tf_op jit(solution)/shard_map/ppermute | solution.py:273
  18.7 29.8 %collective-permute-start.2 = (bf16[64,1024]{1,0:T(8,128)(2,1)S(1)}, bf16[64,1024]{1,0:T(8,128)(2,1)S(1)}, u32[]{:S(2)}, u32[]{:S(2)}) collective-permute-start(bf16[64,1024]{1,0:T(8,128)(2,1)S(1)} %fusion.1), channel_id=1, source_target_pairs={{0,1},{1,2},{2,3},{3,0},{4,5},{5,6},{6,7},{7,4},{8,9},{9,10},{10,1... | collective-permute-start | bytes 393224 | tf_op jit(solution)/shard_map/ppermute | solution.py:273
  50.3 57.4 %all-to-all-start = ((bf16[8,2,256,256]{3,2,1,0:T(8,128)(2,1)}), bf16[8,2,256,256]{3,2,1,0:T(8,128)(2,1)S(1)}, u32[]{:S(2)}, u32[]{:S(2)}) async-start(bf16[8,2,256,256]{3,2,1,0:T(8,128)(2,1)} %get-tuple-element.75), calls=%async_computation | async-start | bytes 4194304 | tf_op jit(solution)/shard_map/all_to_all | solution.py:318
  54.4 17.5 %collective-permute-start.5 = (bf16[2,256,512]{2,1,0:T(8,128)(2,1)}, bf16[2,256,512]{2,1,0:T(8,128)(2,1)S(1)}, u32[]{:S(2)}, u32[]{:S(2)}) collective-permute-start(bf16[2,256,512]{2,1,0:T(8,128)(2,1)} %get-tuple-element.80), channel_id=1, source_target_pairs={{0,0},{1,4},{2,1},{3,5},{4,2},{5,6},{6,3},{7,7},{8,8},{9,12},{10,9... | collective-permute-start | bytes 1572872 | tf_op jit(solution)/shard_map/ppermute | solution.py:273
  58.0 25.4 %collective-permute-start.7 = (bf16[2,256,512]{2,1,0:T(8,128)(2,1)}, bf16[2,256,512]{2,1,0:T(8,128)(2,1)S(1)}, u32[]{:S(2)}, u32[]{:S(2)}) collective-permute-start(bf16[2,256,512]{2,1,0:T(8,128)(2,1)} %get-tuple-element.82), channel_id=1, source_target_pairs={{0,1},{1,5},{2,0},{3,4},{4,3},{5,7},{6,2},{7,6},{8,9},{9,13},{10,8... | collective-permute-start | bytes 1572872 | tf_op jit(solution)/shard_map/ppermute | solution.py:273
  63.5 32.3 %collective-permute-start.9 = (bf16[256,1024]{1,0:T(8,128)(2,1)S(1)}, bf16[256,1024]{1,0:T(8,128)(2,1)S(1)}, u32[]{:S(2)}, u32[]{:S(2)}) collective-permute-start(bf16[256,1024]{1,0:T(8,128)(2,1)S(1)} %broadcast_select_fusion), channel_id=1, source_target_pairs={{0,5},{1,0},{2,3},{5,4},{6,7},{7,2},{8,13},{9,8},{10,11},{13,12},{... | collective-permute-start | bytes 1572872 | tf_op jit(solution)/shard_map/ppermute | solution.py:273
  64.8 42.9 %collective-permute-start.8 = (bf16[256,1024]{1,0:T(8,128)(2,1)S(1)}, bf16[256,1024]{1,0:T(8,128)(2,1)}, u32[]{:S(2)}, u32[]{:S(2)}) collective-permute-start(bf16[256,1024]{1,0:T(8,128)(2,1)S(1)} %broadcast_select_fusion.1), channel_id=1, source_target_pairs={{0,1},{1,0},{2,3},{5,4},{6,7},{7,6},{8,9},{9,8},{10,11},{13,12},{1... | collective-permute-start | bytes 1572872 | tf_op jit(solution)/shard_map/ppermute | solution.py:273
  71.9 49.3 %collective-permute-start.14 = (bf16[256,1024]{1,0:T(8,128)(2,1)}, bf16[256,1024]{1,0:T(8,128)(2,1)}, u32[]{:S(2)}, u32[]{:S(2)}) collective-permute-start(bf16[256,1024]{1,0:T(8,128)(2,1)} %copy-done.6), channel_id=1, source_target_pairs={{0,4},{1,5},{2,6},{3,7},{4,0},{5,1},{6,2},{7,3},{8,12},{9,13},{10,... | collective-permute-start | bytes 1572872 | tf_op jit(solution)/shard_map/ppermute | solution.py:273
  71.9 49.3 %collective-permute-start.15 = (bf16[256,1024]{1,0:T(8,128)(2,1)}, bf16[256,1024]{1,0:T(8,128)(2,1)}, u32[]{:S(2)}, u32[]{:S(2)}) collective-permute-start(bf16[256,1024]{1,0:T(8,128)(2,1)} %copy-done.5), channel_id=1, source_target_pairs={{0,4},{1,5},{2,6},{3,7},{4,0},{5,1},{6,2},{7,3},{8,12},{9,13},{10,... | collective-permute-start | bytes 1572872 | tf_op jit(solution)/shard_map/ppermute | solution.py:273
  83.4 37.8 %collective-permute-start.10 = (bf16[2,256,512]{2,1,0:T(8,128)(2,1)}, bf16[2,256,512]{2,1,0:T(8,128)(2,1)}, u32[]{:S(2)}, u32[]{:S(2)}) collective-permute-start(bf16[2,256,512]{2,1,0:T(8,128)(2,1)} %get-tuple-element.88), channel_id=1, source_target_pairs={{0,4},{1,1},{2,5},{3,0},{4,6},{5,3},{6,7},{7,2},{8,12},{9,9},{10,1... | collective-permute-start | bytes 1572872 | tf_op jit(solution)/shard_map/ppermute | solution.py:273
  121.3 20.8 %collective-permute-start.19 = (bf16[512,1024]{1,0:T(8,128)(2,1)S(1)}, bf16[512,1024]{1,0:T(8,128)(2,1)S(1)}, u32[]{:S(2)}, u32[]{:S(2)}) collective-permute-start(bf16[512,1024]{1,0:T(8,128)(2,1)S(1)} %bitcast.63), channel_id=1, source_target_pairs={{0,4},{1,5},{6,2},{7,3},{8,12},{9,13},{14,10},{15,11},{16,20},{17,... | collective-permute-start | bytes 3145736 | tf_op jit(solution)/shard_map/ppermute | solution.py:273
  161.3 26.8 %collective-permute-start.22 = (bf16[2,256,256]{2,1,0:T(8,128)(2,1)}, bf16[2,256,256]{2,1,0:T(8,128)(2,1)S(1)}, u32[]{:S(2)}, u32[]{:S(2)}) collective-permute-start(bf16[2,256,256]{2,1,0:T(8,128)(2,1)} %get-tuple-element.119), channel_id=1, source_target_pairs={{0,31},{1,29},{2,0},{3,2},{4,12},{5,14},{6,17},{7,19},{8,4},{9,6},... | collective-permute-start | bytes 786440 | tf_op jit(solution)/shard_map/ppermute | solution.py:273
  166.3 21.8 %collective-permute-start.23 = (bf16[2,256,256]{2,1,0:T(8,128)(2,1)}, bf16[2,256,256]{2,1,0:T(8,128)(2,1)S(1)}, u32[]{:S(2)}, u32[]{:S(2)}) collective-permute-start(bf16[2,256,256]{2,1,0:T(8,128)(2,1)} %get-tuple-element.120), channel_id=1, source_target_pairs={{0,27},{1,25},{2,31},{3,29},{4,8},{5,10},{6,12},{7,14},{8,0},{9,2}... | collective-permute-start | bytes 786440 | tf_op jit(solution)/shard_map/ppermute | solution.py:273
  166.4 23.8 %collective-permute-start.24 = (bf16[2,256,256]{2,1,0:T(8,128)(2,1)}, bf16[2,256,256]{2,1,0:T(8,128)(2,1)S(1)}, u32[]{:S(2)}, u32[]{:S(2)}) collective-permute-start(bf16[2,256,256]{2,1,0:T(8,128)(2,1)} %get-tuple-element.121), channel_id=1, source_target_pairs={{0,22},{1,20},{2,27},{3,25},{4,7},{5,5},{6,8},{7,10},{8,31},{9,29}... | collective-permute-start | bytes 786440 | tf_op jit(solution)/shard_map/ppermute | solution.py:273
  171.0 19.2 %collective-permute-start.25 = (bf16[2,256,256]{2,1,0:T(8,128)(2,1)}, bf16[2,256,256]{2,1,0:T(8,128)(2,1)S(1)}, u32[]{:S(2)}, u32[]{:S(2)}) collective-permute-start(bf16[2,256,256]{2,1,0:T(8,128)(2,1)} %get-tuple-element.122), channel_id=1, source_target_pairs={{0,18},{1,16},{2,22},{3,20},{4,3},{5,1},{6,7},{7,5},{8,27},{9,25},... | collective-permute-start | bytes 786440 | tf_op jit(solution)/shard_map/ppermute | solution.py:273
  173.3 18.1 %collective-permute-start.26 = (bf16[2,256,256]{2,1,0:T(8,128)(2,1)}, bf16[2,256,256]{2,1,0:T(8,128)(2,1)}, u32[]{:S(2)}, u32[]{:S(2)}) collective-permute-start(bf16[2,256,256]{2,1,0:T(8,128)(2,1)} %get-tuple-element.131), channel_id=1, source_target_pairs={{0,13},{1,15},{2,18},{3,16},{4,30},{5,28},{6,3},{7,1},{8,22},{9,20... | collective-permute-start | bytes 786440 | tf_op jit(solution)/shard_map/ppermute | solution.py:273
  188.1 21.5 %collective-permute-start.28 = (bf16[2,256,256]{2,1,0:T(8,128)(2,1)}, bf16[2,256,256]{2,1,0:T(8,128)(2,1)}, u32[]{:S(2)}, u32[]{:S(2)}) collective-permute-start(bf16[2,256,256]{2,1,0:T(8,128)(2,1)} %get-tuple-element.133), channel_id=1, source_target_pairs={{0,4},{1,6},{2,9},{3,11},{4,21},{5,23},{6,26},{7,24},{8,13},{9,15}... | collective-permute-start | bytes 786440 | tf_op jit(solution)/shard_map/ppermute | solution.py:273
  223.3 17.0 %collective-permute-start.32 = (bf16[2,256,256]{2,1,0:T(8,128)(2,1)S(1)}, bf16[2,256,256]{2,1,0:T(8,128)(2,1)S(1)}, u32[]{:S(2)}, u32[]{:S(2)}) collective-permute-start(bf16[2,256,256]{2,1,0:T(8,128)(2,1)S(1)} %get-tuple-element.138), channel_id=1, source_target_pairs={{0,16},{1,17},{2,18},{3,19},{4,20},{5,21},{6,22},{7,23},{8,24},{9,... | collective-permute-start | bytes 786440 | tf_op jit(solution)/shard_map/ppermute | solution.py:273
  223.3 24.9 %collective-permute-start.33 = (bf16[2,256,256]{2,1,0:T(8,128)(2,1)S(1)}, bf16[2,256,256]{2,1,0:T(8,128)(2,1)S(1)}, u32[]{:S(2)}, u32[]{:S(2)}) collective-permute-start(bf16[2,256,256]{2,1,0:T(8,128)(2,1)S(1)} %get-tuple-element.139), channel_id=1, source_target_pairs={{0,20},{1,21},{2,22},{3,23},{4,16},{5,17},{6,18},{7,19},{8,28},{9,... | collective-permute-start | bytes 786440 | tf_op jit(solution)/shard_map/ppermute | solution.py:273
  225.1 23.1 %collective-permute-start.34 = (bf16[2,256,256]{2,1,0:T(8,128)(2,1)S(1)}, bf16[2,256,256]{2,1,0:T(8,128)(2,1)S(1)}, u32[]{:S(2)}, u32[]{:S(2)}) collective-permute-start(bf16[2,256,256]{2,1,0:T(8,128)(2,1)S(1)} %get-tuple-element.140), channel_id=1, source_target_pairs={{0,24},{1,25},{2,26},{3,27},{4,28},{5,29},{6,30},{7,31},{8,0},{9,1... | collective-permute-start | bytes 786440 | tf_op jit(solution)/shard_map/ppermute | solution.py:273
  226.0 22.2 %collective-permute-start.35 = (bf16[2,256,256]{2,1,0:T(8,128)(2,1)S(1)}, bf16[2,256,256]{2,1,0:T(8,128)(2,1)S(1)}, u32[]{:S(2)}, u32[]{:S(2)}) collective-permute-start(bf16[2,256,256]{2,1,0:T(8,128)(2,1)S(1)} %get-tuple-element.141), channel_id=1, source_target_pairs={{0,28},{1,29},{2,30},{3,31},{4,24},{5,25},{6,26},{7,27},{8,4},{9,5... | collective-permute-start | bytes 786440 | tf_op jit(solution)/shard_map/ppermute | solution.py:273
  (28 other events, 404.4 us)
Sparse Core Ops, SparseCore 0:
  49.5 48.6 all-gather.2

commit v11 on v8

--- a/solution.py
+++ b/solution.py
@@ -41,6 +41,34 @@
     return 2 * lax.rem(column - shard + columns * 16, columns) + core
 
 
+def sent_piece(shards, ids, r):
+    if shards != 4:
+        return lax.rem(ids[SHARD] - r + shards, shards)
+    side = lax.rem(ids[SHARD], 2)
+    if r < 2:
+        return 2 * (1 - side) + r
+    away = lax.rem(ids[PROC] + ids[CORE], 2)
+    return 2 * side + lax.rem(r + 1 - away, 2)
+
+
+def place_pieces(shards, ids, pieces, store):
+    if shards != 4:
+        for r in range(shards):
+            store(pieces[r], lax.rem(ids[PIECE] + r, shards))
+        return
+    s = ids[SHARD]
+    beside = s + 1 - 2 * lax.rem(s, 2)
+    across = lax.rem(s + 2, 4)
+    for e in range(2):
+
+        @pl.when(ids[CORE] == e)
+        def _():
+            store(pieces[e], beside)
+            store(pieces[2 + e], 3 - s)
+            store(pieces[4 + e], across)
+            store(pieces[5 - e], s)
+
+
 def prep_kernel(shards, ids, w, *out):
     pieces, slices = out[:shards], out[shards]
     _, rows, piece = pieces[0].shape
@@ -48,7 +76,7 @@
     columns = particles // 2
     tiles, per_slice = piece // LANES, cols // LANES
     for r in range(shards):
-        q = lax.rem(ids[SHARD] - r + shards, shards)
+        q = sent_piece(shards, ids, r)
         for j in range(tiles):
             e = q * (tiles // per_slice) + j // per_slice
             column = lax.rem(lax.div(e, 2) + ids[SHARD], columns)
@@ -62,17 +90,19 @@
 
 
 def up_kernel(shards, scale, ids, tokens, *refs):
-    pieces = refs[:shards]
-    act_t, slope_t, down_t, up_w, down_w, up_t = refs[shards:]
+    pieces = refs[:-6]
+    act_t, slope_t, down_t, up_w, down_w, up_t = refs[-6:]
     width, part = up_w.shape
     rows = width // shards
 
     @pl.when(pl.program_id(0) == 0)
     def _():
-        for r in range(shards):
-            at = pl.multiple_of(lax.rem(ids[PIECE] + r, shards) * rows, rows)
-            up_w[pl.ds(at, rows), :] = pieces[r][0]
-            down_w[pl.ds(at, rows), :] = pieces[r][1]
+        def store(piece, shard):
+            at = pl.multiple_of(shard * rows, rows)
+            up_w[pl.ds(at, rows), :] = piece[0]
+            down_w[pl.ds(at, rows), :] = piece[1]
+
+        place_pieces(shards, ids, pieces, store)
         for i in range(width // LANES):
             span = slice(i * LANES, (i + 1) * LANES)
             up_t[:, span] = up_w[span, :].astype(F32).T.astype(BF)
@@ -308,12 +338,24 @@
     )(ids, w_flat)
 
     w_routes = []
-    for r in range(shards):
-        pairs = []
-        for m, c, s in devices:
-            q = (s - r) % shards
-            pairs.append((dev(m, c, s), dev(m, q % 2, c * half + q // 2)))
-        w_routes.append(pairs)
+    if shards == 4:
+        for own, far_by in ((True, 1), (False, 3), (None, 2)):
+            for e in range(2):
+                pairs = []
+                for m, c, s in devices:
+                    at_home = c == s // half
+                    if own is None and at_home:
+                        pairs.append((dev(m, c, s), dev(m, 1 - e, s)))
+                    elif own is None or own == at_home:
+                        pairs.append((dev(m, c, s), dev(m, e, s ^ far_by)))
+                w_routes.append(pairs)
+    else:
+        for r in range(shards):
+            pairs = []
+            for m, c, s in devices:
+                q = (s - r) % shards
+                pairs.append((dev(m, c, s), dev(m, q % 2, c * half + q // 2)))
+            w_routes.append(pairs)
 
     whole = lax.all_to_all(slices, "particle", 0, 0, tiled=True)
 
@@ -378,12 +420,13 @@
         alpha = [move(x, route) for x, route in zip(halves, first_routes)]
         own_c = move(cot, [(dev(m, c, s), dev(m, 1 - c, s)) for m, c, s in devices if c == s // half])
         normed = shift_tokens(normed)
-        alpha, own_c, prepared, normed = lax.optimization_barrier((alpha, own_c, prepared, normed))
+        w_pieces = [move(x, route) for x, route in zip(prepared[:2], w_routes[:2])]
+        alpha, own_c, prepared, normed, w_pieces = lax.optimization_barrier((alpha, own_c, prepared, normed, w_pieces))
         normed = lax.all_gather(normed[None], "particle", axis=0, tiled=True)
-        w_pieces = [move(x, route) for x, route in zip(prepared, w_routes)]
+        w_pieces = w_pieces + [move(x, route) for x, route in zip(prepared, w_routes[2:])]
         beta = [move(jnp.where(inner, a, x), route) for a, x, route in zip(alpha, halves, second_routes)]
         alpha_x = [move(x, swap_of(everyone)) for x in alpha]
-        whole, *w_pieces[:3] = lax.optimization_barrier((whole, *w_pieces[:3]))
+        whole, w_pieces[2:5] = lax.optimization_barrier((whole, w_pieces[2:5]))
         sums = add_over(pair_sums(whole), range(len(hops) - 2))
         w_pieces, normed, sums = lax.optimization_barrier((w_pieces, normed, sums))
         beta_x = [move(x, swap_of(everyone)) for x in beta]
@@ -452,7 +495,7 @@
             jax.ShapeDtypeStruct((part, width), BF),
         ],
         in_specs=[smem_spec(), pl.BlockSpec((BLOCK, width), lambda i: (i, 0))]
-        + [pl.BlockSpec((2, rows, part), lambda i: (0, 0, 0))] * shards,
+        + [pl.BlockSpec((2, rows, part), lambda i: (0, 0, 0))] * len(w_pieces),
         out_specs=[
             pl.BlockSpec((part, BLOCK), lambda i: (0, i)),
             pl.BlockSpec((part, BLOCK), lambda i: (0, i)),

time: 252 us -> 245 us (0.972)
  waiting for transfers between devices: 86.6 us -> 81.8 us
    all_to_all x1, waiting for transfers between devices: 9.72 us -> 0.01 us  [local(): whole = lax.all_to_all(slices, 'particle', 0, 0, tiled=True)]
    ppermute x36 -> x38, waiting for transfers between devices: 76.8 us -> 81.8 us  [move(): return lax.ppermute(x, AXES, pairs)]
    all_to_all x1, starting transfers between devices: 8.07 us -> 3.95 us  [local(): whole = lax.all_to_all(slices, 'particle', 0, 0, tiled=True)]
    ppermute x36 -> x38, starting transfers between devices: 77.1 us -> 79.1 us  [move(): return lax.ppermute(x, AXES, pairs)]
  transfers between devices with their start and end apart: 38 -> 40, of which waited for: 12 -> 10; matrix products, arithmetic and copies ran while one was open for 4% -> 5% of each run, Pallas kernels for 13% -> 14%
where the time goes in v11:
time: 245 us; the launch traced here: 241 us
  starting transfers between devices  83.1 us (34%)
  waiting for transfers between devices  81.8 us (33%)
  Pallas kernels  48.3 us (20%)
  between operations  15.2 us (6%)
  other arithmetic  8.32 us (3%)
  local copies, waits for them, and re-layouts  4.4 us (2%)
    ppermute x38, waiting for transfers between devices, move(): return lax.ppermute(x, AXES, pairs)  81.8 us
    ppermute x38, starting transfers between devices, move(): return lax.ppermute(x, AXES, pairs)  79.1 us
    pallas_call x1, Pallas kernels, local(): pl.pallas_call(functools.partial(grad_kernel, shards, particles, -width *...  13.7 us
    pallas_call x1, Pallas kernels, local(): pl.pallas_call(functools.partial(up_kernel, shards, width ** (-0.5)), gri...  10.7 us
    pallas_call x1, Pallas kernels, local(): pl.pallas_call(functools.partial(adam_kernel, particles), grid=(steps,),...  9.52 us
    pallas_call x1, Pallas kernels, local(): pl.pallas_call(functools.partial(prep_kernel, shards), grid=(steps,), out...  6.9 us
    pallas_call x1, Pallas kernels, local(): pl.pallas_call(functools.partial(stein_kernel, shards, particles), out_sh...  5.37 us
  transfers between devices with their start and end apart: 40, of which 10 were waited for; matrix products, arithmetic and copies ran while one was open for 5% of the time, Pallas kernels for 14%

profile of v11, /device:TPU:23, one launch (start us, length us, event | category | flops | bytes accessed | tf_op | source)
XLA Modules:
  0.0 241.1 jit_solution(1207215194726019743)
XLA Ops:
  7.2 3.7 %collective-permute-start.2 = (bf16[512,1024]{1,0:T(8,128)(2,1)}, bf16[512,1024]{1,0:T(8,128)(2,1)}, u32[]{:S(2)}, u32[]{:S(2)}) collective-permute-start(bf16[512,1024]{1,0:T(8,128)(2,1)} %bitcast.62), channel_id=1, source_target_pairs={{0,4},{1,5},{6,2},{7,3},{8,12},{9,13},{14,10},{15,11},{16,20},{17,... | collective-permute-start | bytes 3145736 | tf_op jit(solution)/shard_map/ppermute | solution.py:303
  12.8 3.4 %collective-permute-start.4 = (bf16[64,1024]{1,0:T(8,128)(2,1)S(1)}, bf16[64,1024]{1,0:T(8,128)(2,1)S(1)}, u32[]{:S(2)}, u32[]{:S(2)}) collective-permute-start(bf16[64,1024]{1,0:T(8,128)(2,1)S(1)} %fusion.1), channel_id=1, source_target_pairs={{0,2},{1,3},{2,0},{3,1},{4,6},{5,7},{6,4},{7,5},{8,10},{9,11},{10,... | collective-permute-start | bytes 393224 | tf_op jit(solution)/shard_map/ppermute | solution.py:303
  20.9 6.9 %prep.1 = (bf16[2,256,512]{2,1,0:T(8,128)(2,1)}, bf16[2,256,512]{2,1,0:T(8,128)(2,1)}, bf16[2,256,512]{2,1,0:T(8,128)(2,1)}, bf16[2,256,512]{2,1,0:T(8,128)(2,1)}, bf16[8,2,256,256]{3,2,1,0:T(8,128)(2,1)}) custom-call(s32[5]{0:T(128)} %stack.36.ids, f32[8192,128]{1,0:T(8,128)} %bitcast.58), custom_call_target="tpu_custom_call" | custom-call | tf_op jit(solution)/shard_map/prep/pallas_call | solution.py:328
  30.0 3.7 %collective-permute-start.6 = (bf16[2,256,512]{2,1,0:T(8,128)(2,1)}, bf16[2,256,512]{2,1,0:T(8,128)(2,1)S(1)}, u32[]{:S(2)}, u32[]{:S(2)}) collective-permute-start(bf16[2,256,512]{2,1,0:T(8,128)(2,1)} %get-tuple-element.81), channel_id=1, source_target_pairs={{0,1},{1,0},{6,3},{7,2},{8,9},{9,8},{14,11},{15,10},{16,17},{17,16... | collective-permute-start | bytes 1572872 | tf_op jit(solution)/shard_map/ppermute | solution.py:303
  33.7 3.8 %collective-permute-start.7 = (bf16[2,256,512]{2,1,0:T(8,128)(2,1)}, bf16[2,256,512]{2,1,0:T(8,128)(2,1)}, u32[]{:S(2)}, u32[]{:S(2)}) collective-permute-start(bf16[2,256,512]{2,1,0:T(8,128)(2,1)} %get-tuple-element.82), channel_id=1, source_target_pairs={{0,5},{1,4},{6,7},{7,6},{8,13},{9,12},{14,15},{15,14},{16,21},{17,... | collective-permute-start | bytes 1572872 | tf_op jit(solution)/shard_map/ppermute | solution.py:303
  38.6 10.7 %collective-permute-done.refs_2_ = bf16[256,1024]{1,0:T(8,128)(2,1)S(1)} collective-permute-done((bf16[256,1024]{1,0:T(8,128)(2,1)S(1)}, bf16[256,1024]{1,0:T(8,128)(2,1)S(1)}, u32[]{:S(2)}, u32[]{:S(2)}) %collective-permute-start) | collective-permute-done | bytes 524320 | tf_op jit(solution)/shard_map/ppermute | solution.py:303
  50.1 4.0 %all-to-all-start = ((bf16[8,2,256,256]{3,2,1,0:T(8,128)(2,1)}), bf16[8,2,256,256]{3,2,1,0:T(8,128)(2,1)S(1)}, u32[]{:S(2)}, u32[]{:S(2)}) async-start(bf16[8,2,256,256]{3,2,1,0:T(8,128)(2,1)} %get-tuple-element.80), calls=%async_computation | async-start | bytes 4194304 | tf_op jit(solution)/shard_map/all_to_all | solution.py:360
  56.0 5.4 %collective-permute-start.10 = (bf16[2,256,512]{2,1,0:T(8,128)(2,1)}, bf16[2,256,512]{2,1,0:T(8,128)(2,1)}, u32[]{:S(2)}, u32[]{:S(2)}) collective-permute-start(bf16[2,256,512]{2,1,0:T(8,128)(2,1)} %get-tuple-element.83), channel_id=1, source_target_pairs={{0,4},{1,5},{2,0},{3,1},{4,2},{5,3},{6,6},{7,7},{8,12},{9,13},{10,... | collective-permute-start | bytes 1572872 | tf_op jit(solution)/shard_map/ppermute | solution.py:303
  66.5 3.4 %collective-permute-start.19 = (bf16[256,1024]{1,0:T(8,128)(2,1)}, bf16[256,1024]{1,0:T(8,128)(2,1)}, u32[]{:S(2)}, u32[]{:S(2)}) collective-permute-start(bf16[256,1024]{1,0:T(8,128)(2,1)} %broadcast_select_fusion.1), channel_id=1, source_target_pairs={{0,1},{1,0},{2,3},{5,4},{6,7},{7,6},{8,9},{9,8},{10,11},{13,12},{1... | collective-permute-start | bytes 1572872 | tf_op jit(solution)/shard_map/ppermute | solution.py:303
  69.9 17.3 %collective-permute-done.9.refs_3_ = bf16[2,256,512]{2,1,0:T(8,128)(2,1)S(1)} collective-permute-done((bf16[2,256,512]{2,1,0:T(8,128)(2,1)}, bf16[2,256,512]{2,1,0:T(8,128)(2,1)S(1)}, u32[]{:S(2)}, u32[]{:S(2)}) %collective-permute-start.9) | collective-permute-done | bytes 524320 | tf_op jit(solution)/shard_map/ppermute | solution.py:303
  90.1 4.8 %collective-permute-start.12 = (f32[8,128]{1,0:T(8,128)S(1)}, f32[8,128]{1,0:T(8,128)S(1)}, u32[]{:S(2)}, u32[]{:S(2)}) collective-permute-start(f32[8,128]{1,0:T(8,128)S(1)} %distances.1), channel_id=1, source_target_pairs={{0,4},{1,5},{2,6},{3,7},{4,0},{5,1},{6,2},{7,3},{8,12},{9,13},{10,... | collective-permute-start | bytes 12296 | tf_op jit(solution)/shard_map/ppermute | solution.py:303
  99.8 5.0 %collective-permute-start.17 = (bf16[256,1024]{1,0:T(8,128)(2,1)S(1)}, bf16[256,1024]{1,0:T(8,128)(2,1)}, u32[]{:S(2)}, u32[]{:S(2)}) collective-permute-start(bf16[256,1024]{1,0:T(8,128)(2,1)S(1)} %collective-permute-done.refs_2_), channel_id=1, source_target_pairs={{0,4},{1,5},{2,6},{3,7},{4,0},{5,1},{6,2},{7,3},{8,12},{9,13},{10,... | collective-permute-start | bytes 1572872 | tf_op jit(solution)/shard_map/ppermute | solution.py:303
  107.8 5.7 %collective-permute-start.15 = (f32[8,128]{1,0:T(8,128)S(1)}, f32[8,128]{1,0:T(8,128)S(1)}, u32[]{:S(2)}, u32[]{:S(2)}) collective-permute-start(f32[8,128]{1,0:T(8,128)S(1)} %add.93), channel_id=1, source_target_pairs={{0,1},{1,0},{2,3},{3,2},{4,5},{5,4},{6,7},{7,6},{8,9},{9,8},{10,11... | collective-permute-start | bytes 12296 | tf_op jit(solution)/shard_map/ppermute | solution.py:303
  113.5 10.7 %up.1 = (bf16[512,2048]{1,0:T(8,128)(2,1)}, bf16[512,2048]{1,0:T(8,128)(2,1)}, bf16[512,1024]{1,0:T(8,128)(2,1)}) custom-call(s32[5]{0:T(128)} %stack.36.ids, bf16[2048,1024]{1,0:T(8,128)(2,1)} %bitcast.60, bf16[2,256,512]{2,1,0:T(8,128)(2,1)} %copy-done.8, bf16[2,256,512]{2,1,0:T(8,128)(2,1)} %collective-permute-done.7.refs_1_, ...), custom_call_target="tpu_custom_call" | custom-call | tf_op jit(solution)/shard_map/up/pallas_call | solution.py:489
  124.3 13.7 %grads.1 = (bf16[2,256,256]{2,1,0:T(8,128)(2,1)}, bf16[2,256,256]{2,1,0:T(8,128)(2,1)}, bf16[2,256,256]{2,1,0:T(8,128)(2,1)}, bf16[2,256,256]{2,1,0:T(8,128)(2,1...) custom-call(s32[5]{0:T(128)} %stack.36.ids, ...), custom_call_target="tpu_custom_call" | custom-call | tf_op jit(solution)/shard_map/grads/pallas_call | solution.py:512
  138.1 4.2 %collective-permute-start.23 = (bf16[2,256,256]{2,1,0:T(8,128)(2,1)}, bf16[2,256,256]{2,1,0:T(8,128)(2,1)S(1)}, u32[]{:S(2)}, u32[]{:S(2)}) collective-permute-start(bf16[2,256,256]{2,1,0:T(8,128)(2,1)} %get-tuple-element.116), channel_id=1, source_target_pairs={{0,0},{1,2},{2,4},{3,6},{4,17},{5,19},{6,21},{7,23},{8,9},{9,11},{... | collective-permute-start | bytes 786440 | tf_op jit(solution)/shard_map/ppermute | solution.py:303
  152.8 15.8 %collective-permute-done.24.refs_1_ = bf16[2,256,256]{2,1,0:T(8,128)(2,1)S(1)} collective-permute-done((bf16[2,256,256]{2,1,0:T(8,128)(2,1)}, bf16[2,256,256]{2,1,0:T(8,128)(2,1)S(1)}, u32[]{:S(2)}, u32[]{:S(2)}) %collective-permute-start.24) | collective-permute-done | bytes 262176 | tf_op jit(solution)/shard_map/ppermute | solution.py:303
  169.9 9.1 %collective-permute-done.29.refs_6_ = bf16[2,256,256]{2,1,0:T(8,128)(2,1)} collective-permute-done((bf16[2,256,256]{2,1,0:T(8,128)(2,1)}, bf16[2,256,256]{2,1,0:T(8,128)(2,1)}, u32[]{:S(2)}, u32[]{:S(2)}) %collective-permute-start.29) | collective-permute-done | bytes 262176 | tf_op jit(solution)/shard_map/ppermute | solution.py:303
  179.0 10.0 %collective-permute-done.30.refs_7_ = bf16[2,256,256]{2,1,0:T(8,128)(2,1)} collective-permute-done((bf16[2,256,256]{2,1,0:T(8,128)(2,1)}, bf16[2,256,256]{2,1,0:T(8,128)(2,1)}, u32[]{:S(2)}, u32[]{:S(2)}) %collective-permute-start.30) | collective-permute-done | bytes 262176 | tf_op jit(solution)/shard_map/ppermute | solution.py:303
  189.1 5.4 %stein.1 = (bf16[2,256,256]{2,1,0:T(8,128)(2,1)S(1)}, bf16[2,256,256]{2,1,0:T(8,128)(2,1)S(1)}, bf16[2,256,256]{2,1,0:T(8,128)(2,1)S(1)}, bf16[2,256,256]{2,1,0:...) custom-call(s32[5]{0:T(128)S(1)} %copy-done.3, ...), custom_call_target="tpu_custom_call" | custom-call | tf_op jit(solution)/shard_map/stein/pallas_call | solution.py:572
  194.8 4.0 %collective-permute-start.32 = (bf16[2,256,256]{2,1,0:T(8,128)(2,1)S(1)}, bf16[2,256,256]{2,1,0:T(8,128)(2,1)S(1)}, u32[]{:S(2)}, u32[]{:S(2)}) collective-permute-start(bf16[2,256,256]{2,1,0:T(8,128)(2,1)S(1)} %get-tuple-element.134), channel_id=1, source_target_pairs={{0,8},{1,9},{2,10},{3,11},{4,12},{5,13},{6,14},{7,15},{8,16},{9,17... | collective-permute-start | bytes 786440 | tf_op jit(solution)/shard_map/ppermute | solution.py:303
  207.1 4.2 %broadcast_multiply_fusion = (f32[8192,128]{1,0:T(8,128)S(1)}, f32[8192,128]{1,0:T(8,128)S(1)}) fusion(f32[8192,128]{1,0:T(8,128)} %bitcast.64, f32[8192,128]{1,0:T(8,128)} %bitcast.65), kind=kLoop, calls=%fused_computation.2 | loop fusion | flops 2097152 | bytes 16777216 | tf_op jit(solution)/shard_map/mul | solution.py:556
  211.3 13.4 %collective-permute-done.35.refs_5_ = bf16[2,256,256]{2,1,0:T(8,128)(2,1)S(1)} collective-permute-done((bf16[2,256,256]{2,1,0:T(8,128)(2,1)S(1)}, bf16[2,256,256]{2,1,0:T(8,128)(2,1)S(1)}, u32[]{:S(2)}, u32[]{:S(2)}) %collective-permute-start.35) | collective-permute-done | bytes 262176 | tf_op jit(solution)/shard_map/ppermute | solution.py:303
  224.7 9.5 %adam.1 = (f32[8192,128]{1,0:T(8,128)}, f32[8192,128]{1,0:T(8,128)}, f32[8192,128]{1,0:T(8,128)}, f32[8192,128]{1,0:T(8,128)}) custom-call(s32[5]{0:T(128)S(1)} %copy-done.3, f32[8192,128]{1,0:T(8,128)S(1)} %bitcast.59, f32[8192,128]{1,0:T(8,128)S(1)} %get-tuple-element.151.first, f32[8192,128]{1,0:T(8,128)S(1)} %get-tuple-element.150.second, ...), custom_call_target="tpu_custom_call" | custom-call | tf_op jit(solution)/shard_map/adam/pallas_call | solution.py:596
  (115 shorter events, 48.0 us)
Async XLA Ops:
  7.2 100.6 %all-gather.3.cloned.1.call-start = ((), (), s32[]{:S(2)}) async-start(), calls=%async_computation.1 | async-start | bytes 4718592 | tf_op jit(solution)/shard_map/all_gather | solution.py:425
  7.2 42.8 %collective-permute-start.2 = (bf16[512,1024]{1,0:T(8,128)(2,1)}, bf16[512,1024]{1,0:T(8,128)(2,1)}, u32[]{:S(2)}, u32[]{:S(2)}) collective-permute-start(bf16[512,1024]{1,0:T(8,128)(2,1)} %bitcast.62), channel_id=1, source_target_pairs={{0,4},{1,5},{6,2},{7,3},{8,12},{9,13},{14,10},{15,11},{16,20},{17,... | collective-permute-start | bytes 3145736 | tf_op jit(solution)/shard_map/ppermute | solution.py:303
  16.2 17.6 %collective-permute-start.3 = (bf16[64,1024]{1,0:T(8,128)(2,1)S(1)}, bf16[64,1024]{1,0:T(8,128)(2,1)S(1)}, u32[]{:S(2)}, u32[]{:S(2)}) collective-permute-start(bf16[64,1024]{1,0:T(8,128)(2,1)S(1)} %fusion.1), channel_id=1, source_target_pairs={{0,1},{1,2},{2,3},{3,0},{4,5},{5,6},{6,7},{7,4},{8,9},{9,10},{10,1... | collective-permute-start | bytes 393224 | tf_op jit(solution)/shard_map/ppermute | solution.py:303
  17.5 21.1 %collective-permute-start.1 = (bf16[256,1024]{1,0:T(8,128)(2,1)S(1)}, bf16[256,1024]{1,0:T(8,128)(2,1)S(1)}, u32[]{:S(2)}, u32[]{:S(2)}) collective-permute-start(bf16[256,1024]{1,0:T(8,128)(2,1)S(1)} %get-tuple-element.146), channel_id=1, source_target_pairs={{1,4},{2,5},{3,1},{4,6},{5,2},{6,3},{9,12},{10,13},{11,9},{12,14},... | collective-permute-start | bytes 1572872 | tf_op jit(solution)/shard_map/ppermute | solution.py:303
  27.8 21.4 %collective-permute-start = (bf16[256,1024]{1,0:T(8,128)(2,1)S(1)}, bf16[256,1024]{1,0:T(8,128)(2,1)S(1)}, u32[]{:S(2)}, u32[]{:S(2)}) collective-permute-start(bf16[256,1024]{1,0:T(8,128)(2,1)S(1)} %get-tuple-element.147), channel_id=1, source_target_pairs={{1,0},{2,1},{3,5},{4,2},{5,6},{6,7},{9,8},{10,9},{11,13},{12,10},{... | collective-permute-start | bytes 1572872 | tf_op jit(solution)/shard_map/ppermute | solution.py:303
  30.0 19.2 %collective-permute-start.6 = (bf16[2,256,512]{2,1,0:T(8,128)(2,1)}, bf16[2,256,512]{2,1,0:T(8,128)(2,1)S(1)}, u32[]{:S(2)}, u32[]{:S(2)}) collective-permute-start(bf16[2,256,512]{2,1,0:T(8,128)(2,1)} %get-tuple-element.81), channel_id=1, source_target_pairs={{0,1},{1,0},{6,3},{7,2},{8,9},{9,8},{14,11},{15,10},{16,17},{17,16... | collective-permute-start | bytes 1572872 | tf_op jit(solution)/shard_map/ppermute | solution.py:303
  50.1 38.0 %all-to-all-start = ((bf16[8,2,256,256]{3,2,1,0:T(8,128)(2,1)}), bf16[8,2,256,256]{3,2,1,0:T(8,128)(2,1)S(1)}, u32[]{:S(2)}, u32[]{:S(2)}) async-start(bf16[8,2,256,256]{3,2,1,0:T(8,128)(2,1)} %get-tuple-element.80), calls=%async_computation | async-start | bytes 4194304 | tf_op jit(solution)/shard_map/all_to_all | solution.py:360
  54.7 32.6 %collective-permute-start.9 = (bf16[2,256,512]{2,1,0:T(8,128)(2,1)}, bf16[2,256,512]{2,1,0:T(8,128)(2,1)S(1)}, u32[]{:S(2)}, u32[]{:S(2)}) collective-permute-start(bf16[2,256,512]{2,1,0:T(8,128)(2,1)} %get-tuple-element.82), channel_id=1, source_target_pairs={{2,5},{3,4},{4,7},{5,6},{10,13},{11,12},{12,15},{13,14},{18,21},{1... | collective-permute-start | bytes 1572872 | tf_op jit(solution)/shard_map/ppermute | solution.py:303
  56.0 32.0 %collective-permute-start.10 = (bf16[2,256,512]{2,1,0:T(8,128)(2,1)}, bf16[2,256,512]{2,1,0:T(8,128)(2,1)}, u32[]{:S(2)}, u32[]{:S(2)}) collective-permute-start(bf16[2,256,512]{2,1,0:T(8,128)(2,1)} %get-tuple-element.83), channel_id=1, source_target_pairs={{0,4},{1,5},{2,0},{3,1},{4,2},{5,3},{6,6},{7,7},{8,12},{9,13},{10,... | collective-permute-start | bytes 1572872 | tf_op jit(solution)/shard_map/ppermute | solution.py:303
  62.3 42.4 %collective-permute-start.20 = (bf16[256,1024]{1,0:T(8,128)(2,1)}, bf16[256,1024]{1,0:T(8,128)(2,1)}, u32[]{:S(2)}, u32[]{:S(2)}) collective-permute-start(bf16[256,1024]{1,0:T(8,128)(2,1)} %broadcast_select_fusion), channel_id=1, source_target_pairs={{0,5},{1,0},{2,3},{5,4},{6,7},{7,2},{8,13},{9,8},{10,11},{13,12},{... | collective-permute-start | bytes 1572872 | tf_op jit(solution)/shard_map/ppermute | solution.py:303
  66.5 38.3 %collective-permute-start.19 = (bf16[256,1024]{1,0:T(8,128)(2,1)}, bf16[256,1024]{1,0:T(8,128)(2,1)}, u32[]{:S(2)}, u32[]{:S(2)}) collective-permute-start(bf16[256,1024]{1,0:T(8,128)(2,1)} %broadcast_select_fusion.1), channel_id=1, source_target_pairs={{0,1},{1,0},{2,3},{5,4},{6,7},{7,6},{8,9},{9,8},{10,11},{13,12},{1... | collective-permute-start | bytes 1572872 | tf_op jit(solution)/shard_map/ppermute | solution.py:303
  99.8 24.5 %collective-permute-start.17 = (bf16[256,1024]{1,0:T(8,128)(2,1)S(1)}, bf16[256,1024]{1,0:T(8,128)(2,1)}, u32[]{:S(2)}, u32[]{:S(2)}) collective-permute-start(bf16[256,1024]{1,0:T(8,128)(2,1)S(1)} %collective-permute-done.refs_2_), channel_id=1, source_target_pairs={{0,4},{1,5},{2,6},{3,7},{4,0},{5,1},{6,2},{7,3},{8,12},{9,13},{10,... | collective-permute-start | bytes 1572872 | tf_op jit(solution)/shard_map/ppermute | solution.py:303
  104.7 19.5 %collective-permute-start.18 = (bf16[256,1024]{1,0:T(8,128)(2,1)S(1)}, bf16[256,1024]{1,0:T(8,128)(2,1)}, u32[]{:S(2)}, u32[]{:S(2)}) collective-permute-start(bf16[256,1024]{1,0:T(8,128)(2,1)S(1)} %collective-permute-done.1.refs_3_), channel_id=1, source_target_pairs={{0,4},{1,5},{2,6},{3,7},{4,0},{5,1},{6,2},{7,3},{8,12},{9,13},{10,... | collective-permute-start | bytes 1572872 | tf_op jit(solution)/shard_map/ppermute | solution.py:303
  104.8 19.5 %collective-permute-start.22 = (bf16[256,1024]{1,0:T(8,128)(2,1)}, bf16[256,1024]{1,0:T(8,128)(2,1)}, u32[]{:S(2)}, u32[]{:S(2)}) collective-permute-start(bf16[256,1024]{1,0:T(8,128)(2,1)} %collective-permute-done.20.refs_7_), channel_id=1, source_target_pairs={{0,4},{1,5},{2,6},{3,7},{4,0},{5,1},{6,2},{7,3},{8,12},{9,13},{10,... | collective-permute-start | bytes 1572872 | tf_op jit(solution)/shard_map/ppermute | solution.py:303
  105.2 19.0 %collective-permute-start.21 = (bf16[256,1024]{1,0:T(8,128)(2,1)}, bf16[256,1024]{1,0:T(8,128)(2,1)}, u32[]{:S(2)}, u32[]{:S(2)}) collective-permute-start(bf16[256,1024]{1,0:T(8,128)(2,1)} %collective-permute-done.19.refs_6_), channel_id=1, source_target_pairs={{0,4},{1,5},{2,6},{3,7},{4,0},{5,1},{6,2},{7,3},{8,12},{9,13},{10,... | collective-permute-start | bytes 1572872 | tf_op jit(solution)/shard_map/ppermute | solution.py:303
  142.3 26.3 %collective-permute-start.24 = (bf16[2,256,256]{2,1,0:T(8,128)(2,1)}, bf16[2,256,256]{2,1,0:T(8,128)(2,1)S(1)}, u32[]{:S(2)}, u32[]{:S(2)}) collective-permute-start(bf16[2,256,256]{2,1,0:T(8,128)(2,1)} %get-tuple-element.117), channel_id=1, source_target_pairs={{0,31},{1,29},{2,0},{3,2},{4,12},{5,14},{6,17},{7,19},{8,4},{9,6},... | collective-permute-start | bytes 786440 | tf_op jit(solution)/shard_map/ppermute | solution.py:303
  144.2 24.4 %collective-permute-start.25 = (bf16[2,256,256]{2,1,0:T(8,128)(2,1)}, bf16[2,256,256]{2,1,0:T(8,128)(2,1)S(1)}, u32[]{:S(2)}, u32[]{:S(2)}) collective-permute-start(bf16[2,256,256]{2,1,0:T(8,128)(2,1)} %get-tuple-element.118), channel_id=1, source_target_pairs={{0,27},{1,25},{2,31},{3,29},{4,8},{5,10},{6,12},{7,14},{8,0},{9,2}... | collective-permute-start | bytes 786440 | tf_op jit(solution)/shard_map/ppermute | solution.py:303
  146.9 21.7 %collective-permute-start.26 = (bf16[2,256,256]{2,1,0:T(8,128)(2,1)}, bf16[2,256,256]{2,1,0:T(8,128)(2,1)S(1)}, u32[]{:S(2)}, u32[]{:S(2)}) collective-permute-start(bf16[2,256,256]{2,1,0:T(8,128)(2,1)} %get-tuple-element.119), channel_id=1, source_target_pairs={{0,22},{1,20},{2,27},{3,25},{4,7},{5,5},{6,8},{7,10},{8,31},{9,29}... | collective-permute-start | bytes 786440 | tf_op jit(solution)/shard_map/ppermute | solution.py:303
  148.8 19.8 %collective-permute-start.27 = (bf16[2,256,256]{2,1,0:T(8,128)(2,1)}, bf16[2,256,256]{2,1,0:T(8,128)(2,1)S(1)}, u32[]{:S(2)}, u32[]{:S(2)}) collective-permute-start(bf16[2,256,256]{2,1,0:T(8,128)(2,1)} %get-tuple-element.120), channel_id=1, source_target_pairs={{0,18},{1,16},{2,22},{3,20},{4,3},{5,1},{6,7},{7,5},{8,27},{9,25},... | collective-permute-start | bytes 786440 | tf_op jit(solution)/shard_map/ppermute | solution.py:303
  151.2 18.7 %collective-permute-start.28 = (bf16[2,256,256]{2,1,0:T(8,128)(2,1)}, bf16[2,256,256]{2,1,0:T(8,128)(2,1)}, u32[]{:S(2)}, u32[]{:S(2)}) collective-permute-start(bf16[2,256,256]{2,1,0:T(8,128)(2,1)} %get-tuple-element.129), channel_id=1, source_target_pairs={{0,13},{1,15},{2,18},{3,16},{4,30},{5,28},{6,3},{7,1},{8,22},{9,20... | collective-permute-start | bytes 786440 | tf_op jit(solution)/shard_map/ppermute | solution.py:303
  168.6 20.4 %collective-permute-start.30 = (bf16[2,256,256]{2,1,0:T(8,128)(2,1)}, bf16[2,256,256]{2,1,0:T(8,128)(2,1)}, u32[]{:S(2)}, u32[]{:S(2)}) collective-permute-start(bf16[2,256,256]{2,1,0:T(8,128)(2,1)} %get-tuple-element.131), channel_id=1, source_target_pairs={{0,4},{1,6},{2,9},{3,11},{4,21},{5,23},{6,26},{7,24},{8,13},{9,15}... | collective-permute-start | bytes 786440 | tf_op jit(solution)/shard_map/ppermute | solution.py:303
  199.8 24.9 %collective-permute-start.35 = (bf16[2,256,256]{2,1,0:T(8,128)(2,1)S(1)}, bf16[2,256,256]{2,1,0:T(8,128)(2,1)S(1)}, u32[]{:S(2)}, u32[]{:S(2)}) collective-permute-start(bf16[2,256,256]{2,1,0:T(8,128)(2,1)S(1)} %get-tuple-element.137), channel_id=1, source_target_pairs={{0,20},{1,21},{2,22},{3,23},{4,16},{5,17},{6,18},{7,19},{8,28},{9,... | collective-permute-start | bytes 786440 | tf_op jit(solution)/shard_map/ppermute | solution.py:303
  201.6 23.1 %collective-permute-start.36 = (bf16[2,256,256]{2,1,0:T(8,128)(2,1)S(1)}, bf16[2,256,256]{2,1,0:T(8,128)(2,1)S(1)}, u32[]{:S(2)}, u32[]{:S(2)}) collective-permute-start(bf16[2,256,256]{2,1,0:T(8,128)(2,1)S(1)} %get-tuple-element.138), channel_id=1, source_target_pairs={{0,24},{1,25},{2,26},{3,27},{4,28},{5,29},{6,30},{7,31},{8,0},{9,1... | collective-permute-start | bytes 786440 | tf_op jit(solution)/shard_map/ppermute | solution.py:303
  204.5 20.2 %collective-permute-start.37 = (bf16[2,256,256]{2,1,0:T(8,128)(2,1)S(1)}, bf16[2,256,256]{2,1,0:T(8,128)(2,1)S(1)}, u32[]{:S(2)}, u32[]{:S(2)}) collective-permute-start(bf16[2,256,256]{2,1,0:T(8,128)(2,1)S(1)} %get-tuple-element.139), channel_id=1, source_target_pairs={{0,28},{1,29},{2,30},{3,31},{4,24},{5,25},{6,26},{7,27},{8,4},{9,5... | collective-permute-start | bytes 786440 | tf_op jit(solution)/shard_map/ppermute | solution.py:303
  (28 other events, 499.7 us)
Sparse Core Ops, SparseCore 0:
  50.1 47.1 all-gather.2

commit v12 on v11

--- a/solution.py
+++ b/solution.py
@@ -13,7 +13,6 @@
 LANES = 128
 BLOCK = 256
 MIB = 1024 * 1024
-NT = (((1,), (1,)), ((), ()))
 
 COL, CORE, SHARD, PROC, PIECE = range(5)
 
@@ -90,8 +89,8 @@
 
 
 def up_kernel(shards, scale, ids, tokens, *refs):
-    pieces = refs[:-6]
-    act_t, slope_t, down_t, up_w, down_w, up_t = refs[-6:]
+    pieces = refs[:-4]
+    act_t, slope, down_w, up_w = refs[-4:]
     width, part = up_w.shape
     rows = width // shards
 
@@ -103,19 +102,15 @@
             down_w[pl.ds(at, rows), :] = piece[1]
 
         place_pieces(shards, ids, pieces, store)
-        for i in range(width // LANES):
-            span = slice(i * LANES, (i + 1) * LANES)
-            up_t[:, span] = up_w[span, :].astype(F32).T.astype(BF)
-            down_t[:, span] = down_w[span, :].astype(F32).T.astype(BF)
-
-    u = lax.dot_general(up_t[...], tokens[...], NT, preferred_element_type=F32) * scale
+
+    u = jnp.dot(tokens[...], up_w[...], preferred_element_type=F32) * scale
     cdf = 0.5 * (1.0 + lax.erf(u * 0.7071067811865476))
     density = jnp.exp(-0.5 * u * u) * 0.3989422804014327
-    act_t[...] = (u * cdf).astype(BF)
-    slope_t[...] = (cdf + u * density).astype(BF)
-
-
-def grad_kernel(shards, particles, up_scale, down_scale, back_scale, pick, ids, normed, act_t, slope_t, down_t, *refs):
+    act_t[...] = (u * cdf).astype(BF).T
+    slope[...] = (cdf + u * density).astype(BF)
+
+
+def grad_kernel(shards, particles, up_scale, down_scale, back_scale, pick, ids, normed, act_t, slope_rows, down_w, *refs):
     n_in = len(refs) - particles - 8
     sources, out = refs[:n_in], refs[n_in : n_in + particles]
     c, n, act, slope, grad, down, score, sems = refs[n_in + particles :]
@@ -123,8 +118,8 @@
     width = c.shape[1]
     chunk = tokens // shards
     first = [
-        pltpu.make_async_copy(down_t, down, sems.at[1]),
-        pltpu.make_async_copy(slope_t, slope, sems.at[2]),
+        pltpu.make_async_copy(down_w, down, sems.at[1]),
+        pltpu.make_async_copy(slope_rows, slope, sems.at[2]),
     ]
     later = [
         pltpu.make_async_copy(act_t, act, sems.at[3]),
@@ -141,8 +136,9 @@
 
     def back(i, carry):
         at = pl.multiple_of(i * chunk, chunk)
-        b = lax.dot_general(down[...], c[pl.ds(at, chunk), :], NT, preferred_element_type=F32)
-        grad[:, pl.ds(at, chunk)] = (b * (slope[:, pl.ds(at, chunk)].astype(F32) * back_scale)).astype(BF)
+        b = jnp.dot(c[pl.ds(at, chunk), :], down[...], preferred_element_type=F32)
+        b = (b * (slope[pl.ds(at, chunk), :].astype(F32) * back_scale)).astype(BF)
+        grad[:, pl.ds(at, chunk)] = b.T
         return carry
 
     lax.fori_loop(0, shards, back, 0)
@@ -427,7 +423,7 @@
         beta = [move(jnp.where(inner, a, x), route) for a, x, route in zip(alpha, halves, second_routes)]
         alpha_x = [move(x, swap_of(everyone)) for x in alpha]
         whole, w_pieces[2:5] = lax.optimization_barrier((whole, w_pieces[2:5]))
-        sums = add_over(pair_sums(whole), range(len(hops) - 2))
+        sums = add_over(pair_sums(whole), range(len(hops) - 3))
         w_pieces, normed, sums = lax.optimization_barrier((w_pieces, normed, sums))
         beta_x = [move(x, swap_of(everyone)) for x in beta]
         sources = [cot, own_c, *alpha, *alpha_x, *beta, *beta_x]
@@ -474,7 +470,7 @@
         sources = [jnp.where(core == proc, full, move(full, swap_of(everyone)))]
         w_pieces = [move(x, route) for x, route in zip(prepared, w_routes)]
         normed = lax.all_gather(shift_tokens(normed)[None], "particle", axis=0, tiled=True)
-        sums = add_over(pair_sums(whole), range(len(hops) - 2))
+        sums = add_over(pair_sums(whole), range(len(hops) - 3))
 
         def pick(ids, refs, held, sem):
             def one(which, carry):
@@ -486,28 +482,28 @@
             lax.fori_loop(0, shards, one, 0)
 
     normed = normed.reshape(tokens, width)
-    act_t, slope_t, down_t = pl.pallas_call(
+    act_t, slope, down_w = pl.pallas_call(
         functools.partial(up_kernel, shards, width ** (-0.5)),
         grid=(blocks,),
         out_shape=[
             jax.ShapeDtypeStruct((part, tokens), BF),
-            jax.ShapeDtypeStruct((part, tokens), BF),
-            jax.ShapeDtypeStruct((part, width), BF),
+            jax.ShapeDtypeStruct((tokens, part), BF),
+            jax.ShapeDtypeStruct((width, part), BF),
         ],
         in_specs=[smem_spec(), pl.BlockSpec((BLOCK, width), lambda i: (i, 0))]
         + [pl.BlockSpec((2, rows, part), lambda i: (0, 0, 0))] * len(w_pieces),
         out_specs=[
             pl.BlockSpec((part, BLOCK), lambda i: (0, i)),
-            pl.BlockSpec((part, BLOCK), lambda i: (0, i)),
-            pl.BlockSpec((part, width), lambda i: (0, 0)),
+            pl.BlockSpec((BLOCK, part), lambda i: (i, 0)),
+            pl.BlockSpec((width, part), lambda i: (0, 0)),
         ],
-        scratch_shapes=[pltpu.VMEM((width, part), BF), pltpu.VMEM((width, part), BF), pltpu.VMEM((part, width), BF)],
+        scratch_shapes=[pltpu.VMEM((width, part), BF)],
         compiler_params=params(56),
         name="up",
     )(ids, normed, *w_pieces)
 
-    sums = add_over(sums, [-2])
-    sums, act_t, slope_t = lax.optimization_barrier((sums, act_t, slope_t))
+    sums = add_over(sums, [-3])
+    sums, act_t, slope = lax.optimization_barrier((sums, act_t, slope))
     grad_scale = 1.0 / (tokens * width)
     scores = pl.pallas_call(
         functools.partial(
@@ -526,17 +522,17 @@
             pltpu.VMEM((tokens, width), BF),
             pltpu.VMEM((tokens, width), BF),
             pltpu.VMEM((part, tokens), BF),
+            pltpu.VMEM((tokens, part), BF),
             pltpu.VMEM((part, tokens), BF),
-            pltpu.VMEM((part, tokens), BF),
-            pltpu.VMEM((part, width), BF),
+            pltpu.VMEM((width, part), BF),
             pltpu.VMEM((2, width, part), BF),
             pltpu.SemaphoreType.DMA((particles + 5,)),
         ],
         compiler_params=params(56),
         name="grads",
-    )(ids, normed, act_t, slope_t, down_t, *sources)
-
-    sums = add_over(sums, [-1])
+    )(ids, normed, act_t, slope, down_w, *sources)
+
+    sums = add_over(sums, [-2])
     sums, *scores = lax.optimization_barrier((sums, *scores))
 
     ratio = particles // shards
@@ -550,6 +546,7 @@
             pairs.append((dev(m, c, s), dev(e // 2 + z, e % 2, z)))
         arrived.append(move(scores[t], pairs))
 
+    sums = add_over(sums, [-1])
     first_moment, second_moment, sums, *arrived[:5] = lax.optimization_barrier(
         (flat(first_moment), flat(second_moment), sums, *arrived[:5])
     )

time: 245 us -> 242 us (0.988)
  waiting for transfers between devices: 81.8 us -> 63.8 us
  starting transfers between devices: 83.1 us -> 101 us
    ppermute x38, waiting for transfers between devices: 81.8 us -> 63.8 us  [move(): return lax.ppermute(x, AXES, pairs)]
    ppermute x38, starting transfers between devices: 79.1 us -> 96.6 us  [move(): return lax.ppermute(x, AXES, pairs)]
  transfers between devices with their start and end apart: 40 -> 40, of which waited for: 10 -> 14; matrix products, arithmetic and copies ran while one was open for 5% -> 5% of each run, Pallas kernels for 14% -> 14%
where the time goes in v12:
time: 242 us; the launch traced here: 240 us
  starting transfers between devices  101 us (42%)
  waiting for transfers between devices  63.8 us (26%)
  Pallas kernels  48 us (20%)
  between operations  15.2 us (6%)
  other arithmetic  8.32 us (3%)
  local copies, waits for them, and re-layouts  4.4 us (2%)
    ppermute x38, starting transfers between devices, move(): return lax.ppermute(x, AXES, pairs)  96.6 us
    ppermute x38, waiting for transfers between devices, move(): return lax.ppermute(x, AXES, pairs)  63.8 us
    pallas_call x1, Pallas kernels, local(): pl.pallas_call(functools.partial(grad_kernel, shards, particles, -width *...  13.9 us
    pallas_call x1, Pallas kernels, local(): pl.pallas_call(functools.partial(up_kernel, shards, width ** (-0.5)), gri...  10.3 us
    pallas_call x1, Pallas kernels, local(): pl.pallas_call(functools.partial(adam_kernel, particles), grid=(steps,),...  9.52 us
    pallas_call x1, Pallas kernels, local(): pl.pallas_call(functools.partial(prep_kernel, shards), grid=(steps,), out...  6.9 us
    pallas_call x1, Pallas kernels, local(): pl.pallas_call(functools.partial(stein_kernel, shards, particles), out_sh...  5.37 us
  transfers between devices with their start and end apart: 40, of which 14 were waited for; matrix products, arithmetic and copies ran while one was open for 5% of the time, Pallas kernels for 14%

profile of v12, /device:TPU:23, one launch (start us, length us, event | category | flops | bytes accessed | tf_op | source)
XLA Modules:
  0.0 240.3 jit_solution(1146797522255613827)
XLA Ops:
  7.2 3.7 %collective-permute-start.2 = (bf16[512,1024]{1,0:T(8,128)(2,1)}, bf16[512,1024]{1,0:T(8,128)(2,1)}, u32[]{:S(2)}, u32[]{:S(2)}) collective-permute-start(bf16[512,1024]{1,0:T(8,128)(2,1)} %bitcast.62), channel_id=1, source_target_pairs={{0,4},{1,5},{6,2},{7,3},{8,12},{9,13},{14,10},{15,11},{16,20},{17,... | collective-permute-start | bytes 3145736 | tf_op jit(solution)/shard_map/ppermute | solution.py:299
  20.9 6.9 %prep.1 = (bf16[2,256,512]{2,1,0:T(8,128)(2,1)}, bf16[2,256,512]{2,1,0:T(8,128)(2,1)}, bf16[2,256,512]{2,1,0:T(8,128)(2,1)}, bf16[2,256,512]{2,1,0:T(8,128)(2,1)}, bf16[8,2,256,256]{3,2,1,0:T(8,128)(2,1)}) custom-call(s32[5]{0:T(128)} %stack.36.ids, f32[8192,128]{1,0:T(8,128)} %bitcast.58), custom_call_target="tpu_custom_call" | custom-call | tf_op jit(solution)/shard_map/prep/pallas_call | solution.py:324
  30.0 3.7 %collective-permute-start.6 = (bf16[2,256,512]{2,1,0:T(8,128)(2,1)}, bf16[2,256,512]{2,1,0:T(8,128)(2,1)S(1)}, u32[]{:S(2)}, u32[]{:S(2)}) collective-permute-start(bf16[2,256,512]{2,1,0:T(8,128)(2,1)} %get-tuple-element.81), channel_id=1, source_target_pairs={{0,1},{1,0},{6,3},{7,2},{8,9},{9,8},{14,11},{15,10},{16,17},{17,16... | collective-permute-start | bytes 1572872 | tf_op jit(solution)/shard_map/ppermute | solution.py:299
  33.7 3.8 %collective-permute-start.7 = (bf16[2,256,512]{2,1,0:T(8,128)(2,1)}, bf16[2,256,512]{2,1,0:T(8,128)(2,1)}, u32[]{:S(2)}, u32[]{:S(2)}) collective-permute-start(bf16[2,256,512]{2,1,0:T(8,128)(2,1)} %get-tuple-element.82), channel_id=1, source_target_pairs={{0,5},{1,4},{6,7},{7,6},{8,13},{9,12},{14,15},{15,14},{16,21},{17,... | collective-permute-start | bytes 1572872 | tf_op jit(solution)/shard_map/ppermute | solution.py:299
  38.6 10.7 %collective-permute-done.refs_2_ = bf16[256,1024]{1,0:T(8,128)(2,1)S(1)} collective-permute-done((bf16[256,1024]{1,0:T(8,128)(2,1)S(1)}, bf16[256,1024]{1,0:T(8,128)(2,1)S(1)}, u32[]{:S(2)}, u32[]{:S(2)}) %collective-permute-start) | collective-permute-done | bytes 524320 | tf_op jit(solution)/shard_map/ppermute | solution.py:299
  50.1 4.0 %all-to-all-start = ((bf16[8,2,256,256]{3,2,1,0:T(8,128)(2,1)}), bf16[8,2,256,256]{3,2,1,0:T(8,128)(2,1)S(1)}, u32[]{:S(2)}, u32[]{:S(2)}) async-start(bf16[8,2,256,256]{3,2,1,0:T(8,128)(2,1)} %get-tuple-element.80), calls=%async_computation | async-start | bytes 4194304 | tf_op jit(solution)/shard_map/all_to_all | solution.py:356
  56.0 5.4 %collective-permute-start.10 = (bf16[2,256,512]{2,1,0:T(8,128)(2,1)}, bf16[2,256,512]{2,1,0:T(8,128)(2,1)}, u32[]{:S(2)}, u32[]{:S(2)}) collective-permute-start(bf16[2,256,512]{2,1,0:T(8,128)(2,1)} %get-tuple-element.83), channel_id=1, source_target_pairs={{0,4},{1,5},{2,0},{3,1},{4,2},{5,3},{6,6},{7,7},{8,12},{9,13},{10,... | collective-permute-start | bytes 1572872 | tf_op jit(solution)/shard_map/ppermute | solution.py:299
  69.9 13.5 %collective-permute-start.11 = (bf16[2,256,512]{2,1,0:T(8,128)(2,1)}, bf16[2,256,512]{2,1,0:T(8,128)(2,1)}, u32[]{:S(2)}, u32[]{:S(2)}) collective-permute-start(bf16[2,256,512]{2,1,0:T(8,128)(2,1)} %get-tuple-element.87), channel_id=1, source_target_pairs={{0,0},{1,1},{2,4},{3,5},{4,6},{5,7},{6,2},{7,3},{8,8},{9,9},{10,12... | collective-permute-start | bytes 1572872 | tf_op jit(solution)/shard_map/ppermute | solution.py:299
  83.5 9.0 %collective-permute-done.9.refs_3_ = bf16[2,256,512]{2,1,0:T(8,128)(2,1)S(1)} collective-permute-done((bf16[2,256,512]{2,1,0:T(8,128)(2,1)}, bf16[2,256,512]{2,1,0:T(8,128)(2,1)S(1)}, u32[]{:S(2)}, u32[]{:S(2)}) %collective-permute-start.9) | collective-permute-done | bytes 524320 | tf_op jit(solution)/shard_map/ppermute | solution.py:299
  95.4 5.2 %collective-permute-start.12 = (f32[8,128]{1,0:T(8,128)S(1)}, f32[8,128]{1,0:T(8,128)S(1)}, u32[]{:S(2)}, u32[]{:S(2)}) collective-permute-start(f32[8,128]{1,0:T(8,128)S(1)} %distances.1), channel_id=1, source_target_pairs={{0,4},{1,5},{2,6},{3,7},{4,0},{5,1},{6,2},{7,3},{8,12},{9,13},{10,... | collective-permute-start | bytes 12296 | tf_op jit(solution)/shard_map/ppermute | solution.py:299
  105.7 10.3 %up.1 = (bf16[512,2048]{1,0:T(8,128)(2,1)}, bf16[2048,512]{1,0:T(8,128)(2,1)}, bf16[1024,512]{1,0:T(8,128)(2,1)}) custom-call(s32[5]{0:T(128)} %stack.36.ids, bf16[2048,1024]{1,0:T(8,128)(2,1)} %bitcast.60, bf16[2,256,512]{2,1,0:T(8,128)(2,1)} %copy-done.8, bf16[2,256,512]{2,1,0:T(8,128)(2,1)} %collective-permute-done.7.refs_1_, ...), custom_call_target="tpu_custom_call" | custom-call | tf_op jit(solution)/shard_map/up/pallas_call | solution.py:485
  117.9 13.9 %grads.1 = (bf16[2,256,256]{2,1,0:T(8,128)(2,1)}, bf16[2,256,256]{2,1,0:T(8,128)(2,1)}, bf16[2,256,256]{2,1,0:T(8,128)(2,1)}, bf16[2,256,256]{2,1,0:T(8,128)(2,1...) custom-call(s32[5]{0:T(128)} %stack.36.ids, ...), custom_call_target="tpu_custom_call" | custom-call | tf_op jit(solution)/shard_map/grads/pallas_call | solution.py:508
  140.5 5.9 %collective-permute-start.26 = (bf16[2,256,256]{2,1,0:T(8,128)(2,1)}, bf16[2,256,256]{2,1,0:T(8,128)(2,1)S(1)}, u32[]{:S(2)}, u32[]{:S(2)}) collective-permute-start(bf16[2,256,256]{2,1,0:T(8,128)(2,1)} %get-tuple-element.119), channel_id=1, source_target_pairs={{0,22},{1,20},{2,27},{3,25},{4,7},{5,5},{6,8},{7,10},{8,31},{9,29}... | collective-permute-start | bytes 786440 | tf_op jit(solution)/shard_map/ppermute | solution.py:299
  151.5 4.0 %collective-permute-done.25.refs_2_ = bf16[2,256,256]{2,1,0:T(8,128)(2,1)S(1)} collective-permute-done((bf16[2,256,256]{2,1,0:T(8,128)(2,1)}, bf16[2,256,256]{2,1,0:T(8,128)(2,1)S(1)}, u32[]{:S(2)}, u32[]{:S(2)}) %collective-permute-start.25) | collective-permute-done | bytes 262176 | tf_op jit(solution)/shard_map/ppermute | solution.py:299
  155.6 6.9 %collective-permute-start.30 = (bf16[2,256,256]{2,1,0:T(8,128)(2,1)}, bf16[2,256,256]{2,1,0:T(8,128)(2,1)}, u32[]{:S(2)}, u32[]{:S(2)}) collective-permute-start(bf16[2,256,256]{2,1,0:T(8,128)(2,1)} %get-tuple-element.131), channel_id=1, source_target_pairs={{0,4},{1,6},{2,9},{3,11},{4,21},{5,23},{6,26},{7,24},{8,13},{9,15}... | collective-permute-start | bytes 786440 | tf_op jit(solution)/shard_map/ppermute | solution.py:299
  164.7 14.9 %collective-permute-done.29.refs_6_ = bf16[2,256,256]{2,1,0:T(8,128)(2,1)} collective-permute-done((bf16[2,256,256]{2,1,0:T(8,128)(2,1)}, bf16[2,256,256]{2,1,0:T(8,128)(2,1)}, u32[]{:S(2)}, u32[]{:S(2)}) %collective-permute-start.29) | collective-permute-done | bytes 262176 | tf_op jit(solution)/shard_map/ppermute | solution.py:299
  179.6 3.9 %collective-permute-done.30.refs_7_ = bf16[2,256,256]{2,1,0:T(8,128)(2,1)} collective-permute-done((bf16[2,256,256]{2,1,0:T(8,128)(2,1)}, bf16[2,256,256]{2,1,0:T(8,128)(2,1)}, u32[]{:S(2)}, u32[]{:S(2)}) %collective-permute-start.30) | collective-permute-done | bytes 262176 | tf_op jit(solution)/shard_map/ppermute | solution.py:299
  183.4 5.4 %stein.1 = (bf16[2,256,256]{2,1,0:T(8,128)(2,1)S(1)}, bf16[2,256,256]{2,1,0:T(8,128)(2,1)S(1)}, bf16[2,256,256]{2,1,0:T(8,128)(2,1)S(1)}, bf16[2,256,256]{2,1,0:...) custom-call(s32[5]{0:T(128)S(1)} %copy-done.3, ...), custom_call_target="tpu_custom_call" | custom-call | tf_op jit(solution)/shard_map/stein/pallas_call | solution.py:569
  190.6 5.9 %collective-permute-start.32 = (bf16[2,256,256]{2,1,0:T(8,128)(2,1)S(1)}, bf16[2,256,256]{2,1,0:T(8,128)(2,1)S(1)}, u32[]{:S(2)}, u32[]{:S(2)}) collective-permute-start(bf16[2,256,256]{2,1,0:T(8,128)(2,1)S(1)} %get-tuple-element.134), channel_id=1, source_target_pairs={{0,8},{1,9},{2,10},{3,11},{4,12},{5,13},{6,14},{7,15},{8,16},{9,17... | collective-permute-start | bytes 786440 | tf_op jit(solution)/shard_map/ppermute | solution.py:299
  202.2 4.1 %collective-permute-start.37 = (bf16[2,256,256]{2,1,0:T(8,128)(2,1)S(1)}, bf16[2,256,256]{2,1,0:T(8,128)(2,1)S(1)}, u32[]{:S(2)}, u32[]{:S(2)}) collective-permute-start(bf16[2,256,256]{2,1,0:T(8,128)(2,1)S(1)} %get-tuple-element.139), channel_id=1, source_target_pairs={{0,28},{1,29},{2,30},{3,31},{4,24},{5,25},{6,26},{7,27},{8,4},{9,5... | collective-permute-start | bytes 786440 | tf_op jit(solution)/shard_map/ppermute | solution.py:299
  206.3 4.2 %broadcast_multiply_fusion = (f32[8192,128]{1,0:T(8,128)S(1)}, f32[8192,128]{1,0:T(8,128)S(1)}) fusion(f32[8192,128]{1,0:T(8,128)} %bitcast.64, f32[8192,128]{1,0:T(8,128)} %bitcast.65), kind=kLoop, calls=%fused_computation.2 | loop fusion | flops 2097152 | bytes 16777216 | tf_op jit(solution)/shard_map/mul | solution.py:553
  210.5 5.4 %collective-permute-done.34.refs_4_ = bf16[2,256,256]{2,1,0:T(8,128)(2,1)S(1)} collective-permute-done((bf16[2,256,256]{2,1,0:T(8,128)(2,1)S(1)}, bf16[2,256,256]{2,1,0:T(8,128)(2,1)S(1)}, u32[]{:S(2)}, u32[]{:S(2)}) %collective-permute-start.34) | collective-permute-done | bytes 262176 | tf_op jit(solution)/shard_map/ppermute | solution.py:299
  215.9 8.0 %collective-permute-done.35.refs_5_ = bf16[2,256,256]{2,1,0:T(8,128)(2,1)S(1)} collective-permute-done((bf16[2,256,256]{2,1,0:T(8,128)(2,1)S(1)}, bf16[2,256,256]{2,1,0:T(8,128)(2,1)S(1)}, u32[]{:S(2)}, u32[]{:S(2)}) %collective-permute-start.35) | collective-permute-done | bytes 262176 | tf_op jit(solution)/shard_map/ppermute | solution.py:299
  223.9 9.5 %adam.1 = (f32[8192,128]{1,0:T(8,128)}, f32[8192,128]{1,0:T(8,128)}, f32[8192,128]{1,0:T(8,128)}, f32[8192,128]{1,0:T(8,128)}) custom-call(s32[5]{0:T(128)S(1)} %copy-done.3, f32[8192,128]{1,0:T(8,128)S(1)} %bitcast.59, f32[8192,128]{1,0:T(8,128)S(1)} %get-tuple-element.151.first, f32[8192,128]{1,0:T(8,128)S(1)} %get-tuple-element.150.second, ...), custom_call_target="tpu_custom_call" | custom-call | tf_op jit(solution)/shard_map/adam/pallas_call | solution.py:593
  (115 shorter events, 57.0 us)
Async XLA Ops:
  7.2 98.2 %all-gather.3.cloned.1.call-start = ((), (), s32[]{:S(2)}) async-start(), calls=%async_computation.1 | async-start | bytes 4718592 | tf_op jit(solution)/shard_map/all_gather | solution.py:421
  7.2 42.8 %collective-permute-start.2 = (bf16[512,1024]{1,0:T(8,128)(2,1)}, bf16[512,1024]{1,0:T(8,128)(2,1)}, u32[]{:S(2)}, u32[]{:S(2)}) collective-permute-start(bf16[512,1024]{1,0:T(8,128)(2,1)} %bitcast.62), channel_id=1, source_target_pairs={{0,4},{1,5},{6,2},{7,3},{8,12},{9,13},{14,10},{15,11},{16,20},{17,... | collective-permute-start | bytes 3145736 | tf_op jit(solution)/shard_map/ppermute | solution.py:299
  12.8 17.2 %collective-permute-start.4 = (bf16[64,1024]{1,0:T(8,128)(2,1)S(1)}, bf16[64,1024]{1,0:T(8,128)(2,1)S(1)}, u32[]{:S(2)}, u32[]{:S(2)}) collective-permute-start(bf16[64,1024]{1,0:T(8,128)(2,1)S(1)} %fusion.1), channel_id=1, source_target_pairs={{0,2},{1,3},{2,0},{3,1},{4,6},{5,7},{6,4},{7,5},{8,10},{9,11},{10,... | collective-permute-start | bytes 393224 | tf_op jit(solution)/shard_map/ppermute | solution.py:299
  16.2 17.6 %collective-permute-start.3 = (bf16[64,1024]{1,0:T(8,128)(2,1)S(1)}, bf16[64,1024]{1,0:T(8,128)(2,1)S(1)}, u32[]{:S(2)}, u32[]{:S(2)}) collective-permute-start(bf16[64,1024]{1,0:T(8,128)(2,1)S(1)} %fusion.1), channel_id=1, source_target_pairs={{0,1},{1,2},{2,3},{3,0},{4,5},{5,6},{6,7},{7,4},{8,9},{9,10},{10,1... | collective-permute-start | bytes 393224 | tf_op jit(solution)/shard_map/ppermute | solution.py:299
  17.5 21.1 %collective-permute-start.1 = (bf16[256,1024]{1,0:T(8,128)(2,1)S(1)}, bf16[256,1024]{1,0:T(8,128)(2,1)S(1)}, u32[]{:S(2)}, u32[]{:S(2)}) collective-permute-start(bf16[256,1024]{1,0:T(8,128)(2,1)S(1)} %get-tuple-element.146), channel_id=1, source_target_pairs={{1,4},{2,5},{3,1},{4,6},{5,2},{6,3},{9,12},{10,13},{11,9},{12,14},... | collective-permute-start | bytes 1572872 | tf_op jit(solution)/shard_map/ppermute | solution.py:299
  27.8 21.4 %collective-permute-start = (bf16[256,1024]{1,0:T(8,128)(2,1)S(1)}, bf16[256,1024]{1,0:T(8,128)(2,1)S(1)}, u32[]{:S(2)}, u32[]{:S(2)}) collective-permute-start(bf16[256,1024]{1,0:T(8,128)(2,1)S(1)} %get-tuple-element.147), channel_id=1, source_target_pairs={{1,0},{2,1},{3,5},{4,2},{5,6},{6,7},{9,8},{10,9},{11,13},{12,10},{... | collective-permute-start | bytes 1572872 | tf_op jit(solution)/shard_map/ppermute | solution.py:299
  30.0 19.2 %collective-permute-start.6 = (bf16[2,256,512]{2,1,0:T(8,128)(2,1)}, bf16[2,256,512]{2,1,0:T(8,128)(2,1)S(1)}, u32[]{:S(2)}, u32[]{:S(2)}) collective-permute-start(bf16[2,256,512]{2,1,0:T(8,128)(2,1)} %get-tuple-element.81), channel_id=1, source_target_pairs={{0,1},{1,0},{6,3},{7,2},{8,9},{9,8},{14,11},{15,10},{16,17},{17,16... | collective-permute-start | bytes 1572872 | tf_op jit(solution)/shard_map/ppermute | solution.py:299
  33.7 16.2 %collective-permute-start.7 = (bf16[2,256,512]{2,1,0:T(8,128)(2,1)}, bf16[2,256,512]{2,1,0:T(8,128)(2,1)}, u32[]{:S(2)}, u32[]{:S(2)}) collective-permute-start(bf16[2,256,512]{2,1,0:T(8,128)(2,1)} %get-tuple-element.82), channel_id=1, source_target_pairs={{0,5},{1,4},{6,7},{7,6},{8,13},{9,12},{14,15},{15,14},{16,21},{17,... | collective-permute-start | bytes 1572872 | tf_op jit(solution)/shard_map/ppermute | solution.py:299
  50.1 43.2 %all-to-all-start = ((bf16[8,2,256,256]{3,2,1,0:T(8,128)(2,1)}), bf16[8,2,256,256]{3,2,1,0:T(8,128)(2,1)S(1)}, u32[]{:S(2)}, u32[]{:S(2)}) async-start(bf16[8,2,256,256]{3,2,1,0:T(8,128)(2,1)} %get-tuple-element.80), calls=%async_computation | async-start | bytes 4194304 | tf_op jit(solution)/shard_map/all_to_all | solution.py:356
  54.0 15.9 %collective-permute-start.8 = (bf16[2,256,512]{2,1,0:T(8,128)(2,1)}, bf16[2,256,512]{2,1,0:T(8,128)(2,1)S(1)}, u32[]{:S(2)}, u32[]{:S(2)}) collective-permute-start(bf16[2,256,512]{2,1,0:T(8,128)(2,1)} %get-tuple-element.81), channel_id=1, source_target_pairs={{2,1},{3,0},{4,3},{5,2},{10,9},{11,8},{12,11},{13,10},{18,17},{19,... | collective-permute-start | bytes 1572872 | tf_op jit(solution)/shard_map/ppermute | solution.py:299
  54.7 37.8 %collective-permute-start.9 = (bf16[2,256,512]{2,1,0:T(8,128)(2,1)}, bf16[2,256,512]{2,1,0:T(8,128)(2,1)S(1)}, u32[]{:S(2)}, u32[]{:S(2)}) collective-permute-start(bf16[2,256,512]{2,1,0:T(8,128)(2,1)} %get-tuple-element.82), channel_id=1, source_target_pairs={{2,5},{3,4},{4,7},{5,6},{10,13},{11,12},{12,15},{13,14},{18,21},{1... | collective-permute-start | bytes 1572872 | tf_op jit(solution)/shard_map/ppermute | solution.py:299
  56.0 37.3 %collective-permute-start.10 = (bf16[2,256,512]{2,1,0:T(8,128)(2,1)}, bf16[2,256,512]{2,1,0:T(8,128)(2,1)}, u32[]{:S(2)}, u32[]{:S(2)}) collective-permute-start(bf16[2,256,512]{2,1,0:T(8,128)(2,1)} %get-tuple-element.83), channel_id=1, source_target_pairs={{0,4},{1,5},{2,0},{3,1},{4,2},{5,3},{6,6},{7,7},{8,12},{9,13},{10,... | collective-permute-start | bytes 1572872 | tf_op jit(solution)/shard_map/ppermute | solution.py:299
  62.3 40.0 %collective-permute-start.19 = (bf16[256,1024]{1,0:T(8,128)(2,1)}, bf16[256,1024]{1,0:T(8,128)(2,1)}, u32[]{:S(2)}, u32[]{:S(2)}) collective-permute-start(bf16[256,1024]{1,0:T(8,128)(2,1)} %broadcast_select_fusion), channel_id=1, source_target_pairs={{0,5},{1,0},{2,3},{5,4},{6,7},{7,2},{8,13},{9,8},{10,11},{13,12},{... | collective-permute-start | bytes 1572872 | tf_op jit(solution)/shard_map/ppermute | solution.py:299
  66.5 35.9 %collective-permute-start.18 = (bf16[256,1024]{1,0:T(8,128)(2,1)}, bf16[256,1024]{1,0:T(8,128)(2,1)}, u32[]{:S(2)}, u32[]{:S(2)}) collective-permute-start(bf16[256,1024]{1,0:T(8,128)(2,1)} %broadcast_select_fusion.1), channel_id=1, source_target_pairs={{0,1},{1,0},{2,3},{5,4},{6,7},{7,6},{8,9},{9,8},{10,11},{13,12},{1... | collective-permute-start | bytes 1572872 | tf_op jit(solution)/shard_map/ppermute | solution.py:299
  69.9 35.4 %collective-permute-start.11 = (bf16[2,256,512]{2,1,0:T(8,128)(2,1)}, bf16[2,256,512]{2,1,0:T(8,128)(2,1)}, u32[]{:S(2)}, u32[]{:S(2)}) collective-permute-start(bf16[2,256,512]{2,1,0:T(8,128)(2,1)} %get-tuple-element.87), channel_id=1, source_target_pairs={{0,0},{1,1},{2,4},{3,5},{4,6},{5,7},{6,2},{7,3},{8,8},{9,9},{10,12... | collective-permute-start | bytes 1572872 | tf_op jit(solution)/shard_map/ppermute | solution.py:299
  101.7 16.1 %collective-permute-start.16 = (bf16[256,1024]{1,0:T(8,128)(2,1)S(1)}, bf16[256,1024]{1,0:T(8,128)(2,1)}, u32[]{:S(2)}, u32[]{:S(2)}) collective-permute-start(bf16[256,1024]{1,0:T(8,128)(2,1)S(1)} %collective-permute-done.refs_2_), channel_id=1, source_target_pairs={{0,4},{1,5},{2,6},{3,7},{4,0},{5,1},{6,2},{7,3},{8,12},{9,13},{10,... | collective-permute-start | bytes 1572872 | tf_op jit(solution)/shard_map/ppermute | solution.py:299
  140.5 22.0 %collective-permute-start.26 = (bf16[2,256,256]{2,1,0:T(8,128)(2,1)}, bf16[2,256,256]{2,1,0:T(8,128)(2,1)S(1)}, u32[]{:S(2)}, u32[]{:S(2)}) collective-permute-start(bf16[2,256,256]{2,1,0:T(8,128)(2,1)} %get-tuple-element.119), channel_id=1, source_target_pairs={{0,22},{1,20},{2,27},{3,25},{4,7},{5,5},{6,8},{7,10},{8,31},{9,29}... | collective-permute-start | bytes 786440 | tf_op jit(solution)/shard_map/ppermute | solution.py:299
  146.4 16.1 %collective-permute-start.27 = (bf16[2,256,256]{2,1,0:T(8,128)(2,1)}, bf16[2,256,256]{2,1,0:T(8,128)(2,1)S(1)}, u32[]{:S(2)}, u32[]{:S(2)}) collective-permute-start(bf16[2,256,256]{2,1,0:T(8,128)(2,1)} %get-tuple-element.120), channel_id=1, source_target_pairs={{0,18},{1,16},{2,22},{3,20},{4,3},{5,1},{6,7},{7,5},{8,27},{9,25},... | collective-permute-start | bytes 786440 | tf_op jit(solution)/shard_map/ppermute | solution.py:299
  151.5 28.0 %collective-permute-start.29 = (bf16[2,256,256]{2,1,0:T(8,128)(2,1)}, bf16[2,256,256]{2,1,0:T(8,128)(2,1)}, u32[]{:S(2)}, u32[]{:S(2)}) collective-permute-start(bf16[2,256,256]{2,1,0:T(8,128)(2,1)} %get-tuple-element.130), channel_id=1, source_target_pairs={{0,9},{1,11},{2,13},{3,15},{4,26},{5,24},{6,30},{7,28},{8,18},{9,1... | collective-permute-start | bytes 786440 | tf_op jit(solution)/shard_map/ppermute | solution.py:299
  155.6 27.9 %collective-permute-start.30 = (bf16[2,256,256]{2,1,0:T(8,128)(2,1)}, bf16[2,256,256]{2,1,0:T(8,128)(2,1)}, u32[]{:S(2)}, u32[]{:S(2)}) collective-permute-start(bf16[2,256,256]{2,1,0:T(8,128)(2,1)} %get-tuple-element.131), channel_id=1, source_target_pairs={{0,4},{1,6},{2,9},{3,11},{4,21},{5,23},{6,26},{7,24},{8,13},{9,15}... | collective-permute-start | bytes 786440 | tf_op jit(solution)/shard_map/ppermute | solution.py:299
  199.0 16.9 %collective-permute-start.34 = (bf16[2,256,256]{2,1,0:T(8,128)(2,1)S(1)}, bf16[2,256,256]{2,1,0:T(8,128)(2,1)S(1)}, u32[]{:S(2)}, u32[]{:S(2)}) collective-permute-start(bf16[2,256,256]{2,1,0:T(8,128)(2,1)S(1)} %get-tuple-element.136), channel_id=1, source_target_pairs={{0,16},{1,17},{2,18},{3,19},{4,20},{5,21},{6,22},{7,23},{8,24},{9,... | collective-permute-start | bytes 786440 | tf_op jit(solution)/shard_map/ppermute | solution.py:299
  199.0 24.9 %collective-permute-start.35 = (bf16[2,256,256]{2,1,0:T(8,128)(2,1)S(1)}, bf16[2,256,256]{2,1,0:T(8,128)(2,1)S(1)}, u32[]{:S(2)}, u32[]{:S(2)}) collective-permute-start(bf16[2,256,256]{2,1,0:T(8,128)(2,1)S(1)} %get-tuple-element.137), channel_id=1, source_target_pairs={{0,20},{1,21},{2,22},{3,23},{4,16},{5,17},{6,18},{7,19},{8,28},{9,... | collective-permute-start | bytes 786440 | tf_op jit(solution)/shard_map/ppermute | solution.py:299
  200.9 23.1 %collective-permute-start.36 = (bf16[2,256,256]{2,1,0:T(8,128)(2,1)S(1)}, bf16[2,256,256]{2,1,0:T(8,128)(2,1)S(1)}, u32[]{:S(2)}, u32[]{:S(2)}) collective-permute-start(bf16[2,256,256]{2,1,0:T(8,128)(2,1)S(1)} %get-tuple-element.138), channel_id=1, source_target_pairs={{0,24},{1,25},{2,26},{3,27},{4,28},{5,29},{6,30},{7,31},{8,0},{9,1... | collective-permute-start | bytes 786440 | tf_op jit(solution)/shard_map/ppermute | solution.py:299
  202.2 21.8 %collective-permute-start.37 = (bf16[2,256,256]{2,1,0:T(8,128)(2,1)S(1)}, bf16[2,256,256]{2,1,0:T(8,128)(2,1)S(1)}, u32[]{:S(2)}, u32[]{:S(2)}) collective-permute-start(bf16[2,256,256]{2,1,0:T(8,128)(2,1)S(1)} %get-tuple-element.139), channel_id=1, source_target_pairs={{0,28},{1,29},{2,30},{3,31},{4,24},{5,25},{6,26},{7,27},{8,4},{9,5... | collective-permute-start | bytes 786440 | tf_op jit(solution)/shard_map/ppermute | solution.py:299
  (28 other events, 532.1 us)
Sparse Core Ops, SparseCore 0:
  50.1 47.1 all-gather.2

commit v13 on v12

--- a/solution.py
+++ b/solution.py
@@ -498,13 +498,14 @@
             pl.BlockSpec((width, part), lambda i: (0, 0)),
         ],
         scratch_shapes=[pltpu.VMEM((width, part), BF)],
-        compiler_params=params(56),
+        compiler_params=params(20),
         name="up",
     )(ids, normed, *w_pieces)
 
     sums = add_over(sums, [-3])
     sums, act_t, slope = lax.optimization_barrier((sums, act_t, slope))
     grad_scale = 1.0 / (tokens * width)
+    held = 2 * (2 * tokens * width + 3 * tokens * part + 3 * width * part)
     scores = pl.pallas_call(
         functools.partial(
             grad_kernel,
@@ -528,7 +529,7 @@
             pltpu.VMEM((2, width, part), BF),
             pltpu.SemaphoreType.DMA((particles + 5,)),
         ],
-        compiler_params=params(56),
+        compiler_params=params(held // MIB + 7),
         name="grads",
     )(ids, normed, act_t, slope, down_w, *sources)
 

time: 242 us -> 250 us (1.033)
  local copies, waits for them, and re-layouts: 4.4 us -> 17.7 us
  starting transfers between devices: 101 us -> 93.2 us
  waiting for transfers between devices: 63.8 us -> 67 us
    unnamed x24 -> x56, local copies, waits for them, and re-layouts: 0.88 us -> 14.2 us
    ppermute x38, starting transfers between devices: 96.6 us -> 89.2 us  [move(): return lax.ppermute(x, AXES, pairs)]
    ppermute x38, waiting for transfers between devices: 63.8 us -> 67 us  [move(): return lax.ppermute(x, AXES, pairs)]
    pallas_call x1, Pallas kernels: 10.3 us -> 7.46 us  [local(): pl.pallas_call(functools.partial(up_kernel, shards, width ** (-0.5)), gri...]
  transfers between devices with their start and end apart: 40 -> 40, of which waited for: 14 -> 11; matrix products, arithmetic and copies ran while one was open for 5% -> 5% of each run, Pallas kernels for 14% -> 13%
where the time goes in v13:
time: 250 us; the launch traced here: 249 us
  starting transfers between devices  93.2 us (37%)
  waiting for transfers between devices  67 us (27%)
  Pallas kernels  46.3 us (19%)
  local copies, waits for them, and re-layouts  17.7 us (7%)
  between operations  15.3 us (6%)
  other arithmetic  9.19 us (4%)
    ppermute x38, starting transfers between devices, move(): return lax.ppermute(x, AXES, pairs)  89.2 us
    ppermute x38, waiting for transfers between devices, move(): return lax.ppermute(x, AXES, pairs)  67 us
    pallas_call x1, Pallas kernels, local(): pl.pallas_call(functools.partial(grad_kernel, shards, particles, -width *...  15 us
    unnamed x56, local copies, waits for them, and re-layouts  14.2 us
    pallas_call x1, Pallas kernels, local(): pl.pallas_call(functools.partial(adam_kernel, particles), grid=(steps,),...  9.52 us
    pallas_call x1, Pallas kernels, local(): pl.pallas_call(functools.partial(up_kernel, shards, width ** (-0.5)), gri...  7.46 us
    pallas_call x1, Pallas kernels, local(): pl.pallas_call(functools.partial(prep_kernel, shards), grid=(steps,), out...  6.9 us
    pallas_call x1, Pallas kernels, local(): pl.pallas_call(functools.partial(stein_kernel, shards, particles), out_sh...  5.37 us
  transfers between devices with their start and end apart: 40, of which 11 were waited for; matrix products, arithmetic and copies ran while one was open for 5% of the time, Pallas kernels for 13%

profile of v13, /device:TPU:23, one launch (start us, length us, event | category | flops | bytes accessed | tf_op | source)
XLA Modules:
  0.0 248.7 jit_solution(6079641293819398972)
XLA Ops:
  7.2 3.7 %collective-permute-start.2 = (bf16[512,1024]{1,0:T(8,128)(2,1)}, bf16[512,1024]{1,0:T(8,128)(2,1)}, u32[]{:S(2)}, u32[]{:S(2)}) collective-permute-start(bf16[512,1024]{1,0:T(8,128)(2,1)} %bitcast.62), channel_id=1, source_target_pairs={{0,4},{1,5},{6,2},{7,3},{8,12},{9,13},{14,10},{15,11},{16,20},{17,... | collective-permute-start | bytes 3145736 | tf_op jit(solution)/shard_map/ppermute | solution.py:299
  20.9 6.9 %prep.1 = (bf16[2,256,512]{2,1,0:T(8,128)(2,1)}, bf16[2,256,512]{2,1,0:T(8,128)(2,1)}, bf16[2,256,512]{2,1,0:T(8,128)(2,1)}, bf16[2,256,512]{2,1,0:T(8,128)(2,1)}, bf16[8,2,256,256]{3,2,1,0:T(8,128)(2,1)}) custom-call(s32[5]{0:T(128)} %stack.36.ids, f32[8192,128]{1,0:T(8,128)} %bitcast.58), custom_call_target="tpu_custom_call" | custom-call | tf_op jit(solution)/shard_map/prep/pallas_call | solution.py:324
  30.1 3.7 %collective-permute-start.6 = (bf16[2,256,512]{2,1,0:T(8,128)(2,1)}, bf16[2,256,512]{2,1,0:T(8,128)(2,1)S(1)}, u32[]{:S(2)}, u32[]{:S(2)}) collective-permute-start(bf16[2,256,512]{2,1,0:T(8,128)(2,1)} %get-tuple-element.81), channel_id=1, source_target_pairs={{0,1},{1,0},{6,3},{7,2},{8,9},{9,8},{14,11},{15,10},{16,17},{17,16... | collective-permute-start | bytes 1572872 | tf_op jit(solution)/shard_map/ppermute | solution.py:299
  34.4 3.8 %collective-permute-start.7 = (bf16[2,256,512]{2,1,0:T(8,128)(2,1)}, bf16[2,256,512]{2,1,0:T(8,128)(2,1)S(1)}, u32[]{:S(2)}, u32[]{:S(2)}) collective-permute-start(bf16[2,256,512]{2,1,0:T(8,128)(2,1)} %get-tuple-element.82), channel_id=1, source_target_pairs={{0,5},{1,4},{6,7},{7,6},{8,13},{9,12},{14,15},{15,14},{16,21},{17,... | collective-permute-start | bytes 1572872 | tf_op jit(solution)/shard_map/ppermute | solution.py:299
  40.2 9.1 %collective-permute-done.refs_2_ = bf16[256,1024]{1,0:T(8,128)(2,1)S(1)} collective-permute-done((bf16[256,1024]{1,0:T(8,128)(2,1)S(1)}, bf16[256,1024]{1,0:T(8,128)(2,1)S(1)}, u32[]{:S(2)}, u32[]{:S(2)}) %collective-permute-start) | collective-permute-done | bytes 524320 | tf_op jit(solution)/shard_map/ppermute | solution.py:299
  51.0 4.0 %all-to-all-start = ((bf16[8,2,256,256]{3,2,1,0:T(8,128)(2,1)}), bf16[8,2,256,256]{3,2,1,0:T(8,128)(2,1)S(1)}, u32[]{:S(2)}, u32[]{:S(2)}) async-start(bf16[8,2,256,256]{3,2,1,0:T(8,128)(2,1)} %get-tuple-element.80), calls=%async_computation | async-start | bytes 4194304 | tf_op jit(solution)/shard_map/all_to_all | solution.py:356
  63.6 7.1 %collective-permute-start.18 = (bf16[256,1024]{1,0:T(8,128)(2,1)}, bf16[256,1024]{1,0:T(8,128)(2,1)}, u32[]{:S(2)}, u32[]{:S(2)}) collective-permute-start(bf16[256,1024]{1,0:T(8,128)(2,1)} %broadcast_select_fusion.1), channel_id=1, source_target_pairs={{0,1},{1,0},{2,3},{5,4},{6,7},{7,6},{8,9},{9,8},{10,11},{13,12},{1... | collective-permute-start | bytes 1572872 | tf_op jit(solution)/shard_map/ppermute | solution.py:299
  71.6 13.6 %collective-permute-start.11 = (bf16[2,256,512]{2,1,0:T(8,128)(2,1)}, bf16[2,256,512]{2,1,0:T(8,128)(2,1)}, u32[]{:S(2)}, u32[]{:S(2)}) collective-permute-start(bf16[2,256,512]{2,1,0:T(8,128)(2,1)} %get-tuple-element.87), channel_id=1, source_target_pairs={{0,0},{1,1},{2,4},{3,5},{4,6},{5,7},{6,2},{7,3},{8,8},{9,9},{10,12... | collective-permute-start | bytes 1572872 | tf_op jit(solution)/shard_map/ppermute | solution.py:299
  85.2 8.2 %collective-permute-done.9.refs_3_ = bf16[2,256,512]{2,1,0:T(8,128)(2,1)S(1)} collective-permute-done((bf16[2,256,512]{2,1,0:T(8,128)(2,1)}, bf16[2,256,512]{2,1,0:T(8,128)(2,1)S(1)}, u32[]{:S(2)}, u32[]{:S(2)}) %collective-permute-start.9) | collective-permute-done | bytes 524320 | tf_op jit(solution)/shard_map/ppermute | solution.py:299
  97.1 5.0 %collective-permute-start.12 = (f32[8,128]{1,0:T(8,128)S(1)}, f32[8,128]{1,0:T(8,128)S(1)}, u32[]{:S(2)}, u32[]{:S(2)}) collective-permute-start(f32[8,128]{1,0:T(8,128)S(1)} %distances.1), channel_id=1, source_target_pairs={{0,4},{1,5},{2,6},{3,7},{4,0},{5,1},{6,2},{7,3},{8,12},{9,13},{10,... | collective-permute-start | bytes 12296 | tf_op jit(solution)/shard_map/ppermute | solution.py:299
  114.7 7.5 %up.1 = (bf16[512,2048]{1,0:T(8,128)(2,1)S(1)}, bf16[2048,512]{1,0:T(8,128)(2,1)S(1)}, bf16[1024,512]{1,0:T(8,128)(2,1)S(1)}) custom-call(s32[5]{0:T(128)S(1)} %copy-done.20, bf16[2048,1024]{1,0:T(8,128)(2,1)S(1)} %bitcast.60, bf16[2,256,512]{2,1,0:T(8,128)(2,1)S(1)} %copy-done.11, bf16[2,256,512]{2,1,0:T(8,128)(2,1)S(1)} %copy-done.13, ...), custom_call_target="tpu_custom_call" | custom-call | tf_op jit(solution)/shard_map/up/pallas_call | solution.py:485
  124.1 15.0 %grads.1 = (bf16[2,256,256]{2,1,0:T(8,128)(2,1)}, bf16[2,256,256]{2,1,0:T(8,128)(2,1)}, bf16[2,256,256]{2,1,0:T(8,128)(2,1)}, bf16[2,256,256]{2,1,0:T(8,128)(2,1...) custom-call(s32[5]{0:T(128)S(1)} %copy-done.20, ...), custom_call_target="tpu_custom_call" | custom-call | tf_op jit(solution)/shard_map/grads/pallas_call | solution.py:509
  141.2 5.2 %collective-permute-start.23 = (bf16[2,256,256]{2,1,0:T(8,128)(2,1)}, bf16[2,256,256]{2,1,0:T(8,128)(2,1)S(1)}, u32[]{:S(2)}, u32[]{:S(2)}) collective-permute-start(bf16[2,256,256]{2,1,0:T(8,128)(2,1)} %get-tuple-element.116), channel_id=1, source_target_pairs={{0,0},{1,2},{2,4},{3,6},{4,17},{5,19},{6,21},{7,23},{8,9},{9,11},{... | collective-permute-start | bytes 786440 | tf_op jit(solution)/shard_map/ppermute | solution.py:299
  149.9 5.7 %collective-permute-start.26 = (bf16[2,256,256]{2,1,0:T(8,128)(2,1)}, bf16[2,256,256]{2,1,0:T(8,128)(2,1)S(1)}, u32[]{:S(2)}, u32[]{:S(2)}) collective-permute-start(bf16[2,256,256]{2,1,0:T(8,128)(2,1)} %get-tuple-element.119), channel_id=1, source_target_pairs={{0,22},{1,20},{2,27},{3,25},{4,7},{5,5},{6,8},{7,10},{8,31},{9,29}... | collective-permute-start | bytes 786440 | tf_op jit(solution)/shard_map/ppermute | solution.py:299
  158.0 18.3 %collective-permute-done.24.refs_1_ = bf16[2,256,256]{2,1,0:T(8,128)(2,1)S(1)} collective-permute-done((bf16[2,256,256]{2,1,0:T(8,128)(2,1)}, bf16[2,256,256]{2,1,0:T(8,128)(2,1)S(1)}, u32[]{:S(2)}, u32[]{:S(2)}) %collective-permute-start.24) | collective-permute-done | bytes 262176 | tf_op jit(solution)/shard_map/ppermute | solution.py:299
  177.6 8.0 %collective-permute-done.29.refs_6_ = bf16[2,256,256]{2,1,0:T(8,128)(2,1)} collective-permute-done((bf16[2,256,256]{2,1,0:T(8,128)(2,1)}, bf16[2,256,256]{2,1,0:T(8,128)(2,1)}, u32[]{:S(2)}, u32[]{:S(2)}) %collective-permute-start.29) | collective-permute-done | bytes 262176 | tf_op jit(solution)/shard_map/ppermute | solution.py:299
  185.6 6.9 %collective-permute-done.30.refs_7_ = bf16[2,256,256]{2,1,0:T(8,128)(2,1)} collective-permute-done((bf16[2,256,256]{2,1,0:T(8,128)(2,1)}, bf16[2,256,256]{2,1,0:T(8,128)(2,1)}, u32[]{:S(2)}, u32[]{:S(2)}) %collective-permute-start.30) | collective-permute-done | bytes 262176 | tf_op jit(solution)/shard_map/ppermute | solution.py:299
  192.5 5.4 %stein.1 = (bf16[2,256,256]{2,1,0:T(8,128)(2,1)S(1)}, bf16[2,256,256]{2,1,0:T(8,128)(2,1)S(1)}, bf16[2,256,256]{2,1,0:T(8,128)(2,1)S(1)}, bf16[2,256,256]{2,1,0:...) custom-call(s32[5]{0:T(128)S(1)} %copy-done.20, ...), custom_call_target="tpu_custom_call" | custom-call | tf_op jit(solution)/shard_map/stein/pallas_call | solution.py:570
  198.3 6.0 %collective-permute-start.32 = (bf16[2,256,256]{2,1,0:T(8,128)(2,1)S(1)}, bf16[2,256,256]{2,1,0:T(8,128)(2,1)S(1)}, u32[]{:S(2)}, u32[]{:S(2)}) collective-permute-start(bf16[2,256,256]{2,1,0:T(8,128)(2,1)S(1)} %get-tuple-element.134), channel_id=1, source_target_pairs={{0,8},{1,9},{2,10},{3,11},{4,12},{5,13},{6,14},{7,15},{8,16},{9,17... | collective-permute-start | bytes 786440 | tf_op jit(solution)/shard_map/ppermute | solution.py:299
  210.1 4.6 %collective-permute-start.37 = (bf16[2,256,256]{2,1,0:T(8,128)(2,1)S(1)}, bf16[2,256,256]{2,1,0:T(8,128)(2,1)S(1)}, u32[]{:S(2)}, u32[]{:S(2)}) collective-permute-start(bf16[2,256,256]{2,1,0:T(8,128)(2,1)S(1)} %get-tuple-element.139), channel_id=1, source_target_pairs={{0,28},{1,29},{2,30},{3,31},{4,24},{5,25},{6,26},{7,27},{8,4},{9,5... | collective-permute-start | bytes 786440 | tf_op jit(solution)/shard_map/ppermute | solution.py:299
  214.7 4.2 %broadcast_multiply_fusion = (f32[8192,128]{1,0:T(8,128)S(1)}, f32[8192,128]{1,0:T(8,128)S(1)}) fusion(f32[8192,128]{1,0:T(8,128)} %bitcast.64, f32[8192,128]{1,0:T(8,128)} %bitcast.65), kind=kLoop, calls=%fused_computation.2 | loop fusion | flops 2097152 | bytes 16777216 | tf_op jit(solution)/shard_map/mul | solution.py:554
  218.9 5.6 %collective-permute-done.34.refs_4_ = bf16[2,256,256]{2,1,0:T(8,128)(2,1)S(1)} collective-permute-done((bf16[2,256,256]{2,1,0:T(8,128)(2,1)S(1)}, bf16[2,256,256]{2,1,0:T(8,128)(2,1)S(1)}, u32[]{:S(2)}, u32[]{:S(2)}) %collective-permute-start.34) | collective-permute-done | bytes 262176 | tf_op jit(solution)/shard_map/ppermute | solution.py:299
  224.4 7.9 %collective-permute-done.35.refs_5_ = bf16[2,256,256]{2,1,0:T(8,128)(2,1)S(1)} collective-permute-done((bf16[2,256,256]{2,1,0:T(8,128)(2,1)S(1)}, bf16[2,256,256]{2,1,0:T(8,128)(2,1)S(1)}, u32[]{:S(2)}, u32[]{:S(2)}) %collective-permute-start.35) | collective-permute-done | bytes 262176 | tf_op jit(solution)/shard_map/ppermute | solution.py:299
  232.3 9.5 %adam.1 = (f32[8192,128]{1,0:T(8,128)}, f32[8192,128]{1,0:T(8,128)}, f32[8192,128]{1,0:T(8,128)}, f32[8192,128]{1,0:T(8,128)}) custom-call(s32[5]{0:T(128)S(1)} %copy-done.20, f32[8192,128]{1,0:T(8,128)S(1)} %bitcast.59, f32[8192,128]{1,0:T(8,128)S(1)} %get-tuple-element.151.first, f32[8192,128]{1,0:T(8,128)S(1)} %get-tuple-element.150.second, ...), custom_call_target="tpu_custom_call" | custom-call | tf_op jit(solution)/shard_map/adam/pallas_call | solution.py:594
  (147 shorter events, 58.6 us)
Async XLA Ops:
  7.2 99.7 %all-gather.3.cloned.1.call-start = ((), (), s32[]{:S(2)}) async-start(), calls=%async_computation.1 | async-start | bytes 4718592 | tf_op jit(solution)/shard_map/all_gather | solution.py:421
  7.2 43.7 %collective-permute-start.2 = (bf16[512,1024]{1,0:T(8,128)(2,1)}, bf16[512,1024]{1,0:T(8,128)(2,1)}, u32[]{:S(2)}, u32[]{:S(2)}) collective-permute-start(bf16[512,1024]{1,0:T(8,128)(2,1)} %bitcast.62), channel_id=1, source_target_pairs={{0,4},{1,5},{6,2},{7,3},{8,12},{9,13},{14,10},{15,11},{16,20},{17,... | collective-permute-start | bytes 3145736 | tf_op jit(solution)/shard_map/ppermute | solution.py:299
  17.5 22.7 %collective-permute-start.1 = (bf16[256,1024]{1,0:T(8,128)(2,1)S(1)}, bf16[256,1024]{1,0:T(8,128)(2,1)S(1)}, u32[]{:S(2)}, u32[]{:S(2)}) collective-permute-start(bf16[256,1024]{1,0:T(8,128)(2,1)S(1)} %get-tuple-element.146), channel_id=1, source_target_pairs={{1,4},{2,5},{3,1},{4,6},{5,2},{6,3},{9,12},{10,13},{11,9},{12,14},... | collective-permute-start | bytes 1572872 | tf_op jit(solution)/shard_map/ppermute | solution.py:299
  27.8 21.4 %collective-permute-start = (bf16[256,1024]{1,0:T(8,128)(2,1)S(1)}, bf16[256,1024]{1,0:T(8,128)(2,1)S(1)}, u32[]{:S(2)}, u32[]{:S(2)}) collective-permute-start(bf16[256,1024]{1,0:T(8,128)(2,1)S(1)} %get-tuple-element.147), channel_id=1, source_target_pairs={{1,0},{2,1},{3,5},{4,2},{5,6},{6,7},{9,8},{10,9},{11,13},{12,10},{... | collective-permute-start | bytes 1572872 | tf_op jit(solution)/shard_map/ppermute | solution.py:299
  30.1 19.2 %collective-permute-start.6 = (bf16[2,256,512]{2,1,0:T(8,128)(2,1)}, bf16[2,256,512]{2,1,0:T(8,128)(2,1)S(1)}, u32[]{:S(2)}, u32[]{:S(2)}) collective-permute-start(bf16[2,256,512]{2,1,0:T(8,128)(2,1)} %get-tuple-element.81), channel_id=1, source_target_pairs={{0,1},{1,0},{6,3},{7,2},{8,9},{9,8},{14,11},{15,10},{16,17},{17,16... | collective-permute-start | bytes 1572872 | tf_op jit(solution)/shard_map/ppermute | solution.py:299
  51.0 44.1 %all-to-all-start = ((bf16[8,2,256,256]{3,2,1,0:T(8,128)(2,1)}), bf16[8,2,256,256]{3,2,1,0:T(8,128)(2,1)S(1)}, u32[]{:S(2)}, u32[]{:S(2)}) async-start(bf16[8,2,256,256]{3,2,1,0:T(8,128)(2,1)} %get-tuple-element.80), calls=%async_computation | async-start | bytes 4194304 | tf_op jit(solution)/shard_map/all_to_all | solution.py:356
  55.6 37.8 %collective-permute-start.9 = (bf16[2,256,512]{2,1,0:T(8,128)(2,1)}, bf16[2,256,512]{2,1,0:T(8,128)(2,1)S(1)}, u32[]{:S(2)}, u32[]{:S(2)}) collective-permute-start(bf16[2,256,512]{2,1,0:T(8,128)(2,1)} %get-tuple-element.82), channel_id=1, source_target_pairs={{2,5},{3,4},{4,7},{5,6},{10,13},{11,12},{12,15},{13,14},{18,21},{1... | collective-permute-start | bytes 1572872 | tf_op jit(solution)/shard_map/ppermute | solution.py:299
  56.9 37.3 %collective-permute-start.10 = (bf16[2,256,512]{2,1,0:T(8,128)(2,1)}, bf16[2,256,512]{2,1,0:T(8,128)(2,1)S(1)}, u32[]{:S(2)}, u32[]{:S(2)}) collective-permute-start(bf16[2,256,512]{2,1,0:T(8,128)(2,1)} %get-tuple-element.83), channel_id=1, source_target_pairs={{0,4},{1,5},{2,0},{3,1},{4,2},{5,3},{6,6},{7,7},{8,12},{9,13},{10,... | collective-permute-start | bytes 1572872 | tf_op jit(solution)/shard_map/ppermute | solution.py:299
  59.5 44.3 %collective-permute-start.19 = (bf16[256,1024]{1,0:T(8,128)(2,1)}, bf16[256,1024]{1,0:T(8,128)(2,1)}, u32[]{:S(2)}, u32[]{:S(2)}) collective-permute-start(bf16[256,1024]{1,0:T(8,128)(2,1)} %broadcast_select_fusion), channel_id=1, source_target_pairs={{0,5},{1,0},{2,3},{5,4},{6,7},{7,2},{8,13},{9,8},{10,11},{13,12},{... | collective-permute-start | bytes 1572872 | tf_op jit(solution)/shard_map/ppermute | solution.py:299
  63.6 40.3 %collective-permute-start.18 = (bf16[256,1024]{1,0:T(8,128)(2,1)}, bf16[256,1024]{1,0:T(8,128)(2,1)}, u32[]{:S(2)}, u32[]{:S(2)}) collective-permute-start(bf16[256,1024]{1,0:T(8,128)(2,1)} %broadcast_select_fusion.1), channel_id=1, source_target_pairs={{0,1},{1,0},{2,3},{5,4},{6,7},{7,6},{8,9},{9,8},{10,11},{13,12},{1... | collective-permute-start | bytes 1572872 | tf_op jit(solution)/shard_map/ppermute | solution.py:299
  71.6 35.3 %collective-permute-start.11 = (bf16[2,256,512]{2,1,0:T(8,128)(2,1)}, bf16[2,256,512]{2,1,0:T(8,128)(2,1)}, u32[]{:S(2)}, u32[]{:S(2)}) collective-permute-start(bf16[2,256,512]{2,1,0:T(8,128)(2,1)} %get-tuple-element.87), channel_id=1, source_target_pairs={{0,0},{1,1},{2,4},{3,5},{4,6},{5,7},{6,2},{7,3},{8,8},{9,9},{10,12... | collective-permute-start | bytes 1572872 | tf_op jit(solution)/shard_map/ppermute | solution.py:299
  103.2 20.8 %collective-permute-start.16 = (bf16[256,1024]{1,0:T(8,128)(2,1)}, bf16[256,1024]{1,0:T(8,128)(2,1)}, u32[]{:S(2)}, u32[]{:S(2)}) collective-permute-start(bf16[256,1024]{1,0:T(8,128)(2,1)} %copy-done.8), channel_id=1, source_target_pairs={{0,4},{1,5},{2,6},{3,7},{4,0},{5,1},{6,2},{7,3},{8,12},{9,13},{10,... | collective-permute-start | bytes 1572872 | tf_op jit(solution)/shard_map/ppermute | solution.py:299
  103.9 20.2 %collective-permute-start.17 = (bf16[256,1024]{1,0:T(8,128)(2,1)}, bf16[256,1024]{1,0:T(8,128)(2,1)}, u32[]{:S(2)}, u32[]{:S(2)}) collective-permute-start(bf16[256,1024]{1,0:T(8,128)(2,1)} %copy-done.6), channel_id=1, source_target_pairs={{0,4},{1,5},{2,6},{3,7},{4,0},{5,1},{6,2},{7,3},{8,12},{9,13},{10,... | collective-permute-start | bytes 1572872 | tf_op jit(solution)/shard_map/ppermute | solution.py:299
  103.9 20.2 %collective-permute-start.21 = (bf16[256,1024]{1,0:T(8,128)(2,1)}, bf16[256,1024]{1,0:T(8,128)(2,1)}, u32[]{:S(2)}, u32[]{:S(2)}) collective-permute-start(bf16[256,1024]{1,0:T(8,128)(2,1)} %collective-permute-done.19.refs_7_), channel_id=1, source_target_pairs={{0,4},{1,5},{2,6},{3,7},{4,0},{5,1},{6,2},{7,3},{8,12},{9,13},{10,... | collective-permute-start | bytes 1572872 | tf_op jit(solution)/shard_map/ppermute | solution.py:299
  105.4 18.6 %collective-permute-start.20 = (bf16[256,1024]{1,0:T(8,128)(2,1)}, bf16[256,1024]{1,0:T(8,128)(2,1)}, u32[]{:S(2)}, u32[]{:S(2)}) collective-permute-start(bf16[256,1024]{1,0:T(8,128)(2,1)} %collective-permute-done.18.refs_6_), channel_id=1, source_target_pairs={{0,4},{1,5},{2,6},{3,7},{4,0},{5,1},{6,2},{7,3},{8,12},{9,13},{10,... | collective-permute-start | bytes 1572872 | tf_op jit(solution)/shard_map/ppermute | solution.py:299
  122.2 19.1 %collective-permute-start.15 = (f32[8,128]{1,0:T(8,128)S(1)}, f32[8,128]{1,0:T(8,128)S(1)}, u32[]{:S(2)}, u32[]{:S(2)}) collective-permute-start(f32[8,128]{1,0:T(8,128)S(1)} %add.93), channel_id=1, source_target_pairs={{0,1},{1,0},{2,3},{3,2},{4,5},{5,4},{6,7},{7,6},{8,9},{9,8},{10,11... | collective-permute-start | bytes 12296 | tf_op jit(solution)/shard_map/ppermute | solution.py:299
  146.4 29.9 %collective-permute-start.24 = (bf16[2,256,256]{2,1,0:T(8,128)(2,1)}, bf16[2,256,256]{2,1,0:T(8,128)(2,1)S(1)}, u32[]{:S(2)}, u32[]{:S(2)}) collective-permute-start(bf16[2,256,256]{2,1,0:T(8,128)(2,1)} %get-tuple-element.117), channel_id=1, source_target_pairs={{0,31},{1,29},{2,0},{3,2},{4,12},{5,14},{6,17},{7,19},{8,4},{9,6},... | collective-permute-start | bytes 786440 | tf_op jit(solution)/shard_map/ppermute | solution.py:299
  149.4 26.9 %collective-permute-start.25 = (bf16[2,256,256]{2,1,0:T(8,128)(2,1)}, bf16[2,256,256]{2,1,0:T(8,128)(2,1)S(1)}, u32[]{:S(2)}, u32[]{:S(2)}) collective-permute-start(bf16[2,256,256]{2,1,0:T(8,128)(2,1)} %get-tuple-element.118), channel_id=1, source_target_pairs={{0,27},{1,25},{2,31},{3,29},{4,8},{5,10},{6,12},{7,14},{8,0},{9,2}... | collective-permute-start | bytes 786440 | tf_op jit(solution)/shard_map/ppermute | solution.py:299
  149.9 26.5 %collective-permute-start.26 = (bf16[2,256,256]{2,1,0:T(8,128)(2,1)}, bf16[2,256,256]{2,1,0:T(8,128)(2,1)S(1)}, u32[]{:S(2)}, u32[]{:S(2)}) collective-permute-start(bf16[2,256,256]{2,1,0:T(8,128)(2,1)} %get-tuple-element.119), channel_id=1, source_target_pairs={{0,22},{1,20},{2,27},{3,25},{4,7},{5,5},{6,8},{7,10},{8,31},{9,29}... | collective-permute-start | bytes 786440 | tf_op jit(solution)/shard_map/ppermute | solution.py:299
  155.6 20.8 %collective-permute-start.27 = (bf16[2,256,256]{2,1,0:T(8,128)(2,1)}, bf16[2,256,256]{2,1,0:T(8,128)(2,1)S(1)}, u32[]{:S(2)}, u32[]{:S(2)}) collective-permute-start(bf16[2,256,256]{2,1,0:T(8,128)(2,1)} %get-tuple-element.120), channel_id=1, source_target_pairs={{0,18},{1,16},{2,22},{3,20},{4,3},{5,1},{6,7},{7,5},{8,27},{9,25},... | collective-permute-start | bytes 786440 | tf_op jit(solution)/shard_map/ppermute | solution.py:299
  157.9 19.7 %collective-permute-start.28 = (bf16[2,256,256]{2,1,0:T(8,128)(2,1)}, bf16[2,256,256]{2,1,0:T(8,128)(2,1)}, u32[]{:S(2)}, u32[]{:S(2)}) collective-permute-start(bf16[2,256,256]{2,1,0:T(8,128)(2,1)} %copy-done.23), channel_id=1, source_target_pairs={{0,13},{1,15},{2,18},{3,16},{4,30},{5,28},{6,3},{7,1},{8,22},{9,20... | collective-permute-start | bytes 786440 | tf_op jit(solution)/shard_map/ppermute | solution.py:299
  207.4 24.9 %collective-permute-start.35 = (bf16[2,256,256]{2,1,0:T(8,128)(2,1)S(1)}, bf16[2,256,256]{2,1,0:T(8,128)(2,1)S(1)}, u32[]{:S(2)}, u32[]{:S(2)}) collective-permute-start(bf16[2,256,256]{2,1,0:T(8,128)(2,1)S(1)} %get-tuple-element.137), channel_id=1, source_target_pairs={{0,20},{1,21},{2,22},{3,23},{4,16},{5,17},{6,18},{7,19},{8,28},{9,... | collective-permute-start | bytes 786440 | tf_op jit(solution)/shard_map/ppermute | solution.py:299
  209.2 23.1 %collective-permute-start.36 = (bf16[2,256,256]{2,1,0:T(8,128)(2,1)S(1)}, bf16[2,256,256]{2,1,0:T(8,128)(2,1)S(1)}, u32[]{:S(2)}, u32[]{:S(2)}) collective-permute-start(bf16[2,256,256]{2,1,0:T(8,128)(2,1)S(1)} %get-tuple-element.138), channel_id=1, source_target_pairs={{0,24},{1,25},{2,26},{3,27},{4,28},{5,29},{6,30},{7,31},{8,0},{9,1... | collective-permute-start | bytes 786440 | tf_op jit(solution)/shard_map/ppermute | solution.py:299
  210.1 22.2 %collective-permute-start.37 = (bf16[2,256,256]{2,1,0:T(8,128)(2,1)S(1)}, bf16[2,256,256]{2,1,0:T(8,128)(2,1)S(1)}, u32[]{:S(2)}, u32[]{:S(2)}) collective-permute-start(bf16[2,256,256]{2,1,0:T(8,128)(2,1)S(1)} %get-tuple-element.139), channel_id=1, source_target_pairs={{0,28},{1,29},{2,30},{3,31},{4,24},{5,25},{6,26},{7,27},{8,4},{9,5... | collective-permute-start | bytes 786440 | tf_op jit(solution)/shard_map/ppermute | solution.py:299
  (44 other events, 579.8 us)
Sparse Core Ops, SparseCore 0:
  51.0 46.9 all-gather.2

commit v14 on v12

--- a/solution.py
+++ b/solution.py
@@ -148,9 +148,9 @@
     def gradient(j, carry):
         at = pl.multiple_of(j * BLOCK, BLOCK)
         g = jnp.dot(grad[...], n[:, pl.ds(at, BLOCK)], preferred_element_type=F32)
-        score[0, pl.ds(at, BLOCK), :] = (g * up_scale).T.astype(BF)
+        score[0, pl.ds(at, BLOCK), :] = (g * up_scale).astype(BF).T
         g = jnp.dot(act[...], c[:, pl.ds(at, BLOCK)], preferred_element_type=F32)
-        score[1, pl.ds(at, BLOCK), :] = (g * down_scale).T.astype(BF)
+        score[1, pl.ds(at, BLOCK), :] = (g * down_scale).astype(BF).T
         return carry
 
     lax.fori_loop(0, width // BLOCK, gradient, 0)
@@ -422,7 +422,7 @@
         w_pieces = w_pieces + [move(x, route) for x, route in zip(prepared, w_routes[2:])]
         beta = [move(jnp.where(inner, a, x), route) for a, x, route in zip(alpha, halves, second_routes)]
         alpha_x = [move(x, swap_of(everyone)) for x in alpha]
-        whole, w_pieces[2:5] = lax.optimization_barrier((whole, w_pieces[2:5]))
+        whole, w_pieces[2:4] = lax.optimization_barrier((whole, w_pieces[2:4]))
         sums = add_over(pair_sums(whole), range(len(hops) - 3))
         w_pieces, normed, sums = lax.optimization_barrier((w_pieces, normed, sums))
         beta_x = [move(x, swap_of(everyone)) for x in beta]

time: 242 us -> 241 us (level)
  transfers between devices with their start and end apart: 40 -> 40, of which waited for: 14 -> 13; matrix products, arithmetic and copies ran while one was open for 5% -> 5% of each run, Pallas kernels for 14% -> 14%
where the time goes in v14:
time: 241 us; the launch traced here: 240 us
  starting transfers between devices  102 us (42%)
  waiting for transfers between devices  62.8 us (26%)
  Pallas kernels  47.9 us (20%)
  between operations  15.2 us (6%)
  other arithmetic  8.32 us (3%)
  local copies, waits for them, and re-layouts  3.61 us (1%)
    ppermute x38, starting transfers between devices, move(): return lax.ppermute(x, AXES, pairs)  98.1 us
    ppermute x38, waiting for transfers between devices, move(): return lax.ppermute(x, AXES, pairs)  62.8 us
    pallas_call x1, Pallas kernels, local(): pl.pallas_call(functools.partial(grad_kernel, shards, particles, -width *...  13.8 us
    pallas_call x1, Pallas kernels, local(): pl.pallas_call(functools.partial(up_kernel, shards, width ** (-0.5)), gri...  10.3 us
    pallas_call x1, Pallas kernels, local(): pl.pallas_call(functools.partial(adam_kernel, particles), grid=(steps,),...  9.52 us
    pallas_call x1, Pallas kernels, local(): pl.pallas_call(functools.partial(prep_kernel, shards), grid=(steps,), out...  6.9 us
    pallas_call x1, Pallas kernels, local(): pl.pallas_call(functools.partial(stein_kernel, shards, particles), out_sh...  5.37 us
  transfers between devices with their start and end apart: 40, of which 13 were waited for; matrix products, arithmetic and copies ran while one was open for 5% of the time, Pallas kernels for 14%

profile of v14, /device:TPU:23, one launch (start us, length us, event | category | flops | bytes accessed | tf_op | source)
XLA Modules:
  0.0 239.9 jit_solution(8006644044218619082)
XLA Ops:
  20.9 6.9 %prep.1 = (bf16[2,256,512]{2,1,0:T(8,128)(2,1)}, bf16[2,256,512]{2,1,0:T(8,128)(2,1)}, bf16[2,256,512]{2,1,0:T(8,128)(2,1)}, bf16[2,256,512]{2,1,0:T(8,128)(2,1)}, bf16[8,2,256,256]{3,2,1,0:T(8,128)(2,1)}) custom-call(s32[5]{0:T(128)} %stack.36.ids, f32[8192,128]{1,0:T(8,128)} %bitcast.58), custom_call_target="tpu_custom_call" | custom-call | tf_op jit(solution)/shard_map/prep/pallas_call | solution.py:324
  33.8 3.8 %collective-permute-start.7 = (bf16[2,256,512]{2,1,0:T(8,128)(2,1)}, bf16[2,256,512]{2,1,0:T(8,128)(2,1)}, u32[]{:S(2)}, u32[]{:S(2)}) collective-permute-start(bf16[2,256,512]{2,1,0:T(8,128)(2,1)} %get-tuple-element.81), channel_id=1, source_target_pairs={{0,5},{1,4},{6,7},{7,6},{8,13},{9,12},{14,15},{15,14},{16,21},{17,... | collective-permute-start | bytes 1572872 | tf_op jit(solution)/shard_map/ppermute | solution.py:299
  38.6 10.7 %collective-permute-done.refs_2_ = bf16[256,1024]{1,0:T(8,128)(2,1)S(1)} collective-permute-done((bf16[256,1024]{1,0:T(8,128)(2,1)S(1)}, bf16[256,1024]{1,0:T(8,128)(2,1)S(1)}, u32[]{:S(2)}, u32[]{:S(2)}) %collective-permute-start) | collective-permute-done | bytes 524320 | tf_op jit(solution)/shard_map/ppermute | solution.py:299
  50.1 4.0 %all-to-all-start = ((bf16[8,2,256,256]{3,2,1,0:T(8,128)(2,1)}), bf16[8,2,256,256]{3,2,1,0:T(8,128)(2,1)S(1)}, u32[]{:S(2)}, u32[]{:S(2)}) async-start(bf16[8,2,256,256]{3,2,1,0:T(8,128)(2,1)} %get-tuple-element.79), calls=%async_computation | async-start | bytes 4194304 | tf_op jit(solution)/shard_map/all_to_all | solution.py:356
  56.0 5.4 %collective-permute-start.10 = (bf16[2,256,512]{2,1,0:T(8,128)(2,1)}, bf16[2,256,512]{2,1,0:T(8,128)(2,1)}, u32[]{:S(2)}, u32[]{:S(2)}) collective-permute-start(bf16[2,256,512]{2,1,0:T(8,128)(2,1)} %get-tuple-element.84), channel_id=1, source_target_pairs={{0,4},{1,5},{2,0},{3,1},{4,2},{5,3},{6,6},{7,7},{8,12},{9,13},{10,... | collective-permute-start | bytes 1572872 | tf_op jit(solution)/shard_map/ppermute | solution.py:299
  66.5 4.2 %collective-permute-start.18 = (bf16[256,1024]{1,0:T(8,128)(2,1)}, bf16[256,1024]{1,0:T(8,128)(2,1)}, u32[]{:S(2)}, u32[]{:S(2)}) collective-permute-start(bf16[256,1024]{1,0:T(8,128)(2,1)} %broadcast_select_fusion.1), channel_id=1, source_target_pairs={{0,1},{1,0},{2,3},{5,4},{6,7},{7,6},{8,9},{9,8},{10,11},{13,12},{1... | collective-permute-start | bytes 1572872 | tf_op jit(solution)/shard_map/ppermute | solution.py:299
  70.7 13.5 %collective-permute-start.11 = (bf16[2,256,512]{2,1,0:T(8,128)(2,1)}, bf16[2,256,512]{2,1,0:T(8,128)(2,1)}, u32[]{:S(2)}, u32[]{:S(2)}) collective-permute-start(bf16[2,256,512]{2,1,0:T(8,128)(2,1)} %get-tuple-element.85), channel_id=1, source_target_pairs={{0,0},{1,1},{2,4},{3,5},{4,6},{5,7},{6,2},{7,3},{8,8},{9,9},{10,12... | collective-permute-start | bytes 1572872 | tf_op jit(solution)/shard_map/ppermute | solution.py:299
  84.2 8.7 %collective-permute-done.9.refs_3_ = bf16[2,256,512]{2,1,0:T(8,128)(2,1)} collective-permute-done((bf16[2,256,512]{2,1,0:T(8,128)(2,1)}, bf16[2,256,512]{2,1,0:T(8,128)(2,1)}, u32[]{:S(2)}, u32[]{:S(2)}) %collective-permute-start.9) | collective-permute-done | bytes 524320 | tf_op jit(solution)/shard_map/ppermute | solution.py:299
  100.3 10.3 %up.1 = (bf16[512,2048]{1,0:T(8,128)(2,1)}, bf16[2048,512]{1,0:T(8,128)(2,1)}, bf16[1024,512]{1,0:T(8,128)(2,1)}) custom-call(s32[5]{0:T(128)} %stack.36.ids, bf16[2048,1024]{1,0:T(8,128)(2,1)} %bitcast.60, bf16[2,256,512]{2,1,0:T(8,128)(2,1)} %copy-done.8, bf16[2,256,512]{2,1,0:T(8,128)(2,1)} %collective-permute-done.7.refs_1_, ...), custom_call_target="tpu_custom_call" | custom-call | tf_op jit(solution)/shard_map/up/pallas_call | solution.py:485
  110.6 6.1 %collective-permute-start.15 = (f32[8,128]{1,0:T(8,128)S(1)}, f32[8,128]{1,0:T(8,128)S(1)}, u32[]{:S(2)}, u32[]{:S(2)}) collective-permute-start(f32[8,128]{1,0:T(8,128)S(1)} %add.93), channel_id=1, source_target_pairs={{0,1},{1,0},{2,3},{3,2},{4,5},{5,4},{6,7},{7,6},{8,9},{9,8},{10,11... | collective-permute-start | bytes 12296 | tf_op jit(solution)/shard_map/ppermute | solution.py:299
  116.8 13.8 %grads.1 = (bf16[2,256,256]{2,1,0:T(8,128)(2,1)}, bf16[2,256,256]{2,1,0:T(8,128)(2,1)}, bf16[2,256,256]{2,1,0:T(8,128)(2,1)}, bf16[2,256,256]{2,1,0:T(8,128)(2,1...) custom-call(s32[5]{0:T(128)} %stack.36.ids, ...), custom_call_target="tpu_custom_call" | custom-call | tf_op jit(solution)/shard_map/grads/pallas_call | solution.py:508
  135.8 4.0 %collective-permute-start.24 = (bf16[2,256,256]{2,1,0:T(8,128)(2,1)}, bf16[2,256,256]{2,1,0:T(8,128)(2,1)S(1)}, u32[]{:S(2)}, u32[]{:S(2)}) collective-permute-start(bf16[2,256,256]{2,1,0:T(8,128)(2,1)} %get-tuple-element.115), channel_id=1, source_target_pairs={{0,31},{1,29},{2,0},{3,2},{4,12},{5,14},{6,17},{7,19},{8,4},{9,6},... | collective-permute-start | bytes 786440 | tf_op jit(solution)/shard_map/ppermute | solution.py:299
  139.8 6.1 %collective-permute-start.26 = (bf16[2,256,256]{2,1,0:T(8,128)(2,1)}, bf16[2,256,256]{2,1,0:T(8,128)(2,1)S(1)}, u32[]{:S(2)}, u32[]{:S(2)}) collective-permute-start(bf16[2,256,256]{2,1,0:T(8,128)(2,1)} %get-tuple-element.117), channel_id=1, source_target_pairs={{0,22},{1,20},{2,27},{3,25},{4,7},{5,5},{6,8},{7,10},{8,31},{9,29}... | collective-permute-start | bytes 786440 | tf_op jit(solution)/shard_map/ppermute | solution.py:299
  151.4 3.7 %collective-permute-done.25.refs_2_ = bf16[2,256,256]{2,1,0:T(8,128)(2,1)S(1)} collective-permute-done((bf16[2,256,256]{2,1,0:T(8,128)(2,1)}, bf16[2,256,256]{2,1,0:T(8,128)(2,1)S(1)}, u32[]{:S(2)}, u32[]{:S(2)}) %collective-permute-start.25) | collective-permute-done | bytes 262176 | tf_op jit(solution)/shard_map/ppermute | solution.py:299
  155.1 6.8 %collective-permute-start.30 = (bf16[2,256,256]{2,1,0:T(8,128)(2,1)}, bf16[2,256,256]{2,1,0:T(8,128)(2,1)}, u32[]{:S(2)}, u32[]{:S(2)}) collective-permute-start(bf16[2,256,256]{2,1,0:T(8,128)(2,1)} %get-tuple-element.129), channel_id=1, source_target_pairs={{0,4},{1,6},{2,9},{3,11},{4,21},{5,23},{6,26},{7,24},{8,13},{9,15}... | collective-permute-start | bytes 786440 | tf_op jit(solution)/shard_map/ppermute | solution.py:299
  164.2 14.8 %collective-permute-done.29.refs_6_ = bf16[2,256,256]{2,1,0:T(8,128)(2,1)} collective-permute-done((bf16[2,256,256]{2,1,0:T(8,128)(2,1)}, bf16[2,256,256]{2,1,0:T(8,128)(2,1)}, u32[]{:S(2)}, u32[]{:S(2)}) %collective-permute-start.29) | collective-permute-done | bytes 262176 | tf_op jit(solution)/shard_map/ppermute | solution.py:299
  179.1 3.9 %collective-permute-done.30.refs_7_ = bf16[2,256,256]{2,1,0:T(8,128)(2,1)} collective-permute-done((bf16[2,256,256]{2,1,0:T(8,128)(2,1)}, bf16[2,256,256]{2,1,0:T(8,128)(2,1)}, u32[]{:S(2)}, u32[]{:S(2)}) %collective-permute-start.30) | collective-permute-done | bytes 262176 | tf_op jit(solution)/shard_map/ppermute | solution.py:299
  183.0 5.4 %stein.1 = (bf16[2,256,256]{2,1,0:T(8,128)(2,1)S(1)}, bf16[2,256,256]{2,1,0:T(8,128)(2,1)S(1)}, bf16[2,256,256]{2,1,0:T(8,128)(2,1)S(1)}, bf16[2,256,256]{2,1,0:...) custom-call(s32[5]{0:T(128)S(1)} %copy-done.3, ...), custom_call_target="tpu_custom_call" | custom-call | tf_op jit(solution)/shard_map/stein/pallas_call | solution.py:569
  190.2 5.8 %collective-permute-start.32 = (bf16[2,256,256]{2,1,0:T(8,128)(2,1)S(1)}, bf16[2,256,256]{2,1,0:T(8,128)(2,1)S(1)}, u32[]{:S(2)}, u32[]{:S(2)}) collective-permute-start(bf16[2,256,256]{2,1,0:T(8,128)(2,1)S(1)} %get-tuple-element.132), channel_id=1, source_target_pairs={{0,8},{1,9},{2,10},{3,11},{4,12},{5,13},{6,14},{7,15},{8,16},{9,17... | collective-permute-start | bytes 786440 | tf_op jit(solution)/shard_map/ppermute | solution.py:299
  201.6 4.3 %collective-permute-start.37 = (bf16[2,256,256]{2,1,0:T(8,128)(2,1)S(1)}, bf16[2,256,256]{2,1,0:T(8,128)(2,1)S(1)}, u32[]{:S(2)}, u32[]{:S(2)}) collective-permute-start(bf16[2,256,256]{2,1,0:T(8,128)(2,1)S(1)} %get-tuple-element.137), channel_id=1, source_target_pairs={{0,28},{1,29},{2,30},{3,31},{4,24},{5,25},{6,26},{7,27},{8,4},{9,5... | collective-permute-start | bytes 786440 | tf_op jit(solution)/shard_map/ppermute | solution.py:299
  205.9 4.2 %broadcast_multiply_fusion = (f32[8192,128]{1,0:T(8,128)S(1)}, f32[8192,128]{1,0:T(8,128)S(1)}) fusion(f32[8192,128]{1,0:T(8,128)} %bitcast.64, f32[8192,128]{1,0:T(8,128)} %bitcast.65), kind=kLoop, calls=%fused_computation.2 | loop fusion | flops 2097152 | bytes 16777216 | tf_op jit(solution)/shard_map/mul | solution.py:553
  210.1 5.6 %collective-permute-done.34.refs_4_ = bf16[2,256,256]{2,1,0:T(8,128)(2,1)S(1)} collective-permute-done((bf16[2,256,256]{2,1,0:T(8,128)(2,1)S(1)}, bf16[2,256,256]{2,1,0:T(8,128)(2,1)S(1)}, u32[]{:S(2)}, u32[]{:S(2)}) %collective-permute-start.34) | collective-permute-done | bytes 262176 | tf_op jit(solution)/shard_map/ppermute | solution.py:299
  215.7 7.9 %collective-permute-done.35.refs_5_ = bf16[2,256,256]{2,1,0:T(8,128)(2,1)S(1)} collective-permute-done((bf16[2,256,256]{2,1,0:T(8,128)(2,1)S(1)}, bf16[2,256,256]{2,1,0:T(8,128)(2,1)S(1)}, u32[]{:S(2)}, u32[]{:S(2)}) %collective-permute-start.35) | collective-permute-done | bytes 262176 | tf_op jit(solution)/shard_map/ppermute | solution.py:299
  223.6 9.5 %adam.1 = (f32[8192,128]{1,0:T(8,128)}, f32[8192,128]{1,0:T(8,128)}, f32[8192,128]{1,0:T(8,128)}, f32[8192,128]{1,0:T(8,128)}) custom-call(s32[5]{0:T(128)S(1)} %copy-done.3, f32[8192,128]{1,0:T(8,128)S(1)} %bitcast.59, f32[8192,128]{1,0:T(8,128)S(1)} %get-tuple-element.149.first, f32[8192,128]{1,0:T(8,128)S(1)} %get-tuple-element.148.second, ...), custom_call_target="tpu_custom_call" | custom-call | tf_op jit(solution)/shard_map/adam/pallas_call | solution.py:593
  (113 shorter events, 55.7 us)
Async XLA Ops:
  7.2 92.8 %all-gather.3.cloned.1.call-start = ((), (), s32[]{:S(2)}) async-start(), calls=%async_computation.1 | async-start | bytes 4718592 | tf_op jit(solution)/shard_map/all_gather | solution.py:421
  7.2 42.8 %collective-permute-start.2 = (bf16[512,1024]{1,0:T(8,128)(2,1)}, bf16[512,1024]{1,0:T(8,128)(2,1)}, u32[]{:S(2)}, u32[]{:S(2)}) collective-permute-start(bf16[512,1024]{1,0:T(8,128)(2,1)} %bitcast.62), channel_id=1, source_target_pairs={{0,4},{1,5},{6,2},{7,3},{8,12},{9,13},{14,10},{15,11},{16,20},{17,... | collective-permute-start | bytes 3145736 | tf_op jit(solution)/shard_map/ppermute | solution.py:299
  12.8 17.2 %collective-permute-start.4 = (bf16[64,1024]{1,0:T(8,128)(2,1)S(1)}, bf16[64,1024]{1,0:T(8,128)(2,1)S(1)}, u32[]{:S(2)}, u32[]{:S(2)}) collective-permute-start(bf16[64,1024]{1,0:T(8,128)(2,1)S(1)} %fusion.1), channel_id=1, source_target_pairs={{0,2},{1,3},{2,0},{3,1},{4,6},{5,7},{6,4},{7,5},{8,10},{9,11},{10,... | collective-permute-start | bytes 393224 | tf_op jit(solution)/shard_map/ppermute | solution.py:299
  16.2 17.6 %collective-permute-start.3 = (bf16[64,1024]{1,0:T(8,128)(2,1)S(1)}, bf16[64,1024]{1,0:T(8,128)(2,1)S(1)}, u32[]{:S(2)}, u32[]{:S(2)}) collective-permute-start(bf16[64,1024]{1,0:T(8,128)(2,1)S(1)} %fusion.1), channel_id=1, source_target_pairs={{0,1},{1,2},{2,3},{3,0},{4,5},{5,6},{6,7},{7,4},{8,9},{9,10},{10,1... | collective-permute-start | bytes 393224 | tf_op jit(solution)/shard_map/ppermute | solution.py:299
  17.5 21.1 %collective-permute-start.1 = (bf16[256,1024]{1,0:T(8,128)(2,1)S(1)}, bf16[256,1024]{1,0:T(8,128)(2,1)S(1)}, u32[]{:S(2)}, u32[]{:S(2)}) collective-permute-start(bf16[256,1024]{1,0:T(8,128)(2,1)S(1)} %get-tuple-element.144), channel_id=1, source_target_pairs={{1,4},{2,5},{3,1},{4,6},{5,2},{6,3},{9,12},{10,13},{11,9},{12,14},... | collective-permute-start | bytes 1572872 | tf_op jit(solution)/shard_map/ppermute | solution.py:299
  27.9 21.4 %collective-permute-start = (bf16[256,1024]{1,0:T(8,128)(2,1)S(1)}, bf16[256,1024]{1,0:T(8,128)(2,1)S(1)}, u32[]{:S(2)}, u32[]{:S(2)}) collective-permute-start(bf16[256,1024]{1,0:T(8,128)(2,1)S(1)} %get-tuple-element.145), channel_id=1, source_target_pairs={{1,0},{2,1},{3,5},{4,2},{5,6},{6,7},{9,8},{10,9},{11,13},{12,10},{... | collective-permute-start | bytes 1572872 | tf_op jit(solution)/shard_map/ppermute | solution.py:299
  30.0 19.2 %collective-permute-start.6 = (bf16[2,256,512]{2,1,0:T(8,128)(2,1)}, bf16[2,256,512]{2,1,0:T(8,128)(2,1)S(1)}, u32[]{:S(2)}, u32[]{:S(2)}) collective-permute-start(bf16[2,256,512]{2,1,0:T(8,128)(2,1)} %get-tuple-element.80), channel_id=1, source_target_pairs={{0,1},{1,0},{6,3},{7,2},{8,9},{9,8},{14,11},{15,10},{16,17},{17,16... | collective-permute-start | bytes 1572872 | tf_op jit(solution)/shard_map/ppermute | solution.py:299
  50.1 42.8 %all-to-all-start = ((bf16[8,2,256,256]{3,2,1,0:T(8,128)(2,1)}), bf16[8,2,256,256]{3,2,1,0:T(8,128)(2,1)S(1)}, u32[]{:S(2)}, u32[]{:S(2)}) async-start(bf16[8,2,256,256]{3,2,1,0:T(8,128)(2,1)} %get-tuple-element.79), calls=%async_computation | async-start | bytes 4194304 | tf_op jit(solution)/shard_map/all_to_all | solution.py:356
  54.7 38.2 %collective-permute-start.9 = (bf16[2,256,512]{2,1,0:T(8,128)(2,1)}, bf16[2,256,512]{2,1,0:T(8,128)(2,1)}, u32[]{:S(2)}, u32[]{:S(2)}) collective-permute-start(bf16[2,256,512]{2,1,0:T(8,128)(2,1)} %get-tuple-element.81), channel_id=1, source_target_pairs={{2,5},{3,4},{4,7},{5,6},{10,13},{11,12},{12,15},{13,14},{18,21},{1... | collective-permute-start | bytes 1572872 | tf_op jit(solution)/shard_map/ppermute | solution.py:299
  56.0 40.5 %collective-permute-start.10 = (bf16[2,256,512]{2,1,0:T(8,128)(2,1)}, bf16[2,256,512]{2,1,0:T(8,128)(2,1)}, u32[]{:S(2)}, u32[]{:S(2)}) collective-permute-start(bf16[2,256,512]{2,1,0:T(8,128)(2,1)} %get-tuple-element.84), channel_id=1, source_target_pairs={{0,4},{1,5},{2,0},{3,1},{4,2},{5,3},{6,6},{7,7},{8,12},{9,13},{10,... | collective-permute-start | bytes 1572872 | tf_op jit(solution)/shard_map/ppermute | solution.py:299
  62.3 36.2 %collective-permute-start.19 = (bf16[256,1024]{1,0:T(8,128)(2,1)}, bf16[256,1024]{1,0:T(8,128)(2,1)}, u32[]{:S(2)}, u32[]{:S(2)}) collective-permute-start(bf16[256,1024]{1,0:T(8,128)(2,1)} %broadcast_select_fusion), channel_id=1, source_target_pairs={{0,5},{1,0},{2,3},{5,4},{6,7},{7,2},{8,13},{9,8},{10,11},{13,12},{... | collective-permute-start | bytes 1572872 | tf_op jit(solution)/shard_map/ppermute | solution.py:299
  66.5 32.1 %collective-permute-start.18 = (bf16[256,1024]{1,0:T(8,128)(2,1)}, bf16[256,1024]{1,0:T(8,128)(2,1)}, u32[]{:S(2)}, u32[]{:S(2)}) collective-permute-start(bf16[256,1024]{1,0:T(8,128)(2,1)} %broadcast_select_fusion.1), channel_id=1, source_target_pairs={{0,1},{1,0},{2,3},{5,4},{6,7},{7,6},{8,9},{9,8},{10,11},{13,12},{1... | collective-permute-start | bytes 1572872 | tf_op jit(solution)/shard_map/ppermute | solution.py:299
  70.7 29.3 %collective-permute-start.11 = (bf16[2,256,512]{2,1,0:T(8,128)(2,1)}, bf16[2,256,512]{2,1,0:T(8,128)(2,1)}, u32[]{:S(2)}, u32[]{:S(2)}) collective-permute-start(bf16[2,256,512]{2,1,0:T(8,128)(2,1)} %get-tuple-element.85), channel_id=1, source_target_pairs={{0,0},{1,1},{2,4},{3,5},{4,6},{5,7},{6,2},{7,3},{8,8},{9,9},{10,12... | collective-permute-start | bytes 1572872 | tf_op jit(solution)/shard_map/ppermute | solution.py:299
  96.5 20.2 %collective-permute-start.16 = (bf16[256,1024]{1,0:T(8,128)(2,1)S(1)}, bf16[256,1024]{1,0:T(8,128)(2,1)}, u32[]{:S(2)}, u32[]{:S(2)}) collective-permute-start(bf16[256,1024]{1,0:T(8,128)(2,1)S(1)} %collective-permute-done.refs_2_), channel_id=1, source_target_pairs={{0,4},{1,5},{2,6},{3,7},{4,0},{5,1},{6,2},{7,3},{8,12},{9,13},{10,... | collective-permute-start | bytes 1572872 | tf_op jit(solution)/shard_map/ppermute | solution.py:299
  98.5 18.3 %collective-permute-start.17 = (bf16[256,1024]{1,0:T(8,128)(2,1)S(1)}, bf16[256,1024]{1,0:T(8,128)(2,1)}, u32[]{:S(2)}, u32[]{:S(2)}) collective-permute-start(bf16[256,1024]{1,0:T(8,128)(2,1)S(1)} %collective-permute-done.1.refs_3_), channel_id=1, source_target_pairs={{0,4},{1,5},{2,6},{3,7},{4,0},{5,1},{6,2},{7,3},{8,12},{9,13},{10,... | collective-permute-start | bytes 1572872 | tf_op jit(solution)/shard_map/ppermute | solution.py:299
  98.6 18.2 %collective-permute-start.21 = (bf16[256,1024]{1,0:T(8,128)(2,1)}, bf16[256,1024]{1,0:T(8,128)(2,1)}, u32[]{:S(2)}, u32[]{:S(2)}) collective-permute-start(bf16[256,1024]{1,0:T(8,128)(2,1)} %collective-permute-done.19.refs_7_), channel_id=1, source_target_pairs={{0,4},{1,5},{2,6},{3,7},{4,0},{5,1},{6,2},{7,3},{8,12},{9,13},{10,... | collective-permute-start | bytes 1572872 | tf_op jit(solution)/shard_map/ppermute | solution.py:299
  99.0 17.7 %collective-permute-start.20 = (bf16[256,1024]{1,0:T(8,128)(2,1)}, bf16[256,1024]{1,0:T(8,128)(2,1)}, u32[]{:S(2)}, u32[]{:S(2)}) collective-permute-start(bf16[256,1024]{1,0:T(8,128)(2,1)} %collective-permute-done.18.refs_6_), channel_id=1, source_target_pairs={{0,4},{1,5},{2,6},{3,7},{4,0},{5,1},{6,2},{7,3},{8,12},{9,13},{10,... | collective-permute-start | bytes 1572872 | tf_op jit(solution)/shard_map/ppermute | solution.py:299
  110.6 19.9 %collective-permute-start.15 = (f32[8,128]{1,0:T(8,128)S(1)}, f32[8,128]{1,0:T(8,128)S(1)}, u32[]{:S(2)}, u32[]{:S(2)}) collective-permute-start(f32[8,128]{1,0:T(8,128)S(1)} %add.93), channel_id=1, source_target_pairs={{0,1},{1,0},{2,3},{3,2},{4,5},{5,4},{6,7},{7,6},{8,9},{9,8},{10,11... | collective-permute-start | bytes 12296 | tf_op jit(solution)/shard_map/ppermute | solution.py:299
  139.8 22.0 %collective-permute-start.26 = (bf16[2,256,256]{2,1,0:T(8,128)(2,1)}, bf16[2,256,256]{2,1,0:T(8,128)(2,1)S(1)}, u32[]{:S(2)}, u32[]{:S(2)}) collective-permute-start(bf16[2,256,256]{2,1,0:T(8,128)(2,1)} %get-tuple-element.117), channel_id=1, source_target_pairs={{0,22},{1,20},{2,27},{3,25},{4,7},{5,5},{6,8},{7,10},{8,31},{9,29}... | collective-permute-start | bytes 786440 | tf_op jit(solution)/shard_map/ppermute | solution.py:299
  151.4 27.7 %collective-permute-start.29 = (bf16[2,256,256]{2,1,0:T(8,128)(2,1)}, bf16[2,256,256]{2,1,0:T(8,128)(2,1)}, u32[]{:S(2)}, u32[]{:S(2)}) collective-permute-start(bf16[2,256,256]{2,1,0:T(8,128)(2,1)} %get-tuple-element.128), channel_id=1, source_target_pairs={{0,9},{1,11},{2,13},{3,15},{4,26},{5,24},{6,30},{7,28},{8,18},{9,1... | collective-permute-start | bytes 786440 | tf_op jit(solution)/shard_map/ppermute | solution.py:299
  155.1 27.9 %collective-permute-start.30 = (bf16[2,256,256]{2,1,0:T(8,128)(2,1)}, bf16[2,256,256]{2,1,0:T(8,128)(2,1)}, u32[]{:S(2)}, u32[]{:S(2)}) collective-permute-start(bf16[2,256,256]{2,1,0:T(8,128)(2,1)} %get-tuple-element.129), channel_id=1, source_target_pairs={{0,4},{1,6},{2,9},{3,11},{4,21},{5,23},{6,26},{7,24},{8,13},{9,15}... | collective-permute-start | bytes 786440 | tf_op jit(solution)/shard_map/ppermute | solution.py:299
  198.7 24.9 %collective-permute-start.35 = (bf16[2,256,256]{2,1,0:T(8,128)(2,1)S(1)}, bf16[2,256,256]{2,1,0:T(8,128)(2,1)S(1)}, u32[]{:S(2)}, u32[]{:S(2)}) collective-permute-start(bf16[2,256,256]{2,1,0:T(8,128)(2,1)S(1)} %get-tuple-element.135), channel_id=1, source_target_pairs={{0,20},{1,21},{2,22},{3,23},{4,16},{5,17},{6,18},{7,19},{8,28},{9,... | collective-permute-start | bytes 786440 | tf_op jit(solution)/shard_map/ppermute | solution.py:299
  200.5 23.1 %collective-permute-start.36 = (bf16[2,256,256]{2,1,0:T(8,128)(2,1)S(1)}, bf16[2,256,256]{2,1,0:T(8,128)(2,1)S(1)}, u32[]{:S(2)}, u32[]{:S(2)}) collective-permute-start(bf16[2,256,256]{2,1,0:T(8,128)(2,1)S(1)} %get-tuple-element.136), channel_id=1, source_target_pairs={{0,24},{1,25},{2,26},{3,27},{4,28},{5,29},{6,30},{7,31},{8,0},{9,1... | collective-permute-start | bytes 786440 | tf_op jit(solution)/shard_map/ppermute | solution.py:299
  201.6 21.9 %collective-permute-start.37 = (bf16[2,256,256]{2,1,0:T(8,128)(2,1)S(1)}, bf16[2,256,256]{2,1,0:T(8,128)(2,1)S(1)}, u32[]{:S(2)}, u32[]{:S(2)}) collective-permute-start(bf16[2,256,256]{2,1,0:T(8,128)(2,1)S(1)} %get-tuple-element.137), channel_id=1, source_target_pairs={{0,28},{1,29},{2,30},{3,31},{4,24},{5,25},{6,26},{7,27},{8,4},{9,5... | collective-permute-start | bytes 786440 | tf_op jit(solution)/shard_map/ppermute | solution.py:299
  (27 other events, 517.6 us)
Sparse Core Ops, SparseCore 0:
  50.1 47.1 all-gather.2

commit v15 on v14

--- a/solution.py
+++ b/solution.py
@@ -134,26 +134,19 @@
         copy.wait()
     pltpu.make_async_copy(c, c, sems.at[0]).wait()
 
-    def back(i, carry):
-        at = pl.multiple_of(i * chunk, chunk)
-        b = jnp.dot(c[pl.ds(at, chunk), :], down[...], preferred_element_type=F32)
-        b = (b * (slope[pl.ds(at, chunk), :].astype(F32) * back_scale)).astype(BF)
-        grad[:, pl.ds(at, chunk)] = b.T
-        return carry
-
-    lax.fori_loop(0, shards, back, 0)
+    for i in range(shards):
+        rows = slice(i * chunk, (i + 1) * chunk)
+        b = jnp.dot(c[rows, :], down[...], preferred_element_type=F32)
+        b = (b * (slope[rows, :].astype(F32) * back_scale)).astype(BF)
+        grad[:, rows] = b.T
     for copy in later:
         copy.wait()
-
-    def gradient(j, carry):
-        at = pl.multiple_of(j * BLOCK, BLOCK)
-        g = jnp.dot(grad[...], n[:, pl.ds(at, BLOCK)], preferred_element_type=F32)
-        score[0, pl.ds(at, BLOCK), :] = (g * up_scale).astype(BF).T
-        g = jnp.dot(act[...], c[:, pl.ds(at, BLOCK)], preferred_element_type=F32)
-        score[1, pl.ds(at, BLOCK), :] = (g * down_scale).astype(BF).T
-        return carry
-
-    lax.fori_loop(0, width // BLOCK, gradient, 0)
+    for j in range(width // BLOCK):
+        span = slice(j * BLOCK, (j + 1) * BLOCK)
+        g = jnp.dot(grad[...], n[:, span], preferred_element_type=F32)
+        score[0, span, :] = (g * up_scale).astype(BF).T
+        g = jnp.dot(act[...], c[:, span], preferred_element_type=F32)
+        score[1, span, :] = (g * down_scale).astype(BF).T
     rows = width // shards
     ratio = particles // shards
     cols = part // ratio

time: 241 us -> 240 us (level)
  transfers between devices with their start and end apart: 40 -> 40, of which waited for: 13 -> 13; matrix products, arithmetic and copies ran while one was open for 5% -> 5% of each run, Pallas kernels for 14% -> 13%
where the time goes in v15:
time: 240 us; the launch traced here: 238 us
  starting transfers between devices  102 us (42%)
  waiting for transfers between devices  62.8 us (26%)
  Pallas kernels  46.3 us (19%)
  between operations  15.2 us (6%)
  other arithmetic  8.32 us (3%)
  local copies, waits for them, and re-layouts  3.61 us (2%)
    ppermute x38, starting transfers between devices, move(): return lax.ppermute(x, AXES, pairs)  98.1 us
    ppermute x38, waiting for transfers between devices, move(): return lax.ppermute(x, AXES, pairs)  62.8 us
    pallas_call x1, Pallas kernels, local(): pl.pallas_call(functools.partial(grad_kernel, shards, particles, -width *...  12.1 us
    pallas_call x1, Pallas kernels, local(): pl.pallas_call(functools.partial(up_kernel, shards, width ** (-0.5)), gri...  10.3 us
    pallas_call x1, Pallas kernels, local(): pl.pallas_call(functools.partial(adam_kernel, particles), grid=(steps,),...  9.52 us
    pallas_call x1, Pallas kernels, local(): pl.pallas_call(functools.partial(prep_kernel, shards), grid=(steps,), out...  6.9 us
    pallas_call x1, Pallas kernels, local(): pl.pallas_call(functools.partial(stein_kernel, shards, particles), out_sh...  5.37 us
  transfers between devices with their start and end apart: 40, of which 13 were waited for; matrix products, arithmetic and copies ran while one was open for 5% of the time, Pallas kernels for 13%

profile of v15, /device:TPU:23, one launch (start us, length us, event | category | flops | bytes accessed | tf_op | source)
XLA Modules:
  0.0 238.3 jit_solution(1705389607986744628)
XLA Ops:
  20.9 6.9 %prep.1 = (bf16[2,256,512]{2,1,0:T(8,128)(2,1)}, bf16[2,256,512]{2,1,0:T(8,128)(2,1)}, bf16[2,256,512]{2,1,0:T(8,128)(2,1)}, bf16[2,256,512]{2,1,0:T(8,128)(2,1)}, bf16[8,2,256,256]{3,2,1,0:T(8,128)(2,1)}) custom-call(s32[5]{0:T(128)} %stack.36.ids, f32[8192,128]{1,0:T(8,128)} %bitcast.58), custom_call_target="tpu_custom_call" | custom-call | tf_op jit(solution)/shard_map/prep/pallas_call | solution.py:317
  33.8 3.8 %collective-permute-start.7 = (bf16[2,256,512]{2,1,0:T(8,128)(2,1)}, bf16[2,256,512]{2,1,0:T(8,128)(2,1)}, u32[]{:S(2)}, u32[]{:S(2)}) collective-permute-start(bf16[2,256,512]{2,1,0:T(8,128)(2,1)} %get-tuple-element.81), channel_id=1, source_target_pairs={{0,5},{1,4},{6,7},{7,6},{8,13},{9,12},{14,15},{15,14},{16,21},{17,... | collective-permute-start | bytes 1572872 | tf_op jit(solution)/shard_map/ppermute | solution.py:292
  38.6 10.7 %collective-permute-done.refs_2_ = bf16[256,1024]{1,0:T(8,128)(2,1)S(1)} collective-permute-done((bf16[256,1024]{1,0:T(8,128)(2,1)S(1)}, bf16[256,1024]{1,0:T(8,128)(2,1)S(1)}, u32[]{:S(2)}, u32[]{:S(2)}) %collective-permute-start) | collective-permute-done | bytes 524320 | tf_op jit(solution)/shard_map/ppermute | solution.py:292
  50.1 4.0 %all-to-all-start = ((bf16[8,2,256,256]{3,2,1,0:T(8,128)(2,1)}), bf16[8,2,256,256]{3,2,1,0:T(8,128)(2,1)S(1)}, u32[]{:S(2)}, u32[]{:S(2)}) async-start(bf16[8,2,256,256]{3,2,1,0:T(8,128)(2,1)} %get-tuple-element.79), calls=%async_computation | async-start | bytes 4194304 | tf_op jit(solution)/shard_map/all_to_all | solution.py:349
  56.0 5.4 %collective-permute-start.10 = (bf16[2,256,512]{2,1,0:T(8,128)(2,1)}, bf16[2,256,512]{2,1,0:T(8,128)(2,1)}, u32[]{:S(2)}, u32[]{:S(2)}) collective-permute-start(bf16[2,256,512]{2,1,0:T(8,128)(2,1)} %get-tuple-element.84), channel_id=1, source_target_pairs={{0,4},{1,5},{2,0},{3,1},{4,2},{5,3},{6,6},{7,7},{8,12},{9,13},{10,... | collective-permute-start | bytes 1572872 | tf_op jit(solution)/shard_map/ppermute | solution.py:292
  66.5 4.2 %collective-permute-start.18 = (bf16[256,1024]{1,0:T(8,128)(2,1)}, bf16[256,1024]{1,0:T(8,128)(2,1)}, u32[]{:S(2)}, u32[]{:S(2)}) collective-permute-start(bf16[256,1024]{1,0:T(8,128)(2,1)} %broadcast_select_fusion.1), channel_id=1, source_target_pairs={{0,1},{1,0},{2,3},{5,4},{6,7},{7,6},{8,9},{9,8},{10,11},{13,12},{1... | collective-permute-start | bytes 1572872 | tf_op jit(solution)/shard_map/ppermute | solution.py:292
  70.7 13.5 %collective-permute-start.11 = (bf16[2,256,512]{2,1,0:T(8,128)(2,1)}, bf16[2,256,512]{2,1,0:T(8,128)(2,1)}, u32[]{:S(2)}, u32[]{:S(2)}) collective-permute-start(bf16[2,256,512]{2,1,0:T(8,128)(2,1)} %get-tuple-element.85), channel_id=1, source_target_pairs={{0,0},{1,1},{2,4},{3,5},{4,6},{5,7},{6,2},{7,3},{8,8},{9,9},{10,12... | collective-permute-start | bytes 1572872 | tf_op jit(solution)/shard_map/ppermute | solution.py:292
  84.2 8.7 %collective-permute-done.9.refs_3_ = bf16[2,256,512]{2,1,0:T(8,128)(2,1)} collective-permute-done((bf16[2,256,512]{2,1,0:T(8,128)(2,1)}, bf16[2,256,512]{2,1,0:T(8,128)(2,1)}, u32[]{:S(2)}, u32[]{:S(2)}) %collective-permute-start.9) | collective-permute-done | bytes 524320 | tf_op jit(solution)/shard_map/ppermute | solution.py:292
  100.3 10.3 %up.1 = (bf16[512,2048]{1,0:T(8,128)(2,1)}, bf16[2048,512]{1,0:T(8,128)(2,1)}, bf16[1024,512]{1,0:T(8,128)(2,1)}) custom-call(s32[5]{0:T(128)} %stack.36.ids, bf16[2048,1024]{1,0:T(8,128)(2,1)} %bitcast.60, bf16[2,256,512]{2,1,0:T(8,128)(2,1)} %copy-done.8, bf16[2,256,512]{2,1,0:T(8,128)(2,1)} %collective-permute-done.7.refs_1_, ...), custom_call_target="tpu_custom_call" | custom-call | tf_op jit(solution)/shard_map/up/pallas_call | solution.py:478
  110.6 6.1 %collective-permute-start.15 = (f32[8,128]{1,0:T(8,128)S(1)}, f32[8,128]{1,0:T(8,128)S(1)}, u32[]{:S(2)}, u32[]{:S(2)}) collective-permute-start(f32[8,128]{1,0:T(8,128)S(1)} %add.93), channel_id=1, source_target_pairs={{0,1},{1,0},{2,3},{3,2},{4,5},{5,4},{6,7},{7,6},{8,9},{9,8},{10,11... | collective-permute-start | bytes 12296 | tf_op jit(solution)/shard_map/ppermute | solution.py:292
  116.8 12.1 %grads.1 = (bf16[2,256,256]{2,1,0:T(8,128)(2,1)}, bf16[2,256,256]{2,1,0:T(8,128)(2,1)}, bf16[2,256,256]{2,1,0:T(8,128)(2,1)}, bf16[2,256,256]{2,1,0:T(8,128)(2,1...) custom-call(s32[5]{0:T(128)} %stack.36.ids, ...), custom_call_target="tpu_custom_call" | custom-call | tf_op jit(solution)/shard_map/grads/pallas_call | solution.py:501
  134.2 4.0 %collective-permute-start.24 = (bf16[2,256,256]{2,1,0:T(8,128)(2,1)}, bf16[2,256,256]{2,1,0:T(8,128)(2,1)S(1)}, u32[]{:S(2)}, u32[]{:S(2)}) collective-permute-start(bf16[2,256,256]{2,1,0:T(8,128)(2,1)} %get-tuple-element.115), channel_id=1, source_target_pairs={{0,31},{1,29},{2,0},{3,2},{4,12},{5,14},{6,17},{7,19},{8,4},{9,6},... | collective-permute-start | bytes 786440 | tf_op jit(solution)/shard_map/ppermute | solution.py:292
  138.2 6.1 %collective-permute-start.26 = (bf16[2,256,256]{2,1,0:T(8,128)(2,1)}, bf16[2,256,256]{2,1,0:T(8,128)(2,1)S(1)}, u32[]{:S(2)}, u32[]{:S(2)}) collective-permute-start(bf16[2,256,256]{2,1,0:T(8,128)(2,1)} %get-tuple-element.117), channel_id=1, source_target_pairs={{0,22},{1,20},{2,27},{3,25},{4,7},{5,5},{6,8},{7,10},{8,31},{9,29}... | collective-permute-start | bytes 786440 | tf_op jit(solution)/shard_map/ppermute | solution.py:292
  149.7 3.7 %collective-permute-done.25.refs_2_ = bf16[2,256,256]{2,1,0:T(8,128)(2,1)S(1)} collective-permute-done((bf16[2,256,256]{2,1,0:T(8,128)(2,1)}, bf16[2,256,256]{2,1,0:T(8,128)(2,1)S(1)}, u32[]{:S(2)}, u32[]{:S(2)}) %collective-permute-start.25) | collective-permute-done | bytes 262176 | tf_op jit(solution)/shard_map/ppermute | solution.py:292
  153.5 6.8 %collective-permute-start.30 = (bf16[2,256,256]{2,1,0:T(8,128)(2,1)}, bf16[2,256,256]{2,1,0:T(8,128)(2,1)}, u32[]{:S(2)}, u32[]{:S(2)}) collective-permute-start(bf16[2,256,256]{2,1,0:T(8,128)(2,1)} %get-tuple-element.129), channel_id=1, source_target_pairs={{0,4},{1,6},{2,9},{3,11},{4,21},{5,23},{6,26},{7,24},{8,13},{9,15}... | collective-permute-start | bytes 786440 | tf_op jit(solution)/shard_map/ppermute | solution.py:292
  162.6 14.8 %collective-permute-done.29.refs_6_ = bf16[2,256,256]{2,1,0:T(8,128)(2,1)} collective-permute-done((bf16[2,256,256]{2,1,0:T(8,128)(2,1)}, bf16[2,256,256]{2,1,0:T(8,128)(2,1)}, u32[]{:S(2)}, u32[]{:S(2)}) %collective-permute-start.29) | collective-permute-done | bytes 262176 | tf_op jit(solution)/shard_map/ppermute | solution.py:292
  177.5 3.9 %collective-permute-done.30.refs_7_ = bf16[2,256,256]{2,1,0:T(8,128)(2,1)} collective-permute-done((bf16[2,256,256]{2,1,0:T(8,128)(2,1)}, bf16[2,256,256]{2,1,0:T(8,128)(2,1)}, u32[]{:S(2)}, u32[]{:S(2)}) %collective-permute-start.30) | collective-permute-done | bytes 262176 | tf_op jit(solution)/shard_map/ppermute | solution.py:292
  181.4 5.4 %stein.1 = (bf16[2,256,256]{2,1,0:T(8,128)(2,1)S(1)}, bf16[2,256,256]{2,1,0:T(8,128)(2,1)S(1)}, bf16[2,256,256]{2,1,0:T(8,128)(2,1)S(1)}, bf16[2,256,256]{2,1,0:...) custom-call(s32[5]{0:T(128)S(1)} %copy-done.3, ...), custom_call_target="tpu_custom_call" | custom-call | tf_op jit(solution)/shard_map/stein/pallas_call | solution.py:562
  188.5 5.8 %collective-permute-start.32 = (bf16[2,256,256]{2,1,0:T(8,128)(2,1)S(1)}, bf16[2,256,256]{2,1,0:T(8,128)(2,1)S(1)}, u32[]{:S(2)}, u32[]{:S(2)}) collective-permute-start(bf16[2,256,256]{2,1,0:T(8,128)(2,1)S(1)} %get-tuple-element.132), channel_id=1, source_target_pairs={{0,8},{1,9},{2,10},{3,11},{4,12},{5,13},{6,14},{7,15},{8,16},{9,17... | collective-permute-start | bytes 786440 | tf_op jit(solution)/shard_map/ppermute | solution.py:292
  200.0 4.3 %collective-permute-start.37 = (bf16[2,256,256]{2,1,0:T(8,128)(2,1)S(1)}, bf16[2,256,256]{2,1,0:T(8,128)(2,1)S(1)}, u32[]{:S(2)}, u32[]{:S(2)}) collective-permute-start(bf16[2,256,256]{2,1,0:T(8,128)(2,1)S(1)} %get-tuple-element.137), channel_id=1, source_target_pairs={{0,28},{1,29},{2,30},{3,31},{4,24},{5,25},{6,26},{7,27},{8,4},{9,5... | collective-permute-start | bytes 786440 | tf_op jit(solution)/shard_map/ppermute | solution.py:292
  204.3 4.2 %broadcast_multiply_fusion = (f32[8192,128]{1,0:T(8,128)S(1)}, f32[8192,128]{1,0:T(8,128)S(1)}) fusion(f32[8192,128]{1,0:T(8,128)} %bitcast.64, f32[8192,128]{1,0:T(8,128)} %bitcast.65), kind=kLoop, calls=%fused_computation.2 | loop fusion | flops 2097152 | bytes 16777216 | tf_op jit(solution)/shard_map/mul | solution.py:546
  208.5 5.6 %collective-permute-done.34.refs_4_ = bf16[2,256,256]{2,1,0:T(8,128)(2,1)S(1)} collective-permute-done((bf16[2,256,256]{2,1,0:T(8,128)(2,1)S(1)}, bf16[2,256,256]{2,1,0:T(8,128)(2,1)S(1)}, u32[]{:S(2)}, u32[]{:S(2)}) %collective-permute-start.34) | collective-permute-done | bytes 262176 | tf_op jit(solution)/shard_map/ppermute | solution.py:292
  214.0 7.9 %collective-permute-done.35.refs_5_ = bf16[2,256,256]{2,1,0:T(8,128)(2,1)S(1)} collective-permute-done((bf16[2,256,256]{2,1,0:T(8,128)(2,1)S(1)}, bf16[2,256,256]{2,1,0:T(8,128)(2,1)S(1)}, u32[]{:S(2)}, u32[]{:S(2)}) %collective-permute-start.35) | collective-permute-done | bytes 262176 | tf_op jit(solution)/shard_map/ppermute | solution.py:292
  221.9 9.5 %adam.1 = (f32[8192,128]{1,0:T(8,128)}, f32[8192,128]{1,0:T(8,128)}, f32[8192,128]{1,0:T(8,128)}, f32[8192,128]{1,0:T(8,128)}) custom-call(s32[5]{0:T(128)S(1)} %copy-done.3, f32[8192,128]{1,0:T(8,128)S(1)} %bitcast.59, f32[8192,128]{1,0:T(8,128)S(1)} %get-tuple-element.149.first, f32[8192,128]{1,0:T(8,128)S(1)} %get-tuple-element.148.second, ...), custom_call_target="tpu_custom_call" | custom-call | tf_op jit(solution)/shard_map/adam/pallas_call | solution.py:586
  (113 shorter events, 55.7 us)
Async XLA Ops:
  7.2 92.8 %all-gather.3.cloned.1.call-start = ((), (), s32[]{:S(2)}) async-start(), calls=%async_computation.1 | async-start | bytes 4718592 | tf_op jit(solution)/shard_map/all_gather | solution.py:414
  7.2 42.8 %collective-permute-start.2 = (bf16[512,1024]{1,0:T(8,128)(2,1)}, bf16[512,1024]{1,0:T(8,128)(2,1)}, u32[]{:S(2)}, u32[]{:S(2)}) collective-permute-start(bf16[512,1024]{1,0:T(8,128)(2,1)} %bitcast.62), channel_id=1, source_target_pairs={{0,4},{1,5},{6,2},{7,3},{8,12},{9,13},{14,10},{15,11},{16,20},{17,... | collective-permute-start | bytes 3145736 | tf_op jit(solution)/shard_map/ppermute | solution.py:292
  12.8 17.2 %collective-permute-start.4 = (bf16[64,1024]{1,0:T(8,128)(2,1)S(1)}, bf16[64,1024]{1,0:T(8,128)(2,1)S(1)}, u32[]{:S(2)}, u32[]{:S(2)}) collective-permute-start(bf16[64,1024]{1,0:T(8,128)(2,1)S(1)} %fusion.1), channel_id=1, source_target_pairs={{0,2},{1,3},{2,0},{3,1},{4,6},{5,7},{6,4},{7,5},{8,10},{9,11},{10,... | collective-permute-start | bytes 393224 | tf_op jit(solution)/shard_map/ppermute | solution.py:292
  16.2 17.6 %collective-permute-start.3 = (bf16[64,1024]{1,0:T(8,128)(2,1)S(1)}, bf16[64,1024]{1,0:T(8,128)(2,1)S(1)}, u32[]{:S(2)}, u32[]{:S(2)}) collective-permute-start(bf16[64,1024]{1,0:T(8,128)(2,1)S(1)} %fusion.1), channel_id=1, source_target_pairs={{0,1},{1,2},{2,3},{3,0},{4,5},{5,6},{6,7},{7,4},{8,9},{9,10},{10,1... | collective-permute-start | bytes 393224 | tf_op jit(solution)/shard_map/ppermute | solution.py:292
  17.5 21.1 %collective-permute-start.1 = (bf16[256,1024]{1,0:T(8,128)(2,1)S(1)}, bf16[256,1024]{1,0:T(8,128)(2,1)S(1)}, u32[]{:S(2)}, u32[]{:S(2)}) collective-permute-start(bf16[256,1024]{1,0:T(8,128)(2,1)S(1)} %get-tuple-element.144), channel_id=1, source_target_pairs={{1,4},{2,5},{3,1},{4,6},{5,2},{6,3},{9,12},{10,13},{11,9},{12,14},... | collective-permute-start | bytes 1572872 | tf_op jit(solution)/shard_map/ppermute | solution.py:292
  27.9 21.4 %collective-permute-start = (bf16[256,1024]{1,0:T(8,128)(2,1)S(1)}, bf16[256,1024]{1,0:T(8,128)(2,1)S(1)}, u32[]{:S(2)}, u32[]{:S(2)}) collective-permute-start(bf16[256,1024]{1,0:T(8,128)(2,1)S(1)} %get-tuple-element.145), channel_id=1, source_target_pairs={{1,0},{2,1},{3,5},{4,2},{5,6},{6,7},{9,8},{10,9},{11,13},{12,10},{... | collective-permute-start | bytes 1572872 | tf_op jit(solution)/shard_map/ppermute | solution.py:292
  30.0 19.2 %collective-permute-start.6 = (bf16[2,256,512]{2,1,0:T(8,128)(2,1)}, bf16[2,256,512]{2,1,0:T(8,128)(2,1)S(1)}, u32[]{:S(2)}, u32[]{:S(2)}) collective-permute-start(bf16[2,256,512]{2,1,0:T(8,128)(2,1)} %get-tuple-element.80), channel_id=1, source_target_pairs={{0,1},{1,0},{6,3},{7,2},{8,9},{9,8},{14,11},{15,10},{16,17},{17,16... | collective-permute-start | bytes 1572872 | tf_op jit(solution)/shard_map/ppermute | solution.py:292
  50.1 42.8 %all-to-all-start = ((bf16[8,2,256,256]{3,2,1,0:T(8,128)(2,1)}), bf16[8,2,256,256]{3,2,1,0:T(8,128)(2,1)S(1)}, u32[]{:S(2)}, u32[]{:S(2)}) async-start(bf16[8,2,256,256]{3,2,1,0:T(8,128)(2,1)} %get-tuple-element.79), calls=%async_computation | async-start | bytes 4194304 | tf_op jit(solution)/shard_map/all_to_all | solution.py:349
  54.7 38.2 %collective-permute-start.9 = (bf16[2,256,512]{2,1,0:T(8,128)(2,1)}, bf16[2,256,512]{2,1,0:T(8,128)(2,1)}, u32[]{:S(2)}, u32[]{:S(2)}) collective-permute-start(bf16[2,256,512]{2,1,0:T(8,128)(2,1)} %get-tuple-element.81), channel_id=1, source_target_pairs={{2,5},{3,4},{4,7},{5,6},{10,13},{11,12},{12,15},{13,14},{18,21},{1... | collective-permute-start | bytes 1572872 | tf_op jit(solution)/shard_map/ppermute | solution.py:292
  56.0 40.5 %collective-permute-start.10 = (bf16[2,256,512]{2,1,0:T(8,128)(2,1)}, bf16[2,256,512]{2,1,0:T(8,128)(2,1)}, u32[]{:S(2)}, u32[]{:S(2)}) collective-permute-start(bf16[2,256,512]{2,1,0:T(8,128)(2,1)} %get-tuple-element.84), channel_id=1, source_target_pairs={{0,4},{1,5},{2,0},{3,1},{4,2},{5,3},{6,6},{7,7},{8,12},{9,13},{10,... | collective-permute-start | bytes 1572872 | tf_op jit(solution)/shard_map/ppermute | solution.py:292
  62.3 36.2 %collective-permute-start.19 = (bf16[256,1024]{1,0:T(8,128)(2,1)}, bf16[256,1024]{1,0:T(8,128)(2,1)}, u32[]{:S(2)}, u32[]{:S(2)}) collective-permute-start(bf16[256,1024]{1,0:T(8,128)(2,1)} %broadcast_select_fusion), channel_id=1, source_target_pairs={{0,5},{1,0},{2,3},{5,4},{6,7},{7,2},{8,13},{9,8},{10,11},{13,12},{... | collective-permute-start | bytes 1572872 | tf_op jit(solution)/shard_map/ppermute | solution.py:292
  66.5 32.1 %collective-permute-start.18 = (bf16[256,1024]{1,0:T(8,128)(2,1)}, bf16[256,1024]{1,0:T(8,128)(2,1)}, u32[]{:S(2)}, u32[]{:S(2)}) collective-permute-start(bf16[256,1024]{1,0:T(8,128)(2,1)} %broadcast_select_fusion.1), channel_id=1, source_target_pairs={{0,1},{1,0},{2,3},{5,4},{6,7},{7,6},{8,9},{9,8},{10,11},{13,12},{1... | collective-permute-start | bytes 1572872 | tf_op jit(solution)/shard_map/ppermute | solution.py:292
  70.7 29.3 %collective-permute-start.11 = (bf16[2,256,512]{2,1,0:T(8,128)(2,1)}, bf16[2,256,512]{2,1,0:T(8,128)(2,1)}, u32[]{:S(2)}, u32[]{:S(2)}) collective-permute-start(bf16[2,256,512]{2,1,0:T(8,128)(2,1)} %get-tuple-element.85), channel_id=1, source_target_pairs={{0,0},{1,1},{2,4},{3,5},{4,6},{5,7},{6,2},{7,3},{8,8},{9,9},{10,12... | collective-permute-start | bytes 1572872 | tf_op jit(solution)/shard_map/ppermute | solution.py:292
  96.5 20.2 %collective-permute-start.16 = (bf16[256,1024]{1,0:T(8,128)(2,1)S(1)}, bf16[256,1024]{1,0:T(8,128)(2,1)}, u32[]{:S(2)}, u32[]{:S(2)}) collective-permute-start(bf16[256,1024]{1,0:T(8,128)(2,1)S(1)} %collective-permute-done.refs_2_), channel_id=1, source_target_pairs={{0,4},{1,5},{2,6},{3,7},{4,0},{5,1},{6,2},{7,3},{8,12},{9,13},{10,... | collective-permute-start | bytes 1572872 | tf_op jit(solution)/shard_map/ppermute | solution.py:292
  98.5 18.3 %collective-permute-start.17 = (bf16[256,1024]{1,0:T(8,128)(2,1)S(1)}, bf16[256,1024]{1,0:T(8,128)(2,1)}, u32[]{:S(2)}, u32[]{:S(2)}) collective-permute-start(bf16[256,1024]{1,0:T(8,128)(2,1)S(1)} %collective-permute-done.1.refs_3_), channel_id=1, source_target_pairs={{0,4},{1,5},{2,6},{3,7},{4,0},{5,1},{6,2},{7,3},{8,12},{9,13},{10,... | collective-permute-start | bytes 1572872 | tf_op jit(solution)/shard_map/ppermute | solution.py:292
  98.6 18.2 %collective-permute-start.21 = (bf16[256,1024]{1,0:T(8,128)(2,1)}, bf16[256,1024]{1,0:T(8,128)(2,1)}, u32[]{:S(2)}, u32[]{:S(2)}) collective-permute-start(bf16[256,1024]{1,0:T(8,128)(2,1)} %collective-permute-done.19.refs_7_), channel_id=1, source_target_pairs={{0,4},{1,5},{2,6},{3,7},{4,0},{5,1},{6,2},{7,3},{8,12},{9,13},{10,... | collective-permute-start | bytes 1572872 | tf_op jit(solution)/shard_map/ppermute | solution.py:292
  99.0 17.7 %collective-permute-start.20 = (bf16[256,1024]{1,0:T(8,128)(2,1)}, bf16[256,1024]{1,0:T(8,128)(2,1)}, u32[]{:S(2)}, u32[]{:S(2)}) collective-permute-start(bf16[256,1024]{1,0:T(8,128)(2,1)} %collective-permute-done.18.refs_6_), channel_id=1, source_target_pairs={{0,4},{1,5},{2,6},{3,7},{4,0},{5,1},{6,2},{7,3},{8,12},{9,13},{10,... | collective-permute-start | bytes 1572872 | tf_op jit(solution)/shard_map/ppermute | solution.py:292
  110.6 18.3 %collective-permute-start.15 = (f32[8,128]{1,0:T(8,128)S(1)}, f32[8,128]{1,0:T(8,128)S(1)}, u32[]{:S(2)}, u32[]{:S(2)}) collective-permute-start(f32[8,128]{1,0:T(8,128)S(1)} %add.93), channel_id=1, source_target_pairs={{0,1},{1,0},{2,3},{3,2},{4,5},{5,4},{6,7},{7,6},{8,9},{9,8},{10,11... | collective-permute-start | bytes 12296 | tf_op jit(solution)/shard_map/ppermute | solution.py:292
  138.2 22.0 %collective-permute-start.26 = (bf16[2,256,256]{2,1,0:T(8,128)(2,1)}, bf16[2,256,256]{2,1,0:T(8,128)(2,1)S(1)}, u32[]{:S(2)}, u32[]{:S(2)}) collective-permute-start(bf16[2,256,256]{2,1,0:T(8,128)(2,1)} %get-tuple-element.117), channel_id=1, source_target_pairs={{0,22},{1,20},{2,27},{3,25},{4,7},{5,5},{6,8},{7,10},{8,31},{9,29}... | collective-permute-start | bytes 786440 | tf_op jit(solution)/shard_map/ppermute | solution.py:292
  149.7 27.7 %collective-permute-start.29 = (bf16[2,256,256]{2,1,0:T(8,128)(2,1)}, bf16[2,256,256]{2,1,0:T(8,128)(2,1)}, u32[]{:S(2)}, u32[]{:S(2)}) collective-permute-start(bf16[2,256,256]{2,1,0:T(8,128)(2,1)} %get-tuple-element.128), channel_id=1, source_target_pairs={{0,9},{1,11},{2,13},{3,15},{4,26},{5,24},{6,30},{7,28},{8,18},{9,1... | collective-permute-start | bytes 786440 | tf_op jit(solution)/shard_map/ppermute | solution.py:292
  153.5 27.9 %collective-permute-start.30 = (bf16[2,256,256]{2,1,0:T(8,128)(2,1)}, bf16[2,256,256]{2,1,0:T(8,128)(2,1)}, u32[]{:S(2)}, u32[]{:S(2)}) collective-permute-start(bf16[2,256,256]{2,1,0:T(8,128)(2,1)} %get-tuple-element.129), channel_id=1, source_target_pairs={{0,4},{1,6},{2,9},{3,11},{4,21},{5,23},{6,26},{7,24},{8,13},{9,15}... | collective-permute-start | bytes 786440 | tf_op jit(solution)/shard_map/ppermute | solution.py:292
  197.0 24.9 %collective-permute-start.35 = (bf16[2,256,256]{2,1,0:T(8,128)(2,1)S(1)}, bf16[2,256,256]{2,1,0:T(8,128)(2,1)S(1)}, u32[]{:S(2)}, u32[]{:S(2)}) collective-permute-start(bf16[2,256,256]{2,1,0:T(8,128)(2,1)S(1)} %get-tuple-element.135), channel_id=1, source_target_pairs={{0,20},{1,21},{2,22},{3,23},{4,16},{5,17},{6,18},{7,19},{8,28},{9,... | collective-permute-start | bytes 786440 | tf_op jit(solution)/shard_map/ppermute | solution.py:292
  198.8 23.1 %collective-permute-start.36 = (bf16[2,256,256]{2,1,0:T(8,128)(2,1)S(1)}, bf16[2,256,256]{2,1,0:T(8,128)(2,1)S(1)}, u32[]{:S(2)}, u32[]{:S(2)}) collective-permute-start(bf16[2,256,256]{2,1,0:T(8,128)(2,1)S(1)} %get-tuple-element.136), channel_id=1, source_target_pairs={{0,24},{1,25},{2,26},{3,27},{4,28},{5,29},{6,30},{7,31},{8,0},{9,1... | collective-permute-start | bytes 786440 | tf_op jit(solution)/shard_map/ppermute | solution.py:292
  200.0 21.9 %collective-permute-start.37 = (bf16[2,256,256]{2,1,0:T(8,128)(2,1)S(1)}, bf16[2,256,256]{2,1,0:T(8,128)(2,1)S(1)}, u32[]{:S(2)}, u32[]{:S(2)}) collective-permute-start(bf16[2,256,256]{2,1,0:T(8,128)(2,1)S(1)} %get-tuple-element.137), channel_id=1, source_target_pairs={{0,28},{1,29},{2,30},{3,31},{4,24},{5,25},{6,26},{7,27},{8,4},{9,5... | collective-permute-start | bytes 786440 | tf_op jit(solution)/shard_map/ppermute | solution.py:292
  (27 other events, 516.0 us)
Sparse Core Ops, SparseCore 0:
  50.1 47.1 all-gather.2
